TPU v7x, 32 devices: a whole 2x2x4 slice. The times are simulated.
32 devices in a mesh: groups: 2 (over x), grid: 8 (over z, y), layer: 2 (over core).
Axes of the slice: x: 2, y: 2, z: 4, core: 2. Of those that a mesh axis runs over, the one named last changes fastest.
Arguments:
- leaf_rhs: float32 [384, 128, 256], P(('groups', 'grid', 'layer')), parts along dimension 0, may hold values from -6 to 6
- leaf_lower_inverse: float32 [384, 128, 128], P(('groups', 'grid', 'layer')), parts along dimension 0, as said below
- leaf_upper_inverse: float32 [384, 128, 128], P(('groups', 'grid', 'layer')), parts along dimension 0, as said below
- leaf_lower: float32 [384, 4, 128, 128], P(('groups', 'grid', 'layer')), parts along dimension 0, may hold values from -0.109375 to 0.109375
- leaf_upper: float32 [384, 4, 128, 128], P(('groups', 'grid', 'layer')), parts along dimension 0, may hold values from -0.25 to 0.25
- leaf_rows: int32 [384, 4], P(('groups', 'grid', 'layer')), parts along dimension 0, may hold values from 0 to 6, as said below
- separator_right_sides: float32 [32, 128, 256], P(('groups', 'grid', 'layer')), parts along dimension 0, may hold values from -6 to 6
- separator_lower_inverse: float32 [32, 128, 128], P(('groups', 'grid', 'layer')), parts along dimension 0, as said below
- separator_upper_inverse: float32 [32, 128, 128], P(('groups', 'grid', 'layer')), parts along dimension 0, as said below
- separator_lower_blocks: float32 [32, 3, 128, 128], P(('groups', 'grid', 'layer')), parts along dimension 0, may hold values from -0.21875 to 0.21875
- sep_upper: float32 [32, 3, 128, 128], P(('groups', 'grid', 'layer')), parts along dimension 0, may hold values from -0.3125 to 0.3125
- sep_rows: int32 [32, 3], P(('groups', 'grid', 'layer')), parts along dimension 0, may hold values from 0 to 3, as said below
- root_rhs: float32 [8, 128, 256], P('groups'), parts along dimension 0, may hold values from -6 to 6
- root_lower_inverse: float32 [8, 128, 128], P('groups'), parts along dimension 0, as said below
- root_upper_inverse: float32 [8, 128, 128], P('groups'), parts along dimension 0, as said below
- root_lower: float32 [1024, 512], P('groups'), parts along dimension 0, may hold values from -0.25 to 0.25
- root_upper: float32 [1024, 512], P('groups'), parts along dimension 0, may hold values from -0.25 to 0.25
Outputs:
- leaf_sol: float32 [384, 128, 256], P(('groups', 'grid', 'layer')), parts along dimension 0
- separator_solution_rows: float32 [32, 128, 256], P(('groups', 'grid', 'layer')), parts along dimension 0
- root_sol: float32 [8, 128, 256], P('groups'), parts along dimension 0
There are 2 independent parts, one for each index of `groups`. A program takes and returns all parts, laid end to end along the dimension named above; each array names one. Nothing has to cross between parts.
Inputs may be any that keep to these rules, and one draw needn't show every extreme that they name: `leaf_rows`: in each row the first value is 0, 1 or 2 and the other 3 values are different values of 3 to 6; among the 12 leaves of one home each of 0, 1 and 2 stands in the first column. `sep_rows`: each row names 3 different values. `leaf_lower_inverse`: zero above the diagonal; diagonal entries between 0.5 and 1.5. `leaf_upper_inverse`: zero below the diagonal; diagonal entries between 0.5 and 1.5. `separator_lower_inverse`: zero above the diagonal; diagonal entries between 0.5 and 1.5. `separator_upper_inverse`: zero below the diagonal; diagonal entries between 0.5 and 1.5. `root_lower_inverse`: zero above the diagonal; diagonal entries between 0.5 and 1.5. `root_upper_inverse`: zero below the diagonal; diagonal entries between 0.5 and 1.5.
All inputs are finite; a program needn't handle non-finite values.
Results may differ from a plain program's by a relative error of at most 0.0001.
Values sent between devices are 32-bit elements; how exact they have to be, the bound alone decides.
No kernel may reach another device: no remote copies, remote signals or barrier semaphores. Data moves between devices by JAX's collectives and lax.ppermute only.
A program may use at most 128 MiB of HBM per device.

v0:
```python
import jax
import jax.numpy as jnp
from jax import lax
from jax.sharding import PartitionSpec as P

precise_mode = lax.Precision.HIGHEST


def passed_along(array, axis, by):
    peers = lax.axis_size(axis)
    return lax.ppermute(array, axis, [(i, (i + by) % peers) for i in range(peers)])


def times_blocks(blocks, vectors):
    return jnp.einsum("kab,kbr->kar", blocks, vectors, precision=precise_mode)


def per_device(
    leaf_rhs,
    leaf_lower_inverse,
    leaf_upper_inverse,
    leaf_lower,
    leaf_upper,
    leaf_rows,
    separator_right_sides,
    separator_lower_inverse,
    separator_upper_inverse,
    separator_lower_blocks,
    sep_upper,
    sep_rows,
    root_rhs,
    root_lower_inverse,
    root_upper_inverse,
    root_lower,
    root_upper,
):
    grid_count = lax.axis_size("grid")
    half_way = grid_count // 2
    block_width = leaf_rhs.shape[1]
    column_count = leaf_rhs.shape[2]
    root_count = root_rhs.shape[0]
    targets = root_count + 3
    leaf_solved = times_blocks(leaf_lower_inverse, leaf_rhs)
    leaf_terms = jnp.einsum("knab,kbr->knar", leaf_lower, leaf_solved, precision=precise_mode)
    selector = (leaf_rows[:, :, None] == jnp.arange(targets, dtype=jnp.int32)).astype(jnp.float32)
    pending = jnp.einsum("knu,knar->uar", selector, leaf_terms, precision=precise_mode)
    root_pending = pending[3:]
    arrived = passed_along(pending[1], "grid", -1)
    far_arrived = passed_along(pending[2], "grid", -half_way)
    sep_sums = (pending[0] + arrived + far_arrived)[None]
    separator_solved_rows = times_blocks(separator_lower_inverse, separator_right_sides - sep_sums)
    separator_update_terms = jnp.einsum(
        "nab,br->nar", separator_lower_blocks[0], separator_solved_rows[0], precision=precise_mode
    )
    sep_selector = (sep_rows[0][:, None] == jnp.arange(root_count, dtype=jnp.int32)).astype(
        jnp.float32
    )
    root_pending = root_pending + jnp.einsum(
        "nu,nar->uar", sep_selector, separator_update_terms, precision=precise_mode
    )
    root_sums = lax.psum(root_pending, ("grid", "layer"))
    pending_rhs = root_rhs - root_sums

    def forward_step(index, solved):
        row_block = lax.dynamic_slice_in_dim(root_lower, index * block_width, block_width, 0)
        earlier = jnp.dot(
            row_block,
            solved.reshape(root_count * block_width, column_count),
            precision=precise_mode,
        )
        rest = lax.dynamic_slice_in_dim(pending_rhs, index, 1, 0)[0] - earlier
        inverse = lax.dynamic_slice_in_dim(root_lower_inverse, index, 1, 0)[0]
        value = jnp.dot(inverse, rest, precision=precise_mode)
        return lax.dynamic_update_slice_in_dim(solved, value[None], index, 0)

    blank = jnp.zeros((root_count, block_width, column_count), jnp.float32)
    root_solved = lax.fori_loop(0, root_count, forward_step, blank)

    def backward_step(counter, solution):
        index = root_count - 1 - counter
        row_block = lax.dynamic_slice_in_dim(root_upper, index * block_width, block_width, 0)
        later = jnp.dot(
            row_block,
            solution.reshape(root_count * block_width, column_count),
            precision=precise_mode,
        )
        rest = lax.dynamic_slice_in_dim(root_solved, index, 1, 0)[0] - later
        inverse = lax.dynamic_slice_in_dim(root_upper_inverse, index, 1, 0)[0]
        value = jnp.dot(inverse, rest, precision=precise_mode)
        return lax.dynamic_update_slice_in_dim(solution, value[None], index, 0)

    root_sol = lax.fori_loop(0, root_count, backward_step, blank)
    linked = jnp.einsum("nu,uar->nar", sep_selector, root_sol, precision=precise_mode)
    separator_remainder = separator_solved_rows[0] - jnp.einsum(
        "nab,nbr->ar", sep_upper[0], linked, precision=precise_mode
    )
    separator_solution_rows = jnp.dot(
        separator_upper_inverse[0], separator_remainder, precision=precise_mode
    )[None]
    root_picked = jnp.einsum("knu,uar->knar", selector[:, :, 3:], root_sol, precision=precise_mode)
    previous = passed_along(separator_solution_rows[0], "grid", 1)
    far_rows = passed_along(separator_solution_rows[0], "grid", half_way)
    near = jnp.stack([separator_solution_rows[0], previous, far_rows], axis=0)
    picked = root_picked + jnp.einsum(
        "knu,uar->knar", selector[:, :, :3], near, precision=precise_mode
    )
    leaf_rest = leaf_solved - jnp.einsum(
        "knab,knbr->kar", leaf_upper, picked, precision=precise_mode
    )
    leaf_sol = times_blocks(leaf_upper_inverse, leaf_rest)
    return (leaf_sol, separator_solution_rows, root_sol)


def solution(mesh):
    placed = (
        P(("groups", "grid", "layer"), None, None),
        P(("groups", "grid", "layer"), None, None),
        P(("groups", "grid", "layer"), None, None),
        P(("groups", "grid", "layer"), None, None, None),
        P(("groups", "grid", "layer"), None, None, None),
        P(("groups", "grid", "layer"), None),
        P(("groups", "grid", "layer"), None, None),
        P(("groups", "grid", "layer"), None, None),
        P(("groups", "grid", "layer"), None, None),
        P(("groups", "grid", "layer"), None, None, None),
        P(("groups", "grid", "layer"), None, None, None),
        P(("groups", "grid", "layer"), None),
        P("groups", None, None),
        P("groups", None, None),
        P("groups", None, None),
        P("groups", None),
        P("groups", None),
    )
    return jax.shard_map(
        per_device,
        mesh=mesh,
        in_specs=placed,
        out_specs=(
            P(("groups", "grid", "layer"), None, None),
            P(("groups", "grid", "layer"), None, None),
            P("groups", None, None),
        ),
        check_vma=False,
    )
```

profile of v0, /device:TPU:6, one launch (start us, length us, event | category | flops | bytes accessed | tf_op | source)
XLA Modules:
  0.0 231.3 jit_solution(8827971962526876989)
XLA Ops:
  7.2 0.0 copy-start
  7.2 0.0 all-reduce.2.cloned.1.call-start
  7.2 3.3 %fusion.52 = f32[12,128,256]{2,1,0:T(8,128)S(1)} fusion(f32[12,128,128]{2,1,0:T(8,128)} %param.22, f32[12,128,256]{2,1,0:T(8,128)} %param.21), kind=kOutput, calls=%fused_computation.66 | convolution fusion | flops 603979776 | bytes 3932160 | tf_op jit(solution)/shard_map/kab,kbr->kar/dot_general | solution.py:15
  10.5 0.0 copy-start.2
  10.5 1.1 copy-done.2
  11.6 7.3 %fusion.17 = f32[12,256,4,128]{3,1,2,0:T(8,128)} fusion(f32[12,4,128,128]{3,2,1,0:T(8,128)S(1)} %copy-done, f32[12,128,256]{2,1,0:T(8,128)S(1)} %fusion.52), kind=kOutput, calls=%fused_computation.25 | convolution fusion | flops 2415919104 | bytes 11010048 | tf_op jit(solution)/shard_map/knab,kbr->knar/dot_general | solution.py:44
  18.9 9.5 %copy.28 = f32[12,256,4,128]{1,0,2,3:T(8,128)} copy(f32[12,256,4,128]{3,1,2,0:T(8,128)} %fusion.17) | data formatting | bytes 12582912 | tf_op jit(solution)/shard_map/knab,kbr->knar/dot_general | solution.py:44
  28.5 0.0 copy-start.9
  28.5 5.4 %fusion.20 = f32[7,128,256]{2,0,1:T(8,128)S(1)} fusion(f32[12,256,4,128]{1,0,2,3:T(8,128)} %copy.28, s32[12,4]{0,1:T(4,128)S(1)} %copy-done.16), kind=kOutput, calls=%fused_computation.28 | convolution fusion | flops 132120912 | bytes 7209152 | tf_op jit(solution)/shard_map/knu,knar->uar/dot_general | solution.py:46
  33.9 1.0 copy-done.4
  34.9 0.3 fusion.51
  35.1 0.7 collective-permute-start
  35.9 2.7 %collective-permute-start.1 = (f32[128,256]{1,0:T(8,128)S(1)}, f32[128,256]{1,0:T(8,128)S(1)}, u32[]{:S(2)}, u32[]{:S(2)}) collective-permute-start(f32[128,256]{1,0:T(8,128)S(1)} %bitcast.165), channel_id=1, source_target_pairs={{0,8},{2,10},{4,12},{6,14},{8,0},{10,2},{12,4},{14,6},{1,9},{3,11}... | collective-permute-start | bytes 393224 | tf_op jit(solution)/shard_map/ppermute | solution.py:11
  38.6 3.0 %collective-permute-done = f32[128,256]{1,0:T(8,128)S(1)} collective-permute-done((f32[128,256]{1,0:T(8,128)S(1)}, f32[128,256]{1,0:T(8,128)S(1)}, u32[]{:S(2)}, u32[]{:S(2)}) %collective-permute-start) | collective-permute-done | bytes 131104 | tf_op jit(solution)/shard_map/ppermute | solution.py:11
  41.5 3.1 %collective-permute-done.1 = f32[128,256]{1,0:T(8,128)S(1)} collective-permute-done((f32[128,256]{1,0:T(8,128)S(1)}, f32[128,256]{1,0:T(8,128)S(1)}, u32[]{:S(2)}, u32[]{:S(2)}) %collective-permute-start.1) | collective-permute-done | bytes 131104 | tf_op jit(solution)/shard_map/ppermute | solution.py:11
  44.6 0.4 fusion.38
  45.1 0.6 copy-done.6
  45.7 0.5 fusion.31
  46.2 1.0 copy.30
  47.2 2.9 %convolution_add_fusion = f32[4,128,256]{2,0,1:T(4,128)} fusion(f32[7,128,256]{2,0,1:T(8,128)} %copy-done.4, f32[256,3,128]{0,1,2:T(4,128)} %copy.30, s32[3]{0:T(128)S(1)} %bitcast.168), kind=kOutput, calls=%fused_computation.29 | convolution fusion | flops 4849676 | bytes 1441804 | tf_op jit(solution)/shard_map/nu,nar->uar/dot_general | solution.py:58
  50.0 0.0 all-reduce.2.cloned.1.call-update
  50.1 93.3 %all-reduce.2.cloned.1.call-done = f32[4,128,256]{2,0,1:T(4,128)} async-done(((f32[4,128,256]{2,0,1:T(4,128)}), f32[4,128,256]{2,0,1:T(4,128)}) %all-reduce.2.cloned.1.call-update) | async-done | bytes 524304 | tf_op jit(solution)/shard_map/psum | solution.py:61
  143.4 2.4 %copy_subtract_fusion = f32[4,128,256]{2,0,1:T(4,128)} fusion(f32[4,128,256]{2,0,1:T(4,128)} %all-reduce.2.cloned.1.call-done, f32[4,128,256]{2,1,0:T(8,128)} %param.33), kind=kLoop, calls=%fused_computation.37 | loop fusion | flops 131072 | bytes 1572864 | tf_op jit(solution)/shard_map/sub | solution.py:62
  145.8 0.8 broadcast_in_dim.29.clone
  146.6 17.8 %while.28 = (s32[]{:T(128)}, f32[4,128,256]{2,1,0:T(8,128)}, f32[4,128,128]{2,1,0:T(8,128)}, f32[4,128,256]{2,0,1:T(4,128)}, f32[512,512]{1,0:T(8,128)}, /*index=5*/s32[]{:T(128)}, s32[]{:T(128)}, s32[]{:T(128)}, s32[]{:T(128)}) while((s32[]{:T(128)}, f32[4,128,256]{2,1,0:T(8,128)}, f32[4,128,128]{2,1,0:T(8,128)}, f32[4,128,256]{2,0,1:T(4,128)}, ...), condition=%wide.region_2.0_spmd, body=%wide.region_1.0_spmd.sunk | while | flops 251691008 | bytes 1639579 | solution.py:77
  146.6 1.2 constant_dynamic-slice_fusion.2
  147.8 1.5 convolution_subtract_fusion.4
  149.3 1.8 fusion.78
  151.1 1.2 constant_dynamic-slice_fusion.2
  152.2 1.5 convolution_subtract_fusion.4
  153.8 1.8 fusion.78
  155.5 1.2 constant_dynamic-slice_fusion.2
  156.7 1.5 convolution_subtract_fusion.4
  158.2 1.8 fusion.78
  160.0 1.2 constant_dynamic-slice_fusion.2
  161.1 1.5 convolution_subtract_fusion.4
  162.7 1.8 fusion.78
  164.4 0.8 broadcast_in_dim.29
  165.3 13.3 %while.29 = (s32[]{:T(128)}, f32[4,128,256]{2,1,0:T(8,128)}, f32[4,128,128]{2,1,0:T(8,128)}, f32[4,128,256]{2,1,0:T(8,128)}, f32[512,512]{1,0:T(8,128)}, /*index...) while((s32[]{:T(128)}, f32[4,128,256]{2,1,0:T(8,128)}, ...), condition=%wide.region_4.0_spmd, body=%wide.region_3.0_spmd.sunk | while | flops 251691024 | bytes 1377497 | solution.py:92
  165.3 1.6 convolution_subtract_fusion.5
  166.9 1.8 fusion.83
  168.6 1.5 convolution_subtract_fusion.5
  170.2 1.8 fusion.83
  172.0 1.5 convolution_subtract_fusion.5
  173.5 1.8 fusion.83
  175.3 1.5 convolution_subtract_fusion.5
  176.8 1.8 fusion.83
  178.6 2.0 fusion.25
  180.6 0.8 fusion.23
  181.5 0.3 fusion.41
  181.8 3.8 %collective-permute-start.2 = (f32[128,256]{0,1:T(8,128)S(1)}, f32[128,256]{0,1:T(8,128)S(1)}, u32[]{:S(2)}, u32[]{:S(2)}) collective-permute-start(f32[128,256]{0,1:T(8,128)S(1)} %bitcast.160), channel_id=1, source_target_pairs={{0,2},{2,4},{4,6},{6,8},{8,10},{10,12},{12,14},{14,0},{1,3},{3,5},... | collective-permute-start | bytes 393224 | tf_op jit(solution)/shard_map/ppermute | solution.py:11
  185.6 1.4 collective-permute-start.3
  187.0 6.8 %fusion.27 = f32[12,4,128,256]{3,0,2,1:T(8,128)} fusion(f32[4,128,256,1]{2,1,0,3:T(8,128)} %bitcast.158, pred[12,4,7]{0,2,1:T(8,128)(4,1)S(1)} %iota_compare_fusion), kind=kOutput, calls=%fused_computation.35 | convolution fusion | flops 75497472 | bytes 6817792 | tf_op jit(solution)/shard_map/knu,uar->knar/dot_general | solution.py:100
  193.9 0.8 copy.26
  194.6 0.5 collective-permute-done.3
  195.1 0.2 copy-done.12
  195.3 0.5 copy-done.13
  195.7 1.1 maximum_bitcast_fusion
  196.8 1.1 copy.37
  197.9 4.8 %fusion.45 = f32[12,4,128,256]{3,0,2,1:T(8,128)S(1)} fusion(f32[3,128,256,1]{2,0,1,3:T(4,128)} %copy.37, pred[12,4,7]{0,2,1:T(8,128)(4,1)S(1)} %iota_compare_fusion), kind=kOutput, calls=%fused_computation.59 | convolution fusion | flops 56623104 | bytes 6686720 | tf_op jit(solution)/shard_map/knu,uar->knar/dot_general | solution.py:104
  202.7 0.0 copy-start.3
  202.7 14.7 %fusion.14 = f32[12,256,128,1]{1,2,3,0:T(8,128)S(1)} fusion(f32[12,4,128,128]{3,2,1,0:T(8,128)} %param.25, f32[12,4,128,256]{3,0,2,1:T(8,128)S(1)} %fusion.45, f32[12,4,128,256]{3,0,2,1:T(8,128)S(1)} %copy-done.1), kind=kOutput, calls=%fused_computation.21 | convolution fusion | flops 2417491968 | bytes 17301504 | tf_op jit(solution)/shard_map/knab,knbr->kar/dot_general | solution.py:107
  217.4 4.0 %fusion.19 = f32[12,128,256]{1,2,0:T(8,128)} fusion(f32[12,128,128]{2,1,0:T(8,128)S(1)} %copy-done.8, f32[12,128,256]{2,1,0:T(8,128)S(1)} %copy-done.3, f32[12,256,128,1]{1,2,3,0:T(8,128)S(1)} %fusion.14), kind=kOutput, calls=%fused_computation.27 | convolution fusion | flops 604372992 | bytes 5505024 | tf_op jit(solution)/shard_map/kab,kbr->kar/dot_general | solution.py:15
  221.4 3.0 %copy.25 = f32[12,128,256]{2,1,0:T(8,128)} copy(f32[12,128,256]{1,2,0:T(8,128)} %fusion.19) | data formatting | bytes 3145728
  (31 shorter events, 0.1 us)
Async XLA Ops:
  7.2 4.5 %copy-start = (f32[12,4,128,128]{3,2,1,0:T(8,128)S(1)}, f32[12,4,128,128]{3,2,1,0:T(8,128)}, u32[]{:S(2)}) copy-start(f32[12,4,128,128]{3,2,1,0:T(8,128)} %param.24) | copy-start | bytes 9437188
  7.2 136.2 %all-reduce.2.cloned.1.call-start = ((), (), s32[]{:S(2)}) async-start(), calls=%async_computation | async-start | bytes 1048576 | tf_op jit(solution)/shard_map/psum | solution.py:61
  10.5 1.1 copy-start.2
  18.9 9.5 %copy-start.16 = (s32[12,4]{0,1:T(4,128)S(1)}, s32[12,4]{0,1:T(4,128)}, u32[]{:S(2)}) copy-start(s32[12,4]{0,1:T(4,128)} %param.26) | copy-start | bytes 580
  28.5 16.2 %copy-start.11 = (f32[1,128,256]{2,1,0:T(8,128)S(1)}, f32[1,128,256]{2,1,0:T(8,128)}, u32[]{:S(2)}) copy-start(f32[1,128,256]{2,1,0:T(8,128)} %param.27) | copy-start | bytes 393220
  28.5 16.2 %copy-start.15 = (f32[1,128,128]{2,1,0:T(8,128)S(1)}, f32[1,128,128]{2,1,0:T(8,128)}, u32[]{:S(2)}) copy-start(f32[1,128,128]{2,1,0:T(8,128)} %param.28) | copy-start | bytes 196612
  28.5 17.2 %copy-start.9 = (f32[1,3,128,128]{3,2,1,0:T(8,128)S(1)}, f32[1,3,128,128]{3,2,1,0:T(8,128)}, u32[]{:S(2)}) copy-start(f32[1,3,128,128]{3,2,1,0:T(8,128)} %param.30) | copy-start | bytes 589828
  33.8 1.0 copy-start.4
  34.9 12.3 %copy-start.17 = (s32[1,3]{1,0:T(1,128)S(1)}, s32[1,3]{1,0:T(1,128)}, u32[]{:S(2)}) copy-start(s32[1,3]{1,0:T(1,128)} %param.32) | copy-start | bytes 40
  35.1 6.4 %collective-permute-start = (f32[128,256]{1,0:T(8,128)S(1)}, f32[128,256]{1,0:T(8,128)S(1)}, u32[]{:S(2)}, u32[]{:S(2)}) collective-permute-start(f32[128,256]{1,0:T(8,128)S(1)} %bitcast.164), channel_id=1, source_target_pairs={{0,14},{2,0},{4,2},{6,4},{8,6},{10,8},{12,10},{14,12},{1,15},{3,1}... | collective-permute-start | bytes 393224 | tf_op jit(solution)/shard_map/ppermute | solution.py:11
  35.9 8.7 %collective-permute-start.1 = (f32[128,256]{1,0:T(8,128)S(1)}, f32[128,256]{1,0:T(8,128)S(1)}, u32[]{:S(2)}, u32[]{:S(2)}) collective-permute-start(f32[128,256]{1,0:T(8,128)S(1)} %bitcast.165), channel_id=1, source_target_pairs={{0,8},{2,10},{4,12},{6,14},{8,0},{10,2},{12,4},{14,6},{1,9},{3,11}... | collective-permute-start | bytes 393224 | tf_op jit(solution)/shard_map/ppermute | solution.py:11
  45.0 0.7 copy-start.6
  165.3 15.3 %copy-start.7 = (f32[256,128]{1,0:T(8,128)S(1)}, f32[256,128]{1,0:T(8,128)}, u32[]{:S(2)}) copy-start(f32[256,128]{1,0:T(8,128)} %copy-done.6) | copy-start | bytes 393220
  165.3 15.4 %copy-start.10 = (f32[1,3,128,128]{3,2,1,0:T(8,128)S(1)}, f32[1,3,128,128]{3,2,1,0:T(8,128)}, u32[]{:S(2)}) copy-start(f32[1,3,128,128]{3,2,1,0:T(8,128)} %param.31) | copy-start | bytes 589828
  165.3 16.2 %copy-start.14 = (f32[1,128,128]{2,1,0:T(8,128)S(1)}, f32[1,128,128]{2,1,0:T(8,128)}, u32[]{:S(2)}) copy-start(f32[1,128,128]{2,1,0:T(8,128)} %param.29) | copy-start | bytes 196612
  181.8 12.1 %copy-start.5 = (f32[256,128]{1,0:T(8,128)}, f32[256,128]{1,0:T(8,128)S(1)}, u32[]{:S(2)}) copy-start(f32[256,128]{1,0:T(8,128)S(1)} %fusion.41) | copy-start | bytes 393220
  181.8 12.8 %collective-permute-start.2 = (f32[128,256]{0,1:T(8,128)S(1)}, f32[128,256]{0,1:T(8,128)S(1)}, u32[]{:S(2)}, u32[]{:S(2)}) collective-permute-start(f32[128,256]{0,1:T(8,128)S(1)} %bitcast.160), channel_id=1, source_target_pairs={{0,2},{2,4},{4,6},{6,8},{8,10},{10,12},{12,14},{14,0},{1,3},{3,5},... | collective-permute-start | bytes 393224 | tf_op jit(solution)/shard_map/ppermute | solution.py:11
  185.6 9.5 %collective-permute-start.3 = (f32[128,256]{0,1:T(8,128)S(1)}, f32[128,256]{0,1:T(8,128)S(1)}, u32[]{:S(2)}, u32[]{:S(2)}) collective-permute-start(f32[128,256]{0,1:T(8,128)S(1)} %bitcast.161), channel_id=1, source_target_pairs={{0,8},{2,10},{4,12},{6,14},{8,0},{10,2},{12,4},{14,6},{1,9},{3,11}... | collective-permute-start | bytes 393224 | tf_op jit(solution)/shard_map/ppermute | solution.py:11
  194.6 0.7 copy-start.12
  195.1 0.6 copy-start.13
  197.9 4.8 %copy-start.1 = (f32[12,4,128,256]{3,0,2,1:T(8,128)S(1)}, f32[12,4,128,256]{3,0,2,1:T(8,128)}, u32[]{:S(2)}) copy-start(f32[12,4,128,256]{3,0,2,1:T(8,128)} %fusion.27) | copy-start | bytes 18874372
  202.7 14.7 %copy-start.3 = (f32[12,128,256]{2,1,0:T(8,128)S(1)}, f32[12,128,256]{2,1,0:T(8,128)}, u32[]{:S(2)}) copy-start(f32[12,128,256]{2,1,0:T(8,128)} %copy-done.2) | copy-start | bytes 4718596
  202.7 14.7 %copy-start.8 = (f32[12,128,128]{2,1,0:T(8,128)S(1)}, f32[12,128,128]{2,1,0:T(8,128)}, u32[]{:S(2)}) copy-start(f32[12,128,128]{2,1,0:T(8,128)} %param.23) | copy-start | bytes 2359300
Sparse Core Ops, SparseCore 0:
  50.2 93.1 all-reduce.1
where the time goes:
time: 234 us; the launch traced here: 231 us
  waiting for transfers between devices  99.9 us (43%)
  matrix products  79.5 us (34%)
  local copies, waits for them, and re-layouts  25.4 us (11%)
  between operations  14.3 us (6%)
  starting transfers between devices  8.69 us (4%)
  other arithmetic  3.45 us (1%)
    psum x1, waiting for transfers between devices, per_device(): root_sums = lax.psum(root_pending, ('grid', 'layer'))  93.3 us
    dot_general x1, matrix products, per_device(): jnp.einsum('knab,knbr->kar', leaf_upper, picked, precision=precise_mode)  14.7 us
    dot_general x1, local copies, waits for them, and re-layouts, per_device(): jnp.einsum('knab,kbr->knar', leaf_lower, leaf_solved, precision=precise_m...  9.53 us
    ppermute x4, starting transfers between devices, passed_along(): lax.ppermute(array, axis, [(i, (i + by) % peers) for i in range(peers)])  8.65 us
    dot_general x3, matrix products, times_blocks(): return jnp.einsum('kab,kbr->kar', blocks, vectors, precision=precise_mode)  7.68 us
    dot_general x1, matrix products, per_device(): jnp.einsum('knab,kbr->knar', leaf_lower, leaf_solved, precision=precise_m...  7.3 us
    unnamed x40, local copies, waits for them, and re-layouts  7.29 us
    dot_general x4, matrix products, backward_step(): value = jnp.dot(inverse, rest, precision=precise_mode)  7.06 us
  transfers between devices with their start and end apart: 5, of which 4 were waited for; matrix products, arithmetic and copies ran while one was open for 3% of the time, Pallas kernels for 0%

commit v1 on v0

v1 whole, which is shorter than its diff:
```python
import functools

import jax
import jax.numpy as jnp
from jax import lax
from jax.experimental import pallas as pl
from jax.experimental.pallas import tpu as pltpu
from jax.sharding import PartitionSpec as P

VMEM = pltpu.VMEM
SMEM = pltpu.SMEM
F32 = jnp.float32
BF16 = jnp.bfloat16


def parts_of(x):
    high = x.astype(BF16)
    low = (x - high.astype(F32)).astype(BF16)
    return high, low


def as_left(x):
    high, low = parts_of(x)
    count = x.shape[1] // 128
    pieces = [slice(j * 128, j * 128 + 128) for j in range(count)]
    top = jnp.concatenate([high[:, s] for s in pieces for _ in range(2)], axis=1)
    bottom = jnp.concatenate([low[:, s] for s in pieces for _ in range(2)], axis=1)
    return jnp.concatenate([top, bottom], axis=0)


def as_right(x):
    high, low = parts_of(x)
    count = x.shape[0] // 128
    pieces = [slice(j * 128, j * 128 + 128) for j in range(count)]
    return jnp.concatenate([y[s] for s in pieces for y in (high, low)], axis=0)


def left_times(left, right):
    both = jnp.dot(left, right, preferred_element_type=F32)
    rows = left.shape[0] // 2
    return both[:rows] + both[rows:]


def times(a, b):
    return left_times(as_left(a), as_right(b))


def cost(units):
    return pl.CostEstimate(
        flops=units * 2 * 128 * 128 * 256 * 3, bytes_accessed=units * 65536, transcendentals=0
    )


def forward_leaf_kernel(rows, rhs, inverse, first, solved, pending):
    step = pl.program_id(0)

    @pl.when(step == 0)
    def _():
        pending[...] = jnp.zeros_like(pending)

    batch = rhs.shape[0]
    for i in range(batch):
        value = times(inverse[i], rhs[i])
        solved[i] = value
        slot = rows[(step * batch + i) * 4]
        pending[slot] += times(first[i, 0], value)


def root_terms_kernel(rows, one, two, three, solved, after, pending):
    step = pl.program_id(0)

    @pl.when(step == 0)
    def _():
        pending[...] = jnp.zeros_like(pending)

    batch = solved.shape[0]
    for i in range(batch):
        blocks = jnp.concatenate([one[i, 0], two[i, 0], three[i, 0]], axis=0)
        terms = times(blocks, solved[i])
        for n in range(3):
            slot = rows[(step * batch + i) * 4 + n + 1] - 3
            pending[slot] += terms[n * 128 : n * 128 + 128]


def operators_kernel(lower_inverse, upper_inverse, lower, upper, after, forward, backward):
    count = lower_inverse.shape[0]
    w = lower_inverse.shape[1]
    forward[...] = jnp.zeros_like(forward)
    backward[...] = jnp.zeros_like(backward)
    for r in range(count):
        here = slice(r * w, r * w + w)
        forward[here, here] = lower_inverse[r]
        if r > 0:
            done = slice(0, r * w)
            inner = times(lower[here, done], forward[done, done])
            forward[here, done] = -times(lower_inverse[r], inner)
    for r in reversed(range(count)):
        here = slice(r * w, r * w + w)
        backward[here, here] = upper_inverse[r]
        if r < count - 1:
            done = slice((r + 1) * w, count * w)
            inner = times(upper[here, done], backward[done, done])
            backward[here, done] = -times(upper_inverse[r], inner)


def separator_kernel(
    rows, core, rhs, inverse, blocks, own, near, far, root_pending, solved, mine, theirs, sums
):
    value = times(inverse[0], rhs[0] - own[...] - near[...] - far[...])
    solved[...] = value
    terms = times(blocks[0].reshape(3 * 128, 128), value)
    sums[...] = root_pending[...]
    for n in range(3):
        sums[rows[n]] += terms[n * 128 : n * 128 + 128]
    total = sums[...]
    first_half, second_half = total[:, :, :128], total[:, :, 128:]
    is_first = core[0] == 0

    @pl.when(is_first)
    def _():
        mine[...] = first_half
        theirs[...] = second_half

    @pl.when(jnp.logical_not(is_first))
    def _():
        mine[...] = second_half
        theirs[...] = first_half


def root_kernel(place, rhs, forward, backward, own, one, two, three, out, pending):
    count, w = rhs.shape[0], rhs.shape[1]
    position = place[0]
    is_first = place[1] == 0
    for j, piece in enumerate((own, one, two, three)):
        root = position ^ j
        right = rhs[root]
        right = jnp.where(is_first, right[:, :128], right[:, 128:])
        pending[pl.ds(pl.multiple_of(root * w, w), w), :] = right - piece[...]
    solved = times(forward[...], pending[...])
    solution = times(backward[...], solved)
    out[...] = solution.reshape(count, w, 128)


def separator_back_kernel(rows, core, mine, theirs, upper, inverse, solved, root_sol, out):
    is_first = core[0] == 0

    @pl.when(is_first)
    def _():
        root_sol[:, :, :128] = mine[...]
        root_sol[:, :, 128:] = theirs[...]

    @pl.when(jnp.logical_not(is_first))
    def _():
        root_sol[:, :, :128] = theirs[...]
        root_sol[:, :, 128:] = mine[...]

    blocks = jnp.concatenate([upper[0, n] for n in range(3)], axis=1)
    linked = jnp.concatenate([root_sol[rows[n]] for n in range(3)], axis=0)
    out[0] = times(inverse[0], solved[...] - times(blocks, linked))


def leaf_root_part_kernel(rows, one, two, three, solved, root_sol, rest):
    step = pl.program_id(0)
    batch = solved.shape[0]
    for i in range(batch):
        base = (step * batch + i) * 4
        blocks = jnp.concatenate([one[i, 0], two[i, 0], three[i, 0]], axis=1)
        linked = jnp.concatenate([root_sol[rows[base + n] - 3] for n in (1, 2, 3)], axis=0)
        rest[i] = solved[i] - times(blocks, linked)


def leaf_final_kernel(rows, first, inverse, rest, own, near, far, out, seps):
    step = pl.program_id(0)

    @pl.when(step == 0)
    def _():
        seps[0] = own[0]
        seps[1] = near[...]
        seps[2] = far[...]

    batch = rest.shape[0]
    for i in range(batch):
        slot = rows[(step * batch + i) * 4]
        out[i] = times(inverse[i], rest[i] - times(first[i, 0], seps[slot]))


def whole(memory=VMEM):
    return pl.BlockSpec(memory_space=memory)


ANY = pl.BlockSpec(memory_space=pl.ANY)


def leafwise(batch, *tail):
    return pl.BlockSpec((batch,) + tail, lambda k: (k,) + (0,) * len(tail))


def link(batch, n, w):
    return pl.BlockSpec((batch, 1, w, w), lambda k: (k, n, 0, 0))


def kept(*shape):
    return pl.BlockSpec(shape, lambda k: (0,) * len(shape))


def per_device(
    leaf_rhs,
    leaf_lower_inverse,
    leaf_upper_inverse,
    leaf_lower,
    leaf_upper,
    leaf_rows,
    separator_right_sides,
    separator_lower_inverse,
    separator_upper_inverse,
    separator_lower_blocks,
    sep_upper,
    sep_rows,
    root_rhs,
    root_lower_inverse,
    root_upper_inverse,
    root_lower,
    root_upper,
):
    peers = lax.axis_size("grid")
    leaves, w, columns = leaf_rhs.shape
    roots = root_rhs.shape[0]
    half = columns // 2
    batch = 3
    steps = leaves // batch
    position = lax.axis_index("grid") % 4
    core = lax.axis_index("layer")
    core_ref = core.astype(jnp.int32).reshape(1)
    place = jnp.stack([position, core]).astype(jnp.int32)
    leaf_links = leaf_rows.reshape(-1)
    sep_links = sep_rows.reshape(-1)

    def shifted(x, by):
        return lax.ppermute(x, "grid", [(i, (i + by) % peers) for i in range(peers)])

    def crossed(x, bit):
        return lax.ppermute(x, "grid", [(i, i ^ bit) for i in range(peers)])

    def swapped(x):
        return lax.ppermute(x, "layer", [(0, 1), (1, 0)])

    shape = jax.ShapeDtypeStruct

    leaf_solved, pending = pl.pallas_call(
        forward_leaf_kernel,
        grid=(steps,),
        in_specs=[
            whole(SMEM),
            leafwise(batch, w, columns),
            leafwise(batch, w, w),
            link(batch, 0, w),
        ],
        out_specs=[leafwise(batch, w, columns), kept(3, w, columns)],
        out_shape=[shape((leaves, w, columns), F32), shape((3, w, columns), F32)],
        cost_estimate=cost(24),
        name="leaf_forward",
    )(leaf_links, leaf_rhs, leaf_lower_inverse, leaf_lower)

    near_sum = shifted(pending[1], -1)
    far_sum = shifted(pending[2], -(peers // 2))

    root_pending = pl.pallas_call(
        root_terms_kernel,
        grid=(steps,),
        in_specs=[
            whole(SMEM),
            link(batch, 1, w),
            link(batch, 2, w),
            link(batch, 3, w),
            leafwise(batch, w, columns),
            ANY,
        ],
        out_specs=kept(roots, w, columns),
        out_shape=shape((roots, w, columns), F32),
        cost_estimate=cost(36),
        name="root_terms",
    )(leaf_links, leaf_lower, leaf_lower, leaf_lower, leaf_solved, pending)

    forward, backward = pl.pallas_call(
        operators_kernel,
        in_specs=[whole(), whole(), whole(), whole(), ANY],
        out_specs=[whole(), whole()],
        out_shape=[shape((roots * w, roots * w), F32)] * 2,
        cost_estimate=cost(32),
        name="root_operators",
    )(root_lower_inverse, root_upper_inverse, root_lower, root_upper, pending)

    sep_solved, mine, theirs = pl.pallas_call(
        separator_kernel,
        in_specs=[whole(SMEM), whole(SMEM)] + [whole()] * 7,
        out_specs=[whole()] * 3,
        out_shape=[
            shape((w, columns), F32),
            shape((roots, w, half), F32),
            shape((roots, w, half), F32),
        ],
        scratch_shapes=[VMEM((roots, w, columns), F32)],
        cost_estimate=cost(4),
        name="separator_forward",
    )(
        sep_links,
        core_ref,
        separator_right_sides,
        separator_lower_inverse,
        separator_lower_blocks,
        pending[0],
        near_sum,
        far_sum,
        root_pending,
    )

    both = mine + swapped(theirs)
    total = lax.dynamic_index_in_dim(both, position, 0, keepdims=False)
    for j in (1, 2, 3):
        total = total + crossed(
            lax.dynamic_index_in_dim(both, position ^ j, 0, keepdims=False), j
        )
    bit = 4
    while bit < peers:
        total = total + crossed(total, bit)
        bit *= 2
    others = [crossed(total, j) for j in (1, 2, 3)]

    solution_half = pl.pallas_call(
        root_kernel,
        in_specs=[whole(SMEM)] + [whole()] * 7,
        out_specs=whole(),
        out_shape=shape((roots, w, half), F32),
        scratch_shapes=[VMEM((roots * w, half), F32)],
        cost_estimate=cost(16),
        name="root_solve",
    )(place, root_rhs, forward, backward, total, *others)

    other_half = swapped(solution_half)

    root_sol, separator_solution_rows = pl.pallas_call(
        separator_back_kernel,
        in_specs=[whole(SMEM), whole(SMEM)] + [whole()] * 5,
        out_specs=[whole()] * 2,
        out_shape=[shape((roots, w, columns), F32), shape((1, w, columns), F32)],
        cost_estimate=cost(4),
        name="separator_backward",
    )(
        sep_links,
        core_ref,
        solution_half,
        other_half,
        sep_upper,
        separator_upper_inverse,
        sep_solved,
    )

    near_rows = shifted(separator_solution_rows[0], 1)
    far_rows = shifted(separator_solution_rows[0], peers // 2)

    leaf_rest = pl.pallas_call(
        leaf_root_part_kernel,
        grid=(steps,),
        in_specs=[
            whole(SMEM),
            link(batch, 1, w),
            link(batch, 2, w),
            link(batch, 3, w),
            leafwise(batch, w, columns),
            kept(roots, w, columns),
        ],
        out_specs=leafwise(batch, w, columns),
        out_shape=shape((leaves, w, columns), F32),
        cost_estimate=cost(36),
        name="leaf_root_part",
    )(leaf_links, leaf_upper, leaf_upper, leaf_upper, leaf_solved, root_sol)

    leaf_sol = pl.pallas_call(
        leaf_final_kernel,
        grid=(steps,),
        in_specs=[
            whole(SMEM),
            link(batch, 0, w),
            leafwise(batch, w, w),
            leafwise(batch, w, columns),
            kept(1, w, columns),
            kept(w, columns),
            kept(w, columns),
        ],
        out_specs=leafwise(batch, w, columns),
        out_shape=shape((leaves, w, columns), F32),
        scratch_shapes=[VMEM((3, w, columns), F32)],
        cost_estimate=cost(24),
        name="leaf_backward",
    )(
        leaf_links,
        leaf_upper,
        leaf_upper_inverse,
        leaf_rest,
        separator_solution_rows,
        near_rows,
        far_rows,
    )
    return (leaf_sol, separator_solution_rows, root_sol)


def solution(mesh):
    by_device = P(("groups", "grid", "layer"))
    by_group = P("groups")
    return jax.shard_map(
        per_device,
        mesh=mesh,
        in_specs=(by_device,) * 12 + (by_group,) * 5,
        out_specs=(by_device, by_device, by_group),
        check_vma=False,
    )
```

time: 234 us -> 77.4 us (0.33)
  waiting for transfers between devices: 99.9 us -> 15.3 us
  matrix products: 79.5 us -> 0 us
  Pallas kernels: 0 us -> 35.7 us
  local copies, waits for them, and re-layouts: 25.4 us -> 6.39 us
  between operations: 14.3 us -> 0.72 us
  starting transfers between devices: 8.69 us -> 17.1 us
    psum x1 -> x0, waiting for transfers between devices: 93.3 us -> none  [per_device(): root_sums = lax.psum(root_pending, ('grid', 'layer'))]
    dot_general x29 -> x0, matrix products: 79.5 us -> none  [the longest x1 14.7 us: per_device(): jnp.einsum('knab,knbr->kar', leaf_upper, picked, precision=precise_mode)]
    pallas_call x0 -> x8, Pallas kernels: none -> 35.7 us  [the longest x1 5.41 us: per_device(): pl.pallas_call(operators_kernel, in_specs=[whole(), whole(), whole(), who...]
    dot_general x2 -> x0, local copies, waits for them, and re-layouts: 10.5 us -> none  [the longest x1 9.53 us: per_device(): jnp.einsum('knab,kbr->knar', leaf_lower, leaf_solved, precision=precise_m...]
    ppermute x4 -> x13, waiting for transfers between devices: 6.56 us -> 15.3 us  [the longest x7 7.32 us: crossed(): return lax.ppermute(x, 'grid', [(i, i ^ bit) for i in range(peers)])]
    ppermute x4 -> x13, starting transfers between devices: 8.65 us -> 17.1 us  [the longest x7 9.43 us: crossed(): return lax.ppermute(x, 'grid', [(i, i ^ bit) for i in range(peers)])]
    dynamic_slice x4 -> x0, local copies, waits for them, and re-layouts: 4.62 us -> none  [forward_step(): rest = lax.dynamic_slice_in_dim(pending_rhs, index, 1, 0)[0] - earlier]
    unnamed x40 -> x19, local copies, waits for them, and re-layouts: 7.29 us -> 4.05 us
  transfers between devices with their start and end apart: 5 -> 13, of which waited for: 4 -> 9; matrix products, arithmetic and copies ran while one was open for 3% -> 1% of each run, Pallas kernels for 0% -> 20%
where the time goes in v1:
time: 77.4 us; the launch traced here: 76.8 us
  Pallas kernels  35.7 us (46%)
  starting transfers between devices  17.1 us (22%)
  waiting for transfers between devices  15.3 us (20%)
  local copies, waits for them, and re-layouts  6.39 us (8%)
  other arithmetic  1.66 us (2%)
    ppermute x7, starting transfers between devices, crossed(): return lax.ppermute(x, 'grid', [(i, i ^ bit) for i in range(peers)])  9.43 us
    ppermute x4, starting transfers between devices, shifted(): lax.ppermute(x, 'grid', [(i, (i + by) % peers) for i in range(peers)])  7.63 us
    ppermute x7, waiting for transfers between devices, crossed(): return lax.ppermute(x, 'grid', [(i, i ^ bit) for i in range(peers)])  7.32 us
    pallas_call x1, Pallas kernels, per_device(): pl.pallas_call(operators_kernel, in_specs=[whole(), whole(), whole(), who...  5.41 us
    pallas_call x1, Pallas kernels, per_device(): pl.pallas_call(leaf_root_part_kernel, grid=(steps,), in_specs=[whole(SMEM...  5.23 us
    pallas_call x1, Pallas kernels, per_device(): pl.pallas_call(leaf_final_kernel, grid=(steps,), in_specs=[whole(SMEM), l...  5.16 us
    pallas_call x1, Pallas kernels, per_device(): pl.pallas_call(root_terms_kernel, grid=(steps,), in_specs=[whole(SMEM), l...  5.03 us
    pallas_call x1, Pallas kernels, per_device(): pl.pallas_call(forward_leaf_kernel, grid=(steps,), in_specs=[whole(SMEM),...  4.83 us
  transfers between devices with their start and end apart: 13, of which 9 were waited for; matrix products, arithmetic and copies ran while one was open for 1% of the time, Pallas kernels for 20%

profile of v1, /device:TPU:6, one launch (start us, length us, event | category | flops | bytes accessed | tf_op | source)
XLA Modules:
  0.0 76.8 jit_solution(12106904281244295475)
XLA Ops:
  0.6 0.8 %copy.21 = s32[12,4]{1,0:T(8,128)S(1)} copy(s32[12,4]{0,1:T(4,128)} %param.22) | data formatting | bytes 384 | tf_op args[5]
  1.4 0.6 reshape.15.rows
  2.0 4.8 %leaf_forward.1 = (f32[12,128,256]{2,1,0:T(8,128)}, f32[3,128,256]{2,1,0:T(8,128)}) custom-call(s32[48]{0:T(128)} %reshape.15.rows, f32[12,128,256]{2,1,0:T(8,128)} %rhs.3, f32[12,128,128]{2,1,0:T(8,128)} %inverse.4, f32[12,4,128,128]{3,2,1,0:T(8,128)} %three.2), custom_call_target="tpu_custom_call" | custom-call | flops 603979776 | bytes 1572864 | tf_op jit(solution)/shard_map/leaf_forward/pallas_call | solution.py:249
  6.8 1.7 %slice_bitcast_fusion = (f32[128,256]{1,0:T(8,128)S(1)}, f32[128,256]{1,0:T(8,128)S(1)}, f32[128,256]{1,0:T(8,128)}) fusion(f32[3,128,256]{2,1,0:T(8,128)} %get-tuple-element.13.after), kind=kLoop, calls=%fused_computation | loop fusion | bytes 786432 | tf_op jit(solution)/shard_map/squeeze | solution.py:265
  8.5 2.6 %collective-permute-start.1 = (f32[128,256]{1,0:T(8,128)S(1)}, f32[128,256]{1,0:T(8,128)S(1)}, u32[]{:S(2)}, u32[]{:S(2)}) collective-permute-start(f32[128,256]{1,0:T(8,128)S(1)} %get-tuple-element.21), channel_id=1, source_target_pairs={{0,8},{2,10},{4,12},{6,14},{8,0},{10,2},{12,4},{14,6},{1,9},{3,11}... | collective-permute-start | bytes 393224 | tf_op jit(solution)/shard_map/ppermute | solution.py:239
  11.1 0.5 collective-permute-start
  11.6 5.0 %root_terms.1.root_pending = f32[4,128,256]{2,1,0:T(8,128)} custom-call(s32[48]{0:T(128)} %reshape.15.rows, f32[12,4,128,128]{3,2,1,0:T(8,128)} %three.2, f32[12,4,128,128]{3,2,1,0:T(8,128)} %three.2, f32[12,4,128,128]{3,2,1,0:T(8,128)} %three.2, f32[12,128,256]{2,1,0:T(8,128)} %get-tuple-element.12.solved, f32[3,128,256]{2,1,0:T(8,128)} %get-tuple-element.13.after), custom_call_target="tpu_custom_call" | custom-call | flops 905969664 | bytes 2359296 | tf_op jit(solution)/shard_map/root_terms/pallas_call | solution.py:267
  16.7 0.8 %collective-permute-done.1.far = f32[128,256]{1,0:T(8,128)S(1)} collective-permute-done((f32[128,256]{1,0:T(8,128)S(1)}, f32[128,256]{1,0:T(8,128)S(1)}, u32[]{:S(2)}, u32[]{:S(2)}) %collective-permute-start.1) | collective-permute-done | bytes 131104 | tf_op jit(solution)/shard_map/ppermute | solution.py:239
  17.5 0.0 copy-start.4
  17.5 1.2 %collective-permute-done.near = f32[128,256]{1,0:T(8,128)S(1)} collective-permute-done((f32[128,256]{1,0:T(8,128)S(1)}, f32[128,256]{1,0:T(8,128)S(1)}, u32[]{:S(2)}, u32[]{:S(2)}) %collective-permute-start) | collective-permute-done | bytes 131104 | tf_op jit(solution)/shard_map/ppermute | solution.py:239
  18.7 0.0 copy-start.5
  18.7 0.0 copy-done.4
  18.7 0.6 copy-done.5
  19.3 2.8 %separator_forward.1 = (f32[128,256]{1,0:T(8,128)}, f32[4,128,128]{2,1,0:T(8,128)}, f32[4,128,128]{2,1,0:T(8,128)}) custom-call(s32[3]{0:T(128)} %bitcast.24, s32[1]{0:T(128)} %bitcast.1.core, f32[1,128,256]{2,1,0:T(8,128)} %rhs.4, f32[1,128,128]{2,1,0:T(8,128)} %inverse.5, f32[1,3,128,128]{3,2,1,0:T(8,128)} %blocks.1, f32[128,256]{1,0:T(8,128)} %get-tuple-element.23.own, ...), custom_call_target="tpu_custom_call" | custom-call | flops 100663296 | bytes 262144 | tf_op jit(solution)/shard_map/separator_forward/pallas_call | solution.py:293
  22.2 0.0 collective-permute-start.2
  22.2 1.7 %collective-permute-done.2 = f32[4,128,128]{2,1,0:T(8,128)S(1)} collective-permute-done((f32[4,128,128]{2,1,0:T(8,128)}, f32[4,128,128]{2,1,0:T(8,128)S(1)}, u32[]{:S(2)}, u32[]{:S(2)}) %collective-permute-start.2) | collective-permute-done | bytes 262176 | tf_op jit(solution)/shard_map/ppermute | solution.py:245
  23.9 1.0 %add.33 = f32[4,128,128]{2,1,0:T(8,128)S(1)} add(f32[4,128,128]{2,1,0:T(8,128)} %get-tuple-element.16, f32[4,128,128]{2,1,0:T(8,128)S(1)} %collective-permute-done.2) | non-fusion elementwise | flops 65536 | bytes 786432 | tf_op jit(solution)/shard_map/add | solution.py:317
  24.9 0.6 collective-permute-start.3
  25.5 3.1 %collective-permute-start.5 = (f32[128,128]{1,0:T(8,128)S(1)}, f32[128,128]{1,0:T(8,128)S(1)}, u32[]{:S(2)}, u32[]{:S(2)}) collective-permute-start(f32[128,128]{1,0:T(8,128)S(1)} %get-tuple-element.25), channel_id=1, source_target_pairs={{0,6},{2,4},{4,2},{6,0},{8,14},{10,12},{12,10},{14,8},{1,7},{3,5},... | collective-permute-start | bytes 196616 | tf_op jit(solution)/shard_map/ppermute | solution.py:242
  28.6 0.0 collective-permute-start.4
  28.6 0.7 collective-permute-done.3
  29.2 1.6 %collective-permute-done.5 = f32[128,128]{1,0:T(8,128)S(1)} collective-permute-done((f32[128,128]{1,0:T(8,128)S(1)}, f32[128,128]{1,0:T(8,128)S(1)}, u32[]{:S(2)}, u32[]{:S(2)}) %collective-permute-start.5) | collective-permute-done | bytes 65568 | tf_op jit(solution)/shard_map/ppermute | solution.py:242
  30.8 2.0 %collective-permute-done.4 = f32[128,128]{1,0:T(8,128)S(1)} collective-permute-done((f32[128,128]{1,0:T(8,128)S(1)}, f32[128,128]{1,0:T(8,128)S(1)}, u32[]{:S(2)}, u32[]{:S(2)}) %collective-permute-start.4) | collective-permute-done | bytes 65568 | tf_op jit(solution)/shard_map/ppermute | solution.py:242
  32.9 2.2 %collective-permute-start.6 = (f32[128,128]{1,0:T(8,128)S(1)}, f32[128,128]{1,0:T(8,128)S(1)}, u32[]{:S(2)}, u32[]{:S(2)}) collective-permute-start(f32[128,128]{1,0:T(8,128)S(1)} %fusion.1), channel_id=1, source_target_pairs={{0,8},{2,10},{4,12},{6,14},{8,0},{10,2},{12,4},{14,6},{1,9},{3,11}... | collective-permute-start | bytes 196616 | tf_op jit(solution)/shard_map/ppermute | solution.py:242
  35.1 0.7 pad_add_fusion.place
  35.7 3.1 %collective-permute-done.6 = f32[128,128]{1,0:T(8,128)S(1)} collective-permute-done((f32[128,128]{1,0:T(8,128)S(1)}, f32[128,128]{1,0:T(8,128)S(1)}, u32[]{:S(2)}, u32[]{:S(2)}) %collective-permute-start.6) | collective-permute-done | bytes 65568 | tf_op jit(solution)/shard_map/ppermute | solution.py:242
  38.8 0.0 copy-start.1
  38.8 1.1 %collective-permute-start.9 = (f32[128,128]{1,0:T(8,128)S(1)}, f32[128,128]{1,0:T(8,128)S(1)}, u32[]{:S(2)}, u32[]{:S(2)}) collective-permute-start(f32[128,128]{1,0:T(8,128)S(1)} %add.41.own), channel_id=1, source_target_pairs={{0,6},{2,4},{4,2},{6,0},{8,14},{10,12},{12,10},{14,8},{1,7},{3,5},... | collective-permute-start | bytes 196616 | tf_op jit(solution)/shard_map/ppermute | solution.py:242
  39.9 1.7 %collective-permute-start.8 = (f32[128,128]{1,0:T(8,128)S(1)}, f32[128,128]{1,0:T(8,128)S(1)}, u32[]{:S(2)}, u32[]{:S(2)}) collective-permute-start(f32[128,128]{1,0:T(8,128)S(1)} %add.41.own), channel_id=1, source_target_pairs={{0,4},{2,6},{4,0},{6,2},{8,12},{10,14},{12,8},{14,10},{1,5},{3,7},... | collective-permute-start | bytes 196616 | tf_op jit(solution)/shard_map/ppermute | solution.py:242
  41.6 0.7 collective-permute-start.7
  42.4 5.4 %root_operators.1 = (f32[512,512]{1,0:T(8,128)}, f32[512,512]{1,0:T(8,128)}) custom-call(f32[4,128,128]{2,1,0:T(8,128)} %lower_inverse.1, f32[4,128,128]{2,1,0:T(8,128)} %upper_inverse.1, f32[512,512]{1,0:T(8,128)} %lower.1, f32[512,512]{1,0:T(8,128)} %upper.2, f32[3,128,256]{2,1,0:T(8,128)} %get-tuple-element.13.after), custom_call_target="tpu_custom_call" | custom-call | flops 805306368 | bytes 2097152 | tf_op jit(solution)/shard_map/root_operators/pallas_call | solution.py:284
  47.8 0.0 collective-permute-done.9.three
  47.8 0.0 copy-start.6
  47.8 0.0 collective-permute-done.8.two
  47.8 0.0 copy-start.7
  47.8 0.0 collective-permute-done.7.one
  47.8 0.0 copy-start.8
  47.8 0.0 copy-done.1
  47.8 0.6 copy-done.6
  48.4 0.0 copy-done.7
  48.4 0.0 copy-done.8
  48.5 4.8 %root_solve.1.mine = f32[4,128,128]{2,1,0:T(8,128)} custom-call(s32[2]{0:T(128)} %pad_add_fusion.place, f32[4,128,256]{2,1,0:T(8,128)} %rhs.5, f32[512,512]{1,0:T(8,128)} %get-tuple-element.14.forward, f32[512,512]{1,0:T(8,128)} %get-tuple-element.15.backward, f32[128,128]{1,0:T(8,128)} %copy-done.1, f32[128,128]{1,0:T(8,128)} %copy-done.8, ...), custom_call_target="tpu_custom_call" | custom-call | flops 402653184 | bytes 1048576 | tf_op jit(solution)/shard_map/root_solve/pallas_call | solution.py:329
  53.3 0.0 collective-permute-start.10
  53.3 1.7 %collective-permute-done.10.theirs = f32[4,128,128]{2,1,0:T(8,128)S(1)} collective-permute-done((f32[4,128,128]{2,1,0:T(8,128)}, f32[4,128,128]{2,1,0:T(8,128)S(1)}, u32[]{:S(2)}, u32[]{:S(2)}) %collective-permute-start.10) | collective-permute-done | bytes 262176 | tf_op jit(solution)/shard_map/ppermute | solution.py:245
  55.0 0.0 copy-start
  55.0 0.7 copy-done
  55.7 2.4 %separator_backward.1 = (f32[4,128,256]{2,1,0:T(8,128)}, f32[1,128,256]{2,1,0:T(8,128)}) custom-call(s32[3]{0:T(128)} %bitcast.25, s32[1]{0:T(128)} %bitcast.1.core, f32[4,128,128]{2,1,0:T(8,128)} %root_solve.1.mine, f32[4,128,128]{2,1,0:T(8,128)} %copy-done, f32[1,3,128,128]{3,2,1,0:T(8,128)} %upper.3, f32[1,128,128]{2,1,0:T(8,128)} %inverse.6, ...), custom_call_target="tpu_custom_call" | custom-call | flops 100663296 | bytes 262144 | tf_op jit(solution)/shard_map/separator_backward/pallas_call | solution.py:341
  58.1 1.7 %collective-permute-start.12 = (f32[128,256]{1,0:T(8,128)}, f32[128,256]{1,0:T(8,128)S(1)}, u32[]{:S(2)}, u32[]{:S(2)}) collective-permute-start(f32[128,256]{1,0:T(8,128)} %bitcast.22), channel_id=1, source_target_pairs={{0,8},{2,10},{4,12},{6,14},{8,0},{10,2},{12,4},{14,6},{1,9},{3,11}... | collective-permute-start | bytes 393224 | tf_op jit(solution)/shard_map/ppermute | solution.py:239
  59.8 2.9 %collective-permute-start.11 = (f32[128,256]{1,0:T(8,128)}, f32[128,256]{1,0:T(8,128)S(1)}, u32[]{:S(2)}, u32[]{:S(2)}) collective-permute-start(f32[128,256]{1,0:T(8,128)} %bitcast.23), channel_id=1, source_target_pairs={{0,2},{2,4},{4,6},{6,8},{8,10},{10,12},{12,14},{14,0},{1,3},{3,5},... | collective-permute-start | bytes 393224 | tf_op jit(solution)/shard_map/ppermute | solution.py:239
  62.6 5.2 %leaf_root_part.1.rest = f32[12,128,256]{2,1,0:T(8,128)} custom-call(s32[48]{0:T(128)} %reshape.15.rows, f32[12,4,128,128]{3,2,1,0:T(8,128)} %first.3, f32[12,4,128,128]{3,2,1,0:T(8,128)} %first.3, f32[12,4,128,128]{3,2,1,0:T(8,128)} %first.3, f32[12,128,256]{2,1,0:T(8,128)} %get-tuple-element.12.solved, f32[4,128,256]{2,1,0:T(8,128)} %get-tuple-element.11.root_sol), custom_call_target="tpu_custom_call" | custom-call | flops 905969664 | bytes 2359296 | tf_op jit(solution)/shard_map/leaf_root_part/pallas_call | solution.py:361
  67.8 2.5 %collective-permute-done.12.far = f32[128,256]{1,0:T(8,128)S(1)} collective-permute-done((f32[128,256]{1,0:T(8,128)}, f32[128,256]{1,0:T(8,128)S(1)}, u32[]{:S(2)}, u32[]{:S(2)}) %collective-permute-start.12) | collective-permute-done | bytes 131104 | tf_op jit(solution)/shard_map/ppermute | solution.py:239
  70.4 0.0 copy-start.2
  70.4 0.0 collective-permute-done.11.near
  70.4 0.6 copy-done.2
  71.0 0.0 copy-start.3
  71.0 0.6 copy-done.3
  71.7 5.2 %leaf_backward.1 = f32[12,128,256]{2,1,0:T(8,128)} custom-call(s32[48]{0:T(128)} %reshape.15.rows, f32[12,4,128,128]{3,2,1,0:T(8,128)} %first.3, f32[12,128,128]{2,1,0:T(8,128)} %inverse.7, f32[12,128,256]{2,1,0:T(8,128)} %leaf_root_part.1.rest, f32[1,128,256]{2,1,0:T(8,128)} %get-tuple-element.10.own, f32[128,256]{1,0:T(8,128)} %copy-done.3, ...), custom_call_target="tpu_custom_call" | custom-call | flops 603979776 | bytes 1572864 | tf_op jit(solution)/shard_map/leaf_backward/pallas_call | solution.py:378
  (3 shorter events, 0.0 us)
Async XLA Ops:
  8.5 8.9 %collective-permute-start.1 = (f32[128,256]{1,0:T(8,128)S(1)}, f32[128,256]{1,0:T(8,128)S(1)}, u32[]{:S(2)}, u32[]{:S(2)}) collective-permute-start(f32[128,256]{1,0:T(8,128)S(1)} %get-tuple-element.21), channel_id=1, source_target_pairs={{0,8},{2,10},{4,12},{6,14},{8,0},{10,2},{12,4},{14,6},{1,9},{3,11}... | collective-permute-start | bytes 393224 | tf_op jit(solution)/shard_map/ppermute | solution.py:239
  11.1 7.6 %collective-permute-start = (f32[128,256]{1,0:T(8,128)S(1)}, f32[128,256]{1,0:T(8,128)S(1)}, u32[]{:S(2)}, u32[]{:S(2)}) collective-permute-start(f32[128,256]{1,0:T(8,128)S(1)} %get-tuple-element.22), channel_id=1, source_target_pairs={{0,14},{2,0},{4,2},{6,4},{8,6},{10,8},{12,10},{14,12},{1,15},{3,1}... | collective-permute-start | bytes 393224 | tf_op jit(solution)/shard_map/ppermute | solution.py:239
  17.5 1.2 %copy-start.4 = (f32[128,256]{1,0:T(8,128)}, f32[128,256]{1,0:T(8,128)S(1)}, u32[]{:S(2)}) copy-start(f32[128,256]{1,0:T(8,128)S(1)} %collective-permute-done.1.far) | copy-start | bytes 393220
  18.7 0.7 copy-start.5
  22.2 1.7 %collective-permute-start.2 = (f32[4,128,128]{2,1,0:T(8,128)}, f32[4,128,128]{2,1,0:T(8,128)S(1)}, u32[]{:S(2)}, u32[]{:S(2)}) collective-permute-start(f32[4,128,128]{2,1,0:T(8,128)} %get-tuple-element.17), channel_id=1, source_target_pairs={{0,1},{1,0},{2,3},{3,2},{4,5},{5,4},{6,7},{7,6},{8,9},{9,8},{10,11... | collective-permute-start | bytes 786440 | tf_op jit(solution)/shard_map/ppermute | solution.py:245
  24.9 4.3 %collective-permute-start.3 = (f32[128,128]{1,0:T(8,128)S(1)}, f32[128,128]{1,0:T(8,128)S(1)}, u32[]{:S(2)}, u32[]{:S(2)}) collective-permute-start(f32[128,128]{1,0:T(8,128)S(1)} %get-tuple-element.24), channel_id=1, source_target_pairs={{0,2},{2,0},{4,6},{6,4},{8,10},{10,8},{12,14},{14,12},{1,3},{3,1},... | collective-permute-start | bytes 196616 | tf_op jit(solution)/shard_map/ppermute | solution.py:242
  25.5 5.3 %collective-permute-start.5 = (f32[128,128]{1,0:T(8,128)S(1)}, f32[128,128]{1,0:T(8,128)S(1)}, u32[]{:S(2)}, u32[]{:S(2)}) collective-permute-start(f32[128,128]{1,0:T(8,128)S(1)} %get-tuple-element.25), channel_id=1, source_target_pairs={{0,6},{2,4},{4,2},{6,0},{8,14},{10,12},{12,10},{14,8},{1,7},{3,5},... | collective-permute-start | bytes 196616 | tf_op jit(solution)/shard_map/ppermute | solution.py:242
  28.6 4.3 %collective-permute-start.4 = (f32[128,128]{1,0:T(8,128)S(1)}, f32[128,128]{1,0:T(8,128)S(1)}, u32[]{:S(2)}, u32[]{:S(2)}) collective-permute-start(f32[128,128]{1,0:T(8,128)S(1)} %get-tuple-element.26), channel_id=1, source_target_pairs={{0,4},{2,6},{4,0},{6,2},{8,12},{10,14},{12,8},{14,10},{1,5},{3,7},... | collective-permute-start | bytes 196616 | tf_op jit(solution)/shard_map/ppermute | solution.py:242
  32.9 5.9 %collective-permute-start.6 = (f32[128,128]{1,0:T(8,128)S(1)}, f32[128,128]{1,0:T(8,128)S(1)}, u32[]{:S(2)}, u32[]{:S(2)}) collective-permute-start(f32[128,128]{1,0:T(8,128)S(1)} %fusion.1), channel_id=1, source_target_pairs={{0,8},{2,10},{4,12},{6,14},{8,0},{10,2},{12,4},{14,6},{1,9},{3,11}... | collective-permute-start | bytes 196616 | tf_op jit(solution)/shard_map/ppermute | solution.py:242
  38.8 9.0 %copy-start.1 = (f32[128,128]{1,0:T(8,128)}, f32[128,128]{1,0:T(8,128)S(1)}, u32[]{:S(2)}) copy-start(f32[128,128]{1,0:T(8,128)S(1)} %add.41.own) | copy-start | bytes 196612
  38.8 9.0 %collective-permute-start.9 = (f32[128,128]{1,0:T(8,128)S(1)}, f32[128,128]{1,0:T(8,128)S(1)}, u32[]{:S(2)}, u32[]{:S(2)}) collective-permute-start(f32[128,128]{1,0:T(8,128)S(1)} %add.41.own), channel_id=1, source_target_pairs={{0,6},{2,4},{4,2},{6,0},{8,14},{10,12},{12,10},{14,8},{1,7},{3,5},... | collective-permute-start | bytes 196616 | tf_op jit(solution)/shard_map/ppermute | solution.py:242
  39.9 7.9 %collective-permute-start.8 = (f32[128,128]{1,0:T(8,128)S(1)}, f32[128,128]{1,0:T(8,128)S(1)}, u32[]{:S(2)}, u32[]{:S(2)}) collective-permute-start(f32[128,128]{1,0:T(8,128)S(1)} %add.41.own), channel_id=1, source_target_pairs={{0,4},{2,6},{4,0},{6,2},{8,12},{10,14},{12,8},{14,10},{1,5},{3,7},... | collective-permute-start | bytes 196616 | tf_op jit(solution)/shard_map/ppermute | solution.py:242
  41.6 6.2 %collective-permute-start.7 = (f32[128,128]{1,0:T(8,128)S(1)}, f32[128,128]{1,0:T(8,128)S(1)}, u32[]{:S(2)}, u32[]{:S(2)}) collective-permute-start(f32[128,128]{1,0:T(8,128)S(1)} %add.41.own), channel_id=1, source_target_pairs={{0,2},{2,0},{4,6},{6,4},{8,10},{10,8},{12,14},{14,12},{1,3},{3,1},... | collective-permute-start | bytes 196616 | tf_op jit(solution)/shard_map/ppermute | solution.py:242
  47.8 0.6 copy-start.6
  47.8 0.6 copy-start.7
  47.8 0.6 copy-start.8
  53.3 1.7 %collective-permute-start.10 = (f32[4,128,128]{2,1,0:T(8,128)}, f32[4,128,128]{2,1,0:T(8,128)S(1)}, u32[]{:S(2)}, u32[]{:S(2)}) collective-permute-start(f32[4,128,128]{2,1,0:T(8,128)} %root_solve.1.mine), channel_id=1, source_target_pairs={{0,1},{1,0},{2,3},{3,2},{4,5},{5,4},{6,7},{7,6},{8,9},{9,8},{10,11... | collective-permute-start | bytes 786440 | tf_op jit(solution)/shard_map/ppermute | solution.py:245
  55.0 0.7 copy-start
  58.1 12.3 %collective-permute-start.12 = (f32[128,256]{1,0:T(8,128)}, f32[128,256]{1,0:T(8,128)S(1)}, u32[]{:S(2)}, u32[]{:S(2)}) collective-permute-start(f32[128,256]{1,0:T(8,128)} %bitcast.22), channel_id=1, source_target_pairs={{0,8},{2,10},{4,12},{6,14},{8,0},{10,2},{12,4},{14,6},{1,9},{3,11}... | collective-permute-start | bytes 393224 | tf_op jit(solution)/shard_map/ppermute | solution.py:239
  59.8 10.6 %collective-permute-start.11 = (f32[128,256]{1,0:T(8,128)}, f32[128,256]{1,0:T(8,128)S(1)}, u32[]{:S(2)}, u32[]{:S(2)}) collective-permute-start(f32[128,256]{1,0:T(8,128)} %bitcast.23), channel_id=1, source_target_pairs={{0,2},{2,4},{4,6},{6,8},{8,10},{10,12},{12,14},{14,0},{1,3},{3,5},... | collective-permute-start | bytes 393224 | tf_op jit(solution)/shard_map/ppermute | solution.py:239
  70.4 0.6 copy-start.2
  71.0 0.7 copy-start.3

commit v2 on v1

v2 whole, which is shorter than its diff:
```python
import functools

import jax
import jax.numpy as jnp
from jax import lax
from jax.experimental import pallas as pl
from jax.experimental.pallas import tpu as pltpu
from jax.sharding import PartitionSpec as P

VMEM = pltpu.VMEM
SMEM = pltpu.SMEM
F32 = jnp.float32
BF16 = jnp.bfloat16


def parts_of(x):
    high = x.astype(BF16)
    low = (x - high.astype(F32)).astype(BF16)
    return high, low


def as_left(x):
    high, low = parts_of(x)
    count = x.shape[1] // 128
    pieces = [slice(j * 128, j * 128 + 128) for j in range(count)]
    top = jnp.concatenate([high[:, s] for s in pieces for _ in range(2)], axis=1)
    bottom = jnp.concatenate([low[:, s] for s in pieces for _ in range(2)], axis=1)
    return jnp.concatenate([top, bottom], axis=0)


def as_right(x):
    high, low = parts_of(x)
    count = x.shape[0] // 128
    pieces = [slice(j * 128, j * 128 + 128) for j in range(count)]
    return jnp.concatenate([y[s] for s in pieces for y in (high, low)], axis=0)


def left_times(left, right):
    both = jnp.dot(left, right, preferred_element_type=F32)
    rows = left.shape[0] // 2
    return both[:rows] + both[rows:]


def times(a, b):
    return left_times(as_left(a), as_right(b))


def cost(microseconds):
    return pl.CostEstimate(
        flops=int(microseconds * 1e9),
        bytes_accessed=int(microseconds * 3e6),
        transcendentals=0,
    )


def forward_leaf_kernel(links, rhs, inverse, first, solved, own, near, far, pending):
    step = pl.program_id(0)

    @pl.when(step == 0)
    def _():
        pending[...] = jnp.zeros_like(pending)

    batch = rhs.shape[0]
    values = []
    for i in range(batch):
        value = times(inverse[i], rhs[i])
        solved[i] = value
        values.append(value)
    for i in range(batch):
        pending[links[0, step * batch + i]] += times(first[i, 0], values[i])

    @pl.when(step == pl.num_programs(0) - 1)
    def _():
        own[...] = pending[0]
        near[...] = pending[1]
        far[...] = pending[2]


def root_terms_kernel(links, one, two, three, solved, after, pending):
    step = pl.program_id(0)

    @pl.when(step == 0)
    def _():
        pending[...] = jnp.zeros_like(pending)

    batch = solved.shape[0]
    for i in range(batch):
        blocks = jnp.concatenate([one[i, 0], two[i, 0], three[i, 0]], axis=0)
        terms = times(blocks, solved[i])
        for n in range(3):
            slot = links[n + 1, step * batch + i] - 3
            pending[slot] += terms[n * 128 : n * 128 + 128]


def root_operator_kernel(
    lower_inverse, upper_inverse, lower, upper, after, root_operator, forward, backward
):
    count = lower_inverse.shape[0]
    w = lower_inverse.shape[1]
    forward[...] = jnp.zeros_like(forward)
    backward[...] = jnp.zeros_like(backward)
    for r in range(count):
        here = slice(r * w, r * w + w)
        forward[here, here] = lower_inverse[r]
        if r > 0:
            done = slice(0, r * w)
            inner = times(lower[here, done], forward[done, done])
            forward[here, done] = -times(lower_inverse[r], inner)
    for r in reversed(range(count)):
        here = slice(r * w, r * w + w)
        backward[here, here] = upper_inverse[r]
        if r < count - 1:
            done = slice((r + 1) * w, count * w)
            inner = times(upper[here, done], backward[done, done])
            backward[here, done] = -times(upper_inverse[r], inner)
    for r in range(count):
        here = slice(r * w, r * w + w)
        left = as_left(times(backward[here, r * w :], forward[r * w :, :]))
        root_operator[here, :] = left[:w]
        root_operator[count * w + r * w : count * w + r * w + w, :] = left[w:]


def separator_operators_kernel(
    lower_inverse, upper_inverse, lower, upper, after, forward, backward
):
    blocks = jnp.concatenate([upper_inverse[0]] + [lower[0, n] for n in range(3)], axis=0)
    forward[...] = as_left(times(blocks, lower_inverse[0]))
    blocks = jnp.concatenate([upper[0, n] for n in range(3)], axis=1)
    backward[...] = as_left(times(upper_inverse[0], blocks))


def separator_kernel(
    links, core, rhs, operator, own, near, far, root_pending, solved, mine, theirs, sums
):
    right = as_right(rhs[0] - own[...] - near[...] - far[...])
    terms = left_times(operator[...], right)
    solved[...] = terms[:128]
    sums[...] = root_pending[...]
    for n in range(3):
        sums[links[n]] += terms[n * 128 + 128 : n * 128 + 256]
    is_first = core[0] == 0

    @pl.when(is_first)
    def _():
        mine[...] = sums[:, :, :128]
        theirs[...] = sums[:, :, 128:]

    @pl.when(jnp.logical_not(is_first))
    def _():
        mine[...] = sums[:, :, 128:]
        theirs[...] = sums[:, :, :128]


def pieces_kernel(place, mine, other, *pieces):
    position = place[0]
    for j, piece in enumerate(pieces):
        piece[...] = mine[position ^ j] + other[position ^ j]


def root_kernel(place, rhs, operator, own, one, two, three, out, pending):
    count, w = rhs.shape[0], rhs.shape[1]
    position = place[0]
    is_first = place[1] == 0
    for j, piece in enumerate((own, one, two, three)):
        root = position ^ j
        right = rhs[root]
        right = jnp.where(is_first, right[:, :128], right[:, 128:])
        pending[pl.ds(pl.multiple_of(root * 2 * w, 2 * w), 2 * w), :] = as_right(
            right - piece[...]
        )
    out[...] = left_times(operator[...], pending[...]).reshape(count, w, 128)


def separator_back_kernel(links, core, mine, theirs, operator, solved, root_sol, right, out):
    is_first = core[0] == 0

    @pl.when(is_first)
    def _():
        root_sol[:, :, :128] = mine[...]
        root_sol[:, :, 128:] = theirs[...]

    @pl.when(jnp.logical_not(is_first))
    def _():
        root_sol[:, :, :128] = theirs[...]
        root_sol[:, :, 128:] = mine[...]

    for r in range(root_sol.shape[0]):
        right[r] = as_right(root_sol[r])
    linked = jnp.concatenate([right[links[n]] for n in range(3)], axis=0)
    out[0] = solved[...] - left_times(operator[...], linked)


def leaf_operator_kernel(inverse, first, after, operator):
    for i in range(inverse.shape[0]):
        operator[i] = as_left(times(inverse[i], first[i, 0]))


def leaf_root_part_kernel(links, one, two, three, inverse, solved, root_right, part):
    step = pl.program_id(0)
    batch = solved.shape[0]
    rests = []
    for i in range(batch):
        leaf = step * batch + i
        blocks = jnp.concatenate([one[i, 0], two[i, 0], three[i, 0]], axis=1)
        linked = jnp.concatenate([root_right[links[n, leaf] - 3] for n in (1, 2, 3)], axis=0)
        rests.append(solved[i] - left_times(as_left(blocks), linked))
    for i in range(batch):
        part[i] = times(inverse[i], rests[i])


def leaf_final_kernel(links, operator, part, own, near, far, out, seps):
    step = pl.program_id(0)

    @pl.when(step == 0)
    def _():
        seps[0] = as_right(own[0])
        seps[1] = as_right(near[...])
        seps[2] = as_right(far[...])

    batch = part.shape[0]
    for i in range(batch):
        slot = links[0, step * batch + i]
        out[i] = part[i] - left_times(operator[i], seps[slot])


def whole(memory=VMEM):
    return pl.BlockSpec(memory_space=memory)


ANY = pl.BlockSpec(memory_space=pl.ANY)


def limit(megabytes):
    return pltpu.CompilerParams(vmem_limit_bytes=megabytes * 1024 * 1024)


def leafwise(batch, *tail):
    return pl.BlockSpec((batch,) + tail, lambda k: (k,) + (0,) * len(tail))


def link(batch, n, w):
    return pl.BlockSpec((batch, 1, w, w), lambda k: (k, n, 0, 0))


def kept(*shape):
    return pl.BlockSpec(shape, lambda k: (0,) * len(shape))


def per_device(
    leaf_rhs,
    leaf_lower_inverse,
    leaf_upper_inverse,
    leaf_lower,
    leaf_upper,
    leaf_rows,
    separator_right_sides,
    separator_lower_inverse,
    separator_upper_inverse,
    separator_lower_blocks,
    sep_upper,
    sep_rows,
    root_rhs,
    root_lower_inverse,
    root_upper_inverse,
    root_lower,
    root_upper,
):
    peers = lax.axis_size("grid")
    leaves, w, columns = leaf_rhs.shape
    roots = root_rhs.shape[0]
    half = columns // 2
    batch = leaves // 2
    position = lax.axis_index("grid") % 4
    core = lax.axis_index("layer")
    core_ref = core.astype(jnp.int32).reshape(1)
    place = jnp.stack([position, core]).astype(jnp.int32)
    leaf_links = leaf_rows.T
    sep_links = sep_rows.reshape(-1)

    def shifted(x, by):
        return lax.ppermute(x, "grid", [(i, (i + by) % peers) for i in range(peers)])

    def crossed(x, bit):
        return lax.ppermute(x, "grid", [(i, i ^ bit) for i in range(peers)])

    def swapped(x):
        return lax.ppermute(x, "layer", [(0, 1), (1, 0)])

    shape = jax.ShapeDtypeStruct

    leaf_solved, own, near, far = pl.pallas_call(
        forward_leaf_kernel,
        grid=(leaves // batch,),
        in_specs=[
            whole(SMEM),
            leafwise(batch, w, columns),
            leafwise(batch, w, w),
            link(batch, 0, w),
        ],
        out_specs=[leafwise(batch, w, columns)] + [kept(w, columns)] * 3,
        out_shape=[shape((leaves, w, columns), F32)] + [shape((w, columns), F32)] * 3,
        scratch_shapes=[VMEM((3, w, columns), F32)],
        compiler_params=limit(56),
        cost_estimate=cost(4),
        name="leaf_forward",
    )(leaf_links, leaf_rhs, leaf_lower_inverse, leaf_lower)

    near_sum = shifted(near, -1)
    far_sum = shifted(far, -(peers // 2))

    root_pending = pl.pallas_call(
        root_terms_kernel,
        grid=(leaves // batch,),
        in_specs=[
            whole(SMEM),
            link(batch, 1, w),
            link(batch, 2, w),
            link(batch, 3, w),
            leafwise(batch, w, columns),
            ANY,
        ],
        out_specs=kept(roots, w, columns),
        out_shape=shape((roots, w, columns), F32),
        compiler_params=limit(16),
        cost_estimate=cost(3),
        name="root_terms",
    )(leaf_links, leaf_lower, leaf_lower, leaf_lower, leaf_solved, own)

    sep_forward, sep_backward = pl.pallas_call(
        separator_operators_kernel,
        in_specs=[whole()] * 4 + [ANY],
        out_specs=[whole()] * 2,
        out_shape=[shape((8 * w, 2 * w), BF16), shape((2 * w, 6 * w), BF16)],
        compiler_params=limit(16),
        cost_estimate=cost(1),
        name="separator_operators",
    )(
        separator_lower_inverse,
        separator_upper_inverse,
        separator_lower_blocks,
        sep_upper,
        own,
    )

    sep_solved, mine, theirs = pl.pallas_call(
        separator_kernel,
        in_specs=[whole(SMEM), whole(SMEM)] + [whole()] * 6,
        out_specs=[whole()] * 3,
        out_shape=[
            shape((w, columns), F32),
            shape((roots, w, half), F32),
            shape((roots, w, half), F32),
        ],
        scratch_shapes=[VMEM((roots, w, columns), F32)],
        compiler_params=limit(16),
        cost_estimate=cost(2),
        name="separator_forward",
    )(
        sep_links,
        core_ref,
        separator_right_sides,
        sep_forward,
        own,
        near_sum,
        far_sum,
        root_pending,
    )

    other = swapped(theirs)
    pieces = pl.pallas_call(
        pieces_kernel,
        in_specs=[whole(SMEM)] + [whole()] * 2,
        out_specs=[whole()] * 4,
        out_shape=[shape((w, half), F32)] * 4,
        compiler_params=limit(16),
        cost_estimate=cost(0.5),
        name="pieces",
    )(place, mine, other)
    total = pieces[0]
    for j in (1, 2, 3):
        total = total + crossed(pieces[j], j)

    leaf_operator = pl.pallas_call(
        leaf_operator_kernel,
        grid=(leaves // batch,),
        in_specs=[leafwise(batch, w, w), link(batch, 0, w), ANY],
        out_specs=leafwise(batch, 2 * w, 2 * w),
        out_shape=shape((leaves, 2 * w, 2 * w), BF16),
        compiler_params=limit(16),
        cost_estimate=cost(1),
        name="leaf_operators",
    )(leaf_upper_inverse, leaf_upper, total)

    root_operator = pl.pallas_call(
        root_operator_kernel,
        in_specs=[whole()] * 4 + [ANY],
        out_specs=whole(),
        out_shape=shape((2 * roots * w, 2 * roots * w), BF16),
        scratch_shapes=[VMEM((roots * w, roots * w), F32)] * 2,
        compiler_params=limit(16),
        cost_estimate=cost(3),
        name="root_operator",
    )(root_lower_inverse, root_upper_inverse, root_lower, root_upper, total)

    bit = 4
    while bit < peers:
        total = total + crossed(total, bit)
        bit *= 2
    others = [crossed(total, j) for j in (1, 2, 3)]

    solution_half = pl.pallas_call(
        root_kernel,
        in_specs=[whole(SMEM)] + [whole()] * 6,
        out_specs=whole(),
        out_shape=shape((roots, w, half), F32),
        scratch_shapes=[VMEM((2 * roots * w, half), BF16)],
        compiler_params=limit(16),
        cost_estimate=cost(1),
        name="root_solve",
    )(place, root_rhs, root_operator, total, *others)

    other_half = swapped(solution_half)

    root_sol, root_right, separator_solution_rows = pl.pallas_call(
        separator_back_kernel,
        in_specs=[whole(SMEM), whole(SMEM)] + [whole()] * 4,
        out_specs=[whole()] * 3,
        out_shape=[
            shape((roots, w, columns), F32),
            shape((roots, 2 * w, columns), BF16),
            shape((1, w, columns), F32),
        ],
        compiler_params=limit(16),
        cost_estimate=cost(1.5),
        name="separator_backward",
    )(sep_links, core_ref, solution_half, other_half, sep_backward, sep_solved)

    near_rows = shifted(separator_solution_rows[0], 1)
    far_rows = shifted(separator_solution_rows[0], peers // 2)

    leaf_part = pl.pallas_call(
        leaf_root_part_kernel,
        grid=(leaves // batch,),
        in_specs=[
            whole(SMEM),
            link(batch, 1, w),
            link(batch, 2, w),
            link(batch, 3, w),
            leafwise(batch, w, w),
            leafwise(batch, w, columns),
            kept(roots, 2 * w, columns),
        ],
        out_specs=leafwise(batch, w, columns),
        out_shape=shape((leaves, w, columns), F32),
        compiler_params=limit(16),
        cost_estimate=cost(3),
        name="leaf_root_part",
    )(
        leaf_links,
        leaf_upper,
        leaf_upper,
        leaf_upper,
        leaf_upper_inverse,
        leaf_solved,
        root_right,
    )

    leaf_sol = pl.pallas_call(
        leaf_final_kernel,
        grid=(leaves // batch,),
        in_specs=[
            whole(SMEM),
            leafwise(batch, 2 * w, 2 * w),
            leafwise(batch, w, columns),
            kept(1, w, columns),
            kept(w, columns),
            kept(w, columns),
        ],
        out_specs=leafwise(batch, w, columns),
        out_shape=shape((leaves, w, columns), F32),
        scratch_shapes=[VMEM((3, 2 * w, columns), BF16)],
        compiler_params=limit(16),
        cost_estimate=cost(2.3),
        name="leaf_backward",
    )(leaf_links, leaf_operator, leaf_part, separator_solution_rows, near_rows, far_rows)
    return (leaf_sol, separator_solution_rows, root_sol)


def solution(mesh):
    by_device = P(("groups", "grid", "layer"))
    by_group = P("groups")
    return jax.shard_map(
        per_device,
        mesh=mesh,
        in_specs=(by_device,) * 12 + (by_group,) * 5,
        out_specs=(by_device, by_device, by_group),
        check_vma=False,
    )
```

time: 77.4 us -> 61.6 us (0.80)
  Pallas kernels: 35.7 us -> 20.2 us
  starting transfers between devices: 17.1 us -> 20 us
  local copies, waits for them, and re-layouts: 6.39 us -> 4.22 us
  other arithmetic: 1.66 us -> 0.1 us
    pallas_call x6 -> x9, Pallas kernels: 30.5 us -> 17.7 us  [the longest x1 3.83 us: per_device(): pl.pallas_call(forward_leaf_kernel, grid=(leaves // batch,), in_specs=[wh...]
    ppermute x7, starting transfers between devices: 9.43 us -> 12.8 us  [crossed(): return lax.ppermute(x, 'grid', [(i, i ^ bit) for i in range(peers)])]
    ppermute x4, waiting for transfers between devices: 4.51 us -> 6.7 us  [shifted(): lax.ppermute(x, 'grid', [(i, (i + by) % peers) for i in range(peers)])]
    pallas_call x1, Pallas kernels: 2.81 us -> 0.91 us  [per_device(): pl.pallas_call(separator_kernel, in_specs=[whole(SMEM), whole(SMEM)] + [w...]
    ppermute x2, waiting for transfers between devices: 3.49 us -> 1.69 us  [swapped(): return lax.ppermute(x, 'layer', [(0, 1), (1, 0)])]
    squeeze x2 -> x0, local copies, waits for them, and re-layouts: 1.74 us -> none  [the longest x1 1.71 us: per_device(): far_sum = shifted(pending[2], -(peers // 2))]
    add x2 -> x1, other arithmetic: 0.99 us -> 0.02 us  [per_device(): total = total + crossed(pieces[j], j)]
    pallas_call x1, Pallas kernels: 2.36 us -> 1.59 us  [per_device(): pl.pallas_call(separator_back_kernel, in_specs=[whole(SMEM), whole(SMEM)]...]
  transfers between devices with their start and end apart: 13 -> 13, of which waited for: 9 -> 8; matrix products, arithmetic and copies ran while one was open for 1% -> 0% of each run, Pallas kernels for 20% -> 16%
where the time goes in v2:
time: 61.6 us; the launch traced here: 61.2 us
  Pallas kernels  20.2 us (33%)
  starting transfers between devices  20 us (32%)
  waiting for transfers between devices  15.8 us (26%)
  local copies, waits for them, and re-layouts  4.22 us (7%)
  between operations  0.94 us (2%)
    ppermute x7, starting transfers between devices, crossed(): return lax.ppermute(x, 'grid', [(i, i ^ bit) for i in range(peers)])  12.8 us
    ppermute x7, waiting for transfers between devices, crossed(): return lax.ppermute(x, 'grid', [(i, i ^ bit) for i in range(peers)])  7.39 us
    ppermute x4, starting transfers between devices, shifted(): lax.ppermute(x, 'grid', [(i, (i + by) % peers) for i in range(peers)])  7.16 us
    ppermute x4, waiting for transfers between devices, shifted(): lax.ppermute(x, 'grid', [(i, (i + by) % peers) for i in range(peers)])  6.7 us
    unnamed x48, local copies, waits for them, and re-layouts  4.22 us
    pallas_call x1, Pallas kernels, per_device(): pl.pallas_call(forward_leaf_kernel, grid=(leaves // batch,), in_specs=[wh...  3.83 us
    pallas_call x1, Pallas kernels, per_device(): pl.pallas_call(root_operator_kernel, in_specs=[whole()] * 4 + [ANY], out_...  3.26 us
    pallas_call x1, Pallas kernels, per_device(): pl.pallas_call(leaf_root_part_kernel, grid=(leaves // batch,), in_specs=[...  2.74 us
  transfers between devices with their start and end apart: 13, of which 8 were waited for; matrix products, arithmetic and copies ran while one was open for 0% of the time, Pallas kernels for 16%

profile of v2, /device:TPU:6, one launch (start us, length us, event | category | flops | bytes accessed | tf_op | source)
XLA Modules:
  0.0 61.2 jit_solution(15112812583841984292)
XLA Ops:
  0.6 0.0 copy-start.1
  0.6 0.0 copy-start.7
  0.7 3.8 %leaf_forward.1 = (f32[12,128,256]{2,1,0:T(8,128)}, f32[128,256]{1,0:T(8,128)}, f32[128,256]{1,0:T(8,128)}, f32[128,256]{1,0:T(8,128)}) custom-call(s32[4,12]{1,0:T(4,128)} %bitcast.5, f32[12,128,256]{2,1,0:T(8,128)} %rhs.3, f32[12,128,128]{2,1,0:T(8,128)} %inverse.3, f32[12,4,128,128]{3,2,1,0:T(8,128)} %three.2), custom_call_target="tpu_custom_call" | custom-call | flops 4000000000 | bytes 12000000 | tf_op jit(solution)/shard_map/leaf_forward/pallas_call | solution.py:291
  4.5 0.5 collective-permute-start
  5.0 2.6 %collective-permute-start.1 = (f32[128,256]{1,0:T(8,128)}, f32[128,256]{1,0:T(8,128)S(1)}, u32[]{:S(2)}, u32[]{:S(2)}) collective-permute-start(f32[128,256]{1,0:T(8,128)} %get-tuple-element.22), channel_id=1, source_target_pairs={{0,8},{2,10},{4,12},{6,14},{8,0},{10,2},{12,4},{14,6},{1,9},{3,11}... | collective-permute-start | bytes 393224 | tf_op jit(solution)/shard_map/ppermute | solution.py:281
  7.6 0.0 copy-done.1
  7.6 0.0 copy-done.7
  7.6 1.4 %copy-done.2 = f32[12,128,256]{2,1,0:T(8,128)S(1)} copy-done((f32[12,128,256]{2,1,0:T(8,128)S(1)}, f32[12,128,256]{2,1,0:T(8,128)}, u32[]{:S(2)}) %copy-start.2) | copy-done | bytes 1572888
  9.0 0.9 %copy-done.5 = f32[128,256]{1,0:T(8,128)S(1)} copy-done((f32[128,256]{1,0:T(8,128)S(1)}, f32[128,256]{1,0:T(8,128)}, u32[]{:S(2)}) %copy-start.5) | copy-done | bytes 131096
  9.9 0.0 copy-start.18
  10.0 2.4 %root_terms.1.root_pending = f32[4,128,256]{2,1,0:T(8,128)S(1)} custom-call(s32[4,12]{1,0:T(4,128)S(1)} %bitcast.6, f32[12,4,128,128]{3,2,1,0:T(8,128)S(1)} %copy-done.1, f32[12,4,128,128]{3,2,1,0:T(8,128)S(1)} %copy-done.1, f32[12,4,128,128]{3,2,1,0:T(8,128)S(1)} %copy-done.1, f32[12,128,256]{2,1,0:T(8,128)S(1)} %copy-done.2, f32[128,256]{1,0:T(8,128)S(1)} %copy-done.5), custom_call_target="tpu_custom_call" | custom-call | flops 3000000000 | bytes 9000000 | tf_op jit(solution)/shard_map/root_terms/pallas_call | solution.py:311
  12.4 0.0 copy-done.6
  12.4 0.0 copy-done.13
  12.4 0.0 copy-done.14
  12.4 0.0 copy-done.17
  12.5 0.0 copy-done.18
  12.5 0.0 copy-start.15
  12.5 0.0 copy-start.19
  12.5 0.4 separator_operators.1
  12.9 0.0 copy-start.20
  12.9 0.7 %copy-done.20 = bf16[256,768]{1,0:T(8,128)(2,1)} copy-done((bf16[256,768]{1,0:T(8,128)(2,1)}, bf16[256,768]{1,0:T(8,128)(2,1)S(1)}, u32[]{:S(2)}) %copy-start.20) | copy-done | bytes 393240
  13.6 0.0 collective-permute-done.near
  13.6 0.3 collective-permute-done.1.far
  13.9 0.0 copy-done.19
  13.9 0.9 %separator_forward.1 = (f32[128,256]{1,0:T(8,128)S(1)}, f32[4,128,128]{2,1,0:T(8,128)S(1)}, f32[4,128,128]{2,1,0:T(8,128)S(1)}) custom-call(s32[3]{0:T(128)S(1)} %bitcast.11, s32[1]{0:T(128)} %bitcast.2.core, f32[1,128,256]{2,1,0:T(8,128)S(1)} %copy-done.15, bf16[1024,256]{1,0:T(8,128)(2,1)S(1)} %get-tuple-element.20.operator, f32[128,256]{1,0:T(8,128)S(1)} %copy-done.6, ...), custom_call_target="tpu_custom_call" | custom-call | flops 2000000000 | bytes 6000000 | tf_op jit(solution)/shard_map/separator_forward/pallas_call | solution.py:345
  14.8 0.0 copy-start.22
  14.8 0.6 %copy-done.22 = f32[128,256]{1,0:T(8,128)} copy-done((f32[128,256]{1,0:T(8,128)}, f32[128,256]{1,0:T(8,128)S(1)}, u32[]{:S(2)}) %copy-start.22) | copy-done | bytes 131096
  15.5 0.0 collective-permute-start.2
  15.5 0.1 pad_add_fusion.place
  15.6 1.4 %collective-permute-done.2.other = f32[4,128,128]{2,1,0:T(8,128)S(1)} collective-permute-done((f32[4,128,128]{2,1,0:T(8,128)S(1)}, f32[4,128,128]{2,1,0:T(8,128)S(1)}, u32[]{:S(2)}, u32[]{:S(2)}) %collective-permute-start.2) | collective-permute-done | bytes 262176 | tf_op jit(solution)/shard_map/ppermute | solution.py:287
  17.0 0.6 pieces.1
  17.6 4.4 %collective-permute-start.3 = (f32[128,128]{1,0:T(8,128)S(1)}, f32[128,128]{1,0:T(8,128)S(1)}, u32[]{:S(2)}, u32[]{:S(2)}) collective-permute-start(f32[128,128]{1,0:T(8,128)S(1)} %get-tuple-element.27), channel_id=1, source_target_pairs={{0,2},{2,0},{4,6},{6,4},{8,10},{10,8},{12,14},{14,12},{1,3},{3,1},... | collective-permute-start | bytes 196616 | tf_op jit(solution)/shard_map/ppermute | solution.py:284
  22.0 0.8 %collective-permute-start.4 = (f32[128,128]{1,0:T(8,128)S(1)}, f32[128,128]{1,0:T(8,128)S(1)}, u32[]{:S(2)}, u32[]{:S(2)}) collective-permute-start(f32[128,128]{1,0:T(8,128)S(1)} %get-tuple-element.28), channel_id=1, source_target_pairs={{0,4},{2,6},{4,0},{6,2},{8,12},{10,14},{12,8},{14,10},{1,5},{3,7},... | collective-permute-start | bytes 196616 | tf_op jit(solution)/shard_map/ppermute | solution.py:284
  22.8 0.7 %collective-permute-start.5 = (f32[128,128]{1,0:T(8,128)S(1)}, f32[128,128]{1,0:T(8,128)S(1)}, u32[]{:S(2)}, u32[]{:S(2)}) collective-permute-start(f32[128,128]{1,0:T(8,128)S(1)} %get-tuple-element.29), channel_id=1, source_target_pairs={{0,6},{2,4},{4,2},{6,0},{8,14},{10,12},{12,10},{14,8},{1,7},{3,5},... | collective-permute-start | bytes 196616 | tf_op jit(solution)/shard_map/ppermute | solution.py:284
  23.5 0.9 %collective-permute-done.3 = f32[128,128]{1,0:T(8,128)S(1)} collective-permute-done((f32[128,128]{1,0:T(8,128)S(1)}, f32[128,128]{1,0:T(8,128)S(1)}, u32[]{:S(2)}, u32[]{:S(2)}) %collective-permute-start.3) | collective-permute-done | bytes 65568 | tf_op jit(solution)/shard_map/ppermute | solution.py:284
  24.4 2.2 %collective-permute-done.4 = f32[128,128]{1,0:T(8,128)S(1)} collective-permute-done((f32[128,128]{1,0:T(8,128)S(1)}, f32[128,128]{1,0:T(8,128)S(1)}, u32[]{:S(2)}, u32[]{:S(2)}) %collective-permute-start.4) | collective-permute-done | bytes 65568 | tf_op jit(solution)/shard_map/ppermute | solution.py:284
  26.5 1.4 %collective-permute-done.5 = f32[128,128]{1,0:T(8,128)S(1)} collective-permute-done((f32[128,128]{1,0:T(8,128)S(1)}, f32[128,128]{1,0:T(8,128)S(1)}, u32[]{:S(2)}, u32[]{:S(2)}) %collective-permute-start.5) | collective-permute-done | bytes 65568 | tf_op jit(solution)/shard_map/ppermute | solution.py:284
  28.0 3.3 %collective-permute-start.6 = (f32[128,128]{1,0:T(8,128)S(1)}, f32[128,128]{1,0:T(8,128)S(1)}, u32[]{:S(2)}, u32[]{:S(2)}) collective-permute-start(f32[128,128]{1,0:T(8,128)S(1)} %add_add_fusion.after), channel_id=1, source_target_pairs={{0,8},{2,10},{4,12},{6,14},{8,0},{10,2},{12,4},{14,6},{1,9},{3,11}... | collective-permute-start | bytes 196616 | tf_op jit(solution)/shard_map/ppermute | solution.py:284
  31.3 2.9 %collective-permute-done.6 = f32[128,128]{1,0:T(8,128)S(1)} collective-permute-done((f32[128,128]{1,0:T(8,128)S(1)}, f32[128,128]{1,0:T(8,128)S(1)}, u32[]{:S(2)}, u32[]{:S(2)}) %collective-permute-start.6) | collective-permute-done | bytes 65568 | tf_op jit(solution)/shard_map/ppermute | solution.py:284
  34.3 0.0 copy-start.10
  34.3 0.1 collective-permute-start.7
  34.4 1.1 %collective-permute-start.8 = (f32[128,128]{1,0:T(8,128)S(1)}, f32[128,128]{1,0:T(8,128)S(1)}, u32[]{:S(2)}, u32[]{:S(2)}) collective-permute-start(f32[128,128]{1,0:T(8,128)S(1)} %add.20.own), channel_id=1, source_target_pairs={{0,4},{2,6},{4,0},{6,2},{8,12},{10,14},{12,8},{14,10},{1,5},{3,7},... | collective-permute-start | bytes 196616 | tf_op jit(solution)/shard_map/ppermute | solution.py:284
  35.4 2.4 %collective-permute-start.9 = (f32[128,128]{1,0:T(8,128)S(1)}, f32[128,128]{1,0:T(8,128)S(1)}, u32[]{:S(2)}, u32[]{:S(2)}) collective-permute-start(f32[128,128]{1,0:T(8,128)S(1)} %add.20.own), channel_id=1, source_target_pairs={{0,6},{2,4},{4,2},{6,0},{8,14},{10,12},{12,10},{14,8},{1,7},{3,5},... | collective-permute-start | bytes 196616 | tf_op jit(solution)/shard_map/ppermute | solution.py:284
  37.8 0.0 copy-start.4
  37.9 3.3 %root_operator.1.operator = bf16[1024,1024]{1,0:T(8,128)(2,1)S(1)} custom-call(f32[4,128,128]{2,1,0:T(8,128)S(1)} %copy-done.11, f32[4,128,128]{2,1,0:T(8,128)S(1)} %copy-done.12, f32[512,512]{1,0:T(8,128)S(1)} %copy-done.8, f32[512,512]{1,0:T(8,128)S(1)} %copy-done.9, f32[128,128]{1,0:T(8,128)S(1)} %add_add_fusion.after), custom_call_target="tpu_custom_call" | custom-call | flops 3000000000 | bytes 9000000 | tf_op jit(solution)/shard_map/root_operator/pallas_call | solution.py:394
  41.1 0.0 copy-start
  41.1 0.0 collective-permute-done.7.one
  41.1 0.0 collective-permute-done.8.two
  41.1 0.0 collective-permute-done.9.three
  41.2 1.3 %root_solve.1.mine = f32[4,128,128]{2,1,0:T(8,128)S(1)} custom-call(s32[2]{0:T(128)S(1)} %pad_add_fusion.place, f32[4,128,256]{2,1,0:T(8,128)S(1)} %copy-done.10, bf16[1024,1024]{1,0:T(8,128)(2,1)S(1)} %root_operator.1.operator, f32[128,128]{1,0:T(8,128)S(1)} %add.20.own, f32[128,128]{1,0:T(8,128)S(1)} %collective-permute-done.7.one, ...), custom_call_target="tpu_custom_call" | custom-call | flops 1000000000 | bytes 3000000 | tf_op jit(solution)/shard_map/root_solve/pallas_call | solution.py:411
  42.5 0.0 copy-start.21
  42.5 0.0 copy-start.23
  42.5 0.1 collective-permute-start.10
  42.6 0.4 copy-done
  43.0 0.8 %leaf_operators.1.operator = bf16[12,256,256]{2,1,0:T(8,128)(2,1)S(1)} custom-call(f32[12,128,128]{2,1,0:T(8,128)S(1)} %copy-done.4, f32[12,4,128,128]{3,2,1,0:T(8,128)S(1)} %copy-done, f32[128,128]{1,0:T(8,128)S(1)} %add_add_fusion.after), custom_call_target="tpu_custom_call" | custom-call | flops 1000000000 | bytes 3000000 | tf_op jit(solution)/shard_map/leaf_operators/pallas_call | solution.py:383
  43.8 0.3 collective-permute-done.10.theirs
  44.1 0.0 copy-done.23
  44.1 1.6 %separator_backward.1 = (f32[4,128,256]{2,1,0:T(8,128)}, bf16[4,256,256]{2,1,0:T(8,128)(2,1)S(1)}, f32[1,128,256]{2,1,0:T(8,128)}) custom-call(s32[3]{0:T(128)S(1)} %bitcast.12, s32[1]{0:T(128)} %bitcast.2.core, f32[4,128,128]{2,1,0:T(8,128)S(1)} %root_solve.1.mine, f32[4,128,128]{2,1,0:T(8,128)S(1)} %collective-permute-done.10.theirs, ...), custom_call_target="tpu_custom_call" | custom-call | flops 1500000000 | bytes 4500000 | tf_op jit(solution)/shard_map/separator_backward/pallas_call | solution.py:424
  45.7 1.8 %collective-permute-start.11 = (f32[128,256]{1,0:T(8,128)}, f32[128,256]{1,0:T(8,128)S(1)}, u32[]{:S(2)}, u32[]{:S(2)}) collective-permute-start(f32[128,256]{1,0:T(8,128)} %bitcast.9), channel_id=1, source_target_pairs={{0,2},{2,4},{4,6},{6,8},{8,10},{10,12},{12,14},{14,0},{1,3},{3,5},... | collective-permute-start | bytes 393224 | tf_op jit(solution)/shard_map/ppermute | solution.py:281
  47.5 2.2 %collective-permute-start.12 = (f32[128,256]{1,0:T(8,128)}, f32[128,256]{1,0:T(8,128)S(1)}, u32[]{:S(2)}, u32[]{:S(2)}) collective-permute-start(f32[128,256]{1,0:T(8,128)} %bitcast.10), channel_id=1, source_target_pairs={{0,8},{2,10},{4,12},{6,14},{8,0},{10,2},{12,4},{14,6},{1,9},{3,11}... | collective-permute-start | bytes 393224 | tf_op jit(solution)/shard_map/ppermute | solution.py:281
  49.7 2.7 %leaf_root_part.1.part = f32[12,128,256]{2,1,0:T(8,128)S(1)} custom-call(s32[4,12]{1,0:T(4,128)S(1)} %bitcast.7, f32[12,4,128,128]{3,2,1,0:T(8,128)S(1)} %copy-done, f32[12,4,128,128]{3,2,1,0:T(8,128)S(1)} %copy-done, f32[12,4,128,128]{3,2,1,0:T(8,128)S(1)} %copy-done, f32[12,128,128]{2,1,0:T(8,128)S(1)} %copy-done.4, f32[12,128,256]{2,1,0:T(8,128)S(1)} %copy-done.3, ...), custom_call_target="tpu_custom_call" | custom-call | flops 3000000000 | bytes 9000000 | tf_op jit(solution)/shard_map/leaf_root_part/pallas_call | solution.py:441
  52.5 0.0 collective-permute-done.11.near
  52.5 6.4 %collective-permute-done.12.far = f32[128,256]{1,0:T(8,128)S(1)} collective-permute-done((f32[128,256]{1,0:T(8,128)}, f32[128,256]{1,0:T(8,128)S(1)}, u32[]{:S(2)}, u32[]{:S(2)}) %collective-permute-start.12) | collective-permute-done | bytes 131104 | tf_op jit(solution)/shard_map/ppermute | solution.py:281
  58.9 2.3 %leaf_backward.1 = f32[12,128,256]{2,1,0:T(8,128)} custom-call(s32[4,12]{1,0:T(4,128)S(1)} %bitcast.8, bf16[12,256,256]{2,1,0:T(8,128)(2,1)S(1)} %leaf_operators.1.operator, f32[12,128,256]{2,1,0:T(8,128)S(1)} %leaf_root_part.1.part, f32[1,128,256]{2,1,0:T(8,128)S(1)} %copy-done.16, f32[128,256]{1,0:T(8,128)S(1)} %collective-permute-done.11.near, ...), custom_call_target="tpu_custom_call" | custom-call | flops 2300000000 | bytes 6899999 | tf_op jit(solution)/shard_map/leaf_backward/pallas_call | solution.py:468
  (24 shorter events, 0.1 us)
Async XLA Ops:
  0.6 7.0 %copy-start.1 = (f32[12,4,128,128]{3,2,1,0:T(8,128)S(1)}, f32[12,4,128,128]{3,2,1,0:T(8,128)}, u32[]{:S(2)}) copy-start(f32[12,4,128,128]{3,2,1,0:T(8,128)} %three.2) | copy-start | bytes 9437188
  0.6 7.0 %copy-start.7 = (s32[12,4]{0,1:T(4,128)S(1)}, s32[12,4]{0,1:T(4,128)}, u32[]{:S(2)}) copy-start(s32[12,4]{0,1:T(4,128)} %param.22) | copy-start | bytes 580
  4.5 9.1 %collective-permute-start = (f32[128,256]{1,0:T(8,128)}, f32[128,256]{1,0:T(8,128)S(1)}, u32[]{:S(2)}, u32[]{:S(2)}) collective-permute-start(f32[128,256]{1,0:T(8,128)} %get-tuple-element.21), channel_id=1, source_target_pairs={{0,14},{2,0},{4,2},{6,4},{8,6},{10,8},{12,10},{14,12},{1,15},{3,1}... | collective-permute-start | bytes 393224 | tf_op jit(solution)/shard_map/ppermute | solution.py:281
  5.0 8.9 %collective-permute-start.1 = (f32[128,256]{1,0:T(8,128)}, f32[128,256]{1,0:T(8,128)S(1)}, u32[]{:S(2)}, u32[]{:S(2)}) collective-permute-start(f32[128,256]{1,0:T(8,128)} %get-tuple-element.22), channel_id=1, source_target_pairs={{0,8},{2,10},{4,12},{6,14},{8,0},{10,2},{12,4},{14,6},{1,9},{3,11}... | collective-permute-start | bytes 393224 | tf_op jit(solution)/shard_map/ppermute | solution.py:281
  7.6 1.4 %copy-start.2 = (f32[12,128,256]{2,1,0:T(8,128)S(1)}, f32[12,128,256]{2,1,0:T(8,128)}, u32[]{:S(2)}) copy-start(f32[12,128,256]{2,1,0:T(8,128)} %get-tuple-element.23.solved) | copy-start | bytes 4718596
  9.0 0.9 %copy-start.5 = (f32[128,256]{1,0:T(8,128)S(1)}, f32[128,256]{1,0:T(8,128)}, u32[]{:S(2)}) copy-start(f32[128,256]{1,0:T(8,128)} %get-tuple-element.19.after.own) | copy-start | bytes 393220
  9.9 2.5 %copy-start.6 = (f32[128,256]{1,0:T(8,128)S(1)}, f32[128,256]{1,0:T(8,128)}, u32[]{:S(2)}) copy-start(f32[128,256]{1,0:T(8,128)} %get-tuple-element.19.after.own) | copy-start | bytes 393220
  9.9 2.5 %copy-start.13 = (f32[1,3,128,128]{3,2,1,0:T(8,128)S(1)}, f32[1,3,128,128]{3,2,1,0:T(8,128)}, u32[]{:S(2)}) copy-start(f32[1,3,128,128]{3,2,1,0:T(8,128)} %lower.2) | copy-start | bytes 589828
  9.9 2.5 %copy-start.14 = (f32[1,3,128,128]{3,2,1,0:T(8,128)S(1)}, f32[1,3,128,128]{3,2,1,0:T(8,128)}, u32[]{:S(2)}) copy-start(f32[1,3,128,128]{3,2,1,0:T(8,128)} %upper.2) | copy-start | bytes 589828
  9.9 2.5 %copy-start.17 = (f32[1,128,128]{2,1,0:T(8,128)S(1)}, f32[1,128,128]{2,1,0:T(8,128)}, u32[]{:S(2)}) copy-start(f32[1,128,128]{2,1,0:T(8,128)} %lower_inverse.2) | copy-start | bytes 196612
  9.9 2.5 %copy-start.18 = (f32[1,128,128]{2,1,0:T(8,128)S(1)}, f32[1,128,128]{2,1,0:T(8,128)}, u32[]{:S(2)}) copy-start(f32[1,128,128]{2,1,0:T(8,128)} %upper_inverse.2) | copy-start | bytes 196612
  12.5 1.4 %copy-start.15 = (f32[1,128,256]{2,1,0:T(8,128)S(1)}, f32[1,128,256]{2,1,0:T(8,128)}, u32[]{:S(2)}) copy-start(f32[1,128,256]{2,1,0:T(8,128)} %rhs.4) | copy-start | bytes 393220
  12.5 1.4 %copy-start.19 = (s32[1,3]{1,0:T(1,128)S(1)}, s32[1,3]{1,0:T(1,128)}, u32[]{:S(2)}) copy-start(s32[1,3]{1,0:T(1,128)} %param.28) | copy-start | bytes 40
  12.9 0.7 %copy-start.20 = (bf16[256,768]{1,0:T(8,128)(2,1)}, bf16[256,768]{1,0:T(8,128)(2,1)S(1)}, u32[]{:S(2)}) copy-start(bf16[256,768]{1,0:T(8,128)(2,1)S(1)} %get-tuple-element.30.operator) | copy-start | bytes 1179652
  13.9 23.9 %copy-start.12 = (f32[4,128,128]{2,1,0:T(8,128)S(1)}, f32[4,128,128]{2,1,0:T(8,128)}, u32[]{:S(2)}) copy-start(f32[4,128,128]{2,1,0:T(8,128)} %upper_inverse.3) | copy-start | bytes 786436
  14.8 0.7 %copy-start.22 = (f32[128,256]{1,0:T(8,128)}, f32[128,256]{1,0:T(8,128)S(1)}, u32[]{:S(2)}) copy-start(f32[128,256]{1,0:T(8,128)S(1)} %get-tuple-element.31.solved) | copy-start | bytes 393220
  15.5 22.4 %copy-start.8 = (f32[512,512]{1,0:T(8,128)S(1)}, f32[512,512]{1,0:T(8,128)}, u32[]{:S(2)}) copy-start(f32[512,512]{1,0:T(8,128)} %lower.3) | copy-start | bytes 3145732
  15.5 22.4 %copy-start.9 = (f32[512,512]{1,0:T(8,128)S(1)}, f32[512,512]{1,0:T(8,128)}, u32[]{:S(2)}) copy-start(f32[512,512]{1,0:T(8,128)} %upper.3) | copy-start | bytes 3145732
  15.5 22.4 %copy-start.11 = (f32[4,128,128]{2,1,0:T(8,128)S(1)}, f32[4,128,128]{2,1,0:T(8,128)}, u32[]{:S(2)}) copy-start(f32[4,128,128]{2,1,0:T(8,128)} %lower_inverse.3) | copy-start | bytes 786436
  15.5 1.5 %collective-permute-start.2 = (f32[4,128,128]{2,1,0:T(8,128)S(1)}, f32[4,128,128]{2,1,0:T(8,128)S(1)}, u32[]{:S(2)}, u32[]{:S(2)}) collective-permute-start(f32[4,128,128]{2,1,0:T(8,128)S(1)} %get-tuple-element.25), channel_id=1, source_target_pairs={{0,1},{1,0},{2,3},{3,2},{4,5},{5,4},{6,7},{7,6},{8,9},{9,8},{10,11... | collective-permute-start | bytes 786440 | tf_op jit(solution)/shard_map/ppermute | solution.py:287
  17.6 6.7 %collective-permute-start.3 = (f32[128,128]{1,0:T(8,128)S(1)}, f32[128,128]{1,0:T(8,128)S(1)}, u32[]{:S(2)}, u32[]{:S(2)}) collective-permute-start(f32[128,128]{1,0:T(8,128)S(1)} %get-tuple-element.27), channel_id=1, source_target_pairs={{0,2},{2,0},{4,6},{6,4},{8,10},{10,8},{12,14},{14,12},{1,3},{3,1},... | collective-permute-start | bytes 196616 | tf_op jit(solution)/shard_map/ppermute | solution.py:284
  22.0 4.6 %collective-permute-start.4 = (f32[128,128]{1,0:T(8,128)S(1)}, f32[128,128]{1,0:T(8,128)S(1)}, u32[]{:S(2)}, u32[]{:S(2)}) collective-permute-start(f32[128,128]{1,0:T(8,128)S(1)} %get-tuple-element.28), channel_id=1, source_target_pairs={{0,4},{2,6},{4,0},{6,2},{8,12},{10,14},{12,8},{14,10},{1,5},{3,7},... | collective-permute-start | bytes 196616 | tf_op jit(solution)/shard_map/ppermute | solution.py:284
  22.8 5.2 %collective-permute-start.5 = (f32[128,128]{1,0:T(8,128)S(1)}, f32[128,128]{1,0:T(8,128)S(1)}, u32[]{:S(2)}, u32[]{:S(2)}) collective-permute-start(f32[128,128]{1,0:T(8,128)S(1)} %get-tuple-element.29), channel_id=1, source_target_pairs={{0,6},{2,4},{4,2},{6,0},{8,14},{10,12},{12,10},{14,8},{1,7},{3,5},... | collective-permute-start | bytes 196616 | tf_op jit(solution)/shard_map/ppermute | solution.py:284
  28.0 6.3 %collective-permute-start.6 = (f32[128,128]{1,0:T(8,128)S(1)}, f32[128,128]{1,0:T(8,128)S(1)}, u32[]{:S(2)}, u32[]{:S(2)}) collective-permute-start(f32[128,128]{1,0:T(8,128)S(1)} %add_add_fusion.after), channel_id=1, source_target_pairs={{0,8},{2,10},{4,12},{6,14},{8,0},{10,2},{12,4},{14,6},{1,9},{3,11}... | collective-permute-start | bytes 196616 | tf_op jit(solution)/shard_map/ppermute | solution.py:284
  34.3 6.9 %copy-start.10 = (f32[4,128,256]{2,1,0:T(8,128)S(1)}, f32[4,128,256]{2,1,0:T(8,128)}, u32[]{:S(2)}) copy-start(f32[4,128,256]{2,1,0:T(8,128)} %rhs.5) | copy-start | bytes 1572868
  34.3 6.9 %collective-permute-start.7 = (f32[128,128]{1,0:T(8,128)S(1)}, f32[128,128]{1,0:T(8,128)S(1)}, u32[]{:S(2)}, u32[]{:S(2)}) collective-permute-start(f32[128,128]{1,0:T(8,128)S(1)} %add.20.own), channel_id=1, source_target_pairs={{0,2},{2,0},{4,6},{6,4},{8,10},{10,8},{12,14},{14,12},{1,3},{3,1},... | collective-permute-start | bytes 196616 | tf_op jit(solution)/shard_map/ppermute | solution.py:284
  34.4 6.8 %collective-permute-start.8 = (f32[128,128]{1,0:T(8,128)S(1)}, f32[128,128]{1,0:T(8,128)S(1)}, u32[]{:S(2)}, u32[]{:S(2)}) collective-permute-start(f32[128,128]{1,0:T(8,128)S(1)} %add.20.own), channel_id=1, source_target_pairs={{0,4},{2,6},{4,0},{6,2},{8,12},{10,14},{12,8},{14,10},{1,5},{3,7},... | collective-permute-start | bytes 196616 | tf_op jit(solution)/shard_map/ppermute | solution.py:284
  35.4 5.7 %collective-permute-start.9 = (f32[128,128]{1,0:T(8,128)S(1)}, f32[128,128]{1,0:T(8,128)S(1)}, u32[]{:S(2)}, u32[]{:S(2)}) collective-permute-start(f32[128,128]{1,0:T(8,128)S(1)} %add.20.own), channel_id=1, source_target_pairs={{0,6},{2,4},{4,2},{6,0},{8,14},{10,12},{12,10},{14,8},{1,7},{3,5},... | collective-permute-start | bytes 196616 | tf_op jit(solution)/shard_map/ppermute | solution.py:284
  37.8 4.7 %copy-start.4 = (f32[12,128,128]{2,1,0:T(8,128)S(1)}, f32[12,128,128]{2,1,0:T(8,128)}, u32[]{:S(2)}) copy-start(f32[12,128,128]{2,1,0:T(8,128)} %inverse.5) | copy-start | bytes 2359300
  41.1 1.9 %copy-start = (f32[12,4,128,128]{3,2,1,0:T(8,128)S(1)}, f32[12,4,128,128]{3,2,1,0:T(8,128)}, u32[]{:S(2)}) copy-start(f32[12,4,128,128]{3,2,1,0:T(8,128)} %three.3) | copy-start | bytes 9437188
  42.5 1.6 %copy-start.21 = (bf16[256,768]{1,0:T(8,128)(2,1)S(1)}, bf16[256,768]{1,0:T(8,128)(2,1)}, u32[]{:S(2)}) copy-start(bf16[256,768]{1,0:T(8,128)(2,1)} %copy-done.20) | copy-start | bytes 1179652
  42.5 1.6 %copy-start.23 = (f32[128,256]{1,0:T(8,128)S(1)}, f32[128,256]{1,0:T(8,128)}, u32[]{:S(2)}) copy-start(f32[128,256]{1,0:T(8,128)} %copy-done.22) | copy-start | bytes 393220
  42.5 1.6 %collective-permute-start.10 = (f32[4,128,128]{2,1,0:T(8,128)S(1)}, f32[4,128,128]{2,1,0:T(8,128)S(1)}, u32[]{:S(2)}, u32[]{:S(2)}) collective-permute-start(f32[4,128,128]{2,1,0:T(8,128)S(1)} %root_solve.1.mine), channel_id=1, source_target_pairs={{0,1},{1,0},{2,3},{3,2},{4,5},{5,4},{6,7},{7,6},{8,9},{9,8},{10,11... | collective-permute-start | bytes 786440 | tf_op jit(solution)/shard_map/ppermute | solution.py:287
  44.1 5.6 %copy-start.3 = (f32[12,128,256]{2,1,0:T(8,128)S(1)}, f32[12,128,256]{2,1,0:T(8,128)}, u32[]{:S(2)}) copy-start(f32[12,128,256]{2,1,0:T(8,128)} %get-tuple-element.23.solved) | copy-start | bytes 4718596
  45.7 6.8 %collective-permute-start.11 = (f32[128,256]{1,0:T(8,128)}, f32[128,256]{1,0:T(8,128)S(1)}, u32[]{:S(2)}, u32[]{:S(2)}) collective-permute-start(f32[128,256]{1,0:T(8,128)} %bitcast.9), channel_id=1, source_target_pairs={{0,2},{2,4},{4,6},{6,8},{8,10},{10,12},{12,14},{14,0},{1,3},{3,5},... | collective-permute-start | bytes 393224 | tf_op jit(solution)/shard_map/ppermute | solution.py:281
  47.5 11.4 %collective-permute-start.12 = (f32[128,256]{1,0:T(8,128)}, f32[128,256]{1,0:T(8,128)S(1)}, u32[]{:S(2)}, u32[]{:S(2)}) collective-permute-start(f32[128,256]{1,0:T(8,128)} %bitcast.10), channel_id=1, source_target_pairs={{0,8},{2,10},{4,12},{6,14},{8,0},{10,2},{12,4},{14,6},{1,9},{3,11}... | collective-permute-start | bytes 393224 | tf_op jit(solution)/shard_map/ppermute | solution.py:281
  49.7 9.2 %copy-start.16 = (f32[1,128,256]{2,1,0:T(8,128)S(1)}, f32[1,128,256]{2,1,0:T(8,128)}, u32[]{:S(2)}) copy-start(f32[1,128,256]{2,1,0:T(8,128)} %get-tuple-element.17.own) | copy-start | bytes 393220

commit v3 on v2

v3 whole, which is shorter than its diff:
```python
import functools

import jax
import jax.numpy as jnp
from jax import lax
from jax.experimental import pallas as pl
from jax.experimental.pallas import tpu as pltpu
from jax.sharding import PartitionSpec as P

VMEM = pltpu.VMEM
SMEM = pltpu.SMEM
F32 = jnp.float32
BF16 = jnp.bfloat16


def parts_of(x):
    high = x.astype(BF16)
    low = (x - high.astype(F32)).astype(BF16)
    return high, low


def as_left(x):
    high, low = parts_of(x)
    count = x.shape[1] // 128
    pieces = [slice(j * 128, j * 128 + 128) for j in range(count)]
    top = jnp.concatenate([high[:, s] for s in pieces for _ in range(2)], axis=1)
    bottom = jnp.concatenate([low[:, s] for s in pieces for _ in range(2)], axis=1)
    return jnp.concatenate([top, bottom], axis=0)


def as_right(x):
    high, low = parts_of(x)
    count = x.shape[0] // 128
    pieces = [slice(j * 128, j * 128 + 128) for j in range(count)]
    return jnp.concatenate([y[s] for s in pieces for y in (high, low)], axis=0)


def left_times(left, right):
    both = jnp.dot(left, right, preferred_element_type=F32)
    rows = left.shape[0] // 2
    return both[:rows] + both[rows:]


def times(a, b):
    return left_times(as_left(a), as_right(b))


def cost(microseconds):
    return pl.CostEstimate(
        flops=int(microseconds * 1e9),
        bytes_accessed=int(microseconds * 3e6),
        transcendentals=0,
    )


def forward_leaf_kernel(links, rhs, inverse, first, solved, own, near, far, pending):
    step = pl.program_id(0)

    @pl.when(step == 0)
    def _():
        pending[...] = jnp.zeros_like(pending)

    batch = rhs.shape[0]
    values = []
    for i in range(batch):
        value = times(inverse[i], rhs[i])
        solved[i] = value
        values.append(value)
    for i in range(batch):
        pending[links[0, step * batch + i]] += times(first[i, 0], values[i])

    @pl.when(step == pl.num_programs(0) - 1)
    def _():
        own[...] = pending[0]
        near[...] = pending[1]
        far[...] = pending[2]


def root_terms_kernel(links, one, two, three, solved, pending):
    step = pl.program_id(0)

    @pl.when(step == 0)
    def _():
        pending[...] = jnp.zeros_like(pending)

    batch = solved.shape[0]
    for i in range(batch):
        blocks = jnp.concatenate([one[i, 0], two[i, 0], three[i, 0]], axis=0)
        terms = times(blocks, solved[i])
        for n in range(3):
            slot = links[n + 1, step * batch + i] - 3
            pending[slot] += terms[n * 128 : n * 128 + 128]


def root_sweeps_kernel(lower_inverse, upper_inverse, lower, upper, after, forward, backward):
    count = lower_inverse.shape[0]
    w = lower_inverse.shape[1]
    forward[...] = jnp.zeros_like(forward)
    backward[...] = jnp.zeros_like(backward)
    for step in range(count):
        r = step
        here = slice(r * w, r * w + w)
        forward[here, here] = lower_inverse[r]
        if step > 0:
            done = slice(0, r * w)
            inner = times(lower[here, done], forward[done, done])
            forward[here, done] = -times(lower_inverse[r], inner)
        r = count - 1 - step
        here = slice(r * w, r * w + w)
        backward[here, here] = upper_inverse[r]
        if step > 0:
            done = slice((r + 1) * w, count * w)
            inner = times(upper[here, done], backward[done, done])
            backward[here, done] = -times(upper_inverse[r], inner)


def root_operator_kernel(forward, backward, after, root_operator):
    w = 128
    size = forward.shape[0]
    for r in range(0, size, w):
        left = as_left(times(backward[r : r + w, r:], forward[r:, :]))
        root_operator[r : r + w, :] = left[:w]
        root_operator[size + r : size + r + w, :] = left[w:]


def separator_operators_kernel(
    lower_inverse, upper_inverse, lower, upper, after, forward, part, backward
):
    blocks = jnp.concatenate([lower[0, n] for n in range(3)], axis=0)
    forward[...] = as_left(times(blocks, lower_inverse[0]))
    part[...] = as_left(times(upper_inverse[0], lower_inverse[0]))
    blocks = jnp.concatenate([upper[0, n] for n in range(3)], axis=1)
    backward[...] = as_left(times(upper_inverse[0], blocks))


def separator_kernel(
    links, place, rhs, operator, own, near, far, root_pending, right, mine, theirs, sums
):
    right[...] = as_right(rhs[0] - own[...] - near[...] - far[...])
    terms = left_times(operator[...], right[...])
    sums[...] = root_pending[...]
    for n in range(3):
        sums[links[n]] += terms[n * 128 : n * 128 + 128]
    position = place[0]
    is_first = place[1] == 0
    for j in range(4):
        block = sums[position ^ j]
        first, second = block[:, :128], block[:, 128:]
        mine[j] = jnp.where(is_first, first, second)
        theirs[j] = jnp.where(is_first, second, first)


def separator_part_kernel(operator, right, out):
    out[...] = left_times(operator[...], right[...])


def root_kernel(place, rhs, operator, own, one, two, three, out, pending):
    count, w = rhs.shape[0], rhs.shape[1]
    position = place[0]
    is_first = place[1] == 0
    for j, piece in enumerate((own, one, two, three)):
        root = position ^ j
        right = rhs[root]
        right = jnp.where(is_first, right[:, :128], right[:, 128:])
        pending[pl.ds(pl.multiple_of(root * 2 * w, 2 * w), 2 * w), :] = as_right(
            right - piece[...]
        )
    out[...] = left_times(operator[...], pending[...]).reshape(count, w, 128)


def separator_back_kernel(links, core, mine, theirs, operator, part, right, out):
    is_first = core[0] == 0
    for r in range(mine.shape[0]):
        one, other = as_right(mine[r]), as_right(theirs[r])
        right[r, :, :128] = jnp.where(is_first, one, other)
        right[r, :, 128:] = jnp.where(is_first, other, one)
    linked = jnp.concatenate([right[links[n]] for n in range(3)], axis=0)
    out[...] = part[...] - left_times(operator[...], linked)


def leaf_operator_kernel(inverse, first, after, operator):
    for i in range(inverse.shape[0]):
        operator[i] = as_left(times(inverse[i], first[i, 0]))


def leaf_root_part_kernel(
    links,
    core,
    one,
    two,
    three,
    inverse,
    solved,
    root_right,
    mine,
    theirs,
    sep_sol,
    part,
    root_sol,
    sep_rows,
):
    step = pl.program_id(0)

    @pl.when(step == 0)
    def _():
        is_first = core[0] == 0
        sep_rows[0] = sep_sol[...]
        root_sol[:, :, :128] = jnp.where(is_first, mine[...], theirs[...])
        root_sol[:, :, 128:] = jnp.where(is_first, theirs[...], mine[...])

    batch = solved.shape[0]
    rests = []
    for i in range(batch):
        leaf = step * batch + i
        blocks = jnp.concatenate([one[i, 0], two[i, 0], three[i, 0]], axis=1)
        linked = jnp.concatenate([root_right[links[n, leaf] - 3] for n in (1, 2, 3)], axis=0)
        rests.append(solved[i] - left_times(as_left(blocks), linked))
    for i in range(batch):
        part[i] = times(inverse[i], rests[i])


def leaf_final_kernel(links, operator, part, own, near, far, out, seps, ready, sems):
    seps[0] = as_right(own[...])
    seps[1] = as_right(near[...])
    seps[2] = as_right(far[...])
    count = part.shape[0]
    copies = []
    for i in range(count):
        ready[i] = part[i] - left_times(operator[i], seps[links[0, i]])
        if i % 2 == 1:
            pair = pl.ds(i - 1, 2)
            copy = pltpu.make_async_copy(ready.at[pair], out.at[pair], sems.at[i // 2])
            copy.start()
            copies.append(copy)
    for copy in copies:
        copy.wait()


def whole(memory=VMEM):
    return pl.BlockSpec(memory_space=memory)


ANY = pl.BlockSpec(memory_space=pl.ANY)


def limit(megabytes):
    return pltpu.CompilerParams(vmem_limit_bytes=megabytes * 1024 * 1024)


def leafwise(batch, *tail):
    return pl.BlockSpec((batch,) + tail, lambda k: (k,) + (0,) * len(tail))


def link(batch, n, w):
    return pl.BlockSpec((batch, 1, w, w), lambda k: (k, n, 0, 0))


def kept(*shape):
    return pl.BlockSpec(shape, lambda k: (0,) * len(shape))


def per_device(
    leaf_rhs,
    leaf_lower_inverse,
    leaf_upper_inverse,
    leaf_lower,
    leaf_upper,
    leaf_rows,
    separator_right_sides,
    separator_lower_inverse,
    separator_upper_inverse,
    separator_lower_blocks,
    sep_upper,
    sep_rows,
    root_rhs,
    root_lower_inverse,
    root_upper_inverse,
    root_lower,
    root_upper,
):
    peers = lax.axis_size("grid")
    leaves, w, columns = leaf_rhs.shape
    roots = root_rhs.shape[0]
    half = columns // 2
    batch = leaves // 2
    position = lax.axis_index("grid") % 4
    core = lax.axis_index("layer")
    core_ref = core.astype(jnp.int32).reshape(1)
    place = jnp.stack([position, core]).astype(jnp.int32)
    leaf_links = leaf_rows.T
    sep_links = sep_rows.reshape(-1)

    def shifted(x, by):
        return lax.ppermute(x, "grid", [(i, (i + by) % peers) for i in range(peers)])

    def crossed(x, bit):
        return lax.ppermute(x, "grid", [(i, i ^ bit) for i in range(peers)])

    def swapped(x):
        return lax.ppermute(x, "layer", [(0, 1), (1, 0)])

    shape = jax.ShapeDtypeStruct

    leaf_solved, own, near, far = pl.pallas_call(
        forward_leaf_kernel,
        grid=(leaves // batch,),
        in_specs=[
            whole(SMEM),
            leafwise(batch, w, columns),
            leafwise(batch, w, w),
            link(batch, 0, w),
        ],
        out_specs=[leafwise(batch, w, columns)] + [kept(w, columns)] * 3,
        out_shape=[shape((leaves, w, columns), F32)] + [shape((w, columns), F32)] * 3,
        scratch_shapes=[VMEM((3, w, columns), F32)],
        compiler_params=limit(56),
        cost_estimate=cost(4),
        name="leaf_forward",
    )(leaf_links, leaf_rhs, leaf_lower_inverse, leaf_lower)

    far_sum = shifted(far, -(peers // 2))
    near_sum = shifted(near, -1)

    root_pending = pl.pallas_call(
        root_terms_kernel,
        grid=(leaves // batch,),
        in_specs=[
            whole(SMEM),
            link(batch, 1, w),
            link(batch, 2, w),
            link(batch, 3, w),
            leafwise(batch, w, columns),
        ],
        out_specs=kept(roots, w, columns),
        out_shape=shape((roots, w, columns), F32),
        compiler_params=limit(16),
        cost_estimate=cost(3),
        name="root_terms",
    )(leaf_links, leaf_lower, leaf_lower, leaf_lower, leaf_solved)

    sep_forward, sep_part, sep_backward = pl.pallas_call(
        separator_operators_kernel,
        in_specs=[whole()] * 4 + [ANY],
        out_specs=[whole()] * 3,
        out_shape=[
            shape((6 * w, 2 * w), BF16),
            shape((2 * w, 2 * w), BF16),
            shape((2 * w, 6 * w), BF16),
        ],
        compiler_params=limit(16),
        cost_estimate=cost(1),
        name="separator_operators",
    )(
        separator_lower_inverse,
        separator_upper_inverse,
        separator_lower_blocks,
        sep_upper,
        leaf_solved,
    )

    sep_right, mine, theirs = pl.pallas_call(
        separator_kernel,
        in_specs=[whole(SMEM), whole(SMEM)] + [whole()] * 6,
        out_specs=[whole()] * 3,
        out_shape=[
            shape((2 * w, columns), BF16),
            shape((roots, w, half), F32),
            shape((roots, w, half), F32),
        ],
        scratch_shapes=[VMEM((roots, w, columns), F32)],
        compiler_params=limit(16),
        cost_estimate=cost(2),
        name="separator_forward",
    )(
        sep_links,
        place,
        separator_right_sides,
        sep_forward,
        own,
        near_sum,
        far_sum,
        root_pending,
    )

    other = swapped(theirs)
    sep_solved = pl.pallas_call(
        separator_part_kernel,
        in_specs=[whole()] * 2,
        out_specs=whole(),
        out_shape=shape((w, columns), F32),
        compiler_params=limit(16),
        cost_estimate=cost(0.4),
        name="separator_part",
    )(sep_part, sep_right)
    pieces = [mine[j] + other[j] for j in range(4)]
    forward, backward = pl.pallas_call(
        root_sweeps_kernel,
        in_specs=[whole()] * 4 + [ANY],
        out_specs=[whole()] * 2,
        out_shape=[shape((roots * w, roots * w), F32)] * 2,
        compiler_params=limit(16),
        cost_estimate=cost(2.3),
        name="root_sweeps",
    )(root_lower_inverse, root_upper_inverse, root_lower, root_upper, pieces[1])
    arrived = [crossed(pieces[j], j) for j in (1, 2, 3)]
    arrived, forward, backward = lax.optimization_barrier((arrived, forward, backward))
    total = pieces[0] + arrived[0] + arrived[1] + arrived[2]

    root_operator = pl.pallas_call(
        root_operator_kernel,
        in_specs=[whole()] * 2 + [ANY],
        out_specs=whole(),
        out_shape=shape((2 * roots * w, 2 * roots * w), BF16),
        compiler_params=limit(16),
        cost_estimate=cost(1),
        name="root_operator",
    )(forward, backward, total)

    bit = 4
    while bit < peers:
        arrived = crossed(total, bit)
        if bit == 4:
            arrived, root_operator = lax.optimization_barrier((arrived, root_operator))
        total = total + arrived
        bit *= 2
    others = [crossed(total, j) for j in (1, 2, 3)]

    solution_half = pl.pallas_call(
        root_kernel,
        in_specs=[whole(SMEM)] + [whole()] * 6,
        out_specs=whole(),
        out_shape=shape((roots, w, half), F32),
        scratch_shapes=[VMEM((2 * roots * w, half), BF16)],
        compiler_params=limit(16),
        cost_estimate=cost(1),
        name="root_solve",
    )(place, root_rhs, root_operator, total, *others)

    other_half = swapped(solution_half)

    root_right, sep_sol = pl.pallas_call(
        separator_back_kernel,
        in_specs=[whole(SMEM), whole(SMEM)] + [whole()] * 4,
        out_specs=[whole()] * 2,
        out_shape=[shape((roots, 2 * w, columns), BF16), shape((w, columns), F32)],
        compiler_params=limit(16),
        cost_estimate=cost(1.5),
        name="separator_backward",
    )(sep_links, core_ref, solution_half, other_half, sep_backward, sep_solved)

    far_rows = shifted(sep_sol, peers // 2)
    near_rows = shifted(sep_sol, 1)

    leaf_operator = pl.pallas_call(
        leaf_operator_kernel,
        grid=(leaves // batch,),
        in_specs=[leafwise(batch, w, w), link(batch, 0, w), ANY],
        out_specs=leafwise(batch, 2 * w, 2 * w),
        out_shape=shape((leaves, 2 * w, 2 * w), BF16),
        compiler_params=limit(16),
        cost_estimate=cost(1),
        name="leaf_operators",
    )(leaf_upper_inverse, leaf_upper, sep_sol)

    leaf_part, root_sol, separator_solution_rows = pl.pallas_call(
        leaf_root_part_kernel,
        grid=(leaves // batch,),
        in_specs=[
            whole(SMEM),
            whole(SMEM),
            link(batch, 1, w),
            link(batch, 2, w),
            link(batch, 3, w),
            leafwise(batch, w, w),
            leafwise(batch, w, columns),
            kept(roots, 2 * w, columns),
            kept(roots, w, half),
            kept(roots, w, half),
            kept(w, columns),
        ],
        out_specs=[
            leafwise(batch, w, columns),
            kept(roots, w, columns),
            kept(1, w, columns),
        ],
        out_shape=[
            shape((leaves, w, columns), F32),
            shape((roots, w, columns), F32),
            shape((1, w, columns), F32),
        ],
        compiler_params=limit(16),
        cost_estimate=cost(3),
        name="leaf_root_part",
    )(
        leaf_links,
        core_ref,
        leaf_upper,
        leaf_upper,
        leaf_upper,
        leaf_upper_inverse,
        leaf_solved,
        root_right,
        solution_half,
        other_half,
        sep_sol,
    )

    leaf_sol = pl.pallas_call(
        leaf_final_kernel,
        in_specs=[whole(SMEM)] + [whole()] * 5,
        out_specs=ANY,
        out_shape=shape((leaves, w, columns), F32),
        scratch_shapes=[
            VMEM((3, 2 * w, columns), BF16),
            VMEM((leaves, w, columns), F32),
            pltpu.SemaphoreType.DMA((leaves // 2,)),
        ],
        compiler_params=limit(16),
        cost_estimate=cost(2),
        name="leaf_backward",
    )(leaf_links, leaf_operator, leaf_part, sep_sol, near_rows, far_rows)
    return (leaf_sol, separator_solution_rows, root_sol)


def solution(mesh):
    by_device = P(("groups", "grid", "layer"))
    by_group = P("groups")
    return jax.shard_map(
        per_device,
        mesh=mesh,
        in_specs=(by_device,) * 12 + (by_group,) * 5,
        out_specs=(by_device, by_device, by_group),
        check_vma=False,
    )
```

time: 61.6 us -> 57.7 us (0.937)
  local copies, waits for them, and re-layouts: 4.22 us -> 1.5 us
  starting transfers between devices: 20 us -> 18.8 us
  waiting for transfers between devices: 15.8 us -> 16.9 us
  Pallas kernels: 20.2 us -> 19.2 us
    unnamed x48 -> x36, local copies, waits for them, and re-layouts: 4.22 us -> 1.5 us
    ppermute x7, starting transfers between devices: 12.8 us -> 11.5 us  [crossed(): return lax.ppermute(x, 'grid', [(i, i ^ bit) for i in range(peers)])]
    ppermute x2, waiting for transfers between devices: 1.69 us -> 2.85 us  [swapped(): return lax.ppermute(x, 'layer', [(0, 1), (1, 0)])]
    ppermute x4, waiting for transfers between devices: 6.7 us -> 5.63 us  [shifted(): lax.ppermute(x, 'grid', [(i, (i + by) % peers) for i in range(peers)])]
    ppermute x7, waiting for transfers between devices: 7.39 us -> 8.38 us  [crossed(): return lax.ppermute(x, 'grid', [(i, i ^ bit) for i in range(peers)])]
    pallas_call x3 -> x4, Pallas kernels: 6.14 us -> 5.15 us  [the longest x1 2.06 us: per_device(): pl.pallas_call(leaf_final_kernel, in_specs=[whole(SMEM)] + [whole()] * 5,...]
    pallas_call x1, Pallas kernels: 2.74 us -> 3.47 us  [per_device(): pl.pallas_call(leaf_root_part_kernel, grid=(leaves // batch,), in_specs=[...]
    pallas_call x1, Pallas kernels: 1.59 us -> 0.93 us  [per_device(): pl.pallas_call(separator_back_kernel, in_specs=[whole(SMEM), whole(SMEM)]...]
  transfers between devices with their start and end apart: 13 -> 13, of which waited for: 8 -> 10; matrix products, arithmetic and copies ran while one was open for 0% -> 0% of each run, Pallas kernels for 16% -> 18%
where the time goes in v3:
time: 57.7 us; the launch traced here: 57.4 us
  Pallas kernels  19.2 us (33%)
  starting transfers between devices  18.8 us (33%)
  waiting for transfers between devices  16.9 us (29%)
  local copies, waits for them, and re-layouts  1.5 us (3%)
  between operations  0.91 us (2%)
    ppermute x7, starting transfers between devices, crossed(): return lax.ppermute(x, 'grid', [(i, i ^ bit) for i in range(peers)])  11.5 us
    ppermute x7, waiting for transfers between devices, crossed(): return lax.ppermute(x, 'grid', [(i, i ^ bit) for i in range(peers)])  8.38 us
    ppermute x4, starting transfers between devices, shifted(): lax.ppermute(x, 'grid', [(i, (i + by) % peers) for i in range(peers)])  7.16 us
    ppermute x4, waiting for transfers between devices, shifted(): lax.ppermute(x, 'grid', [(i, (i + by) % peers) for i in range(peers)])  5.63 us
    pallas_call x1, Pallas kernels, per_device(): pl.pallas_call(forward_leaf_kernel, grid=(leaves // batch,), in_specs=[wh...  3.83 us
    pallas_call x1, Pallas kernels, per_device(): pl.pallas_call(leaf_root_part_kernel, grid=(leaves // batch,), in_specs=[...  3.47 us
    ppermute x2, waiting for transfers between devices, swapped(): return lax.ppermute(x, 'layer', [(0, 1), (1, 0)])  2.85 us
    pallas_call x1, Pallas kernels, per_device(): pl.pallas_call(root_terms_kernel, grid=(leaves // batch,), in_specs=[whol...  2.45 us
  transfers between devices with their start and end apart: 13, of which 10 were waited for; matrix products, arithmetic and copies ran while one was open for 0% of the time, Pallas kernels for 18%

profile of v3, /device:TPU:6, one launch (start us, length us, event | category | flops | bytes accessed | tf_op | source)
XLA Modules:
  0.0 57.4 jit_solution(3052558057859996272)
XLA Ops:
  0.6 0.0 copy-start.1
  0.6 0.0 copy-start.5
  0.7 3.8 %leaf_forward.1 = (f32[12,128,256]{2,1,0:T(8,128)}, f32[128,256]{1,0:T(8,128)}, f32[128,256]{1,0:T(8,128)}, f32[128,256]{1,0:T(8,128)}) custom-call(s32[4,12]{1,0:T(4,128)} %bitcast.18, f32[12,128,256]{2,1,0:T(8,128)} %rhs.3, f32[12,128,128]{2,1,0:T(8,128)} %inverse.3, f32[12,4,128,128]{3,2,1,0:T(8,128)} %three.2), custom_call_target="tpu_custom_call" | custom-call | flops 4000000000 | bytes 12000000 | tf_op jit(solution)/shard_map/leaf_forward/pallas_call | solution.py:304
  4.5 0.5 collective-permute-start
  5.0 2.6 %collective-permute-start.1 = (f32[128,256]{1,0:T(8,128)}, f32[128,256]{1,0:T(8,128)S(1)}, u32[]{:S(2)}, u32[]{:S(2)}) collective-permute-start(f32[128,256]{1,0:T(8,128)} %get-tuple-element.31), channel_id=1, source_target_pairs={{0,8},{2,10},{4,12},{6,14},{8,0},{10,2},{12,4},{14,6},{1,9},{3,11}... | collective-permute-start | bytes 393224 | tf_op jit(solution)/shard_map/ppermute | solution.py:294
  7.6 0.0 copy-done.1
  7.6 0.0 copy-done.5
  7.6 1.4 %copy-done.2 = f32[12,128,256]{2,1,0:T(8,128)S(1)} copy-done((f32[12,128,256]{2,1,0:T(8,128)S(1)}, f32[12,128,256]{2,1,0:T(8,128)}, u32[]{:S(2)}) %copy-start.2) | copy-done | bytes 1572888
  9.0 0.0 copy-start.15
  9.0 2.4 %root_terms.1.root_pending = f32[4,128,256]{2,1,0:T(8,128)S(1)} custom-call(s32[4,12]{1,0:T(4,128)S(1)} %bitcast.19, f32[12,4,128,128]{3,2,1,0:T(8,128)S(1)} %copy-done.1, f32[12,4,128,128]{3,2,1,0:T(8,128)S(1)} %copy-done.1, f32[12,4,128,128]{3,2,1,0:T(8,128)S(1)} %copy-done.1, f32[12,128,256]{2,1,0:T(8,128)S(1)} %copy-done.2), custom_call_target="tpu_custom_call" | custom-call | flops 3000000000 | bytes 9000000 | tf_op jit(solution)/shard_map/root_terms/pallas_call | solution.py:324
  11.5 0.0 copy-done.3
  11.5 0.0 copy-done.11
  11.5 0.0 copy-done.12
  11.5 0.0 copy-done.14
  11.5 0.0 copy-done.15
  11.6 0.0 copy-start.13
  11.6 0.0 copy-start.16
  11.6 0.0 copy-start.17
  11.6 0.4 separator_operators.1
  12.0 0.1 pad_add_fusion.place
  12.0 0.0 collective-permute-done.near
  12.1 1.8 %collective-permute-done.1.far = f32[128,256]{1,0:T(8,128)S(1)} collective-permute-done((f32[128,256]{1,0:T(8,128)}, f32[128,256]{1,0:T(8,128)S(1)}, u32[]{:S(2)}, u32[]{:S(2)}) %collective-permute-start.1) | collective-permute-done | bytes 131104 | tf_op jit(solution)/shard_map/ppermute | solution.py:294
  13.9 0.0 copy-done.13
  13.9 0.0 copy-done.16
  13.9 0.0 copy-done.17
  13.9 0.0 copy-start.6
  13.9 0.0 copy-start.7
  13.9 0.0 copy-start.9
  13.9 0.0 copy-start.10
  14.0 0.9 %separator_forward.1 = (bf16[256,256]{1,0:T(8,128)(2,1)S(1)}, f32[4,128,128]{2,1,0:T(8,128)S(1)}, f32[4,128,128]{2,1,0:T(8,128)S(1)}) custom-call(s32[3]{0:T(128)S(1)} %bitcast.22, s32[2]{0:T(128)S(1)} %pad_add_fusion.place, f32[1,128,256]{2,1,0:T(8,128)S(1)} %copy-done.13, bf16[768,256]{1,0:T(8,128)(2,1)S(1)} %get-tuple-element.28.operator, ...), custom_call_target="tpu_custom_call" | custom-call | flops 2000000000 | bytes 6000000 | tf_op jit(solution)/shard_map/separator_forward/pallas_call | solution.py:361
  14.8 0.1 collective-permute-start.2
  14.9 1.5 %collective-permute-done.2 = f32[4,128,128]{2,1,0:T(8,128)S(1)} collective-permute-done((f32[4,128,128]{2,1,0:T(8,128)S(1)}, f32[4,128,128]{2,1,0:T(8,128)S(1)}, u32[]{:S(2)}, u32[]{:S(2)}) %collective-permute-start.2) | collective-permute-done | bytes 262176 | tf_op jit(solution)/shard_map/ppermute | solution.py:300
  16.5 4.6 %collective-permute-start.5 = (f32[128,128]{1,0:T(8,128)S(1)}, f32[128,128]{1,0:T(8,128)S(1)}, u32[]{:S(2)}, u32[]{:S(2)}) collective-permute-start(f32[128,128]{1,0:T(8,128)S(1)} %get-tuple-element.51), channel_id=1, source_target_pairs={{0,6},{2,4},{4,2},{6,0},{8,14},{10,12},{12,10},{14,8},{1,7},{3,5},... | collective-permute-start | bytes 196616 | tf_op jit(solution)/shard_map/ppermute | solution.py:297
  21.1 1.2 %collective-permute-start.4 = (f32[128,128]{1,0:T(8,128)S(1)}, f32[128,128]{1,0:T(8,128)S(1)}, u32[]{:S(2)}, u32[]{:S(2)}) collective-permute-start(f32[128,128]{1,0:T(8,128)S(1)} %get-tuple-element.52), channel_id=1, source_target_pairs={{0,4},{2,6},{4,0},{6,2},{8,12},{10,14},{12,8},{14,10},{1,5},{3,7},... | collective-permute-start | bytes 196616 | tf_op jit(solution)/shard_map/ppermute | solution.py:297
  22.3 0.0 collective-permute-start.3
  22.3 0.0 copy-done.6
  22.3 0.0 copy-done.7
  22.3 0.0 copy-done.9
  22.3 2.0 %root_sweeps.1 = (f32[512,512]{1,0:T(8,128)S(1)}, f32[512,512]{1,0:T(8,128)S(1)}) custom-call(f32[4,128,128]{2,1,0:T(8,128)S(1)} %copy-done.9, f32[4,128,128]{2,1,0:T(8,128)S(1)} %copy-done.10, f32[512,512]{1,0:T(8,128)S(1)} %copy-done.6, f32[512,512]{1,0:T(8,128)S(1)} %copy-done.7, f32[128,128]{1,0:T(8,128)S(1)} %get-tuple-element.53.after), custom_call_target="tpu_custom_call" | custom-call | flops 2300000000 | bytes 6899999 | tf_op jit(solution)/shard_map/root_sweeps/pallas_call | solution.py:396
  24.3 0.0 collective-permute-done.5
  24.3 1.5 %collective-permute-done.4 = f32[128,128]{1,0:T(8,128)S(1)} collective-permute-done((f32[128,128]{1,0:T(8,128)S(1)}, f32[128,128]{1,0:T(8,128)S(1)}, u32[]{:S(2)}, u32[]{:S(2)}) %collective-permute-start.4) | collective-permute-done | bytes 65568 | tf_op jit(solution)/shard_map/ppermute | solution.py:297
  25.8 0.8 %collective-permute-done.3 = f32[128,128]{1,0:T(8,128)S(1)} collective-permute-done((f32[128,128]{1,0:T(8,128)S(1)}, f32[128,128]{1,0:T(8,128)S(1)}, u32[]{:S(2)}, u32[]{:S(2)}) %collective-permute-start.3) | collective-permute-done | bytes 65568 | tf_op jit(solution)/shard_map/ppermute | solution.py:297
  26.6 0.0 copy-start.8
  26.6 2.1 %collective-permute-start.6 = (f32[128,128]{1,0:T(8,128)S(1)}, f32[128,128]{1,0:T(8,128)S(1)}, u32[]{:S(2)}, u32[]{:S(2)}) collective-permute-start(f32[128,128]{1,0:T(8,128)S(1)} %fusion.6.after), channel_id=1, source_target_pairs={{0,8},{2,10},{4,12},{6,14},{8,0},{10,2},{12,4},{14,6},{1,9},{3,11}... | collective-permute-start | bytes 196616 | tf_op jit(solution)/shard_map/ppermute | solution.py:297
  28.7 0.9 %root_operator.1.operator = bf16[1024,1024]{1,0:T(8,128)(2,1)S(1)} custom-call(f32[512,512]{1,0:T(8,128)S(1)} %get-tuple-element.39.forward, f32[512,512]{1,0:T(8,128)S(1)} %get-tuple-element.40.backward, f32[128,128]{1,0:T(8,128)S(1)} %fusion.6.after), custom_call_target="tpu_custom_call" | custom-call | flops 1000000000 | bytes 3000000 | tf_op jit(solution)/shard_map/root_operator/pallas_call | solution.py:409
  29.6 2.2 %collective-permute-done.6 = f32[128,128]{1,0:T(8,128)S(1)} collective-permute-done((f32[128,128]{1,0:T(8,128)S(1)}, f32[128,128]{1,0:T(8,128)S(1)}, u32[]{:S(2)}, u32[]{:S(2)}) %collective-permute-start.6) | collective-permute-done | bytes 65568 | tf_op jit(solution)/shard_map/ppermute | solution.py:297
  31.8 1.4 %collective-permute-start.9 = (f32[128,128]{1,0:T(8,128)S(1)}, f32[128,128]{1,0:T(8,128)S(1)}, u32[]{:S(2)}, u32[]{:S(2)}) collective-permute-start(f32[128,128]{1,0:T(8,128)S(1)} %add.51.own), channel_id=1, source_target_pairs={{0,6},{2,4},{4,2},{6,0},{8,14},{10,12},{12,10},{14,8},{1,7},{3,5},... | collective-permute-start | bytes 196616 | tf_op jit(solution)/shard_map/ppermute | solution.py:297
  33.2 1.9 %collective-permute-start.8 = (f32[128,128]{1,0:T(8,128)S(1)}, f32[128,128]{1,0:T(8,128)S(1)}, u32[]{:S(2)}, u32[]{:S(2)}) collective-permute-start(f32[128,128]{1,0:T(8,128)S(1)} %add.51.own), channel_id=1, source_target_pairs={{0,4},{2,6},{4,0},{6,2},{8,12},{10,14},{12,8},{14,10},{1,5},{3,7},... | collective-permute-start | bytes 196616 | tf_op jit(solution)/shard_map/ppermute | solution.py:297
  35.1 0.3 collective-permute-start.7
  35.4 1.7 %collective-permute-done.9.three = f32[128,128]{1,0:T(8,128)S(1)} collective-permute-done((f32[128,128]{1,0:T(8,128)S(1)}, f32[128,128]{1,0:T(8,128)S(1)}, u32[]{:S(2)}, u32[]{:S(2)}) %collective-permute-start.9) | collective-permute-done | bytes 65568 | tf_op jit(solution)/shard_map/ppermute | solution.py:297
  37.1 1.0 %collective-permute-done.8.two = f32[128,128]{1,0:T(8,128)S(1)} collective-permute-done((f32[128,128]{1,0:T(8,128)S(1)}, f32[128,128]{1,0:T(8,128)S(1)}, u32[]{:S(2)}, u32[]{:S(2)}) %collective-permute-start.8) | collective-permute-done | bytes 65568 | tf_op jit(solution)/shard_map/ppermute | solution.py:297
  38.0 1.3 %collective-permute-done.7.one = f32[128,128]{1,0:T(8,128)S(1)} collective-permute-done((f32[128,128]{1,0:T(8,128)S(1)}, f32[128,128]{1,0:T(8,128)S(1)}, u32[]{:S(2)}, u32[]{:S(2)}) %collective-permute-start.7) | collective-permute-done | bytes 65568 | tf_op jit(solution)/shard_map/ppermute | solution.py:297
  39.4 1.3 %root_solve.1.mine = f32[4,128,128]{2,1,0:T(8,128)S(1)} custom-call(s32[2]{0:T(128)S(1)} %pad_add_fusion.place, f32[4,128,256]{2,1,0:T(8,128)S(1)} %copy-done.8, bf16[1024,1024]{1,0:T(8,128)(2,1)S(1)} %root_operator.1.operator, f32[128,128]{1,0:T(8,128)S(1)} %add.51.own, f32[128,128]{1,0:T(8,128)S(1)} %collective-permute-done.7.one, ...), custom_call_target="tpu_custom_call" | custom-call | flops 1000000000 | bytes 3000000 | tf_op jit(solution)/shard_map/root_solve/pallas_call | solution.py:428
  40.7 0.1 collective-permute-start.10
  40.7 0.2 separator_part.1.part
  40.9 1.3 %collective-permute-done.10.theirs = f32[4,128,128]{2,1,0:T(8,128)S(1)} collective-permute-done((f32[4,128,128]{2,1,0:T(8,128)S(1)}, f32[4,128,128]{2,1,0:T(8,128)S(1)}, u32[]{:S(2)}, u32[]{:S(2)}) %collective-permute-start.10) | collective-permute-done | bytes 262176 | tf_op jit(solution)/shard_map/ppermute | solution.py:300
  42.3 0.9 %separator_backward.1 = (bf16[4,256,256]{2,1,0:T(8,128)(2,1)S(1)}, f32[128,256]{1,0:T(8,128)S(1)}) custom-call(s32[3]{0:T(128)S(1)} %bitcast.23, s32[1]{0:T(128)} %bitcast.2.core, f32[4,128,128]{2,1,0:T(8,128)S(1)} %root_solve.1.mine, f32[4,128,128]{2,1,0:T(8,128)S(1)} %collective-permute-done.10.theirs, bf16[256,768]{1,0:T(8,128)(2,1)S(1)} %get-tuple-element.43.operator, ...), custom_call_target="tpu_custom_call" | custom-call | flops 1500000000 | bytes 4500000 | tf_op jit(solution)/shard_map/separator_backward/pallas_call | solution.py:441
  43.2 1.2 %collective-permute-start.12 = (f32[128,256]{1,0:T(8,128)S(1)}, f32[128,256]{1,0:T(8,128)S(1)}, u32[]{:S(2)}, u32[]{:S(2)}) collective-permute-start(f32[128,256]{1,0:T(8,128)S(1)} %get-tuple-element.46.after.sep_sol.own), channel_id=1, source_target_pairs={{0,8},{2,10},{4,12},{6,14},{8,0},{10,2},{12,4},{14,6},{1,9},{3,11}... | collective-permute-start | bytes 393224 | tf_op jit(solution)/shard_map/ppermute | solution.py:294
  44.4 2.8 %collective-permute-start.11 = (f32[128,256]{1,0:T(8,128)S(1)}, f32[128,256]{1,0:T(8,128)S(1)}, u32[]{:S(2)}, u32[]{:S(2)}) collective-permute-start(f32[128,256]{1,0:T(8,128)S(1)} %get-tuple-element.46.after.sep_sol.own), channel_id=1, source_target_pairs={{0,2},{2,4},{4,6},{6,8},{8,10},{10,12},{12,14},{14,0},{1,3},{3,5},... | collective-permute-start | bytes 393224 | tf_op jit(solution)/shard_map/ppermute | solution.py:294
  47.2 3.5 %leaf_root_part.1 = (f32[12,128,256]{2,1,0:T(8,128)S(1)}, f32[4,128,256]{2,1,0:T(8,128)}, f32[1,128,256]{2,1,0:T(8,128)}) custom-call(s32[4,12]{1,0:T(4,128)S(1)} %bitcast.20, s32[1]{0:T(128)} %bitcast.2.core, f32[12,4,128,128]{3,2,1,0:T(8,128)S(1)} %copy-done, f32[12,4,128,128]{3,2,1,0:T(8,128)S(1)} %copy-done, f32[12,4,128,128]{3,2,1,0:T(8,128)S(1)} %copy-done, ...), custom_call_target="tpu_custom_call" | custom-call | flops 3000000000 | bytes 9000000 | tf_op jit(solution)/shard_map/leaf_root_part/pallas_call | solution.py:465
  50.7 0.8 %leaf_operators.1.operator = bf16[12,256,256]{2,1,0:T(8,128)(2,1)S(1)} custom-call(f32[12,128,128]{2,1,0:T(8,128)S(1)} %copy-done.4, f32[12,4,128,128]{3,2,1,0:T(8,128)S(1)} %copy-done, f32[128,256]{1,0:T(8,128)S(1)} %get-tuple-element.46.after.sep_sol.own), custom_call_target="tpu_custom_call" | custom-call | flops 1000000000 | bytes 3000000 | tf_op jit(solution)/shard_map/leaf_operators/pallas_call | solution.py:454
  51.5 3.8 %collective-permute-done.12.far = f32[128,256]{1,0:T(8,128)S(1)} collective-permute-done((f32[128,256]{1,0:T(8,128)S(1)}, f32[128,256]{1,0:T(8,128)S(1)}, u32[]{:S(2)}, u32[]{:S(2)}) %collective-permute-start.12) | collective-permute-done | bytes 131104 | tf_op jit(solution)/shard_map/ppermute | solution.py:294
  55.3 0.0 collective-permute-done.11.near
  55.3 2.1 %leaf_backward.1 = f32[12,128,256]{2,1,0:T(8,128)} custom-call(s32[4,12]{1,0:T(4,128)S(1)} %bitcast.21, bf16[12,256,256]{2,1,0:T(8,128)(2,1)S(1)} %leaf_operators.1.operator, f32[12,128,256]{2,1,0:T(8,128)S(1)} %get-tuple-element.48.part, f32[128,256]{1,0:T(8,128)S(1)} %get-tuple-element.46.after.sep_sol.own, f32[128,256]{1,0:T(8,128)S(1)} %collective-permute-done.11.near, ...), custom_call_target="tpu_custom_call" | custom-call | flops 2000000000 | bytes 6000000 | tf_op jit(solution)/shard_map/leaf_backward/pallas_call | solution.py:508
  (14 shorter events, 0.1 us)
Async XLA Ops:
  0.6 7.0 %copy-start.1 = (f32[12,4,128,128]{3,2,1,0:T(8,128)S(1)}, f32[12,4,128,128]{3,2,1,0:T(8,128)}, u32[]{:S(2)}) copy-start(f32[12,4,128,128]{3,2,1,0:T(8,128)} %three.2) | copy-start | bytes 9437188
  0.6 7.0 %copy-start.5 = (s32[12,4]{0,1:T(4,128)S(1)}, s32[12,4]{0,1:T(4,128)}, u32[]{:S(2)}) copy-start(s32[12,4]{0,1:T(4,128)} %param.22) | copy-start | bytes 580
  4.5 7.6 %collective-permute-start = (f32[128,256]{1,0:T(8,128)}, f32[128,256]{1,0:T(8,128)S(1)}, u32[]{:S(2)}, u32[]{:S(2)}) collective-permute-start(f32[128,256]{1,0:T(8,128)} %get-tuple-element.30), channel_id=1, source_target_pairs={{0,14},{2,0},{4,2},{6,4},{8,6},{10,8},{12,10},{14,12},{1,15},{3,1}... | collective-permute-start | bytes 393224 | tf_op jit(solution)/shard_map/ppermute | solution.py:294
  5.0 8.9 %collective-permute-start.1 = (f32[128,256]{1,0:T(8,128)}, f32[128,256]{1,0:T(8,128)S(1)}, u32[]{:S(2)}, u32[]{:S(2)}) collective-permute-start(f32[128,256]{1,0:T(8,128)} %get-tuple-element.31), channel_id=1, source_target_pairs={{0,8},{2,10},{4,12},{6,14},{8,0},{10,2},{12,4},{14,6},{1,9},{3,11}... | collective-permute-start | bytes 393224 | tf_op jit(solution)/shard_map/ppermute | solution.py:294
  7.6 1.4 %copy-start.2 = (f32[12,128,256]{2,1,0:T(8,128)S(1)}, f32[12,128,256]{2,1,0:T(8,128)}, u32[]{:S(2)}) copy-start(f32[12,128,256]{2,1,0:T(8,128)} %get-tuple-element.27.after.solved) | copy-start | bytes 4718596
  9.0 2.5 %copy-start.3 = (f32[12,128,256]{2,1,0:T(8,128)S(1)}, f32[12,128,256]{2,1,0:T(8,128)}, u32[]{:S(2)}) copy-start(f32[12,128,256]{2,1,0:T(8,128)} %get-tuple-element.27.after.solved) | copy-start | bytes 4718596
  9.0 2.5 %copy-start.11 = (f32[1,3,128,128]{3,2,1,0:T(8,128)S(1)}, f32[1,3,128,128]{3,2,1,0:T(8,128)}, u32[]{:S(2)}) copy-start(f32[1,3,128,128]{3,2,1,0:T(8,128)} %lower.2) | copy-start | bytes 589828
  9.0 2.5 %copy-start.12 = (f32[1,3,128,128]{3,2,1,0:T(8,128)S(1)}, f32[1,3,128,128]{3,2,1,0:T(8,128)}, u32[]{:S(2)}) copy-start(f32[1,3,128,128]{3,2,1,0:T(8,128)} %upper.2) | copy-start | bytes 589828
  9.0 2.5 %copy-start.14 = (f32[1,128,128]{2,1,0:T(8,128)S(1)}, f32[1,128,128]{2,1,0:T(8,128)}, u32[]{:S(2)}) copy-start(f32[1,128,128]{2,1,0:T(8,128)} %lower_inverse.2) | copy-start | bytes 196612
  9.0 2.5 %copy-start.15 = (f32[1,128,128]{2,1,0:T(8,128)S(1)}, f32[1,128,128]{2,1,0:T(8,128)}, u32[]{:S(2)}) copy-start(f32[1,128,128]{2,1,0:T(8,128)} %upper_inverse.2) | copy-start | bytes 196612
  11.6 2.3 %copy-start.13 = (f32[1,128,256]{2,1,0:T(8,128)S(1)}, f32[1,128,256]{2,1,0:T(8,128)}, u32[]{:S(2)}) copy-start(f32[1,128,256]{2,1,0:T(8,128)} %rhs.4) | copy-start | bytes 393220
  11.6 2.3 %copy-start.16 = (s32[1,3]{1,0:T(1,128)S(1)}, s32[1,3]{1,0:T(1,128)}, u32[]{:S(2)}) copy-start(s32[1,3]{1,0:T(1,128)} %param.28) | copy-start | bytes 40
  11.6 2.3 %copy-start.17 = (f32[128,256]{1,0:T(8,128)S(1)}, f32[128,256]{1,0:T(8,128)}, u32[]{:S(2)}) copy-start(f32[128,256]{1,0:T(8,128)} %get-tuple-element.29.own) | copy-start | bytes 393220
  13.9 8.4 %copy-start.6 = (f32[512,512]{1,0:T(8,128)S(1)}, f32[512,512]{1,0:T(8,128)}, u32[]{:S(2)}) copy-start(f32[512,512]{1,0:T(8,128)} %lower.3) | copy-start | bytes 3145732
  13.9 8.4 %copy-start.7 = (f32[512,512]{1,0:T(8,128)S(1)}, f32[512,512]{1,0:T(8,128)}, u32[]{:S(2)}) copy-start(f32[512,512]{1,0:T(8,128)} %upper.3) | copy-start | bytes 3145732
  13.9 8.4 %copy-start.9 = (f32[4,128,128]{2,1,0:T(8,128)S(1)}, f32[4,128,128]{2,1,0:T(8,128)}, u32[]{:S(2)}) copy-start(f32[4,128,128]{2,1,0:T(8,128)} %lower_inverse.3) | copy-start | bytes 786436
  13.9 8.4 %copy-start.10 = (f32[4,128,128]{2,1,0:T(8,128)S(1)}, f32[4,128,128]{2,1,0:T(8,128)}, u32[]{:S(2)}) copy-start(f32[4,128,128]{2,1,0:T(8,128)} %upper_inverse.3) | copy-start | bytes 786436
  14.8 1.6 %collective-permute-start.2 = (f32[4,128,128]{2,1,0:T(8,128)S(1)}, f32[4,128,128]{2,1,0:T(8,128)S(1)}, u32[]{:S(2)}, u32[]{:S(2)}) collective-permute-start(f32[4,128,128]{2,1,0:T(8,128)S(1)} %get-tuple-element.33), channel_id=1, source_target_pairs={{0,1},{1,0},{2,3},{3,2},{4,5},{5,4},{6,7},{7,6},{8,9},{9,8},{10,11... | collective-permute-start | bytes 786440 | tf_op jit(solution)/shard_map/ppermute | solution.py:300
  16.5 7.9 %collective-permute-start.5 = (f32[128,128]{1,0:T(8,128)S(1)}, f32[128,128]{1,0:T(8,128)S(1)}, u32[]{:S(2)}, u32[]{:S(2)}) collective-permute-start(f32[128,128]{1,0:T(8,128)S(1)} %get-tuple-element.51), channel_id=1, source_target_pairs={{0,6},{2,4},{4,2},{6,0},{8,14},{10,12},{12,10},{14,8},{1,7},{3,5},... | collective-permute-start | bytes 196616 | tf_op jit(solution)/shard_map/ppermute | solution.py:297
  21.1 4.7 %collective-permute-start.4 = (f32[128,128]{1,0:T(8,128)S(1)}, f32[128,128]{1,0:T(8,128)S(1)}, u32[]{:S(2)}, u32[]{:S(2)}) collective-permute-start(f32[128,128]{1,0:T(8,128)S(1)} %get-tuple-element.52), channel_id=1, source_target_pairs={{0,4},{2,6},{4,0},{6,2},{8,12},{10,14},{12,8},{14,10},{1,5},{3,7},... | collective-permute-start | bytes 196616 | tf_op jit(solution)/shard_map/ppermute | solution.py:297
  22.3 4.3 %collective-permute-start.3 = (f32[128,128]{1,0:T(8,128)S(1)}, f32[128,128]{1,0:T(8,128)S(1)}, u32[]{:S(2)}, u32[]{:S(2)}) collective-permute-start(f32[128,128]{1,0:T(8,128)S(1)} %get-tuple-element.53.after), channel_id=1, source_target_pairs={{0,2},{2,0},{4,6},{6,4},{8,10},{10,8},{12,14},{14,12},{1,3},{3,1},... | collective-permute-start | bytes 196616 | tf_op jit(solution)/shard_map/ppermute | solution.py:297
  26.6 12.8 %copy-start.8 = (f32[4,128,256]{2,1,0:T(8,128)S(1)}, f32[4,128,256]{2,1,0:T(8,128)}, u32[]{:S(2)}) copy-start(f32[4,128,256]{2,1,0:T(8,128)} %rhs.5) | copy-start | bytes 1572868
  26.6 5.2 %collective-permute-start.6 = (f32[128,128]{1,0:T(8,128)S(1)}, f32[128,128]{1,0:T(8,128)S(1)}, u32[]{:S(2)}, u32[]{:S(2)}) collective-permute-start(f32[128,128]{1,0:T(8,128)S(1)} %fusion.6.after), channel_id=1, source_target_pairs={{0,8},{2,10},{4,12},{6,14},{8,0},{10,2},{12,4},{14,6},{1,9},{3,11}... | collective-permute-start | bytes 196616 | tf_op jit(solution)/shard_map/ppermute | solution.py:297
  31.8 5.2 %collective-permute-start.9 = (f32[128,128]{1,0:T(8,128)S(1)}, f32[128,128]{1,0:T(8,128)S(1)}, u32[]{:S(2)}, u32[]{:S(2)}) collective-permute-start(f32[128,128]{1,0:T(8,128)S(1)} %add.51.own), channel_id=1, source_target_pairs={{0,6},{2,4},{4,2},{6,0},{8,14},{10,12},{12,10},{14,8},{1,7},{3,5},... | collective-permute-start | bytes 196616 | tf_op jit(solution)/shard_map/ppermute | solution.py:297
  33.2 4.8 %collective-permute-start.8 = (f32[128,128]{1,0:T(8,128)S(1)}, f32[128,128]{1,0:T(8,128)S(1)}, u32[]{:S(2)}, u32[]{:S(2)}) collective-permute-start(f32[128,128]{1,0:T(8,128)S(1)} %add.51.own), channel_id=1, source_target_pairs={{0,4},{2,6},{4,0},{6,2},{8,12},{10,14},{12,8},{14,10},{1,5},{3,7},... | collective-permute-start | bytes 196616 | tf_op jit(solution)/shard_map/ppermute | solution.py:297
  35.1 4.3 %collective-permute-start.7 = (f32[128,128]{1,0:T(8,128)S(1)}, f32[128,128]{1,0:T(8,128)S(1)}, u32[]{:S(2)}, u32[]{:S(2)}) collective-permute-start(f32[128,128]{1,0:T(8,128)S(1)} %add.51.own), channel_id=1, source_target_pairs={{0,2},{2,0},{4,6},{6,4},{8,10},{10,8},{12,14},{14,12},{1,3},{3,1},... | collective-permute-start | bytes 196616 | tf_op jit(solution)/shard_map/ppermute | solution.py:297
  40.7 1.6 %collective-permute-start.10 = (f32[4,128,128]{2,1,0:T(8,128)S(1)}, f32[4,128,128]{2,1,0:T(8,128)S(1)}, u32[]{:S(2)}, u32[]{:S(2)}) collective-permute-start(f32[4,128,128]{2,1,0:T(8,128)S(1)} %root_solve.1.mine), channel_id=1, source_target_pairs={{0,1},{1,0},{2,3},{3,2},{4,5},{5,4},{6,7},{7,6},{8,9},{9,8},{10,11... | collective-permute-start | bytes 786440 | tf_op jit(solution)/shard_map/ppermute | solution.py:300
  42.3 5.0 %copy-start = (f32[12,4,128,128]{3,2,1,0:T(8,128)S(1)}, f32[12,4,128,128]{3,2,1,0:T(8,128)}, u32[]{:S(2)}) copy-start(f32[12,4,128,128]{3,2,1,0:T(8,128)} %three.3) | copy-start | bytes 9437188
  42.3 5.0 %copy-start.4 = (f32[12,128,128]{2,1,0:T(8,128)S(1)}, f32[12,128,128]{2,1,0:T(8,128)}, u32[]{:S(2)}) copy-start(f32[12,128,128]{2,1,0:T(8,128)} %inverse.5) | copy-start | bytes 2359300
  43.2 12.1 %collective-permute-start.12 = (f32[128,256]{1,0:T(8,128)S(1)}, f32[128,256]{1,0:T(8,128)S(1)}, u32[]{:S(2)}, u32[]{:S(2)}) collective-permute-start(f32[128,256]{1,0:T(8,128)S(1)} %get-tuple-element.46.after.sep_sol.own), channel_id=1, source_target_pairs={{0,8},{2,10},{4,12},{6,14},{8,0},{10,2},{12,4},{14,6},{1,9},{3,11}... | collective-permute-start | bytes 393224 | tf_op jit(solution)/shard_map/ppermute | solution.py:294
  44.4 10.9 %collective-permute-start.11 = (f32[128,256]{1,0:T(8,128)S(1)}, f32[128,256]{1,0:T(8,128)S(1)}, u32[]{:S(2)}, u32[]{:S(2)}) collective-permute-start(f32[128,256]{1,0:T(8,128)S(1)} %get-tuple-element.46.after.sep_sol.own), channel_id=1, source_target_pairs={{0,2},{2,4},{4,6},{6,8},{8,10},{10,12},{12,14},{14,0},{1,3},{3,5},... | collective-permute-start | bytes 393224 | tf_op jit(solution)/shard_map/ppermute | solution.py:294

commit v4 on v3

--- a/solution.py
+++ b/solution.py
@@ -53,7 +53,7 @@
     )
 
 
-def forward_leaf_kernel(links, rhs, inverse, first, solved, own, near, far, pending):
+def forward_leaf_kernel(links, rhs, inverse, first, solved, own, far, near, pending):
     step = pl.program_id(0)
 
     @pl.when(step == 0)
@@ -134,7 +134,7 @@
 
 
 def separator_kernel(
-    links, place, rhs, operator, own, near, far, root_pending, right, mine, theirs, sums
+    links, place, rhs, operator, own, far, near, root_pending, right, mine, theirs, sums
 ):
     right[...] = as_right(rhs[0] - own[...] - near[...] - far[...])
     terms = left_times(operator[...], right[...])
@@ -301,7 +301,7 @@
 
     shape = jax.ShapeDtypeStruct
 
-    leaf_solved, own, near, far = pl.pallas_call(
+    leaf_solved, own, far, near = pl.pallas_call(
         forward_leaf_kernel,
         grid=(leaves // batch,),
         in_specs=[
@@ -377,8 +377,8 @@
         separator_right_sides,
         sep_forward,
         own,
+        far_sum,
         near_sum,
-        far_sum,
         root_pending,
     )
 

time: 57.7 us -> 56.1 us (0.972); the launches traced: 57.4 us -> 55.2 us
  waiting for transfers between devices: 16.9 us -> 14.6 us
    ppermute x7, waiting for transfers between devices: 8.38 us -> 6.15 us  [crossed(): return lax.ppermute(x, 'grid', [(i, i ^ bit) for i in range(peers)])]
    ppermute x4, starting transfers between devices: 7.16 us -> 8.16 us  [shifted(): lax.ppermute(x, 'grid', [(i, (i + by) % peers) for i in range(peers)])]
    ppermute x7, starting transfers between devices: 11.5 us -> 10.6 us  [crossed(): return lax.ppermute(x, 'grid', [(i, i ^ bit) for i in range(peers)])]
where the time goes in v4:
time: 56.1 us; the launch traced here: 55.2 us
  Pallas kernels  19.2 us (34%)
  starting transfers between devices  18.9 us (34%)
  waiting for transfers between devices  14.6 us (26%)
  local copies, waits for them, and re-layouts  1.5 us (3%)
  between operations  0.9 us (2%)
    ppermute x7, starting transfers between devices, crossed(): return lax.ppermute(x, 'grid', [(i, i ^ bit) for i in range(peers)])  10.6 us
    ppermute x4, starting transfers between devices, shifted(): lax.ppermute(x, 'grid', [(i, (i + by) % peers) for i in range(peers)])  8.16 us
    ppermute x7, waiting for transfers between devices, crossed(): return lax.ppermute(x, 'grid', [(i, i ^ bit) for i in range(peers)])  6.15 us
    ppermute x4, waiting for transfers between devices, shifted(): lax.ppermute(x, 'grid', [(i, (i + by) % peers) for i in range(peers)])  5.61 us
    pallas_call x1, Pallas kernels, per_device(): pl.pallas_call(forward_leaf_kernel, grid=(leaves // batch,), in_specs=[wh...  3.83 us
    pallas_call x1, Pallas kernels, per_device(): pl.pallas_call(leaf_root_part_kernel, grid=(leaves // batch,), in_specs=[...  3.47 us
    ppermute x2, waiting for transfers between devices, swapped(): return lax.ppermute(x, 'layer', [(0, 1), (1, 0)])  2.85 us
    pallas_call x1, Pallas kernels, per_device(): pl.pallas_call(root_terms_kernel, grid=(leaves // batch,), in_specs=[whol...  2.44 us
  transfers between devices with their start and end apart: 13, of which 10 were waited for; matrix products, arithmetic and copies ran while one was open for 0% of the time, Pallas kernels for 18%

profile of v4, /device:TPU:6, one launch (start us, length us, event | category | flops | bytes accessed | tf_op | source)
XLA Modules:
  0.0 55.2 jit_solution(16296461724866363765)
XLA Ops:
  0.6 0.0 copy-start.1
  0.6 0.0 copy-start.5
  0.7 3.8 %leaf_forward.1 = (f32[12,128,256]{2,1,0:T(8,128)}, f32[128,256]{1,0:T(8,128)}, f32[128,256]{1,0:T(8,128)}, f32[128,256]{1,0:T(8,128)}) custom-call(s32[4,12]{1,0:T(4,128)} %bitcast.18, f32[12,128,256]{2,1,0:T(8,128)} %rhs.3, f32[12,128,128]{2,1,0:T(8,128)} %inverse.3, f32[12,4,128,128]{3,2,1,0:T(8,128)} %three.2), custom_call_target="tpu_custom_call" | custom-call | flops 4000000000 | bytes 12000000 | tf_op jit(solution)/shard_map/leaf_forward/pallas_call | solution.py:304
  4.5 2.6 %collective-permute-start = (f32[128,256]{1,0:T(8,128)}, f32[128,256]{1,0:T(8,128)S(1)}, u32[]{:S(2)}, u32[]{:S(2)}) collective-permute-start(f32[128,256]{1,0:T(8,128)} %get-tuple-element.30), channel_id=1, source_target_pairs={{0,8},{2,10},{4,12},{6,14},{8,0},{10,2},{12,4},{14,6},{1,9},{3,11}... | collective-permute-start | bytes 393224 | tf_op jit(solution)/shard_map/ppermute | solution.py:294
  7.1 0.5 collective-permute-start.1
  7.6 0.0 copy-done.1
  7.6 0.0 copy-done.5
  7.6 1.4 %copy-done.2 = f32[12,128,256]{2,1,0:T(8,128)S(1)} copy-done((f32[12,128,256]{2,1,0:T(8,128)S(1)}, f32[12,128,256]{2,1,0:T(8,128)}, u32[]{:S(2)}) %copy-start.2) | copy-done | bytes 1572888
  9.1 0.0 copy-start.15
  9.1 2.4 %root_terms.1.root_pending = f32[4,128,256]{2,1,0:T(8,128)S(1)} custom-call(s32[4,12]{1,0:T(4,128)S(1)} %bitcast.19, f32[12,4,128,128]{3,2,1,0:T(8,128)S(1)} %copy-done.1, f32[12,4,128,128]{3,2,1,0:T(8,128)S(1)} %copy-done.1, f32[12,4,128,128]{3,2,1,0:T(8,128)S(1)} %copy-done.1, f32[12,128,256]{2,1,0:T(8,128)S(1)} %copy-done.2), custom_call_target="tpu_custom_call" | custom-call | flops 3000000000 | bytes 9000000 | tf_op jit(solution)/shard_map/root_terms/pallas_call | solution.py:324
  11.5 0.0 copy-done.3
  11.5 0.0 copy-done.11
  11.5 0.0 copy-done.12
  11.5 0.0 copy-done.14
  11.6 0.0 copy-done.15
  11.6 0.0 copy-start.13
  11.6 0.0 copy-start.16
  11.6 0.0 copy-start.17
  11.6 0.4 separator_operators.1
  12.0 0.1 pad_add_fusion.place
  12.1 1.6 %collective-permute-done.far = f32[128,256]{1,0:T(8,128)S(1)} collective-permute-done((f32[128,256]{1,0:T(8,128)}, f32[128,256]{1,0:T(8,128)S(1)}, u32[]{:S(2)}, u32[]{:S(2)}) %collective-permute-start) | collective-permute-done | bytes 131104 | tf_op jit(solution)/shard_map/ppermute | solution.py:294
  13.7 1.2 %collective-permute-done.1.near = f32[128,256]{1,0:T(8,128)S(1)} collective-permute-done((f32[128,256]{1,0:T(8,128)}, f32[128,256]{1,0:T(8,128)S(1)}, u32[]{:S(2)}, u32[]{:S(2)}) %collective-permute-start.1) | collective-permute-done | bytes 131104 | tf_op jit(solution)/shard_map/ppermute | solution.py:294
  14.9 0.0 copy-done.13
  14.9 0.0 copy-done.16
  14.9 0.0 copy-done.17
  14.9 0.0 copy-start.6
  14.9 0.0 copy-start.7
  14.9 0.0 copy-start.9
  14.9 0.0 copy-start.10
  14.9 0.9 %separator_forward.1 = (bf16[256,256]{1,0:T(8,128)(2,1)S(1)}, f32[4,128,128]{2,1,0:T(8,128)S(1)}, f32[4,128,128]{2,1,0:T(8,128)S(1)}) custom-call(s32[3]{0:T(128)S(1)} %bitcast.22, s32[2]{0:T(128)S(1)} %pad_add_fusion.place, f32[1,128,256]{2,1,0:T(8,128)S(1)} %copy-done.13, bf16[768,256]{1,0:T(8,128)(2,1)S(1)} %get-tuple-element.28.operator, ...), custom_call_target="tpu_custom_call" | custom-call | flops 2000000000 | bytes 6000000 | tf_op jit(solution)/shard_map/separator_forward/pallas_call | solution.py:361
  15.8 0.1 collective-permute-start.2
  15.9 1.5 %collective-permute-done.2 = f32[4,128,128]{2,1,0:T(8,128)S(1)} collective-permute-done((f32[4,128,128]{2,1,0:T(8,128)S(1)}, f32[4,128,128]{2,1,0:T(8,128)S(1)}, u32[]{:S(2)}, u32[]{:S(2)}) %collective-permute-start.2) | collective-permute-done | bytes 262176 | tf_op jit(solution)/shard_map/ppermute | solution.py:300
  17.4 2.4 %collective-permute-start.5 = (f32[128,128]{1,0:T(8,128)S(1)}, f32[128,128]{1,0:T(8,128)S(1)}, u32[]{:S(2)}, u32[]{:S(2)}) collective-permute-start(f32[128,128]{1,0:T(8,128)S(1)} %get-tuple-element.51), channel_id=1, source_target_pairs={{0,6},{2,4},{4,2},{6,0},{8,14},{10,12},{12,10},{14,8},{1,7},{3,5},... | collective-permute-start | bytes 196616 | tf_op jit(solution)/shard_map/ppermute | solution.py:297
  19.8 0.0 collective-permute-start.4
  19.8 1.3 %collective-permute-start.3 = (f32[128,128]{1,0:T(8,128)S(1)}, f32[128,128]{1,0:T(8,128)S(1)}, u32[]{:S(2)}, u32[]{:S(2)}) collective-permute-start(f32[128,128]{1,0:T(8,128)S(1)} %get-tuple-element.53.after), channel_id=1, source_target_pairs={{0,2},{2,0},{4,6},{6,4},{8,10},{10,8},{12,14},{14,12},{1,3},{3,1},... | collective-permute-start | bytes 196616 | tf_op jit(solution)/shard_map/ppermute | solution.py:297
  21.1 0.0 copy-done.7
  21.1 2.0 %root_sweeps.1 = (f32[512,512]{1,0:T(8,128)S(1)}, f32[512,512]{1,0:T(8,128)S(1)}) custom-call(f32[4,128,128]{2,1,0:T(8,128)S(1)} %copy-done.9, f32[4,128,128]{2,1,0:T(8,128)S(1)} %copy-done.10, f32[512,512]{1,0:T(8,128)S(1)} %copy-done.6, f32[512,512]{1,0:T(8,128)S(1)} %copy-done.7, f32[128,128]{1,0:T(8,128)S(1)} %get-tuple-element.53.after), custom_call_target="tpu_custom_call" | custom-call | flops 2300000000 | bytes 6899999 | tf_op jit(solution)/shard_map/root_sweeps/pallas_call | solution.py:396
  23.1 0.0 collective-permute-done.5
  23.1 1.0 %collective-permute-done.4 = f32[128,128]{1,0:T(8,128)S(1)} collective-permute-done((f32[128,128]{1,0:T(8,128)S(1)}, f32[128,128]{1,0:T(8,128)S(1)}, u32[]{:S(2)}, u32[]{:S(2)}) %collective-permute-start.4) | collective-permute-done | bytes 65568 | tf_op jit(solution)/shard_map/ppermute | solution.py:297
  24.1 0.0 collective-permute-done.3
  24.1 0.0 copy-start.8
  24.1 3.3 %collective-permute-start.6 = (f32[128,128]{1,0:T(8,128)S(1)}, f32[128,128]{1,0:T(8,128)S(1)}, u32[]{:S(2)}, u32[]{:S(2)}) collective-permute-start(f32[128,128]{1,0:T(8,128)S(1)} %fusion.6.after), channel_id=1, source_target_pairs={{0,8},{2,10},{4,12},{6,14},{8,0},{10,2},{12,4},{14,6},{1,9},{3,11}... | collective-permute-start | bytes 196616 | tf_op jit(solution)/shard_map/ppermute | solution.py:297
  27.5 0.9 %root_operator.1.operator = bf16[1024,1024]{1,0:T(8,128)(2,1)S(1)} custom-call(f32[512,512]{1,0:T(8,128)S(1)} %get-tuple-element.39.forward, f32[512,512]{1,0:T(8,128)S(1)} %get-tuple-element.40.backward, f32[128,128]{1,0:T(8,128)S(1)} %fusion.6.after), custom_call_target="tpu_custom_call" | custom-call | flops 1000000000 | bytes 3000000 | tf_op jit(solution)/shard_map/root_operator/pallas_call | solution.py:409
  28.4 1.5 %collective-permute-done.6 = f32[128,128]{1,0:T(8,128)S(1)} collective-permute-done((f32[128,128]{1,0:T(8,128)S(1)}, f32[128,128]{1,0:T(8,128)S(1)}, u32[]{:S(2)}, u32[]{:S(2)}) %collective-permute-start.6) | collective-permute-done | bytes 65568 | tf_op jit(solution)/shard_map/ppermute | solution.py:297
  29.9 2.2 %collective-permute-start.9 = (f32[128,128]{1,0:T(8,128)S(1)}, f32[128,128]{1,0:T(8,128)S(1)}, u32[]{:S(2)}, u32[]{:S(2)}) collective-permute-start(f32[128,128]{1,0:T(8,128)S(1)} %add.51.own), channel_id=1, source_target_pairs={{0,6},{2,4},{4,2},{6,0},{8,14},{10,12},{12,10},{14,8},{1,7},{3,5},... | collective-permute-start | bytes 196616 | tf_op jit(solution)/shard_map/ppermute | solution.py:297
  32.2 0.7 %collective-permute-start.8 = (f32[128,128]{1,0:T(8,128)S(1)}, f32[128,128]{1,0:T(8,128)S(1)}, u32[]{:S(2)}, u32[]{:S(2)}) collective-permute-start(f32[128,128]{1,0:T(8,128)S(1)} %add.51.own), channel_id=1, source_target_pairs={{0,4},{2,6},{4,0},{6,2},{8,12},{10,14},{12,8},{14,10},{1,5},{3,7},... | collective-permute-start | bytes 196616 | tf_op jit(solution)/shard_map/ppermute | solution.py:297
  32.9 0.6 %collective-permute-start.7 = (f32[128,128]{1,0:T(8,128)S(1)}, f32[128,128]{1,0:T(8,128)S(1)}, u32[]{:S(2)}, u32[]{:S(2)}) collective-permute-start(f32[128,128]{1,0:T(8,128)S(1)} %add.51.own), channel_id=1, source_target_pairs={{0,2},{2,0},{4,6},{6,4},{8,10},{10,8},{12,14},{14,12},{1,3},{3,1},... | collective-permute-start | bytes 196616 | tf_op jit(solution)/shard_map/ppermute | solution.py:297
  33.5 1.7 %collective-permute-done.9.three = f32[128,128]{1,0:T(8,128)S(1)} collective-permute-done((f32[128,128]{1,0:T(8,128)S(1)}, f32[128,128]{1,0:T(8,128)S(1)}, u32[]{:S(2)}, u32[]{:S(2)}) %collective-permute-start.9) | collective-permute-done | bytes 65568 | tf_op jit(solution)/shard_map/ppermute | solution.py:297
  35.2 1.3 %collective-permute-done.8.two = f32[128,128]{1,0:T(8,128)S(1)} collective-permute-done((f32[128,128]{1,0:T(8,128)S(1)}, f32[128,128]{1,0:T(8,128)S(1)}, u32[]{:S(2)}, u32[]{:S(2)}) %collective-permute-start.8) | collective-permute-done | bytes 65568 | tf_op jit(solution)/shard_map/ppermute | solution.py:297
  36.4 0.7 %collective-permute-done.7.one = f32[128,128]{1,0:T(8,128)S(1)} collective-permute-done((f32[128,128]{1,0:T(8,128)S(1)}, f32[128,128]{1,0:T(8,128)S(1)}, u32[]{:S(2)}, u32[]{:S(2)}) %collective-permute-start.7) | collective-permute-done | bytes 65568 | tf_op jit(solution)/shard_map/ppermute | solution.py:297
  37.1 0.0 copy-done.8
  37.1 1.3 %root_solve.1.mine = f32[4,128,128]{2,1,0:T(8,128)S(1)} custom-call(s32[2]{0:T(128)S(1)} %pad_add_fusion.place, f32[4,128,256]{2,1,0:T(8,128)S(1)} %copy-done.8, bf16[1024,1024]{1,0:T(8,128)(2,1)S(1)} %root_operator.1.operator, f32[128,128]{1,0:T(8,128)S(1)} %add.51.own, f32[128,128]{1,0:T(8,128)S(1)} %collective-permute-done.7.one, ...), custom_call_target="tpu_custom_call" | custom-call | flops 1000000000 | bytes 3000000 | tf_op jit(solution)/shard_map/root_solve/pallas_call | solution.py:428
  38.4 0.1 collective-permute-start.10
  38.5 0.2 separator_part.1.part
  38.7 1.3 %collective-permute-done.10.theirs = f32[4,128,128]{2,1,0:T(8,128)S(1)} collective-permute-done((f32[4,128,128]{2,1,0:T(8,128)S(1)}, f32[4,128,128]{2,1,0:T(8,128)S(1)}, u32[]{:S(2)}, u32[]{:S(2)}) %collective-permute-start.10) | collective-permute-done | bytes 262176 | tf_op jit(solution)/shard_map/ppermute | solution.py:300
  40.0 0.9 %separator_backward.1 = (bf16[4,256,256]{2,1,0:T(8,128)(2,1)S(1)}, f32[128,256]{1,0:T(8,128)S(1)}) custom-call(s32[3]{0:T(128)S(1)} %bitcast.23, s32[1]{0:T(128)} %bitcast.2.core, f32[4,128,128]{2,1,0:T(8,128)S(1)} %root_solve.1.mine, f32[4,128,128]{2,1,0:T(8,128)S(1)} %collective-permute-done.10.theirs, bf16[256,768]{1,0:T(8,128)(2,1)S(1)} %get-tuple-element.43.operator, ...), custom_call_target="tpu_custom_call" | custom-call | flops 1500000000 | bytes 4500000 | tf_op jit(solution)/shard_map/separator_backward/pallas_call | solution.py:441
  41.0 2.2 %collective-permute-start.12 = (f32[128,256]{1,0:T(8,128)S(1)}, f32[128,256]{1,0:T(8,128)S(1)}, u32[]{:S(2)}, u32[]{:S(2)}) collective-permute-start(f32[128,256]{1,0:T(8,128)S(1)} %get-tuple-element.46.after.sep_sol.own), channel_id=1, source_target_pairs={{0,8},{2,10},{4,12},{6,14},{8,0},{10,2},{12,4},{14,6},{1,9},{3,11}... | collective-permute-start | bytes 393224 | tf_op jit(solution)/shard_map/ppermute | solution.py:294
  43.2 2.8 %collective-permute-start.11 = (f32[128,256]{1,0:T(8,128)S(1)}, f32[128,256]{1,0:T(8,128)S(1)}, u32[]{:S(2)}, u32[]{:S(2)}) collective-permute-start(f32[128,256]{1,0:T(8,128)S(1)} %get-tuple-element.46.after.sep_sol.own), channel_id=1, source_target_pairs={{0,2},{2,4},{4,6},{6,8},{8,10},{10,12},{12,14},{14,0},{1,3},{3,5},... | collective-permute-start | bytes 393224 | tf_op jit(solution)/shard_map/ppermute | solution.py:294
  46.0 0.0 copy-done.4
  46.0 3.5 %leaf_root_part.1 = (f32[12,128,256]{2,1,0:T(8,128)S(1)}, f32[4,128,256]{2,1,0:T(8,128)}, f32[1,128,256]{2,1,0:T(8,128)}) custom-call(s32[4,12]{1,0:T(4,128)S(1)} %bitcast.20, s32[1]{0:T(128)} %bitcast.2.core, f32[12,4,128,128]{3,2,1,0:T(8,128)S(1)} %copy-done, f32[12,4,128,128]{3,2,1,0:T(8,128)S(1)} %copy-done, f32[12,4,128,128]{3,2,1,0:T(8,128)S(1)} %copy-done, ...), custom_call_target="tpu_custom_call" | custom-call | flops 3000000000 | bytes 9000000 | tf_op jit(solution)/shard_map/leaf_root_part/pallas_call | solution.py:465
  49.5 0.8 %leaf_operators.1.operator = bf16[12,256,256]{2,1,0:T(8,128)(2,1)S(1)} custom-call(f32[12,128,128]{2,1,0:T(8,128)S(1)} %copy-done.4, f32[12,4,128,128]{3,2,1,0:T(8,128)S(1)} %copy-done, f32[128,256]{1,0:T(8,128)S(1)} %get-tuple-element.46.after.sep_sol.own), custom_call_target="tpu_custom_call" | custom-call | flops 1000000000 | bytes 3000000 | tf_op jit(solution)/shard_map/leaf_operators/pallas_call | solution.py:454
  50.3 2.8 %collective-permute-done.12.far = f32[128,256]{1,0:T(8,128)S(1)} collective-permute-done((f32[128,256]{1,0:T(8,128)S(1)}, f32[128,256]{1,0:T(8,128)S(1)}, u32[]{:S(2)}, u32[]{:S(2)}) %collective-permute-start.12) | collective-permute-done | bytes 131104 | tf_op jit(solution)/shard_map/ppermute | solution.py:294
  53.1 0.0 collective-permute-done.11.near
  53.1 2.1 %leaf_backward.1 = f32[12,128,256]{2,1,0:T(8,128)} custom-call(s32[4,12]{1,0:T(4,128)S(1)} %bitcast.21, bf16[12,256,256]{2,1,0:T(8,128)(2,1)S(1)} %leaf_operators.1.operator, f32[12,128,256]{2,1,0:T(8,128)S(1)} %get-tuple-element.48.part, f32[128,256]{1,0:T(8,128)S(1)} %get-tuple-element.46.after.sep_sol.own, f32[128,256]{1,0:T(8,128)S(1)} %collective-permute-done.11.near, ...), custom_call_target="tpu_custom_call" | custom-call | flops 2000000000 | bytes 6000000 | tf_op jit(solution)/shard_map/leaf_backward/pallas_call | solution.py:508
  (14 shorter events, 0.1 us)
Async XLA Ops:
  0.6 7.0 %copy-start.1 = (f32[12,4,128,128]{3,2,1,0:T(8,128)S(1)}, f32[12,4,128,128]{3,2,1,0:T(8,128)}, u32[]{:S(2)}) copy-start(f32[12,4,128,128]{3,2,1,0:T(8,128)} %three.2) | copy-start | bytes 9437188
  0.6 7.0 %copy-start.5 = (s32[12,4]{0,1:T(4,128)S(1)}, s32[12,4]{0,1:T(4,128)}, u32[]{:S(2)}) copy-start(s32[12,4]{0,1:T(4,128)} %param.22) | copy-start | bytes 580
  4.5 9.2 %collective-permute-start = (f32[128,256]{1,0:T(8,128)}, f32[128,256]{1,0:T(8,128)S(1)}, u32[]{:S(2)}, u32[]{:S(2)}) collective-permute-start(f32[128,256]{1,0:T(8,128)} %get-tuple-element.30), channel_id=1, source_target_pairs={{0,8},{2,10},{4,12},{6,14},{8,0},{10,2},{12,4},{14,6},{1,9},{3,11}... | collective-permute-start | bytes 393224 | tf_op jit(solution)/shard_map/ppermute | solution.py:294
  7.1 7.8 %collective-permute-start.1 = (f32[128,256]{1,0:T(8,128)}, f32[128,256]{1,0:T(8,128)S(1)}, u32[]{:S(2)}, u32[]{:S(2)}) collective-permute-start(f32[128,256]{1,0:T(8,128)} %get-tuple-element.31), channel_id=1, source_target_pairs={{0,14},{2,0},{4,2},{6,4},{8,6},{10,8},{12,10},{14,12},{1,15},{3,1}... | collective-permute-start | bytes 393224 | tf_op jit(solution)/shard_map/ppermute | solution.py:294
  7.6 1.4 %copy-start.2 = (f32[12,128,256]{2,1,0:T(8,128)S(1)}, f32[12,128,256]{2,1,0:T(8,128)}, u32[]{:S(2)}) copy-start(f32[12,128,256]{2,1,0:T(8,128)} %get-tuple-element.27.after.solved) | copy-start | bytes 4718596
  9.0 2.5 %copy-start.3 = (f32[12,128,256]{2,1,0:T(8,128)S(1)}, f32[12,128,256]{2,1,0:T(8,128)}, u32[]{:S(2)}) copy-start(f32[12,128,256]{2,1,0:T(8,128)} %get-tuple-element.27.after.solved) | copy-start | bytes 4718596
  9.0 2.5 %copy-start.11 = (f32[1,3,128,128]{3,2,1,0:T(8,128)S(1)}, f32[1,3,128,128]{3,2,1,0:T(8,128)}, u32[]{:S(2)}) copy-start(f32[1,3,128,128]{3,2,1,0:T(8,128)} %lower.2) | copy-start | bytes 589828
  9.0 2.5 %copy-start.12 = (f32[1,3,128,128]{3,2,1,0:T(8,128)S(1)}, f32[1,3,128,128]{3,2,1,0:T(8,128)}, u32[]{:S(2)}) copy-start(f32[1,3,128,128]{3,2,1,0:T(8,128)} %upper.2) | copy-start | bytes 589828
  9.0 2.5 %copy-start.14 = (f32[1,128,128]{2,1,0:T(8,128)S(1)}, f32[1,128,128]{2,1,0:T(8,128)}, u32[]{:S(2)}) copy-start(f32[1,128,128]{2,1,0:T(8,128)} %lower_inverse.2) | copy-start | bytes 196612
  9.1 2.5 %copy-start.15 = (f32[1,128,128]{2,1,0:T(8,128)S(1)}, f32[1,128,128]{2,1,0:T(8,128)}, u32[]{:S(2)}) copy-start(f32[1,128,128]{2,1,0:T(8,128)} %upper_inverse.2) | copy-start | bytes 196612
  11.6 3.3 %copy-start.13 = (f32[1,128,256]{2,1,0:T(8,128)S(1)}, f32[1,128,256]{2,1,0:T(8,128)}, u32[]{:S(2)}) copy-start(f32[1,128,256]{2,1,0:T(8,128)} %rhs.4) | copy-start | bytes 393220
  11.6 3.3 %copy-start.16 = (s32[1,3]{1,0:T(1,128)S(1)}, s32[1,3]{1,0:T(1,128)}, u32[]{:S(2)}) copy-start(s32[1,3]{1,0:T(1,128)} %param.28) | copy-start | bytes 40
  11.6 3.3 %copy-start.17 = (f32[128,256]{1,0:T(8,128)S(1)}, f32[128,256]{1,0:T(8,128)}, u32[]{:S(2)}) copy-start(f32[128,256]{1,0:T(8,128)} %get-tuple-element.29.own) | copy-start | bytes 393220
  14.9 6.2 %copy-start.6 = (f32[512,512]{1,0:T(8,128)S(1)}, f32[512,512]{1,0:T(8,128)}, u32[]{:S(2)}) copy-start(f32[512,512]{1,0:T(8,128)} %lower.3) | copy-start | bytes 3145732
  14.9 6.2 %copy-start.7 = (f32[512,512]{1,0:T(8,128)S(1)}, f32[512,512]{1,0:T(8,128)}, u32[]{:S(2)}) copy-start(f32[512,512]{1,0:T(8,128)} %upper.3) | copy-start | bytes 3145732
  14.9 6.2 %copy-start.9 = (f32[4,128,128]{2,1,0:T(8,128)S(1)}, f32[4,128,128]{2,1,0:T(8,128)}, u32[]{:S(2)}) copy-start(f32[4,128,128]{2,1,0:T(8,128)} %lower_inverse.3) | copy-start | bytes 786436
  14.9 6.2 %copy-start.10 = (f32[4,128,128]{2,1,0:T(8,128)S(1)}, f32[4,128,128]{2,1,0:T(8,128)}, u32[]{:S(2)}) copy-start(f32[4,128,128]{2,1,0:T(8,128)} %upper_inverse.3) | copy-start | bytes 786436
  15.8 1.6 %collective-permute-start.2 = (f32[4,128,128]{2,1,0:T(8,128)S(1)}, f32[4,128,128]{2,1,0:T(8,128)S(1)}, u32[]{:S(2)}, u32[]{:S(2)}) collective-permute-start(f32[4,128,128]{2,1,0:T(8,128)S(1)} %get-tuple-element.33), channel_id=1, source_target_pairs={{0,1},{1,0},{2,3},{3,2},{4,5},{5,4},{6,7},{7,6},{8,9},{9,8},{10,11... | collective-permute-start | bytes 786440 | tf_op jit(solution)/shard_map/ppermute | solution.py:300
  17.4 5.7 %collective-permute-start.5 = (f32[128,128]{1,0:T(8,128)S(1)}, f32[128,128]{1,0:T(8,128)S(1)}, u32[]{:S(2)}, u32[]{:S(2)}) collective-permute-start(f32[128,128]{1,0:T(8,128)S(1)} %get-tuple-element.51), channel_id=1, source_target_pairs={{0,6},{2,4},{4,2},{6,0},{8,14},{10,12},{12,10},{14,8},{1,7},{3,5},... | collective-permute-start | bytes 196616 | tf_op jit(solution)/shard_map/ppermute | solution.py:297
  19.8 4.3 %collective-permute-start.4 = (f32[128,128]{1,0:T(8,128)S(1)}, f32[128,128]{1,0:T(8,128)S(1)}, u32[]{:S(2)}, u32[]{:S(2)}) collective-permute-start(f32[128,128]{1,0:T(8,128)S(1)} %get-tuple-element.52), channel_id=1, source_target_pairs={{0,4},{2,6},{4,0},{6,2},{8,12},{10,14},{12,8},{14,10},{1,5},{3,7},... | collective-permute-start | bytes 196616 | tf_op jit(solution)/shard_map/ppermute | solution.py:297
  19.8 4.3 %collective-permute-start.3 = (f32[128,128]{1,0:T(8,128)S(1)}, f32[128,128]{1,0:T(8,128)S(1)}, u32[]{:S(2)}, u32[]{:S(2)}) collective-permute-start(f32[128,128]{1,0:T(8,128)S(1)} %get-tuple-element.53.after), channel_id=1, source_target_pairs={{0,2},{2,0},{4,6},{6,4},{8,10},{10,8},{12,14},{14,12},{1,3},{3,1},... | collective-permute-start | bytes 196616 | tf_op jit(solution)/shard_map/ppermute | solution.py:297
  24.1 13.0 %copy-start.8 = (f32[4,128,256]{2,1,0:T(8,128)S(1)}, f32[4,128,256]{2,1,0:T(8,128)}, u32[]{:S(2)}) copy-start(f32[4,128,256]{2,1,0:T(8,128)} %rhs.5) | copy-start | bytes 1572868
  24.1 5.8 %collective-permute-start.6 = (f32[128,128]{1,0:T(8,128)S(1)}, f32[128,128]{1,0:T(8,128)S(1)}, u32[]{:S(2)}, u32[]{:S(2)}) collective-permute-start(f32[128,128]{1,0:T(8,128)S(1)} %fusion.6.after), channel_id=1, source_target_pairs={{0,8},{2,10},{4,12},{6,14},{8,0},{10,2},{12,4},{14,6},{1,9},{3,11}... | collective-permute-start | bytes 196616 | tf_op jit(solution)/shard_map/ppermute | solution.py:297
  29.9 5.2 %collective-permute-start.9 = (f32[128,128]{1,0:T(8,128)S(1)}, f32[128,128]{1,0:T(8,128)S(1)}, u32[]{:S(2)}, u32[]{:S(2)}) collective-permute-start(f32[128,128]{1,0:T(8,128)S(1)} %add.51.own), channel_id=1, source_target_pairs={{0,6},{2,4},{4,2},{6,0},{8,14},{10,12},{12,10},{14,8},{1,7},{3,5},... | collective-permute-start | bytes 196616 | tf_op jit(solution)/shard_map/ppermute | solution.py:297
  32.2 4.3 %collective-permute-start.8 = (f32[128,128]{1,0:T(8,128)S(1)}, f32[128,128]{1,0:T(8,128)S(1)}, u32[]{:S(2)}, u32[]{:S(2)}) collective-permute-start(f32[128,128]{1,0:T(8,128)S(1)} %add.51.own), channel_id=1, source_target_pairs={{0,4},{2,6},{4,0},{6,2},{8,12},{10,14},{12,8},{14,10},{1,5},{3,7},... | collective-permute-start | bytes 196616 | tf_op jit(solution)/shard_map/ppermute | solution.py:297
  32.9 4.3 %collective-permute-start.7 = (f32[128,128]{1,0:T(8,128)S(1)}, f32[128,128]{1,0:T(8,128)S(1)}, u32[]{:S(2)}, u32[]{:S(2)}) collective-permute-start(f32[128,128]{1,0:T(8,128)S(1)} %add.51.own), channel_id=1, source_target_pairs={{0,2},{2,0},{4,6},{6,4},{8,10},{10,8},{12,14},{14,12},{1,3},{3,1},... | collective-permute-start | bytes 196616 | tf_op jit(solution)/shard_map/ppermute | solution.py:297
  38.4 1.6 %collective-permute-start.10 = (f32[4,128,128]{2,1,0:T(8,128)S(1)}, f32[4,128,128]{2,1,0:T(8,128)S(1)}, u32[]{:S(2)}, u32[]{:S(2)}) collective-permute-start(f32[4,128,128]{2,1,0:T(8,128)S(1)} %root_solve.1.mine), channel_id=1, source_target_pairs={{0,1},{1,0},{2,3},{3,2},{4,5},{5,4},{6,7},{7,6},{8,9},{9,8},{10,11... | collective-permute-start | bytes 786440 | tf_op jit(solution)/shard_map/ppermute | solution.py:300
  40.0 6.0 %copy-start = (f32[12,4,128,128]{3,2,1,0:T(8,128)S(1)}, f32[12,4,128,128]{3,2,1,0:T(8,128)}, u32[]{:S(2)}) copy-start(f32[12,4,128,128]{3,2,1,0:T(8,128)} %three.3) | copy-start | bytes 9437188
  40.0 6.0 %copy-start.4 = (f32[12,128,128]{2,1,0:T(8,128)S(1)}, f32[12,128,128]{2,1,0:T(8,128)}, u32[]{:S(2)}) copy-start(f32[12,128,128]{2,1,0:T(8,128)} %inverse.5) | copy-start | bytes 2359300
  41.0 12.1 %collective-permute-start.12 = (f32[128,256]{1,0:T(8,128)S(1)}, f32[128,256]{1,0:T(8,128)S(1)}, u32[]{:S(2)}, u32[]{:S(2)}) collective-permute-start(f32[128,256]{1,0:T(8,128)S(1)} %get-tuple-element.46.after.sep_sol.own), channel_id=1, source_target_pairs={{0,8},{2,10},{4,12},{6,14},{8,0},{10,2},{12,4},{14,6},{1,9},{3,11}... | collective-permute-start | bytes 393224 | tf_op jit(solution)/shard_map/ppermute | solution.py:294
  43.2 9.9 %collective-permute-start.11 = (f32[128,256]{1,0:T(8,128)S(1)}, f32[128,256]{1,0:T(8,128)S(1)}, u32[]{:S(2)}, u32[]{:S(2)}) collective-permute-start(f32[128,256]{1,0:T(8,128)S(1)} %get-tuple-element.46.after.sep_sol.own), channel_id=1, source_target_pairs={{0,2},{2,4},{4,6},{6,8},{8,10},{10,12},{12,14},{14,0},{1,3},{3,5},... | collective-permute-start | bytes 393224 | tf_op jit(solution)/shard_map/ppermute | solution.py:294

commit v5 on v4

--- a/solution.py
+++ b/solution.py
@@ -43,6 +43,10 @@
 
 def times(a, b):
     return left_times(as_left(a), as_right(b))
+
+
+def halves(is_first, mine, other):
+    return jnp.where(is_first, mine, other), jnp.where(is_first, other, mine)
 
 
 def cost(microseconds):
@@ -123,14 +127,9 @@
         root_operator[size + r : size + r + w, :] = left[w:]
 
 
-def separator_operators_kernel(
-    lower_inverse, upper_inverse, lower, upper, after, forward, part, backward
-):
+def separator_operator_kernel(lower_inverse, lower, after, forward):
     blocks = jnp.concatenate([lower[0, n] for n in range(3)], axis=0)
     forward[...] = as_left(times(blocks, lower_inverse[0]))
-    part[...] = as_left(times(upper_inverse[0], lower_inverse[0]))
-    blocks = jnp.concatenate([upper[0, n] for n in range(3)], axis=1)
-    backward[...] = as_left(times(upper_inverse[0], blocks))
 
 
 def separator_kernel(
@@ -150,32 +149,61 @@
         theirs[j] = jnp.where(is_first, second, first)
 
 
-def separator_part_kernel(operator, right, out):
-    out[...] = left_times(operator[...], right[...])
-
-
-def root_kernel(place, rhs, operator, own, one, two, three, out, pending):
+def separator_part_kernel(
+    links, place, lower_inverse, upper_inverse, upper, right, mine, pack
+):
+    blocks = jnp.concatenate([upper[0, n] for n in range(3)], axis=1)
+    back = times(upper_inverse[0], blocks)
+    last = pack.shape[0] - 1
+    pack[...] = jnp.zeros_like(pack)
+    for n in range(3):
+        pack[links[n]] = back[:, n * 128 : n * 128 + 128]
+    operator = as_left(times(upper_inverse[0], lower_inverse[0]))
+    part = left_times(operator, right[...])
+    mine[...], pack[last] = halves(place[1] == 0, part[:, :128], part[:, 128:])
+
+
+def separator_factors_kernel(pack, other, backward):
+    for i, blocks in enumerate((pack, other)):
+        backward[i] = as_left(
+            jnp.concatenate([blocks[r] for r in range(blocks.shape[0] - 1)], axis=1)
+        )
+
+
+def root_kernel(
+    place,
+    rhs,
+    operator,
+    three,
+    two,
+    one,
+    own,
+    backward,
+    part,
+    other_pack,
+    out,
+    sep_own,
+    sep_other,
+    pending,
+    right,
+):
     count, w = rhs.shape[0], rhs.shape[1]
     position = place[0]
     is_first = place[1] == 0
     for j, piece in enumerate((own, one, two, three)):
         root = position ^ j
-        right = rhs[root]
-        right = jnp.where(is_first, right[:, :128], right[:, 128:])
+        side = rhs[root]
+        side = jnp.where(is_first, side[:, :128], side[:, 128:])
         pending[pl.ds(pl.multiple_of(root * 2 * w, 2 * w), 2 * w), :] = as_right(
-            right - piece[...]
+            side - piece[...]
         )
-    out[...] = left_times(operator[...], pending[...]).reshape(count, w, 128)
-
-
-def separator_back_kernel(links, core, mine, theirs, operator, part, right, out):
-    is_first = core[0] == 0
-    for r in range(mine.shape[0]):
-        one, other = as_right(mine[r]), as_right(theirs[r])
-        right[r, :, :128] = jnp.where(is_first, one, other)
-        right[r, :, 128:] = jnp.where(is_first, other, one)
-    linked = jnp.concatenate([right[links[n]] for n in range(3)], axis=0)
-    out[...] = part[...] - left_times(operator[...], linked)
+    solution = left_times(operator[...], pending[...])
+    for r in range(count):
+        out[r] = solution[r * w : r * w + w]
+    right[...] = as_right(solution)
+    sep_own[...] = part[...] - left_times(backward[0], right[...])
+    sep_other[...] = other_pack[count] - left_times(backward[1], right[...])
+    out[count] = sep_other[...]
 
 
 def leaf_operator_kernel(inverse, first, after, operator):
@@ -185,44 +213,66 @@
 
 def leaf_root_part_kernel(
     links,
-    core,
+    place,
     one,
     two,
     three,
     inverse,
     solved,
-    root_right,
     mine,
-    theirs,
-    sep_sol,
+    other,
+    sep_own,
     part,
     root_sol,
     sep_rows,
+    right,
 ):
     step = pl.program_id(0)
+    count = root_sol.shape[0]
 
     @pl.when(step == 0)
     def _():
-        is_first = core[0] == 0
-        sep_rows[0] = sep_sol[...]
-        root_sol[:, :, :128] = jnp.where(is_first, mine[...], theirs[...])
-        root_sol[:, :, 128:] = jnp.where(is_first, theirs[...], mine[...])
+        is_first = place[1] == 0
+        for r in range(count):
+            root_sol[r, :, :128], root_sol[r, :, 128:] = halves(is_first, mine[r], other[r])
+            right[r] = as_right(root_sol[r])
+        sep_rows[0, :, :128], sep_rows[0, :, 128:] = halves(is_first, sep_own[...], other[count])
 
     batch = solved.shape[0]
     rests = []
     for i in range(batch):
         leaf = step * batch + i
         blocks = jnp.concatenate([one[i, 0], two[i, 0], three[i, 0]], axis=1)
-        linked = jnp.concatenate([root_right[links[n, leaf] - 3] for n in (1, 2, 3)], axis=0)
+        linked = jnp.concatenate([right[links[n, leaf] - 3] for n in (1, 2, 3)], axis=0)
         rests.append(solved[i] - left_times(as_left(blocks), linked))
     for i in range(batch):
         part[i] = times(inverse[i], rests[i])
 
 
-def leaf_final_kernel(links, operator, part, own, near, far, out, seps, ready, sems):
-    seps[0] = as_right(own[...])
-    seps[1] = as_right(near[...])
-    seps[2] = as_right(far[...])
+def leaf_final_kernel(
+    links,
+    place,
+    operator,
+    part,
+    own,
+    other,
+    far,
+    far_other,
+    near,
+    near_other,
+    out,
+    seps,
+    ready,
+    sems,
+):
+    is_first = place[1] == 0
+    last = other[other.shape[0] - 1]
+    for t, (a, b) in enumerate(
+        ((own[...], last), (near[...], near_other[...]), (far[...], far_other[...]))
+    ):
+        first, second = halves(is_first, a, b)
+        seps[t, :, :128] = as_right(first)
+        seps[t, :, 128:] = as_right(second)
     count = part.shape[0]
     copies = []
     for i in range(count):
@@ -285,13 +335,17 @@
     batch = leaves // 2
     position = lax.axis_index("grid") % 4
     core = lax.axis_index("layer")
-    core_ref = core.astype(jnp.int32).reshape(1)
     place = jnp.stack([position, core]).astype(jnp.int32)
     leaf_links = leaf_rows.T
     sep_links = sep_rows.reshape(-1)
 
-    def shifted(x, by):
-        return lax.ppermute(x, "grid", [(i, (i + by) % peers) for i in range(peers)])
+    def shifted(x, by, to_other=0):
+        pairs = [
+            (2 * i + c, 2 * ((i + by) % peers) + (c ^ to_other))
+            for i in range(peers)
+            for c in range(2)
+        ]
+        return lax.ppermute(x, ("grid", "layer"), pairs)
 
     def crossed(x, bit):
         return lax.ppermute(x, "grid", [(i, i ^ bit) for i in range(peers)])
@@ -300,6 +354,8 @@
         return lax.ppermute(x, "layer", [(0, 1), (1, 0)])
 
     shape = jax.ShapeDtypeStruct
+    half_block = shape((w, half), F32)
+    smem = whole(SMEM)
 
     leaf_solved, own, far, near = pl.pallas_call(
         forward_leaf_kernel,
@@ -338,25 +394,15 @@
         name="root_terms",
     )(leaf_links, leaf_lower, leaf_lower, leaf_lower, leaf_solved)
 
-    sep_forward, sep_part, sep_backward = pl.pallas_call(
-        separator_operators_kernel,
-        in_specs=[whole()] * 4 + [ANY],
-        out_specs=[whole()] * 3,
-        out_shape=[
-            shape((6 * w, 2 * w), BF16),
-            shape((2 * w, 2 * w), BF16),
-            shape((2 * w, 6 * w), BF16),
-        ],
-        compiler_params=limit(16),
-        cost_estimate=cost(1),
-        name="separator_operators",
-    )(
-        separator_lower_inverse,
-        separator_upper_inverse,
-        separator_lower_blocks,
-        sep_upper,
-        leaf_solved,
-    )
+    sep_forward = pl.pallas_call(
+        separator_operator_kernel,
+        in_specs=[whole()] * 2 + [ANY],
+        out_specs=whole(),
+        out_shape=shape((6 * w, 2 * w), BF16),
+        compiler_params=limit(16),
+        cost_estimate=cost(0.5),
+        name="separator_operator",
+    )(separator_lower_inverse, separator_lower_blocks, leaf_solved)
 
     sep_right, mine, theirs = pl.pallas_call(
         separator_kernel,
@@ -383,15 +429,32 @@
     )
 
     other = swapped(theirs)
-    sep_solved = pl.pallas_call(
+    sep_mine, sep_pack = pl.pallas_call(
         separator_part_kernel,
+        in_specs=[smem] * 2 + [whole()] * 4,
+        out_specs=[whole()] * 2,
+        out_shape=[half_block, shape((roots + 1, w, half), F32)],
+        compiler_params=limit(16),
+        cost_estimate=cost(0.7),
+        name="separator_part",
+    )(
+        sep_links,
+        place,
+        separator_lower_inverse,
+        separator_upper_inverse,
+        sep_upper,
+        sep_right,
+    )
+    other_pack = swapped(sep_pack)
+    sep_backward = pl.pallas_call(
+        separator_factors_kernel,
         in_specs=[whole()] * 2,
         out_specs=whole(),
-        out_shape=shape((w, columns), F32),
-        compiler_params=limit(16),
-        cost_estimate=cost(0.4),
-        name="separator_part",
-    )(sep_part, sep_right)
+        out_shape=shape((2, 2 * w, 2 * roots * w), BF16),
+        compiler_params=limit(16),
+        cost_estimate=cost(0.2),
+        name="separator_factors",
+    )(sep_pack, other_pack)
     pieces = [mine[j] + other[j] for j in range(4)]
     forward, backward = pl.pallas_call(
         root_sweeps_kernel,
@@ -402,7 +465,7 @@
         cost_estimate=cost(2.3),
         name="root_sweeps",
     )(root_lower_inverse, root_upper_inverse, root_lower, root_upper, pieces[1])
-    arrived = [crossed(pieces[j], j) for j in (1, 2, 3)]
+    arrived = [crossed(pieces[j], j) for j in (3, 2, 1)]
     arrived, forward, backward = lax.optimization_barrier((arrived, forward, backward))
     total = pieces[0] + arrived[0] + arrived[1] + arrived[2]
 
@@ -423,33 +486,33 @@
             arrived, root_operator = lax.optimization_barrier((arrived, root_operator))
         total = total + arrived
         bit *= 2
-    others = [crossed(total, j) for j in (1, 2, 3)]
-
-    solution_half = pl.pallas_call(
+    others = [crossed(total, j) for j in (3, 2, 1)]
+
+    solution_half, sep_own, sep_other = pl.pallas_call(
         root_kernel,
-        in_specs=[whole(SMEM)] + [whole()] * 6,
-        out_specs=whole(),
-        out_shape=shape((roots, w, half), F32),
-        scratch_shapes=[VMEM((2 * roots * w, half), BF16)],
-        compiler_params=limit(16),
-        cost_estimate=cost(1),
+        in_specs=[smem] + [whole()] * 9,
+        out_specs=[whole()] * 3,
+        out_shape=[shape((roots + 1, w, half), F32)] + [half_block] * 2,
+        scratch_shapes=[VMEM((2 * roots * w, half), BF16)] * 2,
+        compiler_params=limit(16),
+        cost_estimate=cost(2),
         name="root_solve",
-    )(place, root_rhs, root_operator, total, *others)
-
+    )(
+        place,
+        root_rhs,
+        root_operator,
+        *others,
+        total,
+        sep_backward,
+        sep_mine,
+        other_pack,
+    )
+
+    far_rows = shifted(sep_own, peers // 2)
+    far_other_rows = shifted(sep_other, peers // 2, 1)
+    near_rows = shifted(sep_own, 1)
+    near_other_rows = shifted(sep_other, 1, 1)
     other_half = swapped(solution_half)
-
-    root_right, sep_sol = pl.pallas_call(
-        separator_back_kernel,
-        in_specs=[whole(SMEM), whole(SMEM)] + [whole()] * 4,
-        out_specs=[whole()] * 2,
-        out_shape=[shape((roots, 2 * w, columns), BF16), shape((w, columns), F32)],
-        compiler_params=limit(16),
-        cost_estimate=cost(1.5),
-        name="separator_backward",
-    )(sep_links, core_ref, solution_half, other_half, sep_backward, sep_solved)
-
-    far_rows = shifted(sep_sol, peers // 2)
-    near_rows = shifted(sep_sol, 1)
 
     leaf_operator = pl.pallas_call(
         leaf_operator_kernel,
@@ -460,23 +523,22 @@
         compiler_params=limit(16),
         cost_estimate=cost(1),
         name="leaf_operators",
-    )(leaf_upper_inverse, leaf_upper, sep_sol)
+    )(leaf_upper_inverse, leaf_upper, sep_own)
 
     leaf_part, root_sol, separator_solution_rows = pl.pallas_call(
         leaf_root_part_kernel,
         grid=(leaves // batch,),
         in_specs=[
-            whole(SMEM),
-            whole(SMEM),
+            smem,
+            smem,
             link(batch, 1, w),
             link(batch, 2, w),
             link(batch, 3, w),
             leafwise(batch, w, w),
             leafwise(batch, w, columns),
-            kept(roots, 2 * w, columns),
-            kept(roots, w, half),
-            kept(roots, w, half),
-            kept(w, columns),
+            kept(roots + 1, w, half),
+            kept(roots + 1, w, half),
+            kept(w, half),
         ],
         out_specs=[
             leafwise(batch, w, columns),
@@ -488,26 +550,26 @@
             shape((roots, w, columns), F32),
             shape((1, w, columns), F32),
         ],
+        scratch_shapes=[VMEM((roots, 2 * w, columns), BF16)],
         compiler_params=limit(16),
         cost_estimate=cost(3),
         name="leaf_root_part",
     )(
         leaf_links,
-        core_ref,
+        place,
         leaf_upper,
         leaf_upper,
         leaf_upper,
         leaf_upper_inverse,
         leaf_solved,
-        root_right,
         solution_half,
         other_half,
-        sep_sol,
+        sep_own,
     )
 
     leaf_sol = pl.pallas_call(
         leaf_final_kernel,
-        in_specs=[whole(SMEM)] + [whole()] * 5,
+        in_specs=[smem] * 2 + [whole()] * 8,
         out_specs=ANY,
         out_shape=shape((leaves, w, columns), F32),
         scratch_shapes=[
@@ -518,7 +580,18 @@
         compiler_params=limit(16),
         cost_estimate=cost(2),
         name="leaf_backward",
-    )(leaf_links, leaf_operator, leaf_part, sep_sol, near_rows, far_rows)
+    )(
+        leaf_links,
+        place,
+        leaf_operator,
+        leaf_part,
+        sep_own,
+        other_half,
+        far_rows,
+        far_other_rows,
+        near_rows,
+        near_other_rows,
+    )
     return (leaf_sol, separator_solution_rows, root_sol)
 
 

time: 56.1 us -> 55.3 us (0.986)
  waiting for transfers between devices: 14.6 us -> 12.4 us
  starting transfers between devices: 18.9 us -> 19.9 us
  Pallas kernels: 19.2 us -> 19.9 us
    ppermute x2 -> x3, waiting for transfers between devices: 2.85 us -> 0.01 us  [swapped(): return lax.ppermute(x, 'layer', [(0, 1), (1, 0)])]
    pallas_call x5, Pallas kernels: 4.83 us -> 5.58 us  [the longest x1 2.14 us: per_device(): pl.pallas_call(root_kernel, in_specs=[smem] + [whole()] * 9, out_specs=[w...]
    ppermute x4 -> x6, waiting for transfers between devices: 5.61 us -> 6.29 us  [shifted(): return lax.ppermute(x, ('grid', 'layer'), pairs)]
    ppermute x4 -> x6, starting transfers between devices: 8.16 us -> 8.63 us  [shifted(): return lax.ppermute(x, ('grid', 'layer'), pairs)]
  transfers between devices with their start and end apart: 13 -> 16, of which waited for: 10 -> 8; matrix products, arithmetic and copies ran while one was open for 0% -> 0% of each run, Pallas kernels for 18% -> 20%
where the time goes in v5:
time: 55.3 us; the launch traced here: 54.7 us
  Pallas kernels  19.9 us (36%)
  starting transfers between devices  19.9 us (36%)
  waiting for transfers between devices  12.4 us (22%)
  local copies, waits for them, and re-layouts  1.5 us (3%)
  between operations  0.91 us (2%)
    ppermute x7, starting transfers between devices, crossed(): return lax.ppermute(x, 'grid', [(i, i ^ bit) for i in range(peers)])  10.6 us
    ppermute x6, starting transfers between devices, shifted(): return lax.ppermute(x, ('grid', 'layer'), pairs)  8.63 us
    ppermute x6, waiting for transfers between devices, shifted(): return lax.ppermute(x, ('grid', 'layer'), pairs)  6.29 us
    ppermute x7, waiting for transfers between devices, crossed(): return lax.ppermute(x, 'grid', [(i, i ^ bit) for i in range(peers)])  6.06 us
    pallas_call x1, Pallas kernels, per_device(): pl.pallas_call(forward_leaf_kernel, grid=(leaves // batch,), in_specs=[wh...  3.83 us
    pallas_call x1, Pallas kernels, per_device(): pl.pallas_call(leaf_root_part_kernel, grid=(leaves // batch,), in_specs=[...  3.51 us
    pallas_call x1, Pallas kernels, per_device(): pl.pallas_call(root_terms_kernel, grid=(leaves // batch,), in_specs=[whol...  2.43 us
    pallas_call x1, Pallas kernels, per_device(): pl.pallas_call(root_kernel, in_specs=[smem] + [whole()] * 9, out_specs=[w...  2.14 us
  transfers between devices with their start and end apart: 16, of which 8 were waited for; matrix products, arithmetic and copies ran while one was open for 0% of the time, Pallas kernels for 20%

profile of v5, /device:TPU:6, one launch (start us, length us, event | category | flops | bytes accessed | tf_op | source)
XLA Modules:
  0.0 54.7 jit_solution(14127836837172990450)
XLA Ops:
  0.6 0.0 copy-start.1
  0.6 0.0 copy-start.7
  0.7 3.8 %leaf_forward.1 = (f32[12,128,256]{2,1,0:T(8,128)}, f32[128,256]{1,0:T(8,128)}, f32[128,256]{1,0:T(8,128)}, f32[128,256]{1,0:T(8,128)}) custom-call(s32[4,12]{1,0:T(4,128)} %bitcast.18, f32[12,128,256]{2,1,0:T(8,128)} %rhs.3, f32[12,128,128]{2,1,0:T(8,128)} %inverse.3, f32[12,4,128,128]{3,2,1,0:T(8,128)} %three.2), custom_call_target="tpu_custom_call" | custom-call | flops 4000000000 | bytes 12000000 | tf_op jit(solution)/shard_map/leaf_forward/pallas_call | solution.py:360
  4.5 2.6 %collective-permute-start = (f32[128,256]{1,0:T(8,128)}, f32[128,256]{1,0:T(8,128)S(1)}, u32[]{:S(2)}, u32[]{:S(2)}) collective-permute-start(f32[128,256]{1,0:T(8,128)} %get-tuple-element.29), channel_id=1, source_target_pairs={{0,8},{1,9},{2,10},{3,11},{4,12},{5,13},{6,14},{7,15},{8,0},{9,1},... | collective-permute-start | bytes 393224 | tf_op jit(solution)/shard_map/ppermute | solution.py:348
  7.1 0.5 collective-permute-start.1
  7.6 0.0 copy-done.1
  7.6 0.0 copy-done.7
  7.6 1.4 %copy-done.2 = f32[12,128,256]{2,1,0:T(8,128)S(1)} copy-done((f32[12,128,256]{2,1,0:T(8,128)S(1)}, f32[12,128,256]{2,1,0:T(8,128)}, u32[]{:S(2)}) %copy-start.2) | copy-done | bytes 1572888
  9.0 2.4 %root_terms.1.root_pending = f32[4,128,256]{2,1,0:T(8,128)S(1)} custom-call(s32[4,12]{1,0:T(4,128)S(1)} %bitcast.19, f32[12,4,128,128]{3,2,1,0:T(8,128)S(1)} %copy-done.1, f32[12,4,128,128]{3,2,1,0:T(8,128)S(1)} %copy-done.1, f32[12,4,128,128]{3,2,1,0:T(8,128)S(1)} %copy-done.1, f32[12,128,256]{2,1,0:T(8,128)S(1)} %copy-done.2), custom_call_target="tpu_custom_call" | custom-call | flops 3000000000 | bytes 9000000 | tf_op jit(solution)/shard_map/root_terms/pallas_call | solution.py:380
  11.5 0.0 copy-done.3
  11.5 0.0 copy-done.5
  11.5 0.0 copy-done.6
  11.5 0.0 copy-start.14
  11.5 0.0 copy-start.16
  11.5 0.0 copy-start.17
  11.5 0.3 separator_operator.1.operator
  11.8 0.1 pad_add_fusion.place
  11.9 1.8 %collective-permute-done.far = f32[128,256]{1,0:T(8,128)S(1)} collective-permute-done((f32[128,256]{1,0:T(8,128)}, f32[128,256]{1,0:T(8,128)S(1)}, u32[]{:S(2)}, u32[]{:S(2)}) %collective-permute-start) | collective-permute-done | bytes 131104 | tf_op jit(solution)/shard_map/ppermute | solution.py:348
  13.7 1.2 %collective-permute-done.1.near = f32[128,256]{1,0:T(8,128)S(1)} collective-permute-done((f32[128,256]{1,0:T(8,128)}, f32[128,256]{1,0:T(8,128)S(1)}, u32[]{:S(2)}, u32[]{:S(2)}) %collective-permute-start.1) | collective-permute-done | bytes 131104 | tf_op jit(solution)/shard_map/ppermute | solution.py:348
  14.9 0.0 copy-done.16
  14.9 0.0 copy-start.13
  14.9 0.0 copy-start.15
  14.9 0.9 %separator_forward.1 = (bf16[256,256]{1,0:T(8,128)(2,1)S(1)}, f32[4,128,128]{2,1,0:T(8,128)S(1)}, f32[4,128,128]{2,1,0:T(8,128)S(1)}) custom-call(s32[3]{0:T(128)S(1)} %bitcast.22, s32[2]{0:T(128)S(1)} %pad_add_fusion.place, f32[1,128,256]{2,1,0:T(8,128)S(1)} %copy-done.14, bf16[768,256]{1,0:T(8,128)(2,1)S(1)} %separator_operator.1.operator, ...), custom_call_target="tpu_custom_call" | custom-call | flops 2000000000 | bytes 6000000 | tf_op jit(solution)/shard_map/separator_forward/pallas_call | solution.py:407
  15.8 0.1 collective-permute-start.2
  15.9 0.0 copy-start.8
  15.9 0.0 copy-start.9
  15.9 0.0 copy-start.11
  15.9 0.0 copy-start.12
  15.9 1.0 %separator_part.1 = (f32[128,128]{1,0:T(8,128)S(1)}, f32[5,128,128]{2,1,0:T(8,128)S(1)}) custom-call(s32[3]{0:T(128)S(1)} %bitcast.23, s32[2]{0:T(128)S(1)} %pad_add_fusion.place, f32[1,128,128]{2,1,0:T(8,128)S(1)} %copy-done.6, f32[1,128,128]{2,1,0:T(8,128)S(1)} %copy-done.15, f32[1,3,128,128]{3,2,1,0:T(8,128)S(1)} %copy-done.13, ...), custom_call_target="tpu_custom_call" | custom-call | flops 700000000 | bytes 2100000 | tf_op jit(solution)/shard_map/separator_part/pallas_call | solution.py:432
  16.9 0.5 collective-permute-start.10
  17.4 0.0 collective-permute-done.2
  17.5 2.4 %collective-permute-start.3 = (f32[128,128]{1,0:T(8,128)S(1)}, f32[128,128]{1,0:T(8,128)S(1)}, u32[]{:S(2)}, u32[]{:S(2)}) collective-permute-start(f32[128,128]{1,0:T(8,128)S(1)} %get-tuple-element.53), channel_id=1, source_target_pairs={{0,6},{2,4},{4,2},{6,0},{8,14},{10,12},{12,10},{14,8},{1,7},{3,5},... | collective-permute-start | bytes 196616 | tf_op jit(solution)/shard_map/ppermute | solution.py:351
  19.9 0.0 collective-permute-start.4
  19.9 1.3 %collective-permute-start.5 = (f32[128,128]{1,0:T(8,128)S(1)}, f32[128,128]{1,0:T(8,128)S(1)}, u32[]{:S(2)}, u32[]{:S(2)}) collective-permute-start(f32[128,128]{1,0:T(8,128)S(1)} %get-tuple-element.51.after), channel_id=1, source_target_pairs={{0,2},{2,0},{4,6},{6,4},{8,10},{10,8},{12,14},{14,12},{1,3},{3,1},... | collective-permute-start | bytes 196616 | tf_op jit(solution)/shard_map/ppermute | solution.py:351
  21.1 2.0 %root_sweeps.1 = (f32[512,512]{1,0:T(8,128)S(1)}, f32[512,512]{1,0:T(8,128)S(1)}) custom-call(f32[4,128,128]{2,1,0:T(8,128)S(1)} %copy-done.11, f32[4,128,128]{2,1,0:T(8,128)S(1)} %copy-done.12, f32[512,512]{1,0:T(8,128)S(1)} %copy-done.8, f32[512,512]{1,0:T(8,128)S(1)} %copy-done.9, f32[128,128]{1,0:T(8,128)S(1)} %get-tuple-element.51.after), custom_call_target="tpu_custom_call" | custom-call | flops 2300000000 | bytes 6899999 | tf_op jit(solution)/shard_map/root_sweeps/pallas_call | solution.py:459
  23.1 0.0 collective-permute-done.3
  23.1 1.0 %collective-permute-done.4 = f32[128,128]{1,0:T(8,128)S(1)} collective-permute-done((f32[128,128]{1,0:T(8,128)S(1)}, f32[128,128]{1,0:T(8,128)S(1)}, u32[]{:S(2)}, u32[]{:S(2)}) %collective-permute-start.4) | collective-permute-done | bytes 65568 | tf_op jit(solution)/shard_map/ppermute | solution.py:351
  24.1 0.0 collective-permute-done.5
  24.2 3.3 %collective-permute-start.6 = (f32[128,128]{1,0:T(8,128)S(1)}, f32[128,128]{1,0:T(8,128)S(1)}, u32[]{:S(2)}, u32[]{:S(2)}) collective-permute-start(f32[128,128]{1,0:T(8,128)S(1)} %fusion.6.after), channel_id=1, source_target_pairs={{0,8},{2,10},{4,12},{6,14},{8,0},{10,2},{12,4},{14,6},{1,9},{3,11}... | collective-permute-start | bytes 196616 | tf_op jit(solution)/shard_map/ppermute | solution.py:351
  27.5 0.9 %root_operator.1.operator = bf16[1024,1024]{1,0:T(8,128)(2,1)S(1)} custom-call(f32[512,512]{1,0:T(8,128)S(1)} %get-tuple-element.38.forward, f32[512,512]{1,0:T(8,128)S(1)} %get-tuple-element.39.backward, f32[128,128]{1,0:T(8,128)S(1)} %fusion.6.after), custom_call_target="tpu_custom_call" | custom-call | flops 1000000000 | bytes 3000000 | tf_op jit(solution)/shard_map/root_operator/pallas_call | solution.py:472
  28.4 0.0 copy-start.10
  28.4 1.5 %collective-permute-done.6 = f32[128,128]{1,0:T(8,128)S(1)} collective-permute-done((f32[128,128]{1,0:T(8,128)S(1)}, f32[128,128]{1,0:T(8,128)S(1)}, u32[]{:S(2)}, u32[]{:S(2)}) %collective-permute-start.6) | collective-permute-done | bytes 65568 | tf_op jit(solution)/shard_map/ppermute | solution.py:351
  29.9 2.3 %collective-permute-start.7 = (f32[128,128]{1,0:T(8,128)S(1)}, f32[128,128]{1,0:T(8,128)S(1)}, u32[]{:S(2)}, u32[]{:S(2)}) collective-permute-start(f32[128,128]{1,0:T(8,128)S(1)} %add.51.own), channel_id=1, source_target_pairs={{0,6},{2,4},{4,2},{6,0},{8,14},{10,12},{12,10},{14,8},{1,7},{3,5},... | collective-permute-start | bytes 196616 | tf_op jit(solution)/shard_map/ppermute | solution.py:351
  32.2 0.7 %collective-permute-start.8 = (f32[128,128]{1,0:T(8,128)S(1)}, f32[128,128]{1,0:T(8,128)S(1)}, u32[]{:S(2)}, u32[]{:S(2)}) collective-permute-start(f32[128,128]{1,0:T(8,128)S(1)} %add.51.own), channel_id=1, source_target_pairs={{0,4},{2,6},{4,0},{6,2},{8,12},{10,14},{12,8},{14,10},{1,5},{3,7},... | collective-permute-start | bytes 196616 | tf_op jit(solution)/shard_map/ppermute | solution.py:351
  32.9 0.6 %collective-permute-start.9 = (f32[128,128]{1,0:T(8,128)S(1)}, f32[128,128]{1,0:T(8,128)S(1)}, u32[]{:S(2)}, u32[]{:S(2)}) collective-permute-start(f32[128,128]{1,0:T(8,128)S(1)} %add.51.own), channel_id=1, source_target_pairs={{0,2},{2,0},{4,6},{6,4},{8,10},{10,8},{12,14},{14,12},{1,3},{3,1},... | collective-permute-start | bytes 196616 | tf_op jit(solution)/shard_map/ppermute | solution.py:351
  33.5 0.0 collective-permute-done.10.other.other_pack
  33.5 0.1 separator_factors.1.backward
  33.6 1.6 %collective-permute-done.7.three = f32[128,128]{1,0:T(8,128)S(1)} collective-permute-done((f32[128,128]{1,0:T(8,128)S(1)}, f32[128,128]{1,0:T(8,128)S(1)}, u32[]{:S(2)}, u32[]{:S(2)}) %collective-permute-start.7) | collective-permute-done | bytes 65568 | tf_op jit(solution)/shard_map/ppermute | solution.py:351
  35.1 1.3 %collective-permute-done.8.two = f32[128,128]{1,0:T(8,128)S(1)} collective-permute-done((f32[128,128]{1,0:T(8,128)S(1)}, f32[128,128]{1,0:T(8,128)S(1)}, u32[]{:S(2)}, u32[]{:S(2)}) %collective-permute-start.8) | collective-permute-done | bytes 65568 | tf_op jit(solution)/shard_map/ppermute | solution.py:351
  36.4 0.7 %collective-permute-done.9.one = f32[128,128]{1,0:T(8,128)S(1)} collective-permute-done((f32[128,128]{1,0:T(8,128)S(1)}, f32[128,128]{1,0:T(8,128)S(1)}, u32[]{:S(2)}, u32[]{:S(2)}) %collective-permute-start.9) | collective-permute-done | bytes 65568 | tf_op jit(solution)/shard_map/ppermute | solution.py:351
  37.2 2.1 %root_solve.1 = (f32[5,128,128]{2,1,0:T(8,128)S(1)}, f32[128,128]{1,0:T(8,128)S(1)}, f32[128,128]{1,0:T(8,128)S(1)}) custom-call(s32[2]{0:T(128)S(1)} %pad_add_fusion.place, f32[4,128,256]{2,1,0:T(8,128)S(1)} %copy-done.10, bf16[1024,1024]{1,0:T(8,128)(2,1)S(1)} %root_operator.1.operator, f32[128,128]{1,0:T(8,128)S(1)} %collective-permute-done.7.three, ...), custom_call_target="tpu_custom_call" | custom-call | flops 2000000000 | bytes 6000000 | tf_op jit(solution)/shard_map/root_solve/pallas_call | solution.py:491
  39.3 0.1 collective-permute-start.11
  39.4 2.2 %collective-permute-start.12 = (f32[128,128]{1,0:T(8,128)S(1)}, f32[128,128]{1,0:T(8,128)S(1)}, u32[]{:S(2)}, u32[]{:S(2)}) collective-permute-start(f32[128,128]{1,0:T(8,128)S(1)} %get-tuple-element.45.after.sep_own.own), channel_id=1, source_target_pairs={{0,8},{1,9},{2,10},{3,11},{4,12},{5,13},{6,14},{7,15},{8,0},{9,1},... | collective-permute-start | bytes 196616 | tf_op jit(solution)/shard_map/ppermute | solution.py:348
  41.6 2.8 %collective-permute-start.14 = (f32[128,128]{1,0:T(8,128)S(1)}, f32[128,128]{1,0:T(8,128)S(1)}, u32[]{:S(2)}, u32[]{:S(2)}) collective-permute-start(f32[128,128]{1,0:T(8,128)S(1)} %get-tuple-element.45.after.sep_own.own), channel_id=1, source_target_pairs={{0,2},{1,3},{2,4},{3,5},{4,6},{5,7},{6,8},{7,9},{8,10},{9,11},{10,... | collective-permute-start | bytes 196616 | tf_op jit(solution)/shard_map/ppermute | solution.py:348
  44.4 0.0 collective-permute-start.13
  44.4 0.5 collective-permute-start.15
  44.9 0.8 %leaf_operators.1.operator = bf16[12,256,256]{2,1,0:T(8,128)(2,1)S(1)} custom-call(f32[12,128,128]{2,1,0:T(8,128)S(1)} %copy-done.4, f32[12,4,128,128]{3,2,1,0:T(8,128)S(1)} %copy-done, f32[128,128]{1,0:T(8,128)S(1)} %get-tuple-element.45.after.sep_own.own), custom_call_target="tpu_custom_call" | custom-call | flops 1000000000 | bytes 3000000 | tf_op jit(solution)/shard_map/leaf_operators/pallas_call | solution.py:517
  45.7 0.0 collective-permute-done.11.other
  45.7 3.5 %leaf_root_part.1 = (f32[12,128,256]{2,1,0:T(8,128)S(1)}, f32[4,128,256]{2,1,0:T(8,128)}, f32[1,128,256]{2,1,0:T(8,128)}) custom-call(s32[4,12]{1,0:T(4,128)S(1)} %bitcast.20, s32[2]{0:T(128)S(1)} %pad_add_fusion.place, f32[12,4,128,128]{3,2,1,0:T(8,128)S(1)} %copy-done, f32[12,4,128,128]{3,2,1,0:T(8,128)S(1)} %copy-done, f32[12,4,128,128]{3,2,1,0:T(8,128)S(1)} %copy-done, ...), custom_call_target="tpu_custom_call" | custom-call | flops 3000000000 | bytes 9000000 | tf_op jit(solution)/shard_map/leaf_root_part/pallas_call | solution.py:528
  49.2 0.0 collective-permute-done.12.far
  49.2 3.3 %collective-permute-done.13.far_other = f32[128,128]{1,0:T(8,128)S(1)} collective-permute-done((f32[128,128]{1,0:T(8,128)S(1)}, f32[128,128]{1,0:T(8,128)S(1)}, u32[]{:S(2)}, u32[]{:S(2)}) %collective-permute-start.13) | collective-permute-done | bytes 65568 | tf_op jit(solution)/shard_map/ppermute | solution.py:348
  52.6 0.0 collective-permute-done.14.near
  52.6 0.0 collective-permute-done.15.near_other
  52.6 2.1 %leaf_backward.1 = f32[12,128,256]{2,1,0:T(8,128)} custom-call(s32[4,12]{1,0:T(4,128)S(1)} %bitcast.21, s32[2]{0:T(128)S(1)} %pad_add_fusion.place, bf16[12,256,256]{2,1,0:T(8,128)(2,1)S(1)} %leaf_operators.1.operator, f32[12,128,256]{2,1,0:T(8,128)S(1)} %get-tuple-element.47.part, f32[128,128]{1,0:T(8,128)S(1)} %get-tuple-element.45.after.sep_own.own, ...), custom_call_target="tpu_custom_call" | custom-call | flops 2000000000 | bytes 6000000 | tf_op jit(solution)/shard_map/leaf_backward/pallas_call | solution.py:570
  (20 shorter events, 0.1 us)
Async XLA Ops:
  0.6 7.0 %copy-start.1 = (f32[12,4,128,128]{3,2,1,0:T(8,128)S(1)}, f32[12,4,128,128]{3,2,1,0:T(8,128)}, u32[]{:S(2)}) copy-start(f32[12,4,128,128]{3,2,1,0:T(8,128)} %three.2) | copy-start | bytes 9437188
  0.6 7.0 %copy-start.7 = (s32[12,4]{0,1:T(4,128)S(1)}, s32[12,4]{0,1:T(4,128)}, u32[]{:S(2)}) copy-start(s32[12,4]{0,1:T(4,128)} %param.22) | copy-start | bytes 580
  4.5 9.2 %collective-permute-start = (f32[128,256]{1,0:T(8,128)}, f32[128,256]{1,0:T(8,128)S(1)}, u32[]{:S(2)}, u32[]{:S(2)}) collective-permute-start(f32[128,256]{1,0:T(8,128)} %get-tuple-element.29), channel_id=1, source_target_pairs={{0,8},{1,9},{2,10},{3,11},{4,12},{5,13},{6,14},{7,15},{8,0},{9,1},... | collective-permute-start | bytes 393224 | tf_op jit(solution)/shard_map/ppermute | solution.py:348
  7.1 7.8 %collective-permute-start.1 = (f32[128,256]{1,0:T(8,128)}, f32[128,256]{1,0:T(8,128)S(1)}, u32[]{:S(2)}, u32[]{:S(2)}) collective-permute-start(f32[128,256]{1,0:T(8,128)} %get-tuple-element.30), channel_id=1, source_target_pairs={{0,14},{1,15},{2,0},{3,1},{4,2},{5,3},{6,4},{7,5},{8,6},{9,7},{10,... | collective-permute-start | bytes 393224 | tf_op jit(solution)/shard_map/ppermute | solution.py:348
  7.6 1.4 %copy-start.2 = (f32[12,128,256]{2,1,0:T(8,128)S(1)}, f32[12,128,256]{2,1,0:T(8,128)}, u32[]{:S(2)}) copy-start(f32[12,128,256]{2,1,0:T(8,128)} %get-tuple-element.27.after.solved) | copy-start | bytes 4718596
  9.0 2.4 %copy-start.3 = (f32[12,128,256]{2,1,0:T(8,128)S(1)}, f32[12,128,256]{2,1,0:T(8,128)}, u32[]{:S(2)}) copy-start(f32[12,128,256]{2,1,0:T(8,128)} %get-tuple-element.27.after.solved) | copy-start | bytes 4718596
  9.0 2.5 %copy-start.5 = (f32[1,3,128,128]{3,2,1,0:T(8,128)S(1)}, f32[1,3,128,128]{3,2,1,0:T(8,128)}, u32[]{:S(2)}) copy-start(f32[1,3,128,128]{3,2,1,0:T(8,128)} %lower.2) | copy-start | bytes 589828
  9.0 2.5 %copy-start.6 = (f32[1,128,128]{2,1,0:T(8,128)S(1)}, f32[1,128,128]{2,1,0:T(8,128)}, u32[]{:S(2)}) copy-start(f32[1,128,128]{2,1,0:T(8,128)} %lower_inverse.5) | copy-start | bytes 196612
  11.5 3.4 %copy-start.14 = (f32[1,128,256]{2,1,0:T(8,128)S(1)}, f32[1,128,256]{2,1,0:T(8,128)}, u32[]{:S(2)}) copy-start(f32[1,128,256]{2,1,0:T(8,128)} %rhs.4) | copy-start | bytes 393220
  11.5 3.4 %copy-start.16 = (s32[1,3]{1,0:T(1,128)S(1)}, s32[1,3]{1,0:T(1,128)}, u32[]{:S(2)}) copy-start(s32[1,3]{1,0:T(1,128)} %param.28) | copy-start | bytes 40
  11.5 3.3 %copy-start.17 = (f32[128,256]{1,0:T(8,128)S(1)}, f32[128,256]{1,0:T(8,128)}, u32[]{:S(2)}) copy-start(f32[128,256]{1,0:T(8,128)} %get-tuple-element.28.own) | copy-start | bytes 393220
  14.9 1.0 %copy-start.13 = (f32[1,3,128,128]{3,2,1,0:T(8,128)S(1)}, f32[1,3,128,128]{3,2,1,0:T(8,128)}, u32[]{:S(2)}) copy-start(f32[1,3,128,128]{3,2,1,0:T(8,128)} %upper.3) | copy-start | bytes 589828
  14.9 1.0 %copy-start.15 = (f32[1,128,128]{2,1,0:T(8,128)S(1)}, f32[1,128,128]{2,1,0:T(8,128)}, u32[]{:S(2)}) copy-start(f32[1,128,128]{2,1,0:T(8,128)} %upper_inverse.3) | copy-start | bytes 196612
  15.8 1.7 %collective-permute-start.2 = (f32[4,128,128]{2,1,0:T(8,128)S(1)}, f32[4,128,128]{2,1,0:T(8,128)S(1)}, u32[]{:S(2)}, u32[]{:S(2)}) collective-permute-start(f32[4,128,128]{2,1,0:T(8,128)S(1)} %get-tuple-element.32), channel_id=1, source_target_pairs={{0,1},{1,0},{2,3},{3,2},{4,5},{5,4},{6,7},{7,6},{8,9},{9,8},{10,11... | collective-permute-start | bytes 786440 | tf_op jit(solution)/shard_map/ppermute | solution.py:354
  15.9 5.2 %copy-start.8 = (f32[512,512]{1,0:T(8,128)S(1)}, f32[512,512]{1,0:T(8,128)}, u32[]{:S(2)}) copy-start(f32[512,512]{1,0:T(8,128)} %lower.3) | copy-start | bytes 3145732
  15.9 5.2 %copy-start.9 = (f32[512,512]{1,0:T(8,128)S(1)}, f32[512,512]{1,0:T(8,128)}, u32[]{:S(2)}) copy-start(f32[512,512]{1,0:T(8,128)} %upper.2) | copy-start | bytes 3145732
  15.9 5.2 %copy-start.11 = (f32[4,128,128]{2,1,0:T(8,128)S(1)}, f32[4,128,128]{2,1,0:T(8,128)}, u32[]{:S(2)}) copy-start(f32[4,128,128]{2,1,0:T(8,128)} %lower_inverse.4) | copy-start | bytes 786436
  15.9 5.2 %copy-start.12 = (f32[4,128,128]{2,1,0:T(8,128)S(1)}, f32[4,128,128]{2,1,0:T(8,128)}, u32[]{:S(2)}) copy-start(f32[4,128,128]{2,1,0:T(8,128)} %upper_inverse.2) | copy-start | bytes 786436
  16.9 16.6 %collective-permute-start.10 = (f32[5,128,128]{2,1,0:T(8,128)S(1)}, f32[5,128,128]{2,1,0:T(8,128)S(1)}, u32[]{:S(2)}, u32[]{:S(2)}) collective-permute-start(f32[5,128,128]{2,1,0:T(8,128)S(1)} %get-tuple-element.43.pack), channel_id=1, source_target_pairs={{0,1},{1,0},{2,3},{3,2},{4,5},{5,4},{6,7},{7,6},{8,9},{9,8},{10,11... | collective-permute-start | bytes 983048 | tf_op jit(solution)/shard_map/ppermute | solution.py:354
  17.5 5.7 %collective-permute-start.3 = (f32[128,128]{1,0:T(8,128)S(1)}, f32[128,128]{1,0:T(8,128)S(1)}, u32[]{:S(2)}, u32[]{:S(2)}) collective-permute-start(f32[128,128]{1,0:T(8,128)S(1)} %get-tuple-element.53), channel_id=1, source_target_pairs={{0,6},{2,4},{4,2},{6,0},{8,14},{10,12},{12,10},{14,8},{1,7},{3,5},... | collective-permute-start | bytes 196616 | tf_op jit(solution)/shard_map/ppermute | solution.py:351
  19.9 4.3 %collective-permute-start.4 = (f32[128,128]{1,0:T(8,128)S(1)}, f32[128,128]{1,0:T(8,128)S(1)}, u32[]{:S(2)}, u32[]{:S(2)}) collective-permute-start(f32[128,128]{1,0:T(8,128)S(1)} %get-tuple-element.52), channel_id=1, source_target_pairs={{0,4},{2,6},{4,0},{6,2},{8,12},{10,14},{12,8},{14,10},{1,5},{3,7},... | collective-permute-start | bytes 196616 | tf_op jit(solution)/shard_map/ppermute | solution.py:351
  19.9 4.3 %collective-permute-start.5 = (f32[128,128]{1,0:T(8,128)S(1)}, f32[128,128]{1,0:T(8,128)S(1)}, u32[]{:S(2)}, u32[]{:S(2)}) collective-permute-start(f32[128,128]{1,0:T(8,128)S(1)} %get-tuple-element.51.after), channel_id=1, source_target_pairs={{0,2},{2,0},{4,6},{6,4},{8,10},{10,8},{12,14},{14,12},{1,3},{3,1},... | collective-permute-start | bytes 196616 | tf_op jit(solution)/shard_map/ppermute | solution.py:351
  24.2 5.7 %collective-permute-start.6 = (f32[128,128]{1,0:T(8,128)S(1)}, f32[128,128]{1,0:T(8,128)S(1)}, u32[]{:S(2)}, u32[]{:S(2)}) collective-permute-start(f32[128,128]{1,0:T(8,128)S(1)} %fusion.6.after), channel_id=1, source_target_pairs={{0,8},{2,10},{4,12},{6,14},{8,0},{10,2},{12,4},{14,6},{1,9},{3,11}... | collective-permute-start | bytes 196616 | tf_op jit(solution)/shard_map/ppermute | solution.py:351
  28.4 8.8 %copy-start.10 = (f32[4,128,256]{2,1,0:T(8,128)S(1)}, f32[4,128,256]{2,1,0:T(8,128)}, u32[]{:S(2)}) copy-start(f32[4,128,256]{2,1,0:T(8,128)} %rhs.5) | copy-start | bytes 1572868
  29.9 5.2 %collective-permute-start.7 = (f32[128,128]{1,0:T(8,128)S(1)}, f32[128,128]{1,0:T(8,128)S(1)}, u32[]{:S(2)}, u32[]{:S(2)}) collective-permute-start(f32[128,128]{1,0:T(8,128)S(1)} %add.51.own), channel_id=1, source_target_pairs={{0,6},{2,4},{4,2},{6,0},{8,14},{10,12},{12,10},{14,8},{1,7},{3,5},... | collective-permute-start | bytes 196616 | tf_op jit(solution)/shard_map/ppermute | solution.py:351
  32.2 4.3 %collective-permute-start.8 = (f32[128,128]{1,0:T(8,128)S(1)}, f32[128,128]{1,0:T(8,128)S(1)}, u32[]{:S(2)}, u32[]{:S(2)}) collective-permute-start(f32[128,128]{1,0:T(8,128)S(1)} %add.51.own), channel_id=1, source_target_pairs={{0,4},{2,6},{4,0},{6,2},{8,12},{10,14},{12,8},{14,10},{1,5},{3,7},... | collective-permute-start | bytes 196616 | tf_op jit(solution)/shard_map/ppermute | solution.py:351
  32.9 4.3 %collective-permute-start.9 = (f32[128,128]{1,0:T(8,128)S(1)}, f32[128,128]{1,0:T(8,128)S(1)}, u32[]{:S(2)}, u32[]{:S(2)}) collective-permute-start(f32[128,128]{1,0:T(8,128)S(1)} %add.51.own), channel_id=1, source_target_pairs={{0,2},{2,0},{4,6},{6,4},{8,10},{10,8},{12,14},{14,12},{1,3},{3,1},... | collective-permute-start | bytes 196616 | tf_op jit(solution)/shard_map/ppermute | solution.py:351
  37.2 7.7 %copy-start = (f32[12,4,128,128]{3,2,1,0:T(8,128)S(1)}, f32[12,4,128,128]{3,2,1,0:T(8,128)}, u32[]{:S(2)}) copy-start(f32[12,4,128,128]{3,2,1,0:T(8,128)} %three.3) | copy-start | bytes 9437188
  37.2 7.7 %copy-start.4 = (f32[12,128,128]{2,1,0:T(8,128)S(1)}, f32[12,128,128]{2,1,0:T(8,128)}, u32[]{:S(2)}) copy-start(f32[12,128,128]{2,1,0:T(8,128)} %inverse.5) | copy-start | bytes 2359300
  39.3 6.4 %collective-permute-start.11 = (f32[5,128,128]{2,1,0:T(8,128)S(1)}, f32[5,128,128]{2,1,0:T(8,128)S(1)}, u32[]{:S(2)}, u32[]{:S(2)}) collective-permute-start(f32[5,128,128]{2,1,0:T(8,128)S(1)} %get-tuple-element.46.mine), channel_id=1, source_target_pairs={{0,1},{1,0},{2,3},{3,2},{4,5},{5,4},{6,7},{7,6},{8,9},{9,8},{10,11... | collective-permute-start | bytes 983048 | tf_op jit(solution)/shard_map/ppermute | solution.py:354
  39.4 9.9 %collective-permute-start.12 = (f32[128,128]{1,0:T(8,128)S(1)}, f32[128,128]{1,0:T(8,128)S(1)}, u32[]{:S(2)}, u32[]{:S(2)}) collective-permute-start(f32[128,128]{1,0:T(8,128)S(1)} %get-tuple-element.45.after.sep_own.own), channel_id=1, source_target_pairs={{0,8},{1,9},{2,10},{3,11},{4,12},{5,13},{6,14},{7,15},{8,0},{9,1},... | collective-permute-start | bytes 196616 | tf_op jit(solution)/shard_map/ppermute | solution.py:348
  41.6 11.0 %collective-permute-start.14 = (f32[128,128]{1,0:T(8,128)S(1)}, f32[128,128]{1,0:T(8,128)S(1)}, u32[]{:S(2)}, u32[]{:S(2)}) collective-permute-start(f32[128,128]{1,0:T(8,128)S(1)} %get-tuple-element.45.after.sep_own.own), channel_id=1, source_target_pairs={{0,2},{1,3},{2,4},{3,5},{4,6},{5,7},{6,8},{7,9},{8,10},{9,11},{10,... | collective-permute-start | bytes 196616 | tf_op jit(solution)/shard_map/ppermute | solution.py:348
  44.4 8.2 %collective-permute-start.13 = (f32[128,128]{1,0:T(8,128)S(1)}, f32[128,128]{1,0:T(8,128)S(1)}, u32[]{:S(2)}, u32[]{:S(2)}) collective-permute-start(f32[128,128]{1,0:T(8,128)S(1)} %get-tuple-element.48), channel_id=1, source_target_pairs={{0,9},{1,8},{2,11},{3,10},{4,13},{5,12},{6,15},{7,14},{8,1},{9,0},... | collective-permute-start | bytes 196616 | tf_op jit(solution)/shard_map/ppermute | solution.py:348
  44.4 8.2 %collective-permute-start.15 = (f32[128,128]{1,0:T(8,128)S(1)}, f32[128,128]{1,0:T(8,128)S(1)}, u32[]{:S(2)}, u32[]{:S(2)}) collective-permute-start(f32[128,128]{1,0:T(8,128)S(1)} %get-tuple-element.48), channel_id=1, source_target_pairs={{0,3},{1,2},{2,5},{3,4},{4,7},{5,6},{6,9},{7,8},{8,11},{9,10},{10,... | collective-permute-start | bytes 196616 | tf_op jit(solution)/shard_map/ppermute | solution.py:348

commit v6 on v5

--- a/solution.py
+++ b/solution.py
@@ -118,11 +118,13 @@
             backward[here, done] = -times(upper_inverse[r], inner)
 
 
-def root_operator_kernel(forward, backward, after, root_operator):
+def root_operator_kernel(forward, backward, after, root_operator, root_right):
     w = 128
     size = forward.shape[0]
     for r in range(0, size, w):
-        left = as_left(times(backward[r : r + w, r:], forward[r:, :]))
+        block = times(backward[r : r + w, r:], forward[r:, :])
+        root_right[2 * r : 2 * r + 2 * w, :] = as_right(block)
+        left = as_left(block)
         root_operator[r : r + w, :] = left[:w]
         root_operator[size + r : size + r + w, :] = left[w:]
 
@@ -163,11 +165,10 @@
     mine[...], pack[last] = halves(place[1] == 0, part[:, :128], part[:, 128:])
 
 
-def separator_factors_kernel(pack, other, backward):
+def separator_factors_kernel(pack, other, root_right, backward):
     for i, blocks in enumerate((pack, other)):
-        backward[i] = as_left(
-            jnp.concatenate([blocks[r] for r in range(blocks.shape[0] - 1)], axis=1)
-        )
+        row = jnp.concatenate([blocks[r] for r in range(blocks.shape[0] - 1)], axis=1)
+        backward[i] = as_left(left_times(as_left(row), root_right[...]))
 
 
 def root_kernel(
@@ -185,7 +186,6 @@
     sep_own,
     sep_other,
     pending,
-    right,
 ):
     count, w = rhs.shape[0], rhs.shape[1]
     position = place[0]
@@ -200,9 +200,8 @@
     solution = left_times(operator[...], pending[...])
     for r in range(count):
         out[r] = solution[r * w : r * w + w]
-    right[...] = as_right(solution)
-    sep_own[...] = part[...] - left_times(backward[0], right[...])
-    sep_other[...] = other_pack[count] - left_times(backward[1], right[...])
+    sep_own[...] = part[...] - left_times(backward[0], pending[...])
+    sep_other[...] = other_pack[count] - left_times(backward[1], pending[...])
     out[count] = sep_other[...]
 
 
@@ -446,15 +445,6 @@
         sep_right,
     )
     other_pack = swapped(sep_pack)
-    sep_backward = pl.pallas_call(
-        separator_factors_kernel,
-        in_specs=[whole()] * 2,
-        out_specs=whole(),
-        out_shape=shape((2, 2 * w, 2 * roots * w), BF16),
-        compiler_params=limit(16),
-        cost_estimate=cost(0.2),
-        name="separator_factors",
-    )(sep_pack, other_pack)
     pieces = [mine[j] + other[j] for j in range(4)]
     forward, backward = pl.pallas_call(
         root_sweeps_kernel,
@@ -469,11 +459,14 @@
     arrived, forward, backward = lax.optimization_barrier((arrived, forward, backward))
     total = pieces[0] + arrived[0] + arrived[1] + arrived[2]
 
-    root_operator = pl.pallas_call(
+    root_operator, root_right = pl.pallas_call(
         root_operator_kernel,
         in_specs=[whole()] * 2 + [ANY],
-        out_specs=whole(),
-        out_shape=shape((2 * roots * w, 2 * roots * w), BF16),
+        out_specs=[whole()] * 2,
+        out_shape=[
+            shape((2 * roots * w, 2 * roots * w), BF16),
+            shape((2 * roots * w, roots * w), BF16),
+        ],
         compiler_params=limit(16),
         cost_estimate=cost(1),
         name="root_operator",
@@ -486,6 +479,15 @@
             arrived, root_operator = lax.optimization_barrier((arrived, root_operator))
         total = total + arrived
         bit *= 2
+    sep_backward = pl.pallas_call(
+        separator_factors_kernel,
+        in_specs=[whole()] * 3,
+        out_specs=whole(),
+        out_shape=shape((2, 2 * w, 2 * roots * w), BF16),
+        compiler_params=limit(16),
+        cost_estimate=cost(0.5),
+        name="separator_factors",
+    )(sep_pack, other_pack, root_right)
     others = [crossed(total, j) for j in (3, 2, 1)]
 
     solution_half, sep_own, sep_other = pl.pallas_call(
@@ -493,7 +495,7 @@
         in_specs=[smem] + [whole()] * 9,
         out_specs=[whole()] * 3,
         out_shape=[shape((roots + 1, w, half), F32)] + [half_block] * 2,
-        scratch_shapes=[VMEM((2 * roots * w, half), BF16)] * 2,
+        scratch_shapes=[VMEM((2 * roots * w, half), BF16)],
         compiler_params=limit(16),
         cost_estimate=cost(2),
         name="root_solve",

time: 55.3 us -> 54.7 us (0.989)
  waiting for transfers between devices: 12.4 us -> 11.7 us
    ppermute x7, waiting for transfers between devices: 6.06 us -> 5.43 us  [crossed(): return lax.ppermute(x, 'grid', [(i, i ^ bit) for i in range(peers)])]
    pallas_call x1, Pallas kernels: 0.1 us -> 0.72 us  [per_device(): pl.pallas_call(separator_factors_kernel, in_specs=[whole()] * 3, out_spec...]
    pallas_call x1, Pallas kernels: 2.14 us -> 1.59 us  [per_device(): pl.pallas_call(root_kernel, in_specs=[smem] + [whole()] * 9, out_specs=[w...]
  transfers between devices with their start and end apart: 16 -> 16, of which waited for: 8 -> 8; matrix products, arithmetic and copies ran while one was open for 0% -> 0% of each run, Pallas kernels for 20% -> 21%
where the time goes in v6:
time: 54.7 us; the launch traced here: 54.1 us
  Pallas kernels  20 us (37%)
  starting transfers between devices  19.9 us (36%)
  waiting for transfers between devices  11.7 us (21%)
  local copies, waits for them, and re-layouts  1.5 us (3%)
  between operations  0.92 us (2%)
    ppermute x7, starting transfers between devices, crossed(): return lax.ppermute(x, 'grid', [(i, i ^ bit) for i in range(peers)])  10.6 us
    ppermute x6, starting transfers between devices, shifted(): return lax.ppermute(x, ('grid', 'layer'), pairs)  8.64 us
    ppermute x6, waiting for transfers between devices, shifted(): return lax.ppermute(x, ('grid', 'layer'), pairs)  6.29 us
    ppermute x7, waiting for transfers between devices, crossed(): return lax.ppermute(x, 'grid', [(i, i ^ bit) for i in range(peers)])  5.43 us
    pallas_call x1, Pallas kernels, per_device(): pl.pallas_call(forward_leaf_kernel, grid=(leaves // batch,), in_specs=[wh...  3.83 us
    pallas_call x1, Pallas kernels, per_device(): pl.pallas_call(leaf_root_part_kernel, grid=(leaves // batch,), in_specs=[...  3.5 us
    pallas_call x1, Pallas kernels, per_device(): pl.pallas_call(root_terms_kernel, grid=(leaves // batch,), in_specs=[whol...  2.43 us
    pallas_call x1, Pallas kernels, per_device(): pl.pallas_call(leaf_final_kernel, in_specs=[smem] * 2 + [whole()] * 8, ou...  2.09 us
  transfers between devices with their start and end apart: 16, of which 8 were waited for; matrix products, arithmetic and copies ran while one was open for 0% of the time, Pallas kernels for 21%

profile of v6, /device:TPU:6, one launch (start us, length us, event | category | flops | bytes accessed | tf_op | source)
XLA Modules:
  0.0 54.1 jit_solution(3866584905966249951)
XLA Ops:
  0.6 0.0 copy-start.1
  0.6 0.0 copy-start.7
  0.7 3.8 %leaf_forward.1 = (f32[12,128,256]{2,1,0:T(8,128)}, f32[128,256]{1,0:T(8,128)}, f32[128,256]{1,0:T(8,128)}, f32[128,256]{1,0:T(8,128)}) custom-call(s32[4,12]{1,0:T(4,128)} %bitcast.18, f32[12,128,256]{2,1,0:T(8,128)} %rhs.3, f32[12,128,128]{2,1,0:T(8,128)} %inverse.3, f32[12,4,128,128]{3,2,1,0:T(8,128)} %three.2), custom_call_target="tpu_custom_call" | custom-call | flops 4000000000 | bytes 12000000 | tf_op jit(solution)/shard_map/leaf_forward/pallas_call | solution.py:359
  4.5 2.6 %collective-permute-start = (f32[128,256]{1,0:T(8,128)}, f32[128,256]{1,0:T(8,128)S(1)}, u32[]{:S(2)}, u32[]{:S(2)}) collective-permute-start(f32[128,256]{1,0:T(8,128)} %get-tuple-element.31), channel_id=1, source_target_pairs={{0,8},{1,9},{2,10},{3,11},{4,12},{5,13},{6,14},{7,15},{8,0},{9,1},... | collective-permute-start | bytes 393224 | tf_op jit(solution)/shard_map/ppermute | solution.py:347
  7.1 0.5 collective-permute-start.1
  7.6 0.0 copy-done.1
  7.6 0.0 copy-done.7
  7.6 1.4 %copy-done.2 = f32[12,128,256]{2,1,0:T(8,128)S(1)} copy-done((f32[12,128,256]{2,1,0:T(8,128)S(1)}, f32[12,128,256]{2,1,0:T(8,128)}, u32[]{:S(2)}) %copy-start.2) | copy-done | bytes 1572888
  9.0 2.4 %root_terms.1.root_pending = f32[4,128,256]{2,1,0:T(8,128)S(1)} custom-call(s32[4,12]{1,0:T(4,128)S(1)} %bitcast.19, f32[12,4,128,128]{3,2,1,0:T(8,128)S(1)} %copy-done.1, f32[12,4,128,128]{3,2,1,0:T(8,128)S(1)} %copy-done.1, f32[12,4,128,128]{3,2,1,0:T(8,128)S(1)} %copy-done.1, f32[12,128,256]{2,1,0:T(8,128)S(1)} %copy-done.2), custom_call_target="tpu_custom_call" | custom-call | flops 3000000000 | bytes 9000000 | tf_op jit(solution)/shard_map/root_terms/pallas_call | solution.py:379
  11.5 0.0 copy-done.3
  11.5 0.0 copy-done.5
  11.5 0.0 copy-done.6
  11.5 0.0 copy-start.14
  11.5 0.0 copy-start.16
  11.5 0.0 copy-start.17
  11.5 0.3 separator_operator.1.operator
  11.8 0.1 pad_add_fusion.place
  11.9 1.8 %collective-permute-done.far = f32[128,256]{1,0:T(8,128)S(1)} collective-permute-done((f32[128,256]{1,0:T(8,128)}, f32[128,256]{1,0:T(8,128)S(1)}, u32[]{:S(2)}, u32[]{:S(2)}) %collective-permute-start) | collective-permute-done | bytes 131104 | tf_op jit(solution)/shard_map/ppermute | solution.py:347
  13.7 1.2 %collective-permute-done.1.near = f32[128,256]{1,0:T(8,128)S(1)} collective-permute-done((f32[128,256]{1,0:T(8,128)}, f32[128,256]{1,0:T(8,128)S(1)}, u32[]{:S(2)}, u32[]{:S(2)}) %collective-permute-start.1) | collective-permute-done | bytes 131104 | tf_op jit(solution)/shard_map/ppermute | solution.py:347
  14.9 0.0 copy-done.14
  14.9 0.0 copy-start.13
  14.9 0.0 copy-start.15
  14.9 0.9 %separator_forward.1 = (bf16[256,256]{1,0:T(8,128)(2,1)S(1)}, f32[4,128,128]{2,1,0:T(8,128)S(1)}, f32[4,128,128]{2,1,0:T(8,128)S(1)}) custom-call(s32[3]{0:T(128)S(1)} %bitcast.22, s32[2]{0:T(128)S(1)} %pad_add_fusion.place, f32[1,128,256]{2,1,0:T(8,128)S(1)} %copy-done.14, bf16[768,256]{1,0:T(8,128)(2,1)S(1)} %separator_operator.1.operator, ...), custom_call_target="tpu_custom_call" | custom-call | flops 2000000000 | bytes 6000000 | tf_op jit(solution)/shard_map/separator_forward/pallas_call | solution.py:406
  15.8 0.1 collective-permute-start.2
  15.9 0.0 copy-start.8
  15.9 0.0 copy-start.9
  15.9 0.0 copy-start.11
  15.9 0.0 copy-start.12
  15.9 1.0 %separator_part.1 = (f32[128,128]{1,0:T(8,128)S(1)}, f32[5,128,128]{2,1,0:T(8,128)S(1)}) custom-call(s32[3]{0:T(128)S(1)} %bitcast.23, s32[2]{0:T(128)S(1)} %pad_add_fusion.place, f32[1,128,128]{2,1,0:T(8,128)S(1)} %copy-done.6, f32[1,128,128]{2,1,0:T(8,128)S(1)} %copy-done.15, f32[1,3,128,128]{3,2,1,0:T(8,128)S(1)} %copy-done.13, ...), custom_call_target="tpu_custom_call" | custom-call | flops 700000000 | bytes 2100000 | tf_op jit(solution)/shard_map/separator_part/pallas_call | solution.py:431
  16.9 0.5 collective-permute-start.10
  17.4 0.0 collective-permute-done.2
  17.5 2.4 %collective-permute-start.3 = (f32[128,128]{1,0:T(8,128)S(1)}, f32[128,128]{1,0:T(8,128)S(1)}, u32[]{:S(2)}, u32[]{:S(2)}) collective-permute-start(f32[128,128]{1,0:T(8,128)S(1)} %get-tuple-element.57), channel_id=1, source_target_pairs={{0,6},{2,4},{4,2},{6,0},{8,14},{10,12},{12,10},{14,8},{1,7},{3,5},... | collective-permute-start | bytes 196616 | tf_op jit(solution)/shard_map/ppermute | solution.py:350
  19.9 0.0 collective-permute-start.4
  19.9 1.3 %collective-permute-start.5 = (f32[128,128]{1,0:T(8,128)S(1)}, f32[128,128]{1,0:T(8,128)S(1)}, u32[]{:S(2)}, u32[]{:S(2)}) collective-permute-start(f32[128,128]{1,0:T(8,128)S(1)} %get-tuple-element.55.after), channel_id=1, source_target_pairs={{0,2},{2,0},{4,6},{6,4},{8,10},{10,8},{12,14},{14,12},{1,3},{3,1},... | collective-permute-start | bytes 196616 | tf_op jit(solution)/shard_map/ppermute | solution.py:350
  21.1 2.0 %root_sweeps.1 = (f32[512,512]{1,0:T(8,128)S(1)}, f32[512,512]{1,0:T(8,128)S(1)}) custom-call(f32[4,128,128]{2,1,0:T(8,128)S(1)} %copy-done.11, f32[4,128,128]{2,1,0:T(8,128)S(1)} %copy-done.12, f32[512,512]{1,0:T(8,128)S(1)} %copy-done.8, f32[512,512]{1,0:T(8,128)S(1)} %copy-done.9, f32[128,128]{1,0:T(8,128)S(1)} %get-tuple-element.55.after), custom_call_target="tpu_custom_call" | custom-call | flops 2300000000 | bytes 6899999 | tf_op jit(solution)/shard_map/root_sweeps/pallas_call | solution.py:449
  23.1 0.0 collective-permute-done.3
  23.1 1.0 %collective-permute-done.4 = f32[128,128]{1,0:T(8,128)S(1)} collective-permute-done((f32[128,128]{1,0:T(8,128)S(1)}, f32[128,128]{1,0:T(8,128)S(1)}, u32[]{:S(2)}, u32[]{:S(2)}) %collective-permute-start.4) | collective-permute-done | bytes 65568 | tf_op jit(solution)/shard_map/ppermute | solution.py:350
  24.1 0.0 collective-permute-done.5
  24.1 3.3 %collective-permute-start.6 = (f32[128,128]{1,0:T(8,128)S(1)}, f32[128,128]{1,0:T(8,128)S(1)}, u32[]{:S(2)}, u32[]{:S(2)}) collective-permute-start(f32[128,128]{1,0:T(8,128)S(1)} %fusion.6.after), channel_id=1, source_target_pairs={{0,8},{2,10},{4,12},{6,14},{8,0},{10,2},{12,4},{14,6},{1,9},{3,11}... | collective-permute-start | bytes 196616 | tf_op jit(solution)/shard_map/ppermute | solution.py:350
  27.5 0.9 %root_operator.1 = (bf16[1024,1024]{1,0:T(8,128)(2,1)S(1)}, bf16[1024,512]{1,0:T(8,128)(2,1)S(1)}) custom-call(f32[512,512]{1,0:T(8,128)S(1)} %get-tuple-element.40.forward, f32[512,512]{1,0:T(8,128)S(1)} %get-tuple-element.41.backward, f32[128,128]{1,0:T(8,128)S(1)} %fusion.6.after), custom_call_target="tpu_custom_call" | custom-call | flops 1000000000 | bytes 3000000 | tf_op jit(solution)/shard_map/root_operator/pallas_call | solution.py:462
  28.4 0.0 copy-start.10
  28.4 1.5 %collective-permute-done.6 = f32[128,128]{1,0:T(8,128)S(1)} collective-permute-done((f32[128,128]{1,0:T(8,128)S(1)}, f32[128,128]{1,0:T(8,128)S(1)}, u32[]{:S(2)}, u32[]{:S(2)}) %collective-permute-start.6) | collective-permute-done | bytes 65568 | tf_op jit(solution)/shard_map/ppermute | solution.py:350
  29.9 2.3 %collective-permute-start.7 = (f32[128,128]{1,0:T(8,128)S(1)}, f32[128,128]{1,0:T(8,128)S(1)}, u32[]{:S(2)}, u32[]{:S(2)}) collective-permute-start(f32[128,128]{1,0:T(8,128)S(1)} %add.51.own), channel_id=1, source_target_pairs={{0,6},{2,4},{4,2},{6,0},{8,14},{10,12},{12,10},{14,8},{1,7},{3,5},... | collective-permute-start | bytes 196616 | tf_op jit(solution)/shard_map/ppermute | solution.py:350
  32.2 0.7 %collective-permute-start.8 = (f32[128,128]{1,0:T(8,128)S(1)}, f32[128,128]{1,0:T(8,128)S(1)}, u32[]{:S(2)}, u32[]{:S(2)}) collective-permute-start(f32[128,128]{1,0:T(8,128)S(1)} %add.51.own), channel_id=1, source_target_pairs={{0,4},{2,6},{4,0},{6,2},{8,12},{10,14},{12,8},{14,10},{1,5},{3,7},... | collective-permute-start | bytes 196616 | tf_op jit(solution)/shard_map/ppermute | solution.py:350
  32.9 0.6 %collective-permute-start.9 = (f32[128,128]{1,0:T(8,128)S(1)}, f32[128,128]{1,0:T(8,128)S(1)}, u32[]{:S(2)}, u32[]{:S(2)}) collective-permute-start(f32[128,128]{1,0:T(8,128)S(1)} %add.51.own), channel_id=1, source_target_pairs={{0,2},{2,0},{4,6},{6,4},{8,10},{10,8},{12,14},{14,12},{1,3},{3,1},... | collective-permute-start | bytes 196616 | tf_op jit(solution)/shard_map/ppermute | solution.py:350
  33.4 0.0 collective-permute-done.10.other.other_pack
  33.4 0.7 %separator_factors.1.backward = bf16[2,256,1024]{2,1,0:T(8,128)(2,1)S(1)} custom-call(f32[5,128,128]{2,1,0:T(8,128)S(1)} %get-tuple-element.46.pack, f32[5,128,128]{2,1,0:T(8,128)S(1)} %collective-permute-done.10.other.other_pack, bf16[1024,512]{1,0:T(8,128)(2,1)S(1)} %get-tuple-element.47.root_right), custom_call_target="tpu_custom_call" | custom-call | flops 500000000 | bytes 1500000 | tf_op jit(solution)/shard_map/separator_factors/pallas_call | solution.py:482
  34.2 0.9 %collective-permute-done.7.three = f32[128,128]{1,0:T(8,128)S(1)} collective-permute-done((f32[128,128]{1,0:T(8,128)S(1)}, f32[128,128]{1,0:T(8,128)S(1)}, u32[]{:S(2)}, u32[]{:S(2)}) %collective-permute-start.7) | collective-permute-done | bytes 65568 | tf_op jit(solution)/shard_map/ppermute | solution.py:350
  35.1 1.3 %collective-permute-done.8.two = f32[128,128]{1,0:T(8,128)S(1)} collective-permute-done((f32[128,128]{1,0:T(8,128)S(1)}, f32[128,128]{1,0:T(8,128)S(1)}, u32[]{:S(2)}, u32[]{:S(2)}) %collective-permute-start.8) | collective-permute-done | bytes 65568 | tf_op jit(solution)/shard_map/ppermute | solution.py:350
  36.4 0.7 %collective-permute-done.9.one = f32[128,128]{1,0:T(8,128)S(1)} collective-permute-done((f32[128,128]{1,0:T(8,128)S(1)}, f32[128,128]{1,0:T(8,128)S(1)}, u32[]{:S(2)}, u32[]{:S(2)}) %collective-permute-start.9) | collective-permute-done | bytes 65568 | tf_op jit(solution)/shard_map/ppermute | solution.py:350
  37.2 1.6 %root_solve.1 = (f32[5,128,128]{2,1,0:T(8,128)S(1)}, f32[128,128]{1,0:T(8,128)S(1)}, f32[128,128]{1,0:T(8,128)S(1)}) custom-call(s32[2]{0:T(128)S(1)} %pad_add_fusion.place, f32[4,128,256]{2,1,0:T(8,128)S(1)} %copy-done.10, bf16[1024,1024]{1,0:T(8,128)(2,1)S(1)} %get-tuple-element.43.operator, f32[128,128]{1,0:T(8,128)S(1)} %collective-permute-done.7.three, ...), custom_call_target="tpu_custom_call" | custom-call | flops 2000000000 | bytes 6000000 | tf_op jit(solution)/shard_map/root_solve/pallas_call | solution.py:493
  38.7 0.1 collective-permute-start.11
  38.8 2.2 %collective-permute-start.12 = (f32[128,128]{1,0:T(8,128)S(1)}, f32[128,128]{1,0:T(8,128)S(1)}, u32[]{:S(2)}, u32[]{:S(2)}) collective-permute-start(f32[128,128]{1,0:T(8,128)S(1)} %get-tuple-element.49.after.sep_own.own), channel_id=1, source_target_pairs={{0,8},{1,9},{2,10},{3,11},{4,12},{5,13},{6,14},{7,15},{8,0},{9,1},... | collective-permute-start | bytes 196616 | tf_op jit(solution)/shard_map/ppermute | solution.py:347
  41.0 2.8 %collective-permute-start.14 = (f32[128,128]{1,0:T(8,128)S(1)}, f32[128,128]{1,0:T(8,128)S(1)}, u32[]{:S(2)}, u32[]{:S(2)}) collective-permute-start(f32[128,128]{1,0:T(8,128)S(1)} %get-tuple-element.49.after.sep_own.own), channel_id=1, source_target_pairs={{0,2},{1,3},{2,4},{3,5},{4,6},{5,7},{6,8},{7,9},{8,10},{9,11},{10,... | collective-permute-start | bytes 196616 | tf_op jit(solution)/shard_map/ppermute | solution.py:347
  43.8 0.0 collective-permute-start.13
  43.8 0.5 collective-permute-start.15
  44.3 0.8 %leaf_operators.1.operator = bf16[12,256,256]{2,1,0:T(8,128)(2,1)S(1)} custom-call(f32[12,128,128]{2,1,0:T(8,128)S(1)} %copy-done.4, f32[12,4,128,128]{3,2,1,0:T(8,128)S(1)} %copy-done, f32[128,128]{1,0:T(8,128)S(1)} %get-tuple-element.49.after.sep_own.own), custom_call_target="tpu_custom_call" | custom-call | flops 1000000000 | bytes 3000000 | tf_op jit(solution)/shard_map/leaf_operators/pallas_call | solution.py:519
  45.2 0.0 collective-permute-done.11.other
  45.2 3.5 %leaf_root_part.1 = (f32[12,128,256]{2,1,0:T(8,128)S(1)}, f32[4,128,256]{2,1,0:T(8,128)}, f32[1,128,256]{2,1,0:T(8,128)}) custom-call(s32[4,12]{1,0:T(4,128)S(1)} %bitcast.20, s32[2]{0:T(128)S(1)} %pad_add_fusion.place, f32[12,4,128,128]{3,2,1,0:T(8,128)S(1)} %copy-done, f32[12,4,128,128]{3,2,1,0:T(8,128)S(1)} %copy-done, f32[12,4,128,128]{3,2,1,0:T(8,128)S(1)} %copy-done, ...), custom_call_target="tpu_custom_call" | custom-call | flops 3000000000 | bytes 9000000 | tf_op jit(solution)/shard_map/leaf_root_part/pallas_call | solution.py:530
  48.7 0.0 collective-permute-done.12.far
  48.7 3.3 %collective-permute-done.13.far_other = f32[128,128]{1,0:T(8,128)S(1)} collective-permute-done((f32[128,128]{1,0:T(8,128)S(1)}, f32[128,128]{1,0:T(8,128)S(1)}, u32[]{:S(2)}, u32[]{:S(2)}) %collective-permute-start.13) | collective-permute-done | bytes 65568 | tf_op jit(solution)/shard_map/ppermute | solution.py:347
  52.0 0.0 collective-permute-done.14.near
  52.0 0.0 collective-permute-done.15.near_other
  52.0 2.1 %leaf_backward.1 = f32[12,128,256]{2,1,0:T(8,128)} custom-call(s32[4,12]{1,0:T(4,128)S(1)} %bitcast.21, s32[2]{0:T(128)S(1)} %pad_add_fusion.place, bf16[12,256,256]{2,1,0:T(8,128)(2,1)S(1)} %leaf_operators.1.operator, f32[12,128,256]{2,1,0:T(8,128)S(1)} %get-tuple-element.51.part, f32[128,128]{1,0:T(8,128)S(1)} %get-tuple-element.49.after.sep_own.own, ...), custom_call_target="tpu_custom_call" | custom-call | flops 2000000000 | bytes 6000000 | tf_op jit(solution)/shard_map/leaf_backward/pallas_call | solution.py:572
  (20 shorter events, 0.1 us)
Async XLA Ops:
  0.6 7.0 %copy-start.1 = (f32[12,4,128,128]{3,2,1,0:T(8,128)S(1)}, f32[12,4,128,128]{3,2,1,0:T(8,128)}, u32[]{:S(2)}) copy-start(f32[12,4,128,128]{3,2,1,0:T(8,128)} %three.2) | copy-start | bytes 9437188
  0.6 7.0 %copy-start.7 = (s32[12,4]{0,1:T(4,128)S(1)}, s32[12,4]{0,1:T(4,128)}, u32[]{:S(2)}) copy-start(s32[12,4]{0,1:T(4,128)} %param.22) | copy-start | bytes 580
  4.5 9.2 %collective-permute-start = (f32[128,256]{1,0:T(8,128)}, f32[128,256]{1,0:T(8,128)S(1)}, u32[]{:S(2)}, u32[]{:S(2)}) collective-permute-start(f32[128,256]{1,0:T(8,128)} %get-tuple-element.31), channel_id=1, source_target_pairs={{0,8},{1,9},{2,10},{3,11},{4,12},{5,13},{6,14},{7,15},{8,0},{9,1},... | collective-permute-start | bytes 393224 | tf_op jit(solution)/shard_map/ppermute | solution.py:347
  7.1 7.8 %collective-permute-start.1 = (f32[128,256]{1,0:T(8,128)}, f32[128,256]{1,0:T(8,128)S(1)}, u32[]{:S(2)}, u32[]{:S(2)}) collective-permute-start(f32[128,256]{1,0:T(8,128)} %get-tuple-element.32), channel_id=1, source_target_pairs={{0,14},{1,15},{2,0},{3,1},{4,2},{5,3},{6,4},{7,5},{8,6},{9,7},{10,... | collective-permute-start | bytes 393224 | tf_op jit(solution)/shard_map/ppermute | solution.py:347
  7.6 1.4 %copy-start.2 = (f32[12,128,256]{2,1,0:T(8,128)S(1)}, f32[12,128,256]{2,1,0:T(8,128)}, u32[]{:S(2)}) copy-start(f32[12,128,256]{2,1,0:T(8,128)} %get-tuple-element.29.after.solved) | copy-start | bytes 4718596
  9.0 2.4 %copy-start.3 = (f32[12,128,256]{2,1,0:T(8,128)S(1)}, f32[12,128,256]{2,1,0:T(8,128)}, u32[]{:S(2)}) copy-start(f32[12,128,256]{2,1,0:T(8,128)} %get-tuple-element.29.after.solved) | copy-start | bytes 4718596
  9.0 2.5 %copy-start.5 = (f32[1,3,128,128]{3,2,1,0:T(8,128)S(1)}, f32[1,3,128,128]{3,2,1,0:T(8,128)}, u32[]{:S(2)}) copy-start(f32[1,3,128,128]{3,2,1,0:T(8,128)} %lower.2) | copy-start | bytes 589828
  9.0 2.5 %copy-start.6 = (f32[1,128,128]{2,1,0:T(8,128)S(1)}, f32[1,128,128]{2,1,0:T(8,128)}, u32[]{:S(2)}) copy-start(f32[1,128,128]{2,1,0:T(8,128)} %lower_inverse.5) | copy-start | bytes 196612
  11.5 3.4 %copy-start.14 = (f32[1,128,256]{2,1,0:T(8,128)S(1)}, f32[1,128,256]{2,1,0:T(8,128)}, u32[]{:S(2)}) copy-start(f32[1,128,256]{2,1,0:T(8,128)} %rhs.4) | copy-start | bytes 393220
  11.5 3.4 %copy-start.16 = (s32[1,3]{1,0:T(1,128)S(1)}, s32[1,3]{1,0:T(1,128)}, u32[]{:S(2)}) copy-start(s32[1,3]{1,0:T(1,128)} %param.28) | copy-start | bytes 40
  11.5 3.3 %copy-start.17 = (f32[128,256]{1,0:T(8,128)S(1)}, f32[128,256]{1,0:T(8,128)}, u32[]{:S(2)}) copy-start(f32[128,256]{1,0:T(8,128)} %get-tuple-element.30.own) | copy-start | bytes 393220
  14.9 1.0 %copy-start.13 = (f32[1,3,128,128]{3,2,1,0:T(8,128)S(1)}, f32[1,3,128,128]{3,2,1,0:T(8,128)}, u32[]{:S(2)}) copy-start(f32[1,3,128,128]{3,2,1,0:T(8,128)} %upper.3) | copy-start | bytes 589828
  14.9 1.0 %copy-start.15 = (f32[1,128,128]{2,1,0:T(8,128)S(1)}, f32[1,128,128]{2,1,0:T(8,128)}, u32[]{:S(2)}) copy-start(f32[1,128,128]{2,1,0:T(8,128)} %upper_inverse.3) | copy-start | bytes 196612
  15.8 1.7 %collective-permute-start.2 = (f32[4,128,128]{2,1,0:T(8,128)S(1)}, f32[4,128,128]{2,1,0:T(8,128)S(1)}, u32[]{:S(2)}, u32[]{:S(2)}) collective-permute-start(f32[4,128,128]{2,1,0:T(8,128)S(1)} %get-tuple-element.34), channel_id=1, source_target_pairs={{0,1},{1,0},{2,3},{3,2},{4,5},{5,4},{6,7},{7,6},{8,9},{9,8},{10,11... | collective-permute-start | bytes 786440 | tf_op jit(solution)/shard_map/ppermute | solution.py:353
  15.9 5.2 %copy-start.8 = (f32[512,512]{1,0:T(8,128)S(1)}, f32[512,512]{1,0:T(8,128)}, u32[]{:S(2)}) copy-start(f32[512,512]{1,0:T(8,128)} %lower.3) | copy-start | bytes 3145732
  15.9 5.2 %copy-start.9 = (f32[512,512]{1,0:T(8,128)S(1)}, f32[512,512]{1,0:T(8,128)}, u32[]{:S(2)}) copy-start(f32[512,512]{1,0:T(8,128)} %upper.2) | copy-start | bytes 3145732
  15.9 5.2 %copy-start.11 = (f32[4,128,128]{2,1,0:T(8,128)S(1)}, f32[4,128,128]{2,1,0:T(8,128)}, u32[]{:S(2)}) copy-start(f32[4,128,128]{2,1,0:T(8,128)} %lower_inverse.4) | copy-start | bytes 786436
  15.9 5.2 %copy-start.12 = (f32[4,128,128]{2,1,0:T(8,128)S(1)}, f32[4,128,128]{2,1,0:T(8,128)}, u32[]{:S(2)}) copy-start(f32[4,128,128]{2,1,0:T(8,128)} %upper_inverse.2) | copy-start | bytes 786436
  16.9 16.5 %collective-permute-start.10 = (f32[5,128,128]{2,1,0:T(8,128)S(1)}, f32[5,128,128]{2,1,0:T(8,128)S(1)}, u32[]{:S(2)}, u32[]{:S(2)}) collective-permute-start(f32[5,128,128]{2,1,0:T(8,128)S(1)} %get-tuple-element.46.pack), channel_id=1, source_target_pairs={{0,1},{1,0},{2,3},{3,2},{4,5},{5,4},{6,7},{7,6},{8,9},{9,8},{10,11... | collective-permute-start | bytes 983048 | tf_op jit(solution)/shard_map/ppermute | solution.py:353
  17.5 5.7 %collective-permute-start.3 = (f32[128,128]{1,0:T(8,128)S(1)}, f32[128,128]{1,0:T(8,128)S(1)}, u32[]{:S(2)}, u32[]{:S(2)}) collective-permute-start(f32[128,128]{1,0:T(8,128)S(1)} %get-tuple-element.57), channel_id=1, source_target_pairs={{0,6},{2,4},{4,2},{6,0},{8,14},{10,12},{12,10},{14,8},{1,7},{3,5},... | collective-permute-start | bytes 196616 | tf_op jit(solution)/shard_map/ppermute | solution.py:350
  19.9 4.3 %collective-permute-start.4 = (f32[128,128]{1,0:T(8,128)S(1)}, f32[128,128]{1,0:T(8,128)S(1)}, u32[]{:S(2)}, u32[]{:S(2)}) collective-permute-start(f32[128,128]{1,0:T(8,128)S(1)} %get-tuple-element.56), channel_id=1, source_target_pairs={{0,4},{2,6},{4,0},{6,2},{8,12},{10,14},{12,8},{14,10},{1,5},{3,7},... | collective-permute-start | bytes 196616 | tf_op jit(solution)/shard_map/ppermute | solution.py:350
  19.9 4.3 %collective-permute-start.5 = (f32[128,128]{1,0:T(8,128)S(1)}, f32[128,128]{1,0:T(8,128)S(1)}, u32[]{:S(2)}, u32[]{:S(2)}) collective-permute-start(f32[128,128]{1,0:T(8,128)S(1)} %get-tuple-element.55.after), channel_id=1, source_target_pairs={{0,2},{2,0},{4,6},{6,4},{8,10},{10,8},{12,14},{14,12},{1,3},{3,1},... | collective-permute-start | bytes 196616 | tf_op jit(solution)/shard_map/ppermute | solution.py:350
  24.1 5.7 %collective-permute-start.6 = (f32[128,128]{1,0:T(8,128)S(1)}, f32[128,128]{1,0:T(8,128)S(1)}, u32[]{:S(2)}, u32[]{:S(2)}) collective-permute-start(f32[128,128]{1,0:T(8,128)S(1)} %fusion.6.after), channel_id=1, source_target_pairs={{0,8},{2,10},{4,12},{6,14},{8,0},{10,2},{12,4},{14,6},{1,9},{3,11}... | collective-permute-start | bytes 196616 | tf_op jit(solution)/shard_map/ppermute | solution.py:350
  28.4 8.8 %copy-start.10 = (f32[4,128,256]{2,1,0:T(8,128)S(1)}, f32[4,128,256]{2,1,0:T(8,128)}, u32[]{:S(2)}) copy-start(f32[4,128,256]{2,1,0:T(8,128)} %rhs.5) | copy-start | bytes 1572868
  29.9 5.2 %collective-permute-start.7 = (f32[128,128]{1,0:T(8,128)S(1)}, f32[128,128]{1,0:T(8,128)S(1)}, u32[]{:S(2)}, u32[]{:S(2)}) collective-permute-start(f32[128,128]{1,0:T(8,128)S(1)} %add.51.own), channel_id=1, source_target_pairs={{0,6},{2,4},{4,2},{6,0},{8,14},{10,12},{12,10},{14,8},{1,7},{3,5},... | collective-permute-start | bytes 196616 | tf_op jit(solution)/shard_map/ppermute | solution.py:350
  32.2 4.3 %collective-permute-start.8 = (f32[128,128]{1,0:T(8,128)S(1)}, f32[128,128]{1,0:T(8,128)S(1)}, u32[]{:S(2)}, u32[]{:S(2)}) collective-permute-start(f32[128,128]{1,0:T(8,128)S(1)} %add.51.own), channel_id=1, source_target_pairs={{0,4},{2,6},{4,0},{6,2},{8,12},{10,14},{12,8},{14,10},{1,5},{3,7},... | collective-permute-start | bytes 196616 | tf_op jit(solution)/shard_map/ppermute | solution.py:350
  32.9 4.3 %collective-permute-start.9 = (f32[128,128]{1,0:T(8,128)S(1)}, f32[128,128]{1,0:T(8,128)S(1)}, u32[]{:S(2)}, u32[]{:S(2)}) collective-permute-start(f32[128,128]{1,0:T(8,128)S(1)} %add.51.own), channel_id=1, source_target_pairs={{0,2},{2,0},{4,6},{6,4},{8,10},{10,8},{12,14},{14,12},{1,3},{3,1},... | collective-permute-start | bytes 196616 | tf_op jit(solution)/shard_map/ppermute | solution.py:350
  37.1 7.2 %copy-start = (f32[12,4,128,128]{3,2,1,0:T(8,128)S(1)}, f32[12,4,128,128]{3,2,1,0:T(8,128)}, u32[]{:S(2)}) copy-start(f32[12,4,128,128]{3,2,1,0:T(8,128)} %three.3) | copy-start | bytes 9437188
  37.2 7.2 %copy-start.4 = (f32[12,128,128]{2,1,0:T(8,128)S(1)}, f32[12,128,128]{2,1,0:T(8,128)}, u32[]{:S(2)}) copy-start(f32[12,128,128]{2,1,0:T(8,128)} %inverse.5) | copy-start | bytes 2359300
  38.7 6.4 %collective-permute-start.11 = (f32[5,128,128]{2,1,0:T(8,128)S(1)}, f32[5,128,128]{2,1,0:T(8,128)S(1)}, u32[]{:S(2)}, u32[]{:S(2)}) collective-permute-start(f32[5,128,128]{2,1,0:T(8,128)S(1)} %get-tuple-element.50.mine), channel_id=1, source_target_pairs={{0,1},{1,0},{2,3},{3,2},{4,5},{5,4},{6,7},{7,6},{8,9},{9,8},{10,11... | collective-permute-start | bytes 983048 | tf_op jit(solution)/shard_map/ppermute | solution.py:353
  38.8 9.9 %collective-permute-start.12 = (f32[128,128]{1,0:T(8,128)S(1)}, f32[128,128]{1,0:T(8,128)S(1)}, u32[]{:S(2)}, u32[]{:S(2)}) collective-permute-start(f32[128,128]{1,0:T(8,128)S(1)} %get-tuple-element.49.after.sep_own.own), channel_id=1, source_target_pairs={{0,8},{1,9},{2,10},{3,11},{4,12},{5,13},{6,14},{7,15},{8,0},{9,1},... | collective-permute-start | bytes 196616 | tf_op jit(solution)/shard_map/ppermute | solution.py:347
  41.0 11.0 %collective-permute-start.14 = (f32[128,128]{1,0:T(8,128)S(1)}, f32[128,128]{1,0:T(8,128)S(1)}, u32[]{:S(2)}, u32[]{:S(2)}) collective-permute-start(f32[128,128]{1,0:T(8,128)S(1)} %get-tuple-element.49.after.sep_own.own), channel_id=1, source_target_pairs={{0,2},{1,3},{2,4},{3,5},{4,6},{5,7},{6,8},{7,9},{8,10},{9,11},{10,... | collective-permute-start | bytes 196616 | tf_op jit(solution)/shard_map/ppermute | solution.py:347
  43.8 8.2 %collective-permute-start.13 = (f32[128,128]{1,0:T(8,128)S(1)}, f32[128,128]{1,0:T(8,128)S(1)}, u32[]{:S(2)}, u32[]{:S(2)}) collective-permute-start(f32[128,128]{1,0:T(8,128)S(1)} %get-tuple-element.52), channel_id=1, source_target_pairs={{0,9},{1,8},{2,11},{3,10},{4,13},{5,12},{6,15},{7,14},{8,1},{9,0},... | collective-permute-start | bytes 196616 | tf_op jit(solution)/shard_map/ppermute | solution.py:347
  43.8 8.2 %collective-permute-start.15 = (f32[128,128]{1,0:T(8,128)S(1)}, f32[128,128]{1,0:T(8,128)S(1)}, u32[]{:S(2)}, u32[]{:S(2)}) collective-permute-start(f32[128,128]{1,0:T(8,128)S(1)} %get-tuple-element.52), channel_id=1, source_target_pairs={{0,3},{1,2},{2,5},{3,4},{4,7},{5,6},{6,9},{7,8},{8,11},{9,10},{10,... | collective-permute-start | bytes 196616 | tf_op jit(solution)/shard_map/ppermute | solution.py:347

commit v7 on v6

--- a/solution.py
+++ b/solution.py
@@ -185,6 +185,8 @@
     out,
     sep_own,
     sep_other,
+    own_again,
+    other_again,
     pending,
 ):
     count, w = rhs.shape[0], rhs.shape[1]
@@ -203,6 +205,8 @@
     sep_own[...] = part[...] - left_times(backward[0], pending[...])
     sep_other[...] = other_pack[count] - left_times(backward[1], pending[...])
     out[count] = sep_other[...]
+    own_again[...] = sep_own[...]
+    other_again[...] = sep_other[...]
 
 
 def leaf_operator_kernel(inverse, first, after, operator):
@@ -255,10 +259,10 @@
     part,
     own,
     other,
+    near,
     far,
+    near_other,
     far_other,
-    near,
-    near_other,
     out,
     seps,
     ready,
@@ -490,11 +494,11 @@
     )(sep_pack, other_pack, root_right)
     others = [crossed(total, j) for j in (3, 2, 1)]
 
-    solution_half, sep_own, sep_other = pl.pallas_call(
+    solution_half, sep_own, sep_other, own_again, other_again = pl.pallas_call(
         root_kernel,
         in_specs=[smem] + [whole()] * 9,
-        out_specs=[whole()] * 3,
-        out_shape=[shape((roots + 1, w, half), F32)] + [half_block] * 2,
+        out_specs=[whole()] * 5,
+        out_shape=[shape((roots + 1, w, half), F32)] + [half_block] * 4,
         scratch_shapes=[VMEM((2 * roots * w, half), BF16)],
         compiler_params=limit(16),
         cost_estimate=cost(2),
@@ -512,8 +516,8 @@
 
     far_rows = shifted(sep_own, peers // 2)
     far_other_rows = shifted(sep_other, peers // 2, 1)
-    near_rows = shifted(sep_own, 1)
-    near_other_rows = shifted(sep_other, 1, 1)
+    near_rows = shifted(own_again, 1)
+    near_other_rows = shifted(other_again, 1, 1)
     other_half = swapped(solution_half)
 
     leaf_operator = pl.pallas_call(
@@ -589,10 +593,10 @@
         leaf_part,
         sep_own,
         other_half,
+        near_rows,
         far_rows,
+        near_other_rows,
         far_other_rows,
-        near_rows,
-        near_other_rows,
     )
     return (leaf_sol, separator_solution_rows, root_sol)
 

time: 54.7 us -> 54.5 us (level)
  transfers between devices with their start and end apart: 16 -> 16, of which waited for: 8 -> 9; matrix products, arithmetic and copies ran while one was open for 0% -> 0% of each run, Pallas kernels for 21% -> 22%
where the time goes in v7:
time: 54.5 us; the launch traced here: 54 us
  Pallas kernels  20 us (37%)
  starting transfers between devices  19.9 us (37%)
  waiting for transfers between devices  11.7 us (21%)
  local copies, waits for them, and re-layouts  1.5 us (3%)
  between operations  0.92 us (2%)
    ppermute x7, starting transfers between devices, crossed(): return lax.ppermute(x, 'grid', [(i, i ^ bit) for i in range(peers)])  10.6 us
    ppermute x6, starting transfers between devices, shifted(): return lax.ppermute(x, ('grid', 'layer'), pairs)  8.63 us
    ppermute x6, waiting for transfers between devices, shifted(): return lax.ppermute(x, ('grid', 'layer'), pairs)  6.21 us
    ppermute x7, waiting for transfers between devices, crossed(): return lax.ppermute(x, 'grid', [(i, i ^ bit) for i in range(peers)])  5.43 us
    pallas_call x1, Pallas kernels, per_device(): pl.pallas_call(forward_leaf_kernel, grid=(leaves // batch,), in_specs=[wh...  3.83 us
    pallas_call x1, Pallas kernels, per_device(): pl.pallas_call(leaf_root_part_kernel, grid=(leaves // batch,), in_specs=[...  3.51 us
    pallas_call x1, Pallas kernels, per_device(): pl.pallas_call(root_terms_kernel, grid=(leaves // batch,), in_specs=[whol...  2.43 us
    pallas_call x1, Pallas kernels, per_device(): pl.pallas_call(leaf_final_kernel, in_specs=[smem] * 2 + [whole()] * 8, ou...  2.09 us
  transfers between devices with their start and end apart: 16, of which 9 were waited for; matrix products, arithmetic and copies ran while one was open for 0% of the time, Pallas kernels for 22%

profile of v7, /device:TPU:6, one launch (start us, length us, event | category | flops | bytes accessed | tf_op | source)
XLA Modules:
  0.0 54.0 jit_solution(5336478219797110169)
XLA Ops:
  0.6 0.0 copy-start.1
  0.6 0.0 copy-start.7
  0.7 3.8 %leaf_forward.1 = (f32[12,128,256]{2,1,0:T(8,128)}, f32[128,256]{1,0:T(8,128)}, f32[128,256]{1,0:T(8,128)}, f32[128,256]{1,0:T(8,128)}) custom-call(s32[4,12]{1,0:T(4,128)} %bitcast.18, f32[12,128,256]{2,1,0:T(8,128)} %rhs.3, f32[12,128,128]{2,1,0:T(8,128)} %inverse.3, f32[12,4,128,128]{3,2,1,0:T(8,128)} %three.2), custom_call_target="tpu_custom_call" | custom-call | flops 4000000000 | bytes 12000000 | tf_op jit(solution)/shard_map/leaf_forward/pallas_call | solution.py:363
  4.5 2.6 %collective-permute-start = (f32[128,256]{1,0:T(8,128)}, f32[128,256]{1,0:T(8,128)S(1)}, u32[]{:S(2)}, u32[]{:S(2)}) collective-permute-start(f32[128,256]{1,0:T(8,128)} %get-tuple-element.33), channel_id=1, source_target_pairs={{0,8},{1,9},{2,10},{3,11},{4,12},{5,13},{6,14},{7,15},{8,0},{9,1},... | collective-permute-start | bytes 393224 | tf_op jit(solution)/shard_map/ppermute | solution.py:351
  7.1 0.5 collective-permute-start.1
  7.6 0.0 copy-done.1
  7.6 0.0 copy-done.7
  7.6 1.4 %copy-done.2 = f32[12,128,256]{2,1,0:T(8,128)S(1)} copy-done((f32[12,128,256]{2,1,0:T(8,128)S(1)}, f32[12,128,256]{2,1,0:T(8,128)}, u32[]{:S(2)}) %copy-start.2) | copy-done | bytes 1572888
  9.0 2.4 %root_terms.1.root_pending = f32[4,128,256]{2,1,0:T(8,128)S(1)} custom-call(s32[4,12]{1,0:T(4,128)S(1)} %bitcast.19, f32[12,4,128,128]{3,2,1,0:T(8,128)S(1)} %copy-done.1, f32[12,4,128,128]{3,2,1,0:T(8,128)S(1)} %copy-done.1, f32[12,4,128,128]{3,2,1,0:T(8,128)S(1)} %copy-done.1, f32[12,128,256]{2,1,0:T(8,128)S(1)} %copy-done.2), custom_call_target="tpu_custom_call" | custom-call | flops 3000000000 | bytes 9000000 | tf_op jit(solution)/shard_map/root_terms/pallas_call | solution.py:383
  11.5 0.0 copy-done.3
  11.5 0.0 copy-done.5
  11.5 0.0 copy-start.14
  11.5 0.0 copy-start.16
  11.5 0.0 copy-start.17
  11.5 0.3 separator_operator.1.operator
  11.8 0.1 pad_add_fusion.place
  11.9 1.8 %collective-permute-done.far = f32[128,256]{1,0:T(8,128)S(1)} collective-permute-done((f32[128,256]{1,0:T(8,128)}, f32[128,256]{1,0:T(8,128)S(1)}, u32[]{:S(2)}, u32[]{:S(2)}) %collective-permute-start) | collective-permute-done | bytes 131104 | tf_op jit(solution)/shard_map/ppermute | solution.py:351
  13.7 1.2 %collective-permute-done.1.near = f32[128,256]{1,0:T(8,128)S(1)} collective-permute-done((f32[128,256]{1,0:T(8,128)}, f32[128,256]{1,0:T(8,128)S(1)}, u32[]{:S(2)}, u32[]{:S(2)}) %collective-permute-start.1) | collective-permute-done | bytes 131104 | tf_op jit(solution)/shard_map/ppermute | solution.py:351
  14.9 0.0 copy-start.13
  14.9 0.0 copy-start.15
  14.9 0.9 %separator_forward.1 = (bf16[256,256]{1,0:T(8,128)(2,1)S(1)}, f32[4,128,128]{2,1,0:T(8,128)S(1)}, f32[4,128,128]{2,1,0:T(8,128)S(1)}) custom-call(s32[3]{0:T(128)S(1)} %bitcast.22, s32[2]{0:T(128)S(1)} %pad_add_fusion.place, f32[1,128,256]{2,1,0:T(8,128)S(1)} %copy-done.14, bf16[768,256]{1,0:T(8,128)(2,1)S(1)} %separator_operator.1.operator, ...), custom_call_target="tpu_custom_call" | custom-call | flops 2000000000 | bytes 6000000 | tf_op jit(solution)/shard_map/separator_forward/pallas_call | solution.py:410
  15.8 0.1 collective-permute-start.2
  15.9 0.0 copy-start.8
  15.9 0.0 copy-start.9
  15.9 0.0 copy-start.11
  15.9 0.0 copy-start.12
  15.9 1.0 %separator_part.1 = (f32[128,128]{1,0:T(8,128)S(1)}, f32[5,128,128]{2,1,0:T(8,128)S(1)}) custom-call(s32[3]{0:T(128)S(1)} %bitcast.23, s32[2]{0:T(128)S(1)} %pad_add_fusion.place, f32[1,128,128]{2,1,0:T(8,128)S(1)} %copy-done.6, f32[1,128,128]{2,1,0:T(8,128)S(1)} %copy-done.15, f32[1,3,128,128]{3,2,1,0:T(8,128)S(1)} %copy-done.13, ...), custom_call_target="tpu_custom_call" | custom-call | flops 700000000 | bytes 2100000 | tf_op jit(solution)/shard_map/separator_part/pallas_call | solution.py:435
  16.9 0.5 collective-permute-start.10
  17.4 0.0 collective-permute-done.2
  17.5 2.4 %collective-permute-start.3 = (f32[128,128]{1,0:T(8,128)S(1)}, f32[128,128]{1,0:T(8,128)S(1)}, u32[]{:S(2)}, u32[]{:S(2)}) collective-permute-start(f32[128,128]{1,0:T(8,128)S(1)} %get-tuple-element.61), channel_id=1, source_target_pairs={{0,6},{2,4},{4,2},{6,0},{8,14},{10,12},{12,10},{14,8},{1,7},{3,5},... | collective-permute-start | bytes 196616 | tf_op jit(solution)/shard_map/ppermute | solution.py:354
  19.9 0.0 collective-permute-start.4
  19.9 1.3 %collective-permute-start.5 = (f32[128,128]{1,0:T(8,128)S(1)}, f32[128,128]{1,0:T(8,128)S(1)}, u32[]{:S(2)}, u32[]{:S(2)}) collective-permute-start(f32[128,128]{1,0:T(8,128)S(1)} %get-tuple-element.59.after), channel_id=1, source_target_pairs={{0,2},{2,0},{4,6},{6,4},{8,10},{10,8},{12,14},{14,12},{1,3},{3,1},... | collective-permute-start | bytes 196616 | tf_op jit(solution)/shard_map/ppermute | solution.py:354
  21.1 0.0 copy-done.12
  21.1 2.0 %root_sweeps.1 = (f32[512,512]{1,0:T(8,128)S(1)}, f32[512,512]{1,0:T(8,128)S(1)}) custom-call(f32[4,128,128]{2,1,0:T(8,128)S(1)} %copy-done.11, f32[4,128,128]{2,1,0:T(8,128)S(1)} %copy-done.12, f32[512,512]{1,0:T(8,128)S(1)} %copy-done.8, f32[512,512]{1,0:T(8,128)S(1)} %copy-done.9, f32[128,128]{1,0:T(8,128)S(1)} %get-tuple-element.59.after), custom_call_target="tpu_custom_call" | custom-call | flops 2300000000 | bytes 6899999 | tf_op jit(solution)/shard_map/root_sweeps/pallas_call | solution.py:453
  23.1 0.0 collective-permute-done.3
  23.1 1.0 %collective-permute-done.4 = f32[128,128]{1,0:T(8,128)S(1)} collective-permute-done((f32[128,128]{1,0:T(8,128)S(1)}, f32[128,128]{1,0:T(8,128)S(1)}, u32[]{:S(2)}, u32[]{:S(2)}) %collective-permute-start.4) | collective-permute-done | bytes 65568 | tf_op jit(solution)/shard_map/ppermute | solution.py:354
  24.1 0.0 collective-permute-done.5
  24.1 3.3 %collective-permute-start.6 = (f32[128,128]{1,0:T(8,128)S(1)}, f32[128,128]{1,0:T(8,128)S(1)}, u32[]{:S(2)}, u32[]{:S(2)}) collective-permute-start(f32[128,128]{1,0:T(8,128)S(1)} %fusion.6.after), channel_id=1, source_target_pairs={{0,8},{2,10},{4,12},{6,14},{8,0},{10,2},{12,4},{14,6},{1,9},{3,11}... | collective-permute-start | bytes 196616 | tf_op jit(solution)/shard_map/ppermute | solution.py:354
  27.5 0.9 %root_operator.1 = (bf16[1024,1024]{1,0:T(8,128)(2,1)S(1)}, bf16[1024,512]{1,0:T(8,128)(2,1)S(1)}) custom-call(f32[512,512]{1,0:T(8,128)S(1)} %get-tuple-element.42.forward, f32[512,512]{1,0:T(8,128)S(1)} %get-tuple-element.43.backward, f32[128,128]{1,0:T(8,128)S(1)} %fusion.6.after), custom_call_target="tpu_custom_call" | custom-call | flops 1000000000 | bytes 3000000 | tf_op jit(solution)/shard_map/root_operator/pallas_call | solution.py:466
  28.4 0.0 copy-start.10
  28.4 1.5 %collective-permute-done.6 = f32[128,128]{1,0:T(8,128)S(1)} collective-permute-done((f32[128,128]{1,0:T(8,128)S(1)}, f32[128,128]{1,0:T(8,128)S(1)}, u32[]{:S(2)}, u32[]{:S(2)}) %collective-permute-start.6) | collective-permute-done | bytes 65568 | tf_op jit(solution)/shard_map/ppermute | solution.py:354
  29.9 2.3 %collective-permute-start.7 = (f32[128,128]{1,0:T(8,128)S(1)}, f32[128,128]{1,0:T(8,128)S(1)}, u32[]{:S(2)}, u32[]{:S(2)}) collective-permute-start(f32[128,128]{1,0:T(8,128)S(1)} %add.51.own), channel_id=1, source_target_pairs={{0,6},{2,4},{4,2},{6,0},{8,14},{10,12},{12,10},{14,8},{1,7},{3,5},... | collective-permute-start | bytes 196616 | tf_op jit(solution)/shard_map/ppermute | solution.py:354
  32.2 0.7 %collective-permute-start.8 = (f32[128,128]{1,0:T(8,128)S(1)}, f32[128,128]{1,0:T(8,128)S(1)}, u32[]{:S(2)}, u32[]{:S(2)}) collective-permute-start(f32[128,128]{1,0:T(8,128)S(1)} %add.51.own), channel_id=1, source_target_pairs={{0,4},{2,6},{4,0},{6,2},{8,12},{10,14},{12,8},{14,10},{1,5},{3,7},... | collective-permute-start | bytes 196616 | tf_op jit(solution)/shard_map/ppermute | solution.py:354
  32.9 0.6 %collective-permute-start.9 = (f32[128,128]{1,0:T(8,128)S(1)}, f32[128,128]{1,0:T(8,128)S(1)}, u32[]{:S(2)}, u32[]{:S(2)}) collective-permute-start(f32[128,128]{1,0:T(8,128)S(1)} %add.51.own), channel_id=1, source_target_pairs={{0,2},{2,0},{4,6},{6,4},{8,10},{10,8},{12,14},{14,12},{1,3},{3,1},... | collective-permute-start | bytes 196616 | tf_op jit(solution)/shard_map/ppermute | solution.py:354
  33.4 0.0 collective-permute-done.10.other.other_pack
  33.4 0.7 %separator_factors.1.backward = bf16[2,256,1024]{2,1,0:T(8,128)(2,1)S(1)} custom-call(f32[5,128,128]{2,1,0:T(8,128)S(1)} %get-tuple-element.48.pack, f32[5,128,128]{2,1,0:T(8,128)S(1)} %collective-permute-done.10.other.other_pack, bf16[1024,512]{1,0:T(8,128)(2,1)S(1)} %get-tuple-element.49.root_right), custom_call_target="tpu_custom_call" | custom-call | flops 500000000 | bytes 1500000 | tf_op jit(solution)/shard_map/separator_factors/pallas_call | solution.py:486
  34.2 0.9 %collective-permute-done.7.three = f32[128,128]{1,0:T(8,128)S(1)} collective-permute-done((f32[128,128]{1,0:T(8,128)S(1)}, f32[128,128]{1,0:T(8,128)S(1)}, u32[]{:S(2)}, u32[]{:S(2)}) %collective-permute-start.7) | collective-permute-done | bytes 65568 | tf_op jit(solution)/shard_map/ppermute | solution.py:354
  35.1 1.3 %collective-permute-done.8.two = f32[128,128]{1,0:T(8,128)S(1)} collective-permute-done((f32[128,128]{1,0:T(8,128)S(1)}, f32[128,128]{1,0:T(8,128)S(1)}, u32[]{:S(2)}, u32[]{:S(2)}) %collective-permute-start.8) | collective-permute-done | bytes 65568 | tf_op jit(solution)/shard_map/ppermute | solution.py:354
  36.4 0.7 %collective-permute-done.9.one = f32[128,128]{1,0:T(8,128)S(1)} collective-permute-done((f32[128,128]{1,0:T(8,128)S(1)}, f32[128,128]{1,0:T(8,128)S(1)}, u32[]{:S(2)}, u32[]{:S(2)}) %collective-permute-start.9) | collective-permute-done | bytes 65568 | tf_op jit(solution)/shard_map/ppermute | solution.py:354
  37.2 1.6 %root_solve.1 = (f32[5,128,128]{2,1,0:T(8,128)S(1)}, f32[128,128]{1,0:T(8,128)S(1)}, f32[128,128]{1,0:T(8,128)S(1)}, f32[128,128]{1,0:T(8,128)S(1)}, f32[128,128]{1,0:T(8,128)S(1)}) custom-call(s32[2]{0:T(128)S(1)} %pad_add_fusion.place, f32[4,128,256]{2,1,0:T(8,128)S(1)} %copy-done.10, bf16[1024,1024]{1,0:T(8,128)(2,1)S(1)} %get-tuple-element.45.operator, ...), custom_call_target="tpu_custom_call" | custom-call | flops 2000000000 | bytes 6000000 | tf_op jit(solution)/shard_map/root_solve/pallas_call | solution.py:497
  38.8 0.1 collective-permute-start.11
  38.8 1.9 %collective-permute-start.12 = (f32[128,128]{1,0:T(8,128)S(1)}, f32[128,128]{1,0:T(8,128)S(1)}, u32[]{:S(2)}, u32[]{:S(2)}) collective-permute-start(f32[128,128]{1,0:T(8,128)S(1)} %get-tuple-element.54), channel_id=1, source_target_pairs={{0,2},{1,3},{2,4},{3,5},{4,6},{5,7},{6,8},{7,9},{8,10},{9,11},{10,... | collective-permute-start | bytes 196616 | tf_op jit(solution)/shard_map/ppermute | solution.py:351
  40.8 3.1 %collective-permute-start.13 = (f32[128,128]{1,0:T(8,128)S(1)}, f32[128,128]{1,0:T(8,128)S(1)}, u32[]{:S(2)}, u32[]{:S(2)}) collective-permute-start(f32[128,128]{1,0:T(8,128)S(1)} %get-tuple-element.51.after.sep_own.own), channel_id=1, source_target_pairs={{0,8},{1,9},{2,10},{3,11},{4,12},{5,13},{6,14},{7,15},{8,0},{9,1},... | collective-permute-start | bytes 196616 | tf_op jit(solution)/shard_map/ppermute | solution.py:351
  43.8 0.1 collective-permute-start.14
  44.0 0.4 collective-permute-start.15
  44.3 0.0 copy-done.4
  44.3 0.8 %leaf_operators.1.operator = bf16[12,256,256]{2,1,0:T(8,128)(2,1)S(1)} custom-call(f32[12,128,128]{2,1,0:T(8,128)S(1)} %copy-done.4, f32[12,4,128,128]{3,2,1,0:T(8,128)S(1)} %copy-done, f32[128,128]{1,0:T(8,128)S(1)} %get-tuple-element.51.after.sep_own.own), custom_call_target="tpu_custom_call" | custom-call | flops 1000000000 | bytes 3000000 | tf_op jit(solution)/shard_map/leaf_operators/pallas_call | solution.py:523
  45.2 0.0 collective-permute-done.11.other
  45.2 3.5 %leaf_root_part.1 = (f32[12,128,256]{2,1,0:T(8,128)S(1)}, f32[4,128,256]{2,1,0:T(8,128)}, f32[1,128,256]{2,1,0:T(8,128)}) custom-call(s32[4,12]{1,0:T(4,128)S(1)} %bitcast.20, s32[2]{0:T(128)S(1)} %pad_add_fusion.place, f32[12,4,128,128]{3,2,1,0:T(8,128)S(1)} %copy-done, f32[12,4,128,128]{3,2,1,0:T(8,128)S(1)} %copy-done, f32[12,4,128,128]{3,2,1,0:T(8,128)S(1)} %copy-done, ...), custom_call_target="tpu_custom_call" | custom-call | flops 3000000000 | bytes 9000000 | tf_op jit(solution)/shard_map/leaf_root_part/pallas_call | solution.py:534
  48.7 0.0 collective-permute-done.12.near
  48.7 2.3 %collective-permute-done.13.far = f32[128,128]{1,0:T(8,128)S(1)} collective-permute-done((f32[128,128]{1,0:T(8,128)S(1)}, f32[128,128]{1,0:T(8,128)S(1)}, u32[]{:S(2)}, u32[]{:S(2)}) %collective-permute-start.13) | collective-permute-done | bytes 65568 | tf_op jit(solution)/shard_map/ppermute | solution.py:351
  51.0 0.0 collective-permute-done.14.near_other
  51.0 0.9 %collective-permute-done.15.far_other = f32[128,128]{1,0:T(8,128)S(1)} collective-permute-done((f32[128,128]{1,0:T(8,128)S(1)}, f32[128,128]{1,0:T(8,128)S(1)}, u32[]{:S(2)}, u32[]{:S(2)}) %collective-permute-start.15) | collective-permute-done | bytes 65568 | tf_op jit(solution)/shard_map/ppermute | solution.py:351
  51.9 2.1 %leaf_backward.1 = f32[12,128,256]{2,1,0:T(8,128)} custom-call(s32[4,12]{1,0:T(4,128)S(1)} %bitcast.21, s32[2]{0:T(128)S(1)} %pad_add_fusion.place, bf16[12,256,256]{2,1,0:T(8,128)(2,1)S(1)} %leaf_operators.1.operator, f32[12,128,256]{2,1,0:T(8,128)S(1)} %get-tuple-element.53.part, f32[128,128]{1,0:T(8,128)S(1)} %get-tuple-element.51.after.sep_own.own, ...), custom_call_target="tpu_custom_call" | custom-call | flops 2000000000 | bytes 6000000 | tf_op jit(solution)/shard_map/leaf_backward/pallas_call | solution.py:576
  (20 shorter events, 0.1 us)
Async XLA Ops:
  0.6 7.0 %copy-start.1 = (f32[12,4,128,128]{3,2,1,0:T(8,128)S(1)}, f32[12,4,128,128]{3,2,1,0:T(8,128)}, u32[]{:S(2)}) copy-start(f32[12,4,128,128]{3,2,1,0:T(8,128)} %three.2) | copy-start | bytes 9437188
  0.6 7.0 %copy-start.7 = (s32[12,4]{0,1:T(4,128)S(1)}, s32[12,4]{0,1:T(4,128)}, u32[]{:S(2)}) copy-start(s32[12,4]{0,1:T(4,128)} %param.22) | copy-start | bytes 580
  4.5 9.2 %collective-permute-start = (f32[128,256]{1,0:T(8,128)}, f32[128,256]{1,0:T(8,128)S(1)}, u32[]{:S(2)}, u32[]{:S(2)}) collective-permute-start(f32[128,256]{1,0:T(8,128)} %get-tuple-element.33), channel_id=1, source_target_pairs={{0,8},{1,9},{2,10},{3,11},{4,12},{5,13},{6,14},{7,15},{8,0},{9,1},... | collective-permute-start | bytes 393224 | tf_op jit(solution)/shard_map/ppermute | solution.py:351
  7.1 7.8 %collective-permute-start.1 = (f32[128,256]{1,0:T(8,128)}, f32[128,256]{1,0:T(8,128)S(1)}, u32[]{:S(2)}, u32[]{:S(2)}) collective-permute-start(f32[128,256]{1,0:T(8,128)} %get-tuple-element.34), channel_id=1, source_target_pairs={{0,14},{1,15},{2,0},{3,1},{4,2},{5,3},{6,4},{7,5},{8,6},{9,7},{10,... | collective-permute-start | bytes 393224 | tf_op jit(solution)/shard_map/ppermute | solution.py:351
  7.6 1.4 %copy-start.2 = (f32[12,128,256]{2,1,0:T(8,128)S(1)}, f32[12,128,256]{2,1,0:T(8,128)}, u32[]{:S(2)}) copy-start(f32[12,128,256]{2,1,0:T(8,128)} %get-tuple-element.31.after.solved) | copy-start | bytes 4718596
  9.0 2.4 %copy-start.3 = (f32[12,128,256]{2,1,0:T(8,128)S(1)}, f32[12,128,256]{2,1,0:T(8,128)}, u32[]{:S(2)}) copy-start(f32[12,128,256]{2,1,0:T(8,128)} %get-tuple-element.31.after.solved) | copy-start | bytes 4718596
  9.0 2.5 %copy-start.5 = (f32[1,3,128,128]{3,2,1,0:T(8,128)S(1)}, f32[1,3,128,128]{3,2,1,0:T(8,128)}, u32[]{:S(2)}) copy-start(f32[1,3,128,128]{3,2,1,0:T(8,128)} %lower.2) | copy-start | bytes 589828
  9.0 2.5 %copy-start.6 = (f32[1,128,128]{2,1,0:T(8,128)S(1)}, f32[1,128,128]{2,1,0:T(8,128)}, u32[]{:S(2)}) copy-start(f32[1,128,128]{2,1,0:T(8,128)} %lower_inverse.5) | copy-start | bytes 196612
  11.5 3.4 %copy-start.14 = (f32[1,128,256]{2,1,0:T(8,128)S(1)}, f32[1,128,256]{2,1,0:T(8,128)}, u32[]{:S(2)}) copy-start(f32[1,128,256]{2,1,0:T(8,128)} %rhs.4) | copy-start | bytes 393220
  11.5 3.4 %copy-start.16 = (s32[1,3]{1,0:T(1,128)S(1)}, s32[1,3]{1,0:T(1,128)}, u32[]{:S(2)}) copy-start(s32[1,3]{1,0:T(1,128)} %param.28) | copy-start | bytes 40
  11.5 3.3 %copy-start.17 = (f32[128,256]{1,0:T(8,128)S(1)}, f32[128,256]{1,0:T(8,128)}, u32[]{:S(2)}) copy-start(f32[128,256]{1,0:T(8,128)} %get-tuple-element.32.own) | copy-start | bytes 393220
  14.9 1.0 %copy-start.13 = (f32[1,3,128,128]{3,2,1,0:T(8,128)S(1)}, f32[1,3,128,128]{3,2,1,0:T(8,128)}, u32[]{:S(2)}) copy-start(f32[1,3,128,128]{3,2,1,0:T(8,128)} %upper.3) | copy-start | bytes 589828
  14.9 1.0 %copy-start.15 = (f32[1,128,128]{2,1,0:T(8,128)S(1)}, f32[1,128,128]{2,1,0:T(8,128)}, u32[]{:S(2)}) copy-start(f32[1,128,128]{2,1,0:T(8,128)} %upper_inverse.3) | copy-start | bytes 196612
  15.8 1.7 %collective-permute-start.2 = (f32[4,128,128]{2,1,0:T(8,128)S(1)}, f32[4,128,128]{2,1,0:T(8,128)S(1)}, u32[]{:S(2)}, u32[]{:S(2)}) collective-permute-start(f32[4,128,128]{2,1,0:T(8,128)S(1)} %get-tuple-element.36), channel_id=1, source_target_pairs={{0,1},{1,0},{2,3},{3,2},{4,5},{5,4},{6,7},{7,6},{8,9},{9,8},{10,11... | collective-permute-start | bytes 786440 | tf_op jit(solution)/shard_map/ppermute | solution.py:357
  15.9 5.2 %copy-start.8 = (f32[512,512]{1,0:T(8,128)S(1)}, f32[512,512]{1,0:T(8,128)}, u32[]{:S(2)}) copy-start(f32[512,512]{1,0:T(8,128)} %lower.3) | copy-start | bytes 3145732
  15.9 5.2 %copy-start.9 = (f32[512,512]{1,0:T(8,128)S(1)}, f32[512,512]{1,0:T(8,128)}, u32[]{:S(2)}) copy-start(f32[512,512]{1,0:T(8,128)} %upper.2) | copy-start | bytes 3145732
  15.9 5.2 %copy-start.11 = (f32[4,128,128]{2,1,0:T(8,128)S(1)}, f32[4,128,128]{2,1,0:T(8,128)}, u32[]{:S(2)}) copy-start(f32[4,128,128]{2,1,0:T(8,128)} %lower_inverse.4) | copy-start | bytes 786436
  15.9 5.2 %copy-start.12 = (f32[4,128,128]{2,1,0:T(8,128)S(1)}, f32[4,128,128]{2,1,0:T(8,128)}, u32[]{:S(2)}) copy-start(f32[4,128,128]{2,1,0:T(8,128)} %upper_inverse.2) | copy-start | bytes 786436
  16.9 16.5 %collective-permute-start.10 = (f32[5,128,128]{2,1,0:T(8,128)S(1)}, f32[5,128,128]{2,1,0:T(8,128)S(1)}, u32[]{:S(2)}, u32[]{:S(2)}) collective-permute-start(f32[5,128,128]{2,1,0:T(8,128)S(1)} %get-tuple-element.48.pack), channel_id=1, source_target_pairs={{0,1},{1,0},{2,3},{3,2},{4,5},{5,4},{6,7},{7,6},{8,9},{9,8},{10,11... | collective-permute-start | bytes 983048 | tf_op jit(solution)/shard_map/ppermute | solution.py:357
  17.5 5.7 %collective-permute-start.3 = (f32[128,128]{1,0:T(8,128)S(1)}, f32[128,128]{1,0:T(8,128)S(1)}, u32[]{:S(2)}, u32[]{:S(2)}) collective-permute-start(f32[128,128]{1,0:T(8,128)S(1)} %get-tuple-element.61), channel_id=1, source_target_pairs={{0,6},{2,4},{4,2},{6,0},{8,14},{10,12},{12,10},{14,8},{1,7},{3,5},... | collective-permute-start | bytes 196616 | tf_op jit(solution)/shard_map/ppermute | solution.py:354
  19.9 4.3 %collective-permute-start.4 = (f32[128,128]{1,0:T(8,128)S(1)}, f32[128,128]{1,0:T(8,128)S(1)}, u32[]{:S(2)}, u32[]{:S(2)}) collective-permute-start(f32[128,128]{1,0:T(8,128)S(1)} %get-tuple-element.60), channel_id=1, source_target_pairs={{0,4},{2,6},{4,0},{6,2},{8,12},{10,14},{12,8},{14,10},{1,5},{3,7},... | collective-permute-start | bytes 196616 | tf_op jit(solution)/shard_map/ppermute | solution.py:354
  19.9 4.3 %collective-permute-start.5 = (f32[128,128]{1,0:T(8,128)S(1)}, f32[128,128]{1,0:T(8,128)S(1)}, u32[]{:S(2)}, u32[]{:S(2)}) collective-permute-start(f32[128,128]{1,0:T(8,128)S(1)} %get-tuple-element.59.after), channel_id=1, source_target_pairs={{0,2},{2,0},{4,6},{6,4},{8,10},{10,8},{12,14},{14,12},{1,3},{3,1},... | collective-permute-start | bytes 196616 | tf_op jit(solution)/shard_map/ppermute | solution.py:354
  24.1 5.7 %collective-permute-start.6 = (f32[128,128]{1,0:T(8,128)S(1)}, f32[128,128]{1,0:T(8,128)S(1)}, u32[]{:S(2)}, u32[]{:S(2)}) collective-permute-start(f32[128,128]{1,0:T(8,128)S(1)} %fusion.6.after), channel_id=1, source_target_pairs={{0,8},{2,10},{4,12},{6,14},{8,0},{10,2},{12,4},{14,6},{1,9},{3,11}... | collective-permute-start | bytes 196616 | tf_op jit(solution)/shard_map/ppermute | solution.py:354
  28.4 8.8 %copy-start.10 = (f32[4,128,256]{2,1,0:T(8,128)S(1)}, f32[4,128,256]{2,1,0:T(8,128)}, u32[]{:S(2)}) copy-start(f32[4,128,256]{2,1,0:T(8,128)} %rhs.5) | copy-start | bytes 1572868
  29.9 5.2 %collective-permute-start.7 = (f32[128,128]{1,0:T(8,128)S(1)}, f32[128,128]{1,0:T(8,128)S(1)}, u32[]{:S(2)}, u32[]{:S(2)}) collective-permute-start(f32[128,128]{1,0:T(8,128)S(1)} %add.51.own), channel_id=1, source_target_pairs={{0,6},{2,4},{4,2},{6,0},{8,14},{10,12},{12,10},{14,8},{1,7},{3,5},... | collective-permute-start | bytes 196616 | tf_op jit(solution)/shard_map/ppermute | solution.py:354
  32.2 4.3 %collective-permute-start.8 = (f32[128,128]{1,0:T(8,128)S(1)}, f32[128,128]{1,0:T(8,128)S(1)}, u32[]{:S(2)}, u32[]{:S(2)}) collective-permute-start(f32[128,128]{1,0:T(8,128)S(1)} %add.51.own), channel_id=1, source_target_pairs={{0,4},{2,6},{4,0},{6,2},{8,12},{10,14},{12,8},{14,10},{1,5},{3,7},... | collective-permute-start | bytes 196616 | tf_op jit(solution)/shard_map/ppermute | solution.py:354
  32.9 4.3 %collective-permute-start.9 = (f32[128,128]{1,0:T(8,128)S(1)}, f32[128,128]{1,0:T(8,128)S(1)}, u32[]{:S(2)}, u32[]{:S(2)}) collective-permute-start(f32[128,128]{1,0:T(8,128)S(1)} %add.51.own), channel_id=1, source_target_pairs={{0,2},{2,0},{4,6},{6,4},{8,10},{10,8},{12,14},{14,12},{1,3},{3,1},... | collective-permute-start | bytes 196616 | tf_op jit(solution)/shard_map/ppermute | solution.py:354
  37.1 7.2 %copy-start = (f32[12,4,128,128]{3,2,1,0:T(8,128)S(1)}, f32[12,4,128,128]{3,2,1,0:T(8,128)}, u32[]{:S(2)}) copy-start(f32[12,4,128,128]{3,2,1,0:T(8,128)} %three.3) | copy-start | bytes 9437188
  37.2 7.2 %copy-start.4 = (f32[12,128,128]{2,1,0:T(8,128)S(1)}, f32[12,128,128]{2,1,0:T(8,128)}, u32[]{:S(2)}) copy-start(f32[12,128,128]{2,1,0:T(8,128)} %inverse.5) | copy-start | bytes 2359300
  38.8 6.4 %collective-permute-start.11 = (f32[5,128,128]{2,1,0:T(8,128)S(1)}, f32[5,128,128]{2,1,0:T(8,128)S(1)}, u32[]{:S(2)}, u32[]{:S(2)}) collective-permute-start(f32[5,128,128]{2,1,0:T(8,128)S(1)} %get-tuple-element.52.mine), channel_id=1, source_target_pairs={{0,1},{1,0},{2,3},{3,2},{4,5},{5,4},{6,7},{7,6},{8,9},{9,8},{10,11... | collective-permute-start | bytes 983048 | tf_op jit(solution)/shard_map/ppermute | solution.py:357
  38.8 9.9 %collective-permute-start.12 = (f32[128,128]{1,0:T(8,128)S(1)}, f32[128,128]{1,0:T(8,128)S(1)}, u32[]{:S(2)}, u32[]{:S(2)}) collective-permute-start(f32[128,128]{1,0:T(8,128)S(1)} %get-tuple-element.54), channel_id=1, source_target_pairs={{0,2},{1,3},{2,4},{3,5},{4,6},{5,7},{6,8},{7,9},{8,10},{9,11},{10,... | collective-permute-start | bytes 196616 | tf_op jit(solution)/shard_map/ppermute | solution.py:351
  40.8 10.2 %collective-permute-start.13 = (f32[128,128]{1,0:T(8,128)S(1)}, f32[128,128]{1,0:T(8,128)S(1)}, u32[]{:S(2)}, u32[]{:S(2)}) collective-permute-start(f32[128,128]{1,0:T(8,128)S(1)} %get-tuple-element.51.after.sep_own.own), channel_id=1, source_target_pairs={{0,8},{1,9},{2,10},{3,11},{4,12},{5,13},{6,14},{7,15},{8,0},{9,1},... | collective-permute-start | bytes 196616 | tf_op jit(solution)/shard_map/ppermute | solution.py:351
  43.8 7.2 %collective-permute-start.14 = (f32[128,128]{1,0:T(8,128)S(1)}, f32[128,128]{1,0:T(8,128)S(1)}, u32[]{:S(2)}, u32[]{:S(2)}) collective-permute-start(f32[128,128]{1,0:T(8,128)S(1)} %get-tuple-element.55), channel_id=1, source_target_pairs={{0,3},{1,2},{2,5},{3,4},{4,7},{5,6},{6,9},{7,8},{8,11},{9,10},{10,... | collective-permute-start | bytes 196616 | tf_op jit(solution)/shard_map/ppermute | solution.py:351
  44.0 8.0 %collective-permute-start.15 = (f32[128,128]{1,0:T(8,128)S(1)}, f32[128,128]{1,0:T(8,128)S(1)}, u32[]{:S(2)}, u32[]{:S(2)}) collective-permute-start(f32[128,128]{1,0:T(8,128)S(1)} %get-tuple-element.56), channel_id=1, source_target_pairs={{0,9},{1,8},{2,11},{3,10},{4,13},{5,12},{6,15},{7,14},{8,1},{9,0},... | collective-permute-start | bytes 196616 | tf_op jit(solution)/shard_map/ppermute | solution.py:351

commit v8 on v7

--- a/solution.py
+++ b/solution.py
@@ -57,7 +57,7 @@
     )
 
 
-def forward_leaf_kernel(links, rhs, inverse, first, solved, own, far, near, pending):
+def forward_leaf_kernel(links, rhs, inverse, first, own, far, near, pending):
     step = pl.program_id(0)
 
     @pl.when(step == 0)
@@ -67,9 +67,7 @@
     batch = rhs.shape[0]
     values = []
     for i in range(batch):
-        value = times(inverse[i], rhs[i])
-        solved[i] = value
-        values.append(value)
+        values.append(times(inverse[i], rhs[i]))
     for i in range(batch):
         pending[links[0, step * batch + i]] += times(first[i, 0], values[i])
 
@@ -80,17 +78,19 @@
         far[...] = pending[2]
 
 
-def root_terms_kernel(links, one, two, three, solved, pending):
+def root_terms_kernel(links, rhs, inverse, one, two, three, after, solved, pending):
     step = pl.program_id(0)
 
     @pl.when(step == 0)
     def _():
         pending[...] = jnp.zeros_like(pending)
 
-    batch = solved.shape[0]
+    batch = rhs.shape[0]
     for i in range(batch):
+        value = times(inverse[i], rhs[i])
+        solved[i] = value
         blocks = jnp.concatenate([one[i, 0], two[i, 0], three[i, 0]], axis=0)
-        terms = times(blocks, solved[i])
+        terms = times(blocks, value)
         for n in range(3):
             slot = links[n + 1, step * batch + i] - 3
             pending[slot] += terms[n * 128 : n * 128 + 128]
@@ -360,7 +360,7 @@
     half_block = shape((w, half), F32)
     smem = whole(SMEM)
 
-    leaf_solved, own, far, near = pl.pallas_call(
+    own, far, near = pl.pallas_call(
         forward_leaf_kernel,
         grid=(leaves // batch,),
         in_specs=[
@@ -369,8 +369,8 @@
             leafwise(batch, w, w),
             link(batch, 0, w),
         ],
-        out_specs=[leafwise(batch, w, columns)] + [kept(w, columns)] * 3,
-        out_shape=[shape((leaves, w, columns), F32)] + [shape((w, columns), F32)] * 3,
+        out_specs=[kept(w, columns)] * 3,
+        out_shape=[shape((w, columns), F32)] * 3,
         scratch_shapes=[VMEM((3, w, columns), F32)],
         compiler_params=limit(56),
         cost_estimate=cost(4),
@@ -380,22 +380,24 @@
     far_sum = shifted(far, -(peers // 2))
     near_sum = shifted(near, -1)
 
-    root_pending = pl.pallas_call(
+    leaf_solved, root_pending = pl.pallas_call(
         root_terms_kernel,
         grid=(leaves // batch,),
         in_specs=[
-            whole(SMEM),
+            smem,
+            leafwise(batch, w, columns),
+            leafwise(batch, w, w),
             link(batch, 1, w),
             link(batch, 2, w),
             link(batch, 3, w),
-            leafwise(batch, w, columns),
-        ],
-        out_specs=kept(roots, w, columns),
-        out_shape=shape((roots, w, columns), F32),
+            ANY,
+        ],
+        out_specs=[leafwise(batch, w, columns), kept(roots, w, columns)],
+        out_shape=[shape((leaves, w, columns), F32), shape((roots, w, columns), F32)],
         compiler_params=limit(16),
         cost_estimate=cost(3),
         name="root_terms",
-    )(leaf_links, leaf_lower, leaf_lower, leaf_lower, leaf_solved)
+    )(leaf_links, leaf_rhs, leaf_lower_inverse, leaf_lower, leaf_lower, leaf_lower, own)
 
     sep_forward = pl.pallas_call(
         separator_operator_kernel,
@@ -405,7 +407,7 @@
         compiler_params=limit(16),
         cost_estimate=cost(0.5),
         name="separator_operator",
-    )(separator_lower_inverse, separator_lower_blocks, leaf_solved)
+    )(separator_lower_inverse, separator_lower_blocks, own)
 
     sep_right, mine, theirs = pl.pallas_call(
         separator_kernel,

time: 54.5 us -> 54.2 us (level)
  Pallas kernels: 20 us -> 21 us
  waiting for transfers between devices: 11.7 us -> 10.9 us
    pallas_call x1, Pallas kernels: 2.43 us -> 3.73 us  [per_device(): pl.pallas_call(root_terms_kernel, grid=(leaves // batch,), in_specs=[smem...]
    ppermute x6, waiting for transfers between devices: 6.21 us -> 5.45 us  [shifted(): return lax.ppermute(x, ('grid', 'layer'), pairs)]
    unnamed x36 -> x38, local copies, waits for them, and re-layouts: 1.5 us -> 0.99 us
  transfers between devices with their start and end apart: 16 -> 16, of which waited for: 9 -> 9; matrix products, arithmetic and copies ran while one was open for 0% -> 0% of each run, Pallas kernels for 22% -> 24%
where the time goes in v8:
time: 54.2 us; the launch traced here: 53.7 us
  Pallas kernels  21 us (39%)
  starting transfers between devices  19.8 us (37%)
  waiting for transfers between devices  10.9 us (20%)
  local copies, waits for them, and re-layouts  0.99 us (2%)
  between operations  0.92 us (2%)
    ppermute x7, starting transfers between devices, crossed(): return lax.ppermute(x, 'grid', [(i, i ^ bit) for i in range(peers)])  10.5 us
    ppermute x6, starting transfers between devices, shifted(): return lax.ppermute(x, ('grid', 'layer'), pairs)  8.57 us
    ppermute x6, waiting for transfers between devices, shifted(): return lax.ppermute(x, ('grid', 'layer'), pairs)  5.45 us
    ppermute x7, waiting for transfers between devices, crossed(): return lax.ppermute(x, 'grid', [(i, i ^ bit) for i in range(peers)])  5.42 us
    pallas_call x1, Pallas kernels, per_device(): pl.pallas_call(root_terms_kernel, grid=(leaves // batch,), in_specs=[smem...  3.73 us
    pallas_call x1, Pallas kernels, per_device(): pl.pallas_call(forward_leaf_kernel, grid=(leaves // batch,), in_specs=[wh...  3.56 us
    pallas_call x1, Pallas kernels, per_device(): pl.pallas_call(leaf_root_part_kernel, grid=(leaves // batch,), in_specs=[...  3.51 us
    pallas_call x1, Pallas kernels, per_device(): pl.pallas_call(leaf_final_kernel, in_specs=[smem] * 2 + [whole()] * 8, ou...  2.09 us
  transfers between devices with their start and end apart: 16, of which 9 were waited for; matrix products, arithmetic and copies ran while one was open for 0% of the time, Pallas kernels for 24%

profile of v8, /device:TPU:6, one launch (start us, length us, event | category | flops | bytes accessed | tf_op | source)
XLA Modules:
  0.0 53.7 jit_solution(17523043243138400625)
XLA Ops:
  0.6 0.0 copy-start.1
  0.6 0.0 copy-start.3
  0.7 0.0 copy-start.4
  0.7 0.0 copy-start.7
  0.7 3.6 %leaf_forward.1 = (f32[128,256]{1,0:T(8,128)}, f32[128,256]{1,0:T(8,128)}, f32[128,256]{1,0:T(8,128)}) custom-call(s32[4,12]{1,0:T(4,128)} %bitcast.18, f32[12,128,256]{2,1,0:T(8,128)} %rhs.5, f32[12,128,128]{2,1,0:T(8,128)} %inverse.5, f32[12,4,128,128]{3,2,1,0:T(8,128)} %three.2), custom_call_target="tpu_custom_call" | custom-call | flops 4000000000 | bytes 12000000 | tf_op jit(solution)/shard_map/leaf_forward/pallas_call | solution.py:363
  4.2 2.6 %collective-permute-start = (f32[128,256]{1,0:T(8,128)}, f32[128,256]{1,0:T(8,128)S(1)}, u32[]{:S(2)}, u32[]{:S(2)}) collective-permute-start(f32[128,256]{1,0:T(8,128)} %get-tuple-element.33), channel_id=1, source_target_pairs={{0,8},{1,9},{2,10},{3,11},{4,12},{5,13},{6,14},{7,15},{8,0},{9,1},... | collective-permute-start | bytes 393224 | tf_op jit(solution)/shard_map/ppermute | solution.py:351
  6.8 0.5 collective-permute-start.1
  7.3 0.0 copy-done.1
  7.3 0.0 copy-done.3
  7.3 0.0 copy-done.4
  7.3 0.0 copy-done.7
  7.3 0.0 copy-start.5
  7.3 0.9 %copy-done.5 = f32[128,256]{1,0:T(8,128)S(1)} copy-done((f32[128,256]{1,0:T(8,128)S(1)}, f32[128,256]{1,0:T(8,128)}, u32[]{:S(2)}) %copy-start.5) | copy-done | bytes 131096
  8.3 3.7 %root_terms.1 = (f32[12,128,256]{2,1,0:T(8,128)S(1)}, f32[4,128,256]{2,1,0:T(8,128)S(1)}) custom-call(s32[4,12]{1,0:T(4,128)S(1)} %bitcast.19, f32[12,128,256]{2,1,0:T(8,128)S(1)} %copy-done.3, f32[12,128,128]{2,1,0:T(8,128)S(1)} %copy-done.4, f32[12,4,128,128]{3,2,1,0:T(8,128)S(1)} %copy-done.1, f32[12,4,128,128]{3,2,1,0:T(8,128)S(1)} %copy-done.1, ...), custom_call_target="tpu_custom_call" | custom-call | flops 3000000000 | bytes 9000000 | tf_op jit(solution)/shard_map/root_terms/pallas_call | solution.py:383
  12.0 0.0 copy-start.15
  12.0 0.0 copy-start.18
  12.0 0.3 separator_operator.1.operator
  12.3 0.1 pad_add_fusion.place
  12.4 1.0 %collective-permute-done.far = f32[128,256]{1,0:T(8,128)S(1)} collective-permute-done((f32[128,256]{1,0:T(8,128)}, f32[128,256]{1,0:T(8,128)S(1)}, u32[]{:S(2)}, u32[]{:S(2)}) %collective-permute-start) | collective-permute-done | bytes 131104 | tf_op jit(solution)/shard_map/ppermute | solution.py:351
  13.4 1.2 %collective-permute-done.1.near = f32[128,256]{1,0:T(8,128)S(1)} collective-permute-done((f32[128,256]{1,0:T(8,128)}, f32[128,256]{1,0:T(8,128)S(1)}, u32[]{:S(2)}, u32[]{:S(2)}) %collective-permute-start.1) | collective-permute-done | bytes 131104 | tf_op jit(solution)/shard_map/ppermute | solution.py:351
  14.6 0.0 copy-done.18
  14.6 0.9 %separator_forward.1 = (bf16[256,256]{1,0:T(8,128)(2,1)S(1)}, f32[4,128,128]{2,1,0:T(8,128)S(1)}, f32[4,128,128]{2,1,0:T(8,128)S(1)}) custom-call(s32[3]{0:T(128)S(1)} %bitcast.22, s32[2]{0:T(128)S(1)} %pad_add_fusion.place, f32[1,128,256]{2,1,0:T(8,128)S(1)} %copy-done.15, bf16[768,256]{1,0:T(8,128)(2,1)S(1)} %separator_operator.1.operator, ...), custom_call_target="tpu_custom_call" | custom-call | flops 2000000000 | bytes 6000000 | tf_op jit(solution)/shard_map/separator_forward/pallas_call | solution.py:412
  15.5 0.1 collective-permute-start.2
  15.6 0.0 copy-start.8
  15.6 0.0 copy-start.9
  15.6 0.0 copy-start.11
  15.6 0.0 copy-start.12
  15.6 1.0 %separator_part.1 = (f32[128,128]{1,0:T(8,128)S(1)}, f32[5,128,128]{2,1,0:T(8,128)S(1)}) custom-call(s32[3]{0:T(128)S(1)} %bitcast.23, s32[2]{0:T(128)S(1)} %pad_add_fusion.place, f32[1,128,128]{2,1,0:T(8,128)S(1)} %copy-done.16, f32[1,128,128]{2,1,0:T(8,128)S(1)} %copy-done.17, f32[1,3,128,128]{3,2,1,0:T(8,128)S(1)} %copy-done.14, ...), custom_call_target="tpu_custom_call" | custom-call | flops 700000000 | bytes 2100000 | tf_op jit(solution)/shard_map/separator_part/pallas_call | solution.py:437
  16.6 0.5 collective-permute-start.10
  17.1 0.0 collective-permute-done.2
  17.2 2.4 %collective-permute-start.3 = (f32[128,128]{1,0:T(8,128)S(1)}, f32[128,128]{1,0:T(8,128)S(1)}, u32[]{:S(2)}, u32[]{:S(2)}) collective-permute-start(f32[128,128]{1,0:T(8,128)S(1)} %get-tuple-element.63), channel_id=1, source_target_pairs={{0,6},{2,4},{4,2},{6,0},{8,14},{10,12},{12,10},{14,8},{1,7},{3,5},... | collective-permute-start | bytes 196616 | tf_op jit(solution)/shard_map/ppermute | solution.py:354
  19.6 0.0 collective-permute-start.4
  19.6 1.2 %collective-permute-start.5 = (f32[128,128]{1,0:T(8,128)S(1)}, f32[128,128]{1,0:T(8,128)S(1)}, u32[]{:S(2)}, u32[]{:S(2)}) collective-permute-start(f32[128,128]{1,0:T(8,128)S(1)} %get-tuple-element.61.after), channel_id=1, source_target_pairs={{0,2},{2,0},{4,6},{6,4},{8,10},{10,8},{12,14},{14,12},{1,3},{3,1},... | collective-permute-start | bytes 196616 | tf_op jit(solution)/shard_map/ppermute | solution.py:354
  20.8 0.0 copy-done.8
  20.8 2.0 %root_sweeps.1 = (f32[512,512]{1,0:T(8,128)S(1)}, f32[512,512]{1,0:T(8,128)S(1)}) custom-call(f32[4,128,128]{2,1,0:T(8,128)S(1)} %copy-done.11, f32[4,128,128]{2,1,0:T(8,128)S(1)} %copy-done.12, f32[512,512]{1,0:T(8,128)S(1)} %copy-done.8, f32[512,512]{1,0:T(8,128)S(1)} %copy-done.9, f32[128,128]{1,0:T(8,128)S(1)} %get-tuple-element.61.after), custom_call_target="tpu_custom_call" | custom-call | flops 2300000000 | bytes 6899999 | tf_op jit(solution)/shard_map/root_sweeps/pallas_call | solution.py:455
  22.8 0.0 collective-permute-done.3
  22.8 1.0 %collective-permute-done.4 = f32[128,128]{1,0:T(8,128)S(1)} collective-permute-done((f32[128,128]{1,0:T(8,128)S(1)}, f32[128,128]{1,0:T(8,128)S(1)}, u32[]{:S(2)}, u32[]{:S(2)}) %collective-permute-start.4) | collective-permute-done | bytes 65568 | tf_op jit(solution)/shard_map/ppermute | solution.py:354
  23.8 0.0 collective-permute-done.5
  23.9 3.3 %collective-permute-start.6 = (f32[128,128]{1,0:T(8,128)S(1)}, f32[128,128]{1,0:T(8,128)S(1)}, u32[]{:S(2)}, u32[]{:S(2)}) collective-permute-start(f32[128,128]{1,0:T(8,128)S(1)} %fusion.6.after), channel_id=1, source_target_pairs={{0,8},{2,10},{4,12},{6,14},{8,0},{10,2},{12,4},{14,6},{1,9},{3,11}... | collective-permute-start | bytes 196616 | tf_op jit(solution)/shard_map/ppermute | solution.py:354
  27.2 0.9 %root_operator.1 = (bf16[1024,1024]{1,0:T(8,128)(2,1)S(1)}, bf16[1024,512]{1,0:T(8,128)(2,1)S(1)}) custom-call(f32[512,512]{1,0:T(8,128)S(1)} %get-tuple-element.43.forward, f32[512,512]{1,0:T(8,128)S(1)} %get-tuple-element.44.backward, f32[128,128]{1,0:T(8,128)S(1)} %fusion.6.after), custom_call_target="tpu_custom_call" | custom-call | flops 1000000000 | bytes 3000000 | tf_op jit(solution)/shard_map/root_operator/pallas_call | solution.py:468
  28.1 0.0 copy-start.10
  28.1 1.5 %collective-permute-done.6 = f32[128,128]{1,0:T(8,128)S(1)} collective-permute-done((f32[128,128]{1,0:T(8,128)S(1)}, f32[128,128]{1,0:T(8,128)S(1)}, u32[]{:S(2)}, u32[]{:S(2)}) %collective-permute-start.6) | collective-permute-done | bytes 65568 | tf_op jit(solution)/shard_map/ppermute | solution.py:354
  29.6 2.3 %collective-permute-start.7 = (f32[128,128]{1,0:T(8,128)S(1)}, f32[128,128]{1,0:T(8,128)S(1)}, u32[]{:S(2)}, u32[]{:S(2)}) collective-permute-start(f32[128,128]{1,0:T(8,128)S(1)} %add.51.own), channel_id=1, source_target_pairs={{0,6},{2,4},{4,2},{6,0},{8,14},{10,12},{12,10},{14,8},{1,7},{3,5},... | collective-permute-start | bytes 196616 | tf_op jit(solution)/shard_map/ppermute | solution.py:354
  31.9 0.7 %collective-permute-start.8 = (f32[128,128]{1,0:T(8,128)S(1)}, f32[128,128]{1,0:T(8,128)S(1)}, u32[]{:S(2)}, u32[]{:S(2)}) collective-permute-start(f32[128,128]{1,0:T(8,128)S(1)} %add.51.own), channel_id=1, source_target_pairs={{0,4},{2,6},{4,0},{6,2},{8,12},{10,14},{12,8},{14,10},{1,5},{3,7},... | collective-permute-start | bytes 196616 | tf_op jit(solution)/shard_map/ppermute | solution.py:354
  32.6 0.6 %collective-permute-start.9 = (f32[128,128]{1,0:T(8,128)S(1)}, f32[128,128]{1,0:T(8,128)S(1)}, u32[]{:S(2)}, u32[]{:S(2)}) collective-permute-start(f32[128,128]{1,0:T(8,128)S(1)} %add.51.own), channel_id=1, source_target_pairs={{0,2},{2,0},{4,6},{6,4},{8,10},{10,8},{12,14},{14,12},{1,3},{3,1},... | collective-permute-start | bytes 196616 | tf_op jit(solution)/shard_map/ppermute | solution.py:354
  33.1 0.0 collective-permute-done.10.other.other_pack
  33.2 0.7 %separator_factors.1.backward = bf16[2,256,1024]{2,1,0:T(8,128)(2,1)S(1)} custom-call(f32[5,128,128]{2,1,0:T(8,128)S(1)} %get-tuple-element.49.pack, f32[5,128,128]{2,1,0:T(8,128)S(1)} %collective-permute-done.10.other.other_pack, bf16[1024,512]{1,0:T(8,128)(2,1)S(1)} %get-tuple-element.50.root_right), custom_call_target="tpu_custom_call" | custom-call | flops 500000000 | bytes 1500000 | tf_op jit(solution)/shard_map/separator_factors/pallas_call | solution.py:488
  33.9 0.9 %collective-permute-done.7.three = f32[128,128]{1,0:T(8,128)S(1)} collective-permute-done((f32[128,128]{1,0:T(8,128)S(1)}, f32[128,128]{1,0:T(8,128)S(1)}, u32[]{:S(2)}, u32[]{:S(2)}) %collective-permute-start.7) | collective-permute-done | bytes 65568 | tf_op jit(solution)/shard_map/ppermute | solution.py:354
  34.8 1.3 %collective-permute-done.8.two = f32[128,128]{1,0:T(8,128)S(1)} collective-permute-done((f32[128,128]{1,0:T(8,128)S(1)}, f32[128,128]{1,0:T(8,128)S(1)}, u32[]{:S(2)}, u32[]{:S(2)}) %collective-permute-start.8) | collective-permute-done | bytes 65568 | tf_op jit(solution)/shard_map/ppermute | solution.py:354
  36.1 0.7 %collective-permute-done.9.one = f32[128,128]{1,0:T(8,128)S(1)} collective-permute-done((f32[128,128]{1,0:T(8,128)S(1)}, f32[128,128]{1,0:T(8,128)S(1)}, u32[]{:S(2)}, u32[]{:S(2)}) %collective-permute-start.9) | collective-permute-done | bytes 65568 | tf_op jit(solution)/shard_map/ppermute | solution.py:354
  36.8 1.6 %root_solve.1 = (f32[5,128,128]{2,1,0:T(8,128)S(1)}, f32[128,128]{1,0:T(8,128)S(1)}, f32[128,128]{1,0:T(8,128)S(1)}, f32[128,128]{1,0:T(8,128)S(1)}, f32[128,128]{1,0:T(8,128)S(1)}) custom-call(s32[2]{0:T(128)S(1)} %pad_add_fusion.place, f32[4,128,256]{2,1,0:T(8,128)S(1)} %copy-done.10, bf16[1024,1024]{1,0:T(8,128)(2,1)S(1)} %get-tuple-element.46.operator, ...), custom_call_target="tpu_custom_call" | custom-call | flops 2000000000 | bytes 6000000 | tf_op jit(solution)/shard_map/root_solve/pallas_call | solution.py:499
  38.4 0.1 collective-permute-start.11
  38.5 2.0 %collective-permute-start.12 = (f32[128,128]{1,0:T(8,128)S(1)}, f32[128,128]{1,0:T(8,128)S(1)}, u32[]{:S(2)}, u32[]{:S(2)}) collective-permute-start(f32[128,128]{1,0:T(8,128)S(1)} %get-tuple-element.56), channel_id=1, source_target_pairs={{0,2},{1,3},{2,4},{3,5},{4,6},{5,7},{6,8},{7,9},{8,10},{9,11},{10,... | collective-permute-start | bytes 196616 | tf_op jit(solution)/shard_map/ppermute | solution.py:351
  40.5 3.1 %collective-permute-start.13 = (f32[128,128]{1,0:T(8,128)S(1)}, f32[128,128]{1,0:T(8,128)S(1)}, u32[]{:S(2)}, u32[]{:S(2)}) collective-permute-start(f32[128,128]{1,0:T(8,128)S(1)} %get-tuple-element.52.after.sep_own.own), channel_id=1, source_target_pairs={{0,8},{1,9},{2,10},{3,11},{4,12},{5,13},{6,14},{7,15},{8,0},{9,1},... | collective-permute-start | bytes 196616 | tf_op jit(solution)/shard_map/ppermute | solution.py:351
  43.5 0.1 collective-permute-start.14
  43.7 0.3 collective-permute-start.15
  44.0 0.8 %leaf_operators.1.operator = bf16[12,256,256]{2,1,0:T(8,128)(2,1)S(1)} custom-call(f32[12,128,128]{2,1,0:T(8,128)S(1)} %copy-done.2, f32[12,4,128,128]{3,2,1,0:T(8,128)S(1)} %copy-done, f32[128,128]{1,0:T(8,128)S(1)} %get-tuple-element.52.after.sep_own.own), custom_call_target="tpu_custom_call" | custom-call | flops 1000000000 | bytes 3000000 | tf_op jit(solution)/shard_map/leaf_operators/pallas_call | solution.py:525
  44.8 0.0 collective-permute-done.11.other
  44.8 3.5 %leaf_root_part.1 = (f32[12,128,256]{2,1,0:T(8,128)S(1)}, f32[4,128,256]{2,1,0:T(8,128)}, f32[1,128,256]{2,1,0:T(8,128)}) custom-call(s32[4,12]{1,0:T(4,128)S(1)} %bitcast.20, s32[2]{0:T(128)S(1)} %pad_add_fusion.place, f32[12,4,128,128]{3,2,1,0:T(8,128)S(1)} %copy-done, f32[12,4,128,128]{3,2,1,0:T(8,128)S(1)} %copy-done, f32[12,4,128,128]{3,2,1,0:T(8,128)S(1)} %copy-done, ...), custom_call_target="tpu_custom_call" | custom-call | flops 3000000000 | bytes 9000000 | tf_op jit(solution)/shard_map/leaf_root_part/pallas_call | solution.py:536
  48.4 0.0 collective-permute-done.12.near
  48.4 2.3 %collective-permute-done.13.far = f32[128,128]{1,0:T(8,128)S(1)} collective-permute-done((f32[128,128]{1,0:T(8,128)S(1)}, f32[128,128]{1,0:T(8,128)S(1)}, u32[]{:S(2)}, u32[]{:S(2)}) %collective-permute-start.13) | collective-permute-done | bytes 65568 | tf_op jit(solution)/shard_map/ppermute | solution.py:351
  50.7 0.0 collective-permute-done.14.near_other
  50.7 0.9 %collective-permute-done.15.far_other = f32[128,128]{1,0:T(8,128)S(1)} collective-permute-done((f32[128,128]{1,0:T(8,128)S(1)}, f32[128,128]{1,0:T(8,128)S(1)}, u32[]{:S(2)}, u32[]{:S(2)}) %collective-permute-start.15) | collective-permute-done | bytes 65568 | tf_op jit(solution)/shard_map/ppermute | solution.py:351
  51.6 2.1 %leaf_backward.1 = f32[12,128,256]{2,1,0:T(8,128)} custom-call(s32[4,12]{1,0:T(4,128)S(1)} %bitcast.21, s32[2]{0:T(128)S(1)} %pad_add_fusion.place, bf16[12,256,256]{2,1,0:T(8,128)(2,1)S(1)} %leaf_operators.1.operator, f32[12,128,256]{2,1,0:T(8,128)S(1)} %get-tuple-element.55.part, f32[128,128]{1,0:T(8,128)S(1)} %get-tuple-element.52.after.sep_own.own, ...), custom_call_target="tpu_custom_call" | custom-call | flops 2000000000 | bytes 6000000 | tf_op jit(solution)/shard_map/leaf_backward/pallas_call | solution.py:578
  (22 shorter events, 0.1 us)
Async XLA Ops:
  0.6 6.7 %copy-start.1 = (f32[12,4,128,128]{3,2,1,0:T(8,128)S(1)}, f32[12,4,128,128]{3,2,1,0:T(8,128)}, u32[]{:S(2)}) copy-start(f32[12,4,128,128]{3,2,1,0:T(8,128)} %three.2) | copy-start | bytes 9437188
  0.6 6.7 %copy-start.3 = (f32[12,128,256]{2,1,0:T(8,128)S(1)}, f32[12,128,256]{2,1,0:T(8,128)}, u32[]{:S(2)}) copy-start(f32[12,128,256]{2,1,0:T(8,128)} %rhs.5) | copy-start | bytes 4718596
  0.7 6.7 %copy-start.4 = (f32[12,128,128]{2,1,0:T(8,128)S(1)}, f32[12,128,128]{2,1,0:T(8,128)}, u32[]{:S(2)}) copy-start(f32[12,128,128]{2,1,0:T(8,128)} %inverse.5) | copy-start | bytes 2359300
  0.7 6.7 %copy-start.7 = (s32[12,4]{0,1:T(4,128)S(1)}, s32[12,4]{0,1:T(4,128)}, u32[]{:S(2)}) copy-start(s32[12,4]{0,1:T(4,128)} %param.22) | copy-start | bytes 580
  4.2 9.2 %collective-permute-start = (f32[128,256]{1,0:T(8,128)}, f32[128,256]{1,0:T(8,128)S(1)}, u32[]{:S(2)}, u32[]{:S(2)}) collective-permute-start(f32[128,256]{1,0:T(8,128)} %get-tuple-element.33), channel_id=1, source_target_pairs={{0,8},{1,9},{2,10},{3,11},{4,12},{5,13},{6,14},{7,15},{8,0},{9,1},... | collective-permute-start | bytes 393224 | tf_op jit(solution)/shard_map/ppermute | solution.py:351
  6.8 7.8 %collective-permute-start.1 = (f32[128,256]{1,0:T(8,128)}, f32[128,256]{1,0:T(8,128)S(1)}, u32[]{:S(2)}, u32[]{:S(2)}) collective-permute-start(f32[128,256]{1,0:T(8,128)} %get-tuple-element.34), channel_id=1, source_target_pairs={{0,14},{1,15},{2,0},{3,1},{4,2},{5,3},{6,4},{7,5},{8,6},{9,7},{10,... | collective-permute-start | bytes 393224 | tf_op jit(solution)/shard_map/ppermute | solution.py:351
  7.3 0.9 %copy-start.5 = (f32[128,256]{1,0:T(8,128)S(1)}, f32[128,256]{1,0:T(8,128)}, u32[]{:S(2)}) copy-start(f32[128,256]{1,0:T(8,128)} %get-tuple-element.32.after.own) | copy-start | bytes 393220
  8.2 3.7 %copy-start.6 = (f32[128,256]{1,0:T(8,128)S(1)}, f32[128,256]{1,0:T(8,128)}, u32[]{:S(2)}) copy-start(f32[128,256]{1,0:T(8,128)} %get-tuple-element.32.after.own) | copy-start | bytes 393220
  8.2 3.8 %copy-start.13 = (f32[1,3,128,128]{3,2,1,0:T(8,128)S(1)}, f32[1,3,128,128]{3,2,1,0:T(8,128)}, u32[]{:S(2)}) copy-start(f32[1,3,128,128]{3,2,1,0:T(8,128)} %lower.2) | copy-start | bytes 589828
  8.2 3.8 %copy-start.16 = (f32[1,128,128]{2,1,0:T(8,128)S(1)}, f32[1,128,128]{2,1,0:T(8,128)}, u32[]{:S(2)}) copy-start(f32[1,128,128]{2,1,0:T(8,128)} %lower_inverse.5) | copy-start | bytes 196612
  12.0 2.6 %copy-start.15 = (f32[1,128,256]{2,1,0:T(8,128)S(1)}, f32[1,128,256]{2,1,0:T(8,128)}, u32[]{:S(2)}) copy-start(f32[1,128,256]{2,1,0:T(8,128)} %rhs.6) | copy-start | bytes 393220
  12.0 2.6 %copy-start.18 = (s32[1,3]{1,0:T(1,128)S(1)}, s32[1,3]{1,0:T(1,128)}, u32[]{:S(2)}) copy-start(s32[1,3]{1,0:T(1,128)} %param.28) | copy-start | bytes 40
  14.6 1.0 %copy-start.14 = (f32[1,3,128,128]{3,2,1,0:T(8,128)S(1)}, f32[1,3,128,128]{3,2,1,0:T(8,128)}, u32[]{:S(2)}) copy-start(f32[1,3,128,128]{3,2,1,0:T(8,128)} %upper.3) | copy-start | bytes 589828
  14.6 1.0 %copy-start.17 = (f32[1,128,128]{2,1,0:T(8,128)S(1)}, f32[1,128,128]{2,1,0:T(8,128)}, u32[]{:S(2)}) copy-start(f32[1,128,128]{2,1,0:T(8,128)} %upper_inverse.3) | copy-start | bytes 196612
  15.5 1.7 %collective-permute-start.2 = (f32[4,128,128]{2,1,0:T(8,128)S(1)}, f32[4,128,128]{2,1,0:T(8,128)S(1)}, u32[]{:S(2)}, u32[]{:S(2)}) collective-permute-start(f32[4,128,128]{2,1,0:T(8,128)S(1)} %get-tuple-element.37), channel_id=1, source_target_pairs={{0,1},{1,0},{2,3},{3,2},{4,5},{5,4},{6,7},{7,6},{8,9},{9,8},{10,11... | collective-permute-start | bytes 786440 | tf_op jit(solution)/shard_map/ppermute | solution.py:357
  15.6 5.2 %copy-start.8 = (f32[512,512]{1,0:T(8,128)S(1)}, f32[512,512]{1,0:T(8,128)}, u32[]{:S(2)}) copy-start(f32[512,512]{1,0:T(8,128)} %lower.3) | copy-start | bytes 3145732
  15.6 5.2 %copy-start.9 = (f32[512,512]{1,0:T(8,128)S(1)}, f32[512,512]{1,0:T(8,128)}, u32[]{:S(2)}) copy-start(f32[512,512]{1,0:T(8,128)} %upper.2) | copy-start | bytes 3145732
  15.6 5.2 %copy-start.11 = (f32[4,128,128]{2,1,0:T(8,128)S(1)}, f32[4,128,128]{2,1,0:T(8,128)}, u32[]{:S(2)}) copy-start(f32[4,128,128]{2,1,0:T(8,128)} %lower_inverse.4) | copy-start | bytes 786436
  15.6 5.2 %copy-start.12 = (f32[4,128,128]{2,1,0:T(8,128)S(1)}, f32[4,128,128]{2,1,0:T(8,128)}, u32[]{:S(2)}) copy-start(f32[4,128,128]{2,1,0:T(8,128)} %upper_inverse.2) | copy-start | bytes 786436
  16.6 16.6 %collective-permute-start.10 = (f32[5,128,128]{2,1,0:T(8,128)S(1)}, f32[5,128,128]{2,1,0:T(8,128)S(1)}, u32[]{:S(2)}, u32[]{:S(2)}) collective-permute-start(f32[5,128,128]{2,1,0:T(8,128)S(1)} %get-tuple-element.49.pack), channel_id=1, source_target_pairs={{0,1},{1,0},{2,3},{3,2},{4,5},{5,4},{6,7},{7,6},{8,9},{9,8},{10,11... | collective-permute-start | bytes 983048 | tf_op jit(solution)/shard_map/ppermute | solution.py:357
  17.2 5.7 %collective-permute-start.3 = (f32[128,128]{1,0:T(8,128)S(1)}, f32[128,128]{1,0:T(8,128)S(1)}, u32[]{:S(2)}, u32[]{:S(2)}) collective-permute-start(f32[128,128]{1,0:T(8,128)S(1)} %get-tuple-element.63), channel_id=1, source_target_pairs={{0,6},{2,4},{4,2},{6,0},{8,14},{10,12},{12,10},{14,8},{1,7},{3,5},... | collective-permute-start | bytes 196616 | tf_op jit(solution)/shard_map/ppermute | solution.py:354
  19.6 4.3 %collective-permute-start.4 = (f32[128,128]{1,0:T(8,128)S(1)}, f32[128,128]{1,0:T(8,128)S(1)}, u32[]{:S(2)}, u32[]{:S(2)}) collective-permute-start(f32[128,128]{1,0:T(8,128)S(1)} %get-tuple-element.62), channel_id=1, source_target_pairs={{0,4},{2,6},{4,0},{6,2},{8,12},{10,14},{12,8},{14,10},{1,5},{3,7},... | collective-permute-start | bytes 196616 | tf_op jit(solution)/shard_map/ppermute | solution.py:354
  19.6 4.3 %collective-permute-start.5 = (f32[128,128]{1,0:T(8,128)S(1)}, f32[128,128]{1,0:T(8,128)S(1)}, u32[]{:S(2)}, u32[]{:S(2)}) collective-permute-start(f32[128,128]{1,0:T(8,128)S(1)} %get-tuple-element.61.after), channel_id=1, source_target_pairs={{0,2},{2,0},{4,6},{6,4},{8,10},{10,8},{12,14},{14,12},{1,3},{3,1},... | collective-permute-start | bytes 196616 | tf_op jit(solution)/shard_map/ppermute | solution.py:354
  23.9 5.7 %collective-permute-start.6 = (f32[128,128]{1,0:T(8,128)S(1)}, f32[128,128]{1,0:T(8,128)S(1)}, u32[]{:S(2)}, u32[]{:S(2)}) collective-permute-start(f32[128,128]{1,0:T(8,128)S(1)} %fusion.6.after), channel_id=1, source_target_pairs={{0,8},{2,10},{4,12},{6,14},{8,0},{10,2},{12,4},{14,6},{1,9},{3,11}... | collective-permute-start | bytes 196616 | tf_op jit(solution)/shard_map/ppermute | solution.py:354
  28.1 8.7 %copy-start.10 = (f32[4,128,256]{2,1,0:T(8,128)S(1)}, f32[4,128,256]{2,1,0:T(8,128)}, u32[]{:S(2)}) copy-start(f32[4,128,256]{2,1,0:T(8,128)} %rhs.7) | copy-start | bytes 1572868
  29.6 5.2 %collective-permute-start.7 = (f32[128,128]{1,0:T(8,128)S(1)}, f32[128,128]{1,0:T(8,128)S(1)}, u32[]{:S(2)}, u32[]{:S(2)}) collective-permute-start(f32[128,128]{1,0:T(8,128)S(1)} %add.51.own), channel_id=1, source_target_pairs={{0,6},{2,4},{4,2},{6,0},{8,14},{10,12},{12,10},{14,8},{1,7},{3,5},... | collective-permute-start | bytes 196616 | tf_op jit(solution)/shard_map/ppermute | solution.py:354
  31.9 4.3 %collective-permute-start.8 = (f32[128,128]{1,0:T(8,128)S(1)}, f32[128,128]{1,0:T(8,128)S(1)}, u32[]{:S(2)}, u32[]{:S(2)}) collective-permute-start(f32[128,128]{1,0:T(8,128)S(1)} %add.51.own), channel_id=1, source_target_pairs={{0,4},{2,6},{4,0},{6,2},{8,12},{10,14},{12,8},{14,10},{1,5},{3,7},... | collective-permute-start | bytes 196616 | tf_op jit(solution)/shard_map/ppermute | solution.py:354
  32.6 4.3 %collective-permute-start.9 = (f32[128,128]{1,0:T(8,128)S(1)}, f32[128,128]{1,0:T(8,128)S(1)}, u32[]{:S(2)}, u32[]{:S(2)}) collective-permute-start(f32[128,128]{1,0:T(8,128)S(1)} %add.51.own), channel_id=1, source_target_pairs={{0,2},{2,0},{4,6},{6,4},{8,10},{10,8},{12,14},{14,12},{1,3},{3,1},... | collective-permute-start | bytes 196616 | tf_op jit(solution)/shard_map/ppermute | solution.py:354
  36.8 7.2 %copy-start = (f32[12,4,128,128]{3,2,1,0:T(8,128)S(1)}, f32[12,4,128,128]{3,2,1,0:T(8,128)}, u32[]{:S(2)}) copy-start(f32[12,4,128,128]{3,2,1,0:T(8,128)} %three.3) | copy-start | bytes 9437188
  36.8 7.2 %copy-start.2 = (f32[12,128,128]{2,1,0:T(8,128)S(1)}, f32[12,128,128]{2,1,0:T(8,128)}, u32[]{:S(2)}) copy-start(f32[12,128,128]{2,1,0:T(8,128)} %inverse.7) | copy-start | bytes 2359300
  38.4 6.4 %collective-permute-start.11 = (f32[5,128,128]{2,1,0:T(8,128)S(1)}, f32[5,128,128]{2,1,0:T(8,128)S(1)}, u32[]{:S(2)}, u32[]{:S(2)}) collective-permute-start(f32[5,128,128]{2,1,0:T(8,128)S(1)} %get-tuple-element.54.mine), channel_id=1, source_target_pairs={{0,1},{1,0},{2,3},{3,2},{4,5},{5,4},{6,7},{7,6},{8,9},{9,8},{10,11... | collective-permute-start | bytes 983048 | tf_op jit(solution)/shard_map/ppermute | solution.py:357
  38.5 9.8 %collective-permute-start.12 = (f32[128,128]{1,0:T(8,128)S(1)}, f32[128,128]{1,0:T(8,128)S(1)}, u32[]{:S(2)}, u32[]{:S(2)}) collective-permute-start(f32[128,128]{1,0:T(8,128)S(1)} %get-tuple-element.56), channel_id=1, source_target_pairs={{0,2},{1,3},{2,4},{3,5},{4,6},{5,7},{6,8},{7,9},{8,10},{9,11},{10,... | collective-permute-start | bytes 196616 | tf_op jit(solution)/shard_map/ppermute | solution.py:351
  40.5 10.2 %collective-permute-start.13 = (f32[128,128]{1,0:T(8,128)S(1)}, f32[128,128]{1,0:T(8,128)S(1)}, u32[]{:S(2)}, u32[]{:S(2)}) collective-permute-start(f32[128,128]{1,0:T(8,128)S(1)} %get-tuple-element.52.after.sep_own.own), channel_id=1, source_target_pairs={{0,8},{1,9},{2,10},{3,11},{4,12},{5,13},{6,14},{7,15},{8,0},{9,1},... | collective-permute-start | bytes 196616 | tf_op jit(solution)/shard_map/ppermute | solution.py:351
  43.5 7.2 %collective-permute-start.14 = (f32[128,128]{1,0:T(8,128)S(1)}, f32[128,128]{1,0:T(8,128)S(1)}, u32[]{:S(2)}, u32[]{:S(2)}) collective-permute-start(f32[128,128]{1,0:T(8,128)S(1)} %get-tuple-element.57), channel_id=1, source_target_pairs={{0,3},{1,2},{2,5},{3,4},{4,7},{5,6},{6,9},{7,8},{8,11},{9,10},{10,... | collective-permute-start | bytes 196616 | tf_op jit(solution)/shard_map/ppermute | solution.py:351
  43.7 8.0 %collective-permute-start.15 = (f32[128,128]{1,0:T(8,128)S(1)}, f32[128,128]{1,0:T(8,128)S(1)}, u32[]{:S(2)}, u32[]{:S(2)}) collective-permute-start(f32[128,128]{1,0:T(8,128)S(1)} %get-tuple-element.58), channel_id=1, source_target_pairs={{0,9},{1,8},{2,11},{3,10},{4,13},{5,12},{6,15},{7,14},{8,1},{9,0},... | collective-permute-start | bytes 196616 | tf_op jit(solution)/shard_map/ppermute | solution.py:351

commit v9 on v8

--- a/solution.py
+++ b/solution.py
@@ -531,7 +531,7 @@
         compiler_params=limit(16),
         cost_estimate=cost(1),
         name="leaf_operators",
-    )(leaf_upper_inverse, leaf_upper, sep_own)
+    )(leaf_upper_inverse, leaf_upper, total)
 
     leaf_part, root_sol, separator_solution_rows = pl.pallas_call(
         leaf_root_part_kernel,

time: 54.2 us -> 55.2 us (1.018)
  waiting for transfers between devices: 10.9 us -> 11.6 us
    ppermute x6, waiting for transfers between devices: 5.45 us -> 6.15 us  [shifted(): return lax.ppermute(x, ('grid', 'layer'), pairs)]
where the time goes in v9:
time: 55.2 us; the launch traced here: 54.8 us
  Pallas kernels  21 us (38%)
  starting transfers between devices  19.8 us (36%)
  waiting for transfers between devices  11.6 us (21%)
  local copies, waits for them, and re-layouts  1.38 us (2%)
  between operations  0.92 us (2%)
    ppermute x7, starting transfers between devices, crossed(): return lax.ppermute(x, 'grid', [(i, i ^ bit) for i in range(peers)])  10.5 us
    ppermute x6, starting transfers between devices, shifted(): return lax.ppermute(x, ('grid', 'layer'), pairs)  8.57 us
    ppermute x6, waiting for transfers between devices, shifted(): return lax.ppermute(x, ('grid', 'layer'), pairs)  6.15 us
    ppermute x7, waiting for transfers between devices, crossed(): return lax.ppermute(x, 'grid', [(i, i ^ bit) for i in range(peers)])  5.42 us
    pallas_call x1, Pallas kernels, per_device(): pl.pallas_call(root_terms_kernel, grid=(leaves // batch,), in_specs=[smem...  3.73 us
    pallas_call x1, Pallas kernels, per_device(): pl.pallas_call(forward_leaf_kernel, grid=(leaves // batch,), in_specs=[wh...  3.56 us
    pallas_call x1, Pallas kernels, per_device(): pl.pallas_call(leaf_root_part_kernel, grid=(leaves // batch,), in_specs=[...  3.48 us
    pallas_call x1, Pallas kernels, per_device(): pl.pallas_call(leaf_final_kernel, in_specs=[smem] * 2 + [whole()] * 8, ou...  2.09 us
  transfers between devices with their start and end apart: 16, of which 9 were waited for; matrix products, arithmetic and copies ran while one was open for 0% of the time, Pallas kernels for 24%

profile of v9, /device:TPU:6, one launch (start us, length us, event | category | flops | bytes accessed | tf_op | source)
XLA Modules:
  0.0 54.8 jit_solution(12105153333683331208)
XLA Ops:
  0.6 0.0 copy-start.1
  0.6 0.0 copy-start.3
  0.7 0.0 copy-start.4
  0.7 0.0 copy-start.7
  0.7 3.6 %leaf_forward.1 = (f32[128,256]{1,0:T(8,128)}, f32[128,256]{1,0:T(8,128)}, f32[128,256]{1,0:T(8,128)}) custom-call(s32[4,12]{1,0:T(4,128)} %bitcast.18, f32[12,128,256]{2,1,0:T(8,128)} %rhs.5, f32[12,128,128]{2,1,0:T(8,128)} %inverse.5, f32[12,4,128,128]{3,2,1,0:T(8,128)} %three.2), custom_call_target="tpu_custom_call" | custom-call | flops 4000000000 | bytes 12000000 | tf_op jit(solution)/shard_map/leaf_forward/pallas_call | solution.py:363
  4.2 2.6 %collective-permute-start = (f32[128,256]{1,0:T(8,128)}, f32[128,256]{1,0:T(8,128)S(1)}, u32[]{:S(2)}, u32[]{:S(2)}) collective-permute-start(f32[128,256]{1,0:T(8,128)} %get-tuple-element.33), channel_id=1, source_target_pairs={{0,8},{1,9},{2,10},{3,11},{4,12},{5,13},{6,14},{7,15},{8,0},{9,1},... | collective-permute-start | bytes 393224 | tf_op jit(solution)/shard_map/ppermute | solution.py:351
  6.8 0.5 collective-permute-start.1
  7.3 0.0 copy-done.1
  7.3 0.0 copy-done.4
  7.3 0.0 copy-start.5
  7.3 0.9 %copy-done.5 = f32[128,256]{1,0:T(8,128)S(1)} copy-done((f32[128,256]{1,0:T(8,128)S(1)}, f32[128,256]{1,0:T(8,128)}, u32[]{:S(2)}) %copy-start.5) | copy-done | bytes 131096
  8.3 3.7 %root_terms.1 = (f32[12,128,256]{2,1,0:T(8,128)S(1)}, f32[4,128,256]{2,1,0:T(8,128)S(1)}) custom-call(s32[4,12]{1,0:T(4,128)S(1)} %bitcast.19, f32[12,128,256]{2,1,0:T(8,128)S(1)} %copy-done.3, f32[12,128,128]{2,1,0:T(8,128)S(1)} %copy-done.4, f32[12,4,128,128]{3,2,1,0:T(8,128)S(1)} %copy-done.1, f32[12,4,128,128]{3,2,1,0:T(8,128)S(1)} %copy-done.1, ...), custom_call_target="tpu_custom_call" | custom-call | flops 3000000000 | bytes 9000000 | tf_op jit(solution)/shard_map/root_terms/pallas_call | solution.py:383
  12.0 0.0 copy-start.15
  12.0 0.0 copy-start.18
  12.0 0.3 separator_operator.1.operator
  12.3 0.1 pad_add_fusion.place
  12.4 1.0 %collective-permute-done.far = f32[128,256]{1,0:T(8,128)S(1)} collective-permute-done((f32[128,256]{1,0:T(8,128)}, f32[128,256]{1,0:T(8,128)S(1)}, u32[]{:S(2)}, u32[]{:S(2)}) %collective-permute-start) | collective-permute-done | bytes 131104 | tf_op jit(solution)/shard_map/ppermute | solution.py:351
  13.4 1.2 %collective-permute-done.1.near = f32[128,256]{1,0:T(8,128)S(1)} collective-permute-done((f32[128,256]{1,0:T(8,128)}, f32[128,256]{1,0:T(8,128)S(1)}, u32[]{:S(2)}, u32[]{:S(2)}) %collective-permute-start.1) | collective-permute-done | bytes 131104 | tf_op jit(solution)/shard_map/ppermute | solution.py:351
  14.6 0.0 copy-done.18
  14.6 0.9 %separator_forward.1 = (bf16[256,256]{1,0:T(8,128)(2,1)S(1)}, f32[4,128,128]{2,1,0:T(8,128)S(1)}, f32[4,128,128]{2,1,0:T(8,128)S(1)}) custom-call(s32[3]{0:T(128)S(1)} %bitcast.22, s32[2]{0:T(128)S(1)} %pad_add_fusion.place, f32[1,128,256]{2,1,0:T(8,128)S(1)} %copy-done.15, bf16[768,256]{1,0:T(8,128)(2,1)S(1)} %separator_operator.1.operator, ...), custom_call_target="tpu_custom_call" | custom-call | flops 2000000000 | bytes 6000000 | tf_op jit(solution)/shard_map/separator_forward/pallas_call | solution.py:412
  15.5 0.1 collective-permute-start.2
  15.6 0.0 copy-start.8
  15.6 0.0 copy-start.9
  15.6 0.0 copy-start.11
  15.6 0.0 copy-start.12
  15.6 1.0 %separator_part.1 = (f32[128,128]{1,0:T(8,128)S(1)}, f32[5,128,128]{2,1,0:T(8,128)S(1)}) custom-call(s32[3]{0:T(128)S(1)} %bitcast.23, s32[2]{0:T(128)S(1)} %pad_add_fusion.place, f32[1,128,128]{2,1,0:T(8,128)S(1)} %copy-done.16, f32[1,128,128]{2,1,0:T(8,128)S(1)} %copy-done.17, f32[1,3,128,128]{3,2,1,0:T(8,128)S(1)} %copy-done.14, ...), custom_call_target="tpu_custom_call" | custom-call | flops 700000000 | bytes 2100000 | tf_op jit(solution)/shard_map/separator_part/pallas_call | solution.py:437
  16.6 0.5 collective-permute-start.10
  17.1 0.0 collective-permute-done.2
  17.2 2.4 %collective-permute-start.3 = (f32[128,128]{1,0:T(8,128)S(1)}, f32[128,128]{1,0:T(8,128)S(1)}, u32[]{:S(2)}, u32[]{:S(2)}) collective-permute-start(f32[128,128]{1,0:T(8,128)S(1)} %get-tuple-element.63), channel_id=1, source_target_pairs={{0,6},{2,4},{4,2},{6,0},{8,14},{10,12},{12,10},{14,8},{1,7},{3,5},... | collective-permute-start | bytes 196616 | tf_op jit(solution)/shard_map/ppermute | solution.py:354
  19.6 0.0 collective-permute-start.4
  19.6 1.2 %collective-permute-start.5 = (f32[128,128]{1,0:T(8,128)S(1)}, f32[128,128]{1,0:T(8,128)S(1)}, u32[]{:S(2)}, u32[]{:S(2)}) collective-permute-start(f32[128,128]{1,0:T(8,128)S(1)} %get-tuple-element.61.after), channel_id=1, source_target_pairs={{0,2},{2,0},{4,6},{6,4},{8,10},{10,8},{12,14},{14,12},{1,3},{3,1},... | collective-permute-start | bytes 196616 | tf_op jit(solution)/shard_map/ppermute | solution.py:354
  20.8 0.0 copy-done.8
  20.8 2.0 %root_sweeps.1 = (f32[512,512]{1,0:T(8,128)S(1)}, f32[512,512]{1,0:T(8,128)S(1)}) custom-call(f32[4,128,128]{2,1,0:T(8,128)S(1)} %copy-done.11, f32[4,128,128]{2,1,0:T(8,128)S(1)} %copy-done.12, f32[512,512]{1,0:T(8,128)S(1)} %copy-done.8, f32[512,512]{1,0:T(8,128)S(1)} %copy-done.9, f32[128,128]{1,0:T(8,128)S(1)} %get-tuple-element.61.after), custom_call_target="tpu_custom_call" | custom-call | flops 2300000000 | bytes 6899999 | tf_op jit(solution)/shard_map/root_sweeps/pallas_call | solution.py:455
  22.8 0.0 collective-permute-done.3
  22.8 1.0 %collective-permute-done.4 = f32[128,128]{1,0:T(8,128)S(1)} collective-permute-done((f32[128,128]{1,0:T(8,128)S(1)}, f32[128,128]{1,0:T(8,128)S(1)}, u32[]{:S(2)}, u32[]{:S(2)}) %collective-permute-start.4) | collective-permute-done | bytes 65568 | tf_op jit(solution)/shard_map/ppermute | solution.py:354
  23.8 0.0 collective-permute-done.5
  23.9 3.3 %collective-permute-start.6 = (f32[128,128]{1,0:T(8,128)S(1)}, f32[128,128]{1,0:T(8,128)S(1)}, u32[]{:S(2)}, u32[]{:S(2)}) collective-permute-start(f32[128,128]{1,0:T(8,128)S(1)} %fusion.6.after), channel_id=1, source_target_pairs={{0,8},{2,10},{4,12},{6,14},{8,0},{10,2},{12,4},{14,6},{1,9},{3,11}... | collective-permute-start | bytes 196616 | tf_op jit(solution)/shard_map/ppermute | solution.py:354
  27.2 0.9 %root_operator.1 = (bf16[1024,1024]{1,0:T(8,128)(2,1)S(1)}, bf16[1024,512]{1,0:T(8,128)(2,1)S(1)}) custom-call(f32[512,512]{1,0:T(8,128)S(1)} %get-tuple-element.43.forward, f32[512,512]{1,0:T(8,128)S(1)} %get-tuple-element.44.backward, f32[128,128]{1,0:T(8,128)S(1)} %fusion.6.after), custom_call_target="tpu_custom_call" | custom-call | flops 1000000000 | bytes 3000000 | tf_op jit(solution)/shard_map/root_operator/pallas_call | solution.py:468
  28.1 0.0 copy-start.10
  28.1 1.5 %collective-permute-done.6 = f32[128,128]{1,0:T(8,128)S(1)} collective-permute-done((f32[128,128]{1,0:T(8,128)S(1)}, f32[128,128]{1,0:T(8,128)S(1)}, u32[]{:S(2)}, u32[]{:S(2)}) %collective-permute-start.6) | collective-permute-done | bytes 65568 | tf_op jit(solution)/shard_map/ppermute | solution.py:354
  29.6 2.3 %collective-permute-start.7 = (f32[128,128]{1,0:T(8,128)S(1)}, f32[128,128]{1,0:T(8,128)S(1)}, u32[]{:S(2)}, u32[]{:S(2)}) collective-permute-start(f32[128,128]{1,0:T(8,128)S(1)} %add.51.after.own), channel_id=1, source_target_pairs={{0,6},{2,4},{4,2},{6,0},{8,14},{10,12},{12,10},{14,8},{1,7},{3,5},... | collective-permute-start | bytes 196616 | tf_op jit(solution)/shard_map/ppermute | solution.py:354
  31.9 0.7 %collective-permute-start.8 = (f32[128,128]{1,0:T(8,128)S(1)}, f32[128,128]{1,0:T(8,128)S(1)}, u32[]{:S(2)}, u32[]{:S(2)}) collective-permute-start(f32[128,128]{1,0:T(8,128)S(1)} %add.51.after.own), channel_id=1, source_target_pairs={{0,4},{2,6},{4,0},{6,2},{8,12},{10,14},{12,8},{14,10},{1,5},{3,7},... | collective-permute-start | bytes 196616 | tf_op jit(solution)/shard_map/ppermute | solution.py:354
  32.6 0.6 %collective-permute-start.9 = (f32[128,128]{1,0:T(8,128)S(1)}, f32[128,128]{1,0:T(8,128)S(1)}, u32[]{:S(2)}, u32[]{:S(2)}) collective-permute-start(f32[128,128]{1,0:T(8,128)S(1)} %add.51.after.own), channel_id=1, source_target_pairs={{0,2},{2,0},{4,6},{6,4},{8,10},{10,8},{12,14},{14,12},{1,3},{3,1},... | collective-permute-start | bytes 196616 | tf_op jit(solution)/shard_map/ppermute | solution.py:354
  33.1 0.0 collective-permute-done.10.other.other_pack
  33.2 0.7 %separator_factors.1.backward = bf16[2,256,1024]{2,1,0:T(8,128)(2,1)S(1)} custom-call(f32[5,128,128]{2,1,0:T(8,128)S(1)} %get-tuple-element.50.pack, f32[5,128,128]{2,1,0:T(8,128)S(1)} %collective-permute-done.10.other.other_pack, bf16[1024,512]{1,0:T(8,128)(2,1)S(1)} %get-tuple-element.51.root_right), custom_call_target="tpu_custom_call" | custom-call | flops 500000000 | bytes 1500000 | tf_op jit(solution)/shard_map/separator_factors/pallas_call | solution.py:488
  33.9 0.9 %collective-permute-done.7.three = f32[128,128]{1,0:T(8,128)S(1)} collective-permute-done((f32[128,128]{1,0:T(8,128)S(1)}, f32[128,128]{1,0:T(8,128)S(1)}, u32[]{:S(2)}, u32[]{:S(2)}) %collective-permute-start.7) | collective-permute-done | bytes 65568 | tf_op jit(solution)/shard_map/ppermute | solution.py:354
  34.8 1.3 %collective-permute-done.8.two = f32[128,128]{1,0:T(8,128)S(1)} collective-permute-done((f32[128,128]{1,0:T(8,128)S(1)}, f32[128,128]{1,0:T(8,128)S(1)}, u32[]{:S(2)}, u32[]{:S(2)}) %collective-permute-start.8) | collective-permute-done | bytes 65568 | tf_op jit(solution)/shard_map/ppermute | solution.py:354
  36.1 0.7 %collective-permute-done.9.one = f32[128,128]{1,0:T(8,128)S(1)} collective-permute-done((f32[128,128]{1,0:T(8,128)S(1)}, f32[128,128]{1,0:T(8,128)S(1)}, u32[]{:S(2)}, u32[]{:S(2)}) %collective-permute-start.9) | collective-permute-done | bytes 65568 | tf_op jit(solution)/shard_map/ppermute | solution.py:354
  36.8 1.6 %root_solve.1 = (f32[5,128,128]{2,1,0:T(8,128)S(1)}, f32[128,128]{1,0:T(8,128)S(1)}, f32[128,128]{1,0:T(8,128)S(1)}, f32[128,128]{1,0:T(8,128)S(1)}, f32[128,128]{1,0:T(8,128)S(1)}) custom-call(s32[2]{0:T(128)S(1)} %pad_add_fusion.place, f32[4,128,256]{2,1,0:T(8,128)S(1)} %copy-done.10, bf16[1024,1024]{1,0:T(8,128)(2,1)S(1)} %get-tuple-element.48.operator, ...), custom_call_target="tpu_custom_call" | custom-call | flops 2000000000 | bytes 6000000 | tf_op jit(solution)/shard_map/root_solve/pallas_call | solution.py:499
  38.4 0.1 collective-permute-start.11
  38.5 0.2 copy-done
  38.7 0.2 copy-done.2
  38.9 0.8 %leaf_operators.1.operator = bf16[12,256,256]{2,1,0:T(8,128)(2,1)S(1)} custom-call(f32[12,128,128]{2,1,0:T(8,128)S(1)} %copy-done.2, f32[12,4,128,128]{3,2,1,0:T(8,128)S(1)} %copy-done, f32[128,128]{1,0:T(8,128)S(1)} %add.51.after.own), custom_call_target="tpu_custom_call" | custom-call | flops 1000000000 | bytes 3000000 | tf_op jit(solution)/shard_map/leaf_operators/pallas_call | solution.py:525
  39.8 2.0 %collective-permute-start.12 = (f32[128,128]{1,0:T(8,128)S(1)}, f32[128,128]{1,0:T(8,128)S(1)}, u32[]{:S(2)}, u32[]{:S(2)}) collective-permute-start(f32[128,128]{1,0:T(8,128)S(1)} %get-tuple-element.56), channel_id=1, source_target_pairs={{0,2},{1,3},{2,4},{3,5},{4,6},{5,7},{6,8},{7,9},{8,10},{9,11},{10,... | collective-permute-start | bytes 196616 | tf_op jit(solution)/shard_map/ppermute | solution.py:351
  41.7 3.1 %collective-permute-start.13 = (f32[128,128]{1,0:T(8,128)S(1)}, f32[128,128]{1,0:T(8,128)S(1)}, u32[]{:S(2)}, u32[]{:S(2)}) collective-permute-start(f32[128,128]{1,0:T(8,128)S(1)} %get-tuple-element.54.sep_own.own), channel_id=1, source_target_pairs={{0,8},{1,9},{2,10},{3,11},{4,12},{5,13},{6,14},{7,15},{8,0},{9,1},... | collective-permute-start | bytes 196616 | tf_op jit(solution)/shard_map/ppermute | solution.py:351
  44.8 0.0 collective-permute-start.14
  44.8 0.4 collective-permute-start.15
  45.2 0.0 collective-permute-done.11.other
  45.2 3.5 %leaf_root_part.1 = (f32[12,128,256]{2,1,0:T(8,128)S(1)}, f32[4,128,256]{2,1,0:T(8,128)}, f32[1,128,256]{2,1,0:T(8,128)}) custom-call(s32[4,12]{1,0:T(4,128)S(1)} %bitcast.20, s32[2]{0:T(128)S(1)} %pad_add_fusion.place, f32[12,4,128,128]{3,2,1,0:T(8,128)S(1)} %copy-done, f32[12,4,128,128]{3,2,1,0:T(8,128)S(1)} %copy-done, f32[12,4,128,128]{3,2,1,0:T(8,128)S(1)} %copy-done, ...), custom_call_target="tpu_custom_call" | custom-call | flops 3000000000 | bytes 9000000 | tf_op jit(solution)/shard_map/leaf_root_part/pallas_call | solution.py:536
  48.7 0.0 collective-permute-done.12.near
  48.7 3.0 %collective-permute-done.13.far = f32[128,128]{1,0:T(8,128)S(1)} collective-permute-done((f32[128,128]{1,0:T(8,128)S(1)}, f32[128,128]{1,0:T(8,128)S(1)}, u32[]{:S(2)}, u32[]{:S(2)}) %collective-permute-start.13) | collective-permute-done | bytes 65568 | tf_op jit(solution)/shard_map/ppermute | solution.py:351
  51.7 0.0 collective-permute-done.14.near_other
  51.7 1.0 %collective-permute-done.15.far_other = f32[128,128]{1,0:T(8,128)S(1)} collective-permute-done((f32[128,128]{1,0:T(8,128)S(1)}, f32[128,128]{1,0:T(8,128)S(1)}, u32[]{:S(2)}, u32[]{:S(2)}) %collective-permute-start.15) | collective-permute-done | bytes 65568 | tf_op jit(solution)/shard_map/ppermute | solution.py:351
  52.7 2.1 %leaf_backward.1 = f32[12,128,256]{2,1,0:T(8,128)} custom-call(s32[4,12]{1,0:T(4,128)S(1)} %bitcast.21, s32[2]{0:T(128)S(1)} %pad_add_fusion.place, bf16[12,256,256]{2,1,0:T(8,128)(2,1)S(1)} %leaf_operators.1.operator, f32[12,128,256]{2,1,0:T(8,128)S(1)} %get-tuple-element.55.part, f32[128,128]{1,0:T(8,128)S(1)} %get-tuple-element.54.sep_own.own, ...), custom_call_target="tpu_custom_call" | custom-call | flops 2000000000 | bytes 6000000 | tf_op jit(solution)/shard_map/leaf_backward/pallas_call | solution.py:578
  (22 shorter events, 0.1 us)
Async XLA Ops:
  0.6 6.7 %copy-start.1 = (f32[12,4,128,128]{3,2,1,0:T(8,128)S(1)}, f32[12,4,128,128]{3,2,1,0:T(8,128)}, u32[]{:S(2)}) copy-start(f32[12,4,128,128]{3,2,1,0:T(8,128)} %three.2) | copy-start | bytes 9437188
  0.6 6.7 %copy-start.3 = (f32[12,128,256]{2,1,0:T(8,128)S(1)}, f32[12,128,256]{2,1,0:T(8,128)}, u32[]{:S(2)}) copy-start(f32[12,128,256]{2,1,0:T(8,128)} %rhs.5) | copy-start | bytes 4718596
  0.7 6.7 %copy-start.4 = (f32[12,128,128]{2,1,0:T(8,128)S(1)}, f32[12,128,128]{2,1,0:T(8,128)}, u32[]{:S(2)}) copy-start(f32[12,128,128]{2,1,0:T(8,128)} %inverse.5) | copy-start | bytes 2359300
  0.7 6.7 %copy-start.7 = (s32[12,4]{0,1:T(4,128)S(1)}, s32[12,4]{0,1:T(4,128)}, u32[]{:S(2)}) copy-start(s32[12,4]{0,1:T(4,128)} %param.22) | copy-start | bytes 580
  4.2 9.2 %collective-permute-start = (f32[128,256]{1,0:T(8,128)}, f32[128,256]{1,0:T(8,128)S(1)}, u32[]{:S(2)}, u32[]{:S(2)}) collective-permute-start(f32[128,256]{1,0:T(8,128)} %get-tuple-element.33), channel_id=1, source_target_pairs={{0,8},{1,9},{2,10},{3,11},{4,12},{5,13},{6,14},{7,15},{8,0},{9,1},... | collective-permute-start | bytes 393224 | tf_op jit(solution)/shard_map/ppermute | solution.py:351
  6.8 7.8 %collective-permute-start.1 = (f32[128,256]{1,0:T(8,128)}, f32[128,256]{1,0:T(8,128)S(1)}, u32[]{:S(2)}, u32[]{:S(2)}) collective-permute-start(f32[128,256]{1,0:T(8,128)} %get-tuple-element.34), channel_id=1, source_target_pairs={{0,14},{1,15},{2,0},{3,1},{4,2},{5,3},{6,4},{7,5},{8,6},{9,7},{10,... | collective-permute-start | bytes 393224 | tf_op jit(solution)/shard_map/ppermute | solution.py:351
  7.3 0.9 %copy-start.5 = (f32[128,256]{1,0:T(8,128)S(1)}, f32[128,256]{1,0:T(8,128)}, u32[]{:S(2)}) copy-start(f32[128,256]{1,0:T(8,128)} %get-tuple-element.32.after.own) | copy-start | bytes 393220
  8.2 3.7 %copy-start.6 = (f32[128,256]{1,0:T(8,128)S(1)}, f32[128,256]{1,0:T(8,128)}, u32[]{:S(2)}) copy-start(f32[128,256]{1,0:T(8,128)} %get-tuple-element.32.after.own) | copy-start | bytes 393220
  8.2 3.8 %copy-start.13 = (f32[1,3,128,128]{3,2,1,0:T(8,128)S(1)}, f32[1,3,128,128]{3,2,1,0:T(8,128)}, u32[]{:S(2)}) copy-start(f32[1,3,128,128]{3,2,1,0:T(8,128)} %lower.2) | copy-start | bytes 589828
  8.2 3.8 %copy-start.16 = (f32[1,128,128]{2,1,0:T(8,128)S(1)}, f32[1,128,128]{2,1,0:T(8,128)}, u32[]{:S(2)}) copy-start(f32[1,128,128]{2,1,0:T(8,128)} %lower_inverse.5) | copy-start | bytes 196612
  12.0 2.6 %copy-start.15 = (f32[1,128,256]{2,1,0:T(8,128)S(1)}, f32[1,128,256]{2,1,0:T(8,128)}, u32[]{:S(2)}) copy-start(f32[1,128,256]{2,1,0:T(8,128)} %rhs.6) | copy-start | bytes 393220
  12.0 2.6 %copy-start.18 = (s32[1,3]{1,0:T(1,128)S(1)}, s32[1,3]{1,0:T(1,128)}, u32[]{:S(2)}) copy-start(s32[1,3]{1,0:T(1,128)} %param.28) | copy-start | bytes 40
  14.6 1.0 %copy-start.14 = (f32[1,3,128,128]{3,2,1,0:T(8,128)S(1)}, f32[1,3,128,128]{3,2,1,0:T(8,128)}, u32[]{:S(2)}) copy-start(f32[1,3,128,128]{3,2,1,0:T(8,128)} %upper.3) | copy-start | bytes 589828
  14.6 1.0 %copy-start.17 = (f32[1,128,128]{2,1,0:T(8,128)S(1)}, f32[1,128,128]{2,1,0:T(8,128)}, u32[]{:S(2)}) copy-start(f32[1,128,128]{2,1,0:T(8,128)} %upper_inverse.3) | copy-start | bytes 196612
  15.5 1.7 %collective-permute-start.2 = (f32[4,128,128]{2,1,0:T(8,128)S(1)}, f32[4,128,128]{2,1,0:T(8,128)S(1)}, u32[]{:S(2)}, u32[]{:S(2)}) collective-permute-start(f32[4,128,128]{2,1,0:T(8,128)S(1)} %get-tuple-element.37), channel_id=1, source_target_pairs={{0,1},{1,0},{2,3},{3,2},{4,5},{5,4},{6,7},{7,6},{8,9},{9,8},{10,11... | collective-permute-start | bytes 786440 | tf_op jit(solution)/shard_map/ppermute | solution.py:357
  15.6 5.2 %copy-start.8 = (f32[512,512]{1,0:T(8,128)S(1)}, f32[512,512]{1,0:T(8,128)}, u32[]{:S(2)}) copy-start(f32[512,512]{1,0:T(8,128)} %lower.3) | copy-start | bytes 3145732
  15.6 5.2 %copy-start.9 = (f32[512,512]{1,0:T(8,128)S(1)}, f32[512,512]{1,0:T(8,128)}, u32[]{:S(2)}) copy-start(f32[512,512]{1,0:T(8,128)} %upper.2) | copy-start | bytes 3145732
  15.6 5.2 %copy-start.11 = (f32[4,128,128]{2,1,0:T(8,128)S(1)}, f32[4,128,128]{2,1,0:T(8,128)}, u32[]{:S(2)}) copy-start(f32[4,128,128]{2,1,0:T(8,128)} %lower_inverse.4) | copy-start | bytes 786436
  15.6 5.2 %copy-start.12 = (f32[4,128,128]{2,1,0:T(8,128)S(1)}, f32[4,128,128]{2,1,0:T(8,128)}, u32[]{:S(2)}) copy-start(f32[4,128,128]{2,1,0:T(8,128)} %upper_inverse.2) | copy-start | bytes 786436
  16.6 16.6 %collective-permute-start.10 = (f32[5,128,128]{2,1,0:T(8,128)S(1)}, f32[5,128,128]{2,1,0:T(8,128)S(1)}, u32[]{:S(2)}, u32[]{:S(2)}) collective-permute-start(f32[5,128,128]{2,1,0:T(8,128)S(1)} %get-tuple-element.50.pack), channel_id=1, source_target_pairs={{0,1},{1,0},{2,3},{3,2},{4,5},{5,4},{6,7},{7,6},{8,9},{9,8},{10,11... | collective-permute-start | bytes 983048 | tf_op jit(solution)/shard_map/ppermute | solution.py:357
  17.2 5.7 %collective-permute-start.3 = (f32[128,128]{1,0:T(8,128)S(1)}, f32[128,128]{1,0:T(8,128)S(1)}, u32[]{:S(2)}, u32[]{:S(2)}) collective-permute-start(f32[128,128]{1,0:T(8,128)S(1)} %get-tuple-element.63), channel_id=1, source_target_pairs={{0,6},{2,4},{4,2},{6,0},{8,14},{10,12},{12,10},{14,8},{1,7},{3,5},... | collective-permute-start | bytes 196616 | tf_op jit(solution)/shard_map/ppermute | solution.py:354
  19.6 4.3 %collective-permute-start.4 = (f32[128,128]{1,0:T(8,128)S(1)}, f32[128,128]{1,0:T(8,128)S(1)}, u32[]{:S(2)}, u32[]{:S(2)}) collective-permute-start(f32[128,128]{1,0:T(8,128)S(1)} %get-tuple-element.62), channel_id=1, source_target_pairs={{0,4},{2,6},{4,0},{6,2},{8,12},{10,14},{12,8},{14,10},{1,5},{3,7},... | collective-permute-start | bytes 196616 | tf_op jit(solution)/shard_map/ppermute | solution.py:354
  19.6 4.3 %collective-permute-start.5 = (f32[128,128]{1,0:T(8,128)S(1)}, f32[128,128]{1,0:T(8,128)S(1)}, u32[]{:S(2)}, u32[]{:S(2)}) collective-permute-start(f32[128,128]{1,0:T(8,128)S(1)} %get-tuple-element.61.after), channel_id=1, source_target_pairs={{0,2},{2,0},{4,6},{6,4},{8,10},{10,8},{12,14},{14,12},{1,3},{3,1},... | collective-permute-start | bytes 196616 | tf_op jit(solution)/shard_map/ppermute | solution.py:354
  23.9 5.7 %collective-permute-start.6 = (f32[128,128]{1,0:T(8,128)S(1)}, f32[128,128]{1,0:T(8,128)S(1)}, u32[]{:S(2)}, u32[]{:S(2)}) collective-permute-start(f32[128,128]{1,0:T(8,128)S(1)} %fusion.6.after), channel_id=1, source_target_pairs={{0,8},{2,10},{4,12},{6,14},{8,0},{10,2},{12,4},{14,6},{1,9},{3,11}... | collective-permute-start | bytes 196616 | tf_op jit(solution)/shard_map/ppermute | solution.py:354
  28.1 8.7 %copy-start.10 = (f32[4,128,256]{2,1,0:T(8,128)S(1)}, f32[4,128,256]{2,1,0:T(8,128)}, u32[]{:S(2)}) copy-start(f32[4,128,256]{2,1,0:T(8,128)} %rhs.7) | copy-start | bytes 1572868
  29.6 5.2 %collective-permute-start.7 = (f32[128,128]{1,0:T(8,128)S(1)}, f32[128,128]{1,0:T(8,128)S(1)}, u32[]{:S(2)}, u32[]{:S(2)}) collective-permute-start(f32[128,128]{1,0:T(8,128)S(1)} %add.51.after.own), channel_id=1, source_target_pairs={{0,6},{2,4},{4,2},{6,0},{8,14},{10,12},{12,10},{14,8},{1,7},{3,5},... | collective-permute-start | bytes 196616 | tf_op jit(solution)/shard_map/ppermute | solution.py:354
  31.9 4.3 %collective-permute-start.8 = (f32[128,128]{1,0:T(8,128)S(1)}, f32[128,128]{1,0:T(8,128)S(1)}, u32[]{:S(2)}, u32[]{:S(2)}) collective-permute-start(f32[128,128]{1,0:T(8,128)S(1)} %add.51.after.own), channel_id=1, source_target_pairs={{0,4},{2,6},{4,0},{6,2},{8,12},{10,14},{12,8},{14,10},{1,5},{3,7},... | collective-permute-start | bytes 196616 | tf_op jit(solution)/shard_map/ppermute | solution.py:354
  32.6 4.3 %collective-permute-start.9 = (f32[128,128]{1,0:T(8,128)S(1)}, f32[128,128]{1,0:T(8,128)S(1)}, u32[]{:S(2)}, u32[]{:S(2)}) collective-permute-start(f32[128,128]{1,0:T(8,128)S(1)} %add.51.after.own), channel_id=1, source_target_pairs={{0,2},{2,0},{4,6},{6,4},{8,10},{10,8},{12,14},{14,12},{1,3},{3,1},... | collective-permute-start | bytes 196616 | tf_op jit(solution)/shard_map/ppermute | solution.py:354
  36.8 1.9 %copy-start = (f32[12,4,128,128]{3,2,1,0:T(8,128)S(1)}, f32[12,4,128,128]{3,2,1,0:T(8,128)}, u32[]{:S(2)}) copy-start(f32[12,4,128,128]{3,2,1,0:T(8,128)} %three.3) | copy-start | bytes 9437188
  36.8 2.1 %copy-start.2 = (f32[12,128,128]{2,1,0:T(8,128)S(1)}, f32[12,128,128]{2,1,0:T(8,128)}, u32[]{:S(2)}) copy-start(f32[12,128,128]{2,1,0:T(8,128)} %inverse.7) | copy-start | bytes 2359300
  38.4 6.8 %collective-permute-start.11 = (f32[5,128,128]{2,1,0:T(8,128)S(1)}, f32[5,128,128]{2,1,0:T(8,128)S(1)}, u32[]{:S(2)}, u32[]{:S(2)}) collective-permute-start(f32[5,128,128]{2,1,0:T(8,128)S(1)} %get-tuple-element.53.mine), channel_id=1, source_target_pairs={{0,1},{1,0},{2,3},{3,2},{4,5},{5,4},{6,7},{7,6},{8,9},{9,8},{10,11... | collective-permute-start | bytes 983048 | tf_op jit(solution)/shard_map/ppermute | solution.py:357
  39.8 9.0 %collective-permute-start.12 = (f32[128,128]{1,0:T(8,128)S(1)}, f32[128,128]{1,0:T(8,128)S(1)}, u32[]{:S(2)}, u32[]{:S(2)}) collective-permute-start(f32[128,128]{1,0:T(8,128)S(1)} %get-tuple-element.56), channel_id=1, source_target_pairs={{0,2},{1,3},{2,4},{3,5},{4,6},{5,7},{6,8},{7,9},{8,10},{9,11},{10,... | collective-permute-start | bytes 196616 | tf_op jit(solution)/shard_map/ppermute | solution.py:351
  41.7 10.0 %collective-permute-start.13 = (f32[128,128]{1,0:T(8,128)S(1)}, f32[128,128]{1,0:T(8,128)S(1)}, u32[]{:S(2)}, u32[]{:S(2)}) collective-permute-start(f32[128,128]{1,0:T(8,128)S(1)} %get-tuple-element.54.sep_own.own), channel_id=1, source_target_pairs={{0,8},{1,9},{2,10},{3,11},{4,12},{5,13},{6,14},{7,15},{8,0},{9,1},... | collective-permute-start | bytes 196616 | tf_op jit(solution)/shard_map/ppermute | solution.py:351
  44.8 6.9 %collective-permute-start.14 = (f32[128,128]{1,0:T(8,128)S(1)}, f32[128,128]{1,0:T(8,128)S(1)}, u32[]{:S(2)}, u32[]{:S(2)}) collective-permute-start(f32[128,128]{1,0:T(8,128)S(1)} %get-tuple-element.57), channel_id=1, source_target_pairs={{0,3},{1,2},{2,5},{3,4},{4,7},{5,6},{6,9},{7,8},{8,11},{9,10},{10,... | collective-permute-start | bytes 196616 | tf_op jit(solution)/shard_map/ppermute | solution.py:351
  44.8 7.9 %collective-permute-start.15 = (f32[128,128]{1,0:T(8,128)S(1)}, f32[128,128]{1,0:T(8,128)S(1)}, u32[]{:S(2)}, u32[]{:S(2)}) collective-permute-start(f32[128,128]{1,0:T(8,128)S(1)} %get-tuple-element.58), channel_id=1, source_target_pairs={{0,9},{1,8},{2,11},{3,10},{4,13},{5,12},{6,15},{7,14},{8,1},{9,0},... | collective-permute-start | bytes 196616 | tf_op jit(solution)/shard_map/ppermute | solution.py:351
